TPU v7x, 512 devices: a whole 4x8x8 slice. The times are simulated.
512 devices in a mesh: grp: 4 (over x), ado: 128 (over z, y, core).
Axes of the slice: x: 4, y: 8, z: 8, core: 2. Of those that a mesh axis runs over, the one named last changes fastest.
Arguments:
- states: bfloat16 [4, 128, 128, 64, 128], P('grp', 'ado'), may hold values from -6 to 6
- send_slot: int32 [4, 128, 128, 3], P('grp', 'ado'), may hold values from -1 to 127, as said below
- window_tier_states: bfloat16 [2048, 64, 128], P('ado', 'grp'), may hold values from -6 to 6
- modes_tri: int32 [2048, 3], P('ado'), may hold values from 0 to 127, as said below
- use_up: int32 [2048, 128], P('ado', 'grp'), may hold values from 0 to 383, as said below
- use_down: int32 [2048, 3], P('ado'), may hold values from 0 to 383, as said below
- hamiltonian: bfloat16 [64, 64], replicated, may hold values from -4 to 4, as said below
- coupling: bfloat16 [128, 64, 64], P('grp'), may hold values from -1 to 1, as said below
- coup_re: float32 [128], P('grp'), may hold values from 1 to 4
- coup_im: float32 [128], P('grp'), may hold values from -6 to 6
- decay_rate: float32 [128], replicated, may hold values from 0.1 to 2
Outputs:
- increment: float32 [2048, 64, 128], P('ado', 'grp')
Inputs may be any that keep to these rules, and one draw needn't show every extreme that they name: send_slot[g, j, i, c] is a slot of the stored states of the device (g, j); -1 marks an empty place. For each sending device (g, j) and receiving ado index i the live places come first, 1 to 3 of them; for every receiving device some owner fills all 3. `modes_tri`: each row lists a tier-3 multi-index in rising order, a mode repeated as often as it is occupied. use_up[w, k] names a live place, and every live place received by a device is named by some entry of use_up for that device. use_down[w, t] names a live place of the device of grp index modes_tri[w, t] // 32. `hamiltonian`: Symmetric. `coupling`: each mode's matrix is symmetric.
All inputs are finite; a program needn't handle non-finite values.
Results may differ from a plain program's by a relative error of at most 0.0003.
Values may be sent and summed in bfloat16 or wider, within the bound.
No kernel may reach another device: no remote copies, remote signals or barrier semaphores. Data moves between devices by JAX's collectives and lax.ppermute only.
A program may use at most 64 MiB of HBM per device.

v0:
```python
import jax
import jax.numpy as jnp
from jax import lax
from jax.sharding import PartitionSpec as P

STEP_WEIGHT = 0.5


def rotate(parts, width):
    return jnp.concatenate([parts[..., width:], -parts[..., :width]], axis=-1)


def doubled(matrices):
    empty = jnp.zeros_like(matrices)
    upper_half = jnp.concatenate([matrices, empty], axis=-1)
    lower_half = jnp.concatenate([empty, matrices], axis=-1)
    return jnp.concatenate([upper_half, lower_half], axis=-2)


def on_device(
    states,
    send_slot,
    window_tier_states,
    modes_tri,
    use_up,
    use_down,
    hamiltonian,
    coupling,
    coup_re,
    coup_im,
    decay_rate,
):
    width = hamiltonian.shape[0]
    windows = window_tier_states.shape[0]
    share = window_tier_states.shape[1]
    modes_present = coupling.shape[0]
    group = lax.axis_index("grp")
    store = states[0, 0]
    slots = send_slot[0, 0]
    picked = jnp.take(store, jnp.maximum(slots, 0), axis=0)
    picked = jnp.where((slots >= 0)[:, :, None, None], picked, jnp.zeros((), picked.dtype))
    received = lax.all_to_all(picked, "ado", split_axis=0, concat_axis=0, tiled=True)
    flat = received.reshape(-1, width, 2 * width)
    ham_wide = doubled(hamiltonian)
    maps_wide = doubled(coupling)
    right_part = jnp.einsum(
        "wab,bc->wac", window_tier_states, ham_wide, preferred_element_type=jnp.float32
    )
    every_mode = jnp.arange(decay_rate.shape[0], dtype=jnp.int32)
    hits = modes_tri[:, :, None] == every_mode
    damping = jnp.sum(jnp.where(hits, decay_rate, 0.0), axis=(1, 2))
    block = min(8, modes_present)
    upper = jnp.zeros((windows, width, 2 * width), jnp.float32)
    for start in range(0, modes_present, block):
        places = use_up[:, start : start + block]
        pulled = jnp.take(flat, places, axis=0)
        maps = coupling[start : start + block]
        wide = maps_wide[start : start + block]
        left = jnp.einsum("mab,wmbc->wac", maps, pulled, preferred_element_type=jnp.float32)
        right = jnp.einsum("wmab,mbc->wac", pulled, wide, preferred_element_type=jnp.float32)
        upper = upper + left - right
    lowered = modes_tri - group * modes_present
    mine = (lowered >= 0) & (lowered < modes_present)
    index_here = jnp.clip(lowered, 0, modes_present - 1)
    pick_local = index_here[:, :, None] == jnp.arange(modes_present, dtype=jnp.int32)
    real_coef = jnp.where(mine, jnp.sum(jnp.where(pick_local, coup_re, 0.0), axis=2), 0.0)
    imag_coef = jnp.where(mine, jnp.sum(jnp.where(pick_local, coup_im, 0.0), axis=2), 0.0)
    lower_states = jnp.take(flat, use_down, axis=0)
    lower_tier_lookup = jnp.take(coupling, index_here, axis=0)
    lower_wide = jnp.take(maps_wide, index_here, axis=0)
    left_factor = jnp.einsum(
        "wtab,wtbc->wtac", lower_tier_lookup, lower_states, preferred_element_type=jnp.float32
    )
    right_d = jnp.einsum(
        "wtab,wtbc->wtac", lower_states, lower_wide, preferred_element_type=jnp.float32
    )
    minus = left_factor - right_d
    plus = left_factor + right_d
    real_b = real_coef[:, :, None, None]
    imag_b = imag_coef[:, :, None, None]
    dreal = jnp.sum(real_b * minus[..., :width] - imag_b * plus[..., width:], axis=1)
    dimag = jnp.sum(real_b * minus[..., width:] + imag_b * plus[..., :width], axis=1)
    partial_value = jnp.concatenate(
        [upper[..., width:] + dimag, -(upper[..., :width] + dreal)], axis=-1
    )
    whole = lax.all_gather(window_tier_states, "grp", axis=1, tiled=True)
    head_rows = lax.dynamic_slice_in_dim(hamiltonian, group * share, share, 0)
    left_h = jnp.einsum("ab,wbc->wac", head_rows, whole, preferred_element_type=jnp.float32)
    summed = lax.psum_scatter(partial_value, "grp", scatter_dimension=1, tiled=True)
    total = summed + rotate(left_h - right_part, width)
    total = total - damping[:, None, None] * window_tier_states.astype(jnp.float32)
    return STEP_WEIGHT * total


def solution(mesh):
    in_specs = (
        P("grp", "ado", None, None, None),
        P("grp", "ado", None, None),
        P("ado", "grp", None),
        P("ado", None),
        P("ado", "grp"),
        P("ado", None),
        P(),
        P("grp", None, None),
        P("grp"),
        P("grp"),
        P(),
    )
    out_specs = P("ado", "grp", None)
    return jax.shard_map(
        on_device, mesh=mesh, in_specs=in_specs, out_specs=out_specs, check_vma=False
    )
```

profile of v0, /device:TPU:1, one launch (start us, length us, event | category | flops | bytes accessed | tf_op | source)
XLA Modules:
  0.0 294.1 jit_solution(17896489941185772080)
XLA Ops:
  6.5 0.8 broadcast_compare_fusion.1
  7.4 0.7 broadcast_maximum_fusion
  8.1 0.1 copy.53
  8.2 0.1 copy.54
  8.3 0.1 copy.37
  8.4 0.2 reshape.87
  8.7 13.3 %gather_fusion = bf16[384,64,128]{2,1,0:T(8,128)(2,1)} fusion(bf16[128,64,128]{2,1,0:T(8,128)(2,1)S(1)} %bitcast.98, s32[1024]{0:T(1024)S(1)} %pad_clamp_fusion.6), kind=kCustom, calls=%fused_computation.4 | custom fusion | bytes 12584448 | tf_op jit(solution)/shard_map/jit(_take)/gather | solution.py:40
  22.0 6.9 %select_select_fusion = bf16[128,3,64,128]{3,2,1,0:T(8,128)(2,1)} fusion(bf16[128,3,64,128]{3,2,1,0:T(8,128)(2,1)} %bitcast.99, pred[128,3]{1,0:T(8,128)(4,1)S(1)} %bitcast.113, pred[128,3]{1,0:T(8,128)(4,1)S(1)} %bitcast.112), kind=kLoop, calls=%fused_computation.8 | loop fusion | flops 6291456 | bytes 12583680 | tf_op jit(solution)/shard_map/jit(_where)/select_n | solution.py:41
  28.9 19.0 %all-to-all-start = ((bf16[128,3,64,128]{3,2,1,0:T(8,128)(2,1)}), bf16[128,3,64,128]{3,2,1,0:T(8,128)(2,1)}, u32[]{:S(2)}, u32[]{:S(2)}) async-start(bf16[128,3,64,128]{3,2,1,0:T(8,128)(2,1)} %select_select_fusion), calls=%async_computation | async-start | bytes 12582912 | tf_op jit(solution)/shard_map/all_to_all | solution.py:42
  47.9 0.2 reduce-scatter.2.cloned.1.call-start
  48.2 0.1 reshape.137
  48.8 1.6 gather_fusion.1
  50.4 1.6 fusion.33
  52.0 2.0 gather_fusion.3
  54.2 0.1 copy.39
  54.3 0.1 copy.41
  54.4 0.2 select_reduce_fusion.2
  54.9 143.6 %all-to-all-done = bf16[128,3,64,128]{3,2,1,0:T(8,128)(2,1)} async-done(((bf16[128,3,64,128]{3,2,1,0:T(8,128)(2,1)}), bf16[128,3,64,128]{3,2,1,0:T(8,128)(2,1)}, u32[]{:S(2)}, u32[]{:S(2)}) %all-to-all-start) | async-done | bytes 6291488 | tf_op jit(solution)/shard_map/all_to_all | solution.py:42
  198.5 5.0 %gather_fusion.5 = bf16[128,64,128]{2,1,0:T(8,128)(2,1)} fusion(bf16[384,64,128]{2,1,0:T(8,128)(2,1)} %bitcast.4, s32[1024]{0:T(1024)S(1)} %pad_clamp_fusion.4), kind=kCustom, calls=%fused_computation.1.clone | custom fusion | bytes 4194816 | tf_op jit(solution)/shard_map/jit(_take)/gather | solution.py:56
  203.4 3.3 %fusion.22 = f32[16,64,128]{2,1,0:T(8,128)} fusion(bf16[16,8,64,128]{3,2,1,0:T(8,128)(2,1)} %bitcast.108, pred[16,8]{1,0:T(8,128)(4,1)S(1)} %get-tuple-element.22, bf16[32,128,128]{2,1,0:T(8,128)(2,1)S(1)} %fusion.33), kind=kOutput, calls=%fused_computation.41 | convolution fusion | flops 269484032 | bytes 2885632 | tf_op jit(solution)/shard_map/wmab,mbc->wac/dot_general | solution.py:60
  206.7 2.3 fusion.21
  209.1 5.0 %gather_fusion.7 = bf16[128,64,128]{2,1,0:T(8,128)(2,1)} fusion(bf16[384,64,128]{2,1,0:T(8,128)(2,1)} %bitcast.4, s32[1024]{0:T(1024)S(1)} %pad_clamp_fusion.2), kind=kCustom, calls=%fused_computation.3.clone | custom fusion | bytes 4194816 | tf_op jit(solution)/shard_map/jit(_take)/gather | solution.py:56
  214.0 3.3 %fusion.18 = f32[16,64,128]{2,1,0:T(8,128)} fusion(bf16[16,8,64,128]{3,2,1,0:T(8,128)(2,1)} %bitcast.110, pred[16,8]{1,0:T(8,128)(4,1)S(1)} %get-tuple-element.21, bf16[32,128,128]{2,1,0:T(8,128)(2,1)S(1)} %fusion.33), kind=kOutput, calls=%fused_computation.37 | convolution fusion | flops 269484032 | bytes 2885632 | tf_op jit(solution)/shard_map/wmab,mbc->wac/dot_general | solution.py:60
  217.3 2.4 fusion.17
  219.7 5.0 %gather_fusion.4 = bf16[128,64,128]{2,1,0:T(8,128)(2,1)} fusion(bf16[384,64,128]{2,1,0:T(8,128)(2,1)} %bitcast.4, s32[1024]{0:T(1024)S(1)} %pad_clamp_fusion.5), kind=kCustom, calls=%fused_computation.clone | custom fusion | bytes 4194816 | tf_op jit(solution)/shard_map/jit(_take)/gather | solution.py:56
  224.7 5.0 %gather_fusion.6 = bf16[128,64,128]{2,1,0:T(8,128)(2,1)} fusion(bf16[384,64,128]{2,1,0:T(8,128)(2,1)} %bitcast.4, s32[1024]{0:T(1024)S(1)} %pad_clamp_fusion.3), kind=kCustom, calls=%fused_computation.2.clone | custom fusion | bytes 4194816 | tf_op jit(solution)/shard_map/jit(_take)/gather | solution.py:56
  229.7 3.5 %gather_fusion.2 = bf16[48,64,128]{2,1,0:T(8,128)(2,1)S(1)} fusion(bf16[384,64,128]{2,1,0:T(8,128)(2,1)} %bitcast.4, s32[1024]{0:T(1024)S(1)} %pad_clamp_fusion), kind=kCustom, calls=%fused_computation.6 | custom fusion | bytes 1573056 | tf_op jit(solution)/shard_map/jit(_take)/gather | solution.py:68
  233.2 2.4 fusion.23
  235.6 0.6 fusion.14
  236.2 0.5 copy-done.6
  236.7 0.5 fusion.86
  237.2 0.8 copy-done.2
  237.9 0.7 copy-done.8
  238.7 0.2 copy-done.22
  238.9 0.8 fusion.27
  239.6 0.8 copy-done.7
  240.5 0.7 fusion.31
  241.1 0.8 fusion.30
  241.9 1.1 fusion.13
  243.1 0.2 slice_add_fusion.1
  243.3 1.0 pad_maximum_fusion
  244.4 9.7 %all_gather.3 = bf16[16,64,128]{2,1,0:T(8,128)(2,1)S(1)} all-gather(bf16[16,16,128]{2,1,0:T(8,128)(2,1)S(1)} %copy-done.12), channel_id=1, replica_groups=mesh['grp'=4,'ado'=128] {'grp'}, dimensions={1}, use_global_device_ids=true | all-gather | bytes 327680 | tf_op jit(solution)/shard_map/all_gather | solution.py:86
  254.1 0.2 select_reduce_fusion
  254.3 0.2 convolution_bitcast_fusion.1
  254.5 0.2 fusion.32
  254.6 0.1 fusion.87
  254.8 30.8 %reduce-scatter.2.cloned.1.call-done = f32[16,16,128]{2,1,0:T(8,128)} async-done(((f32[16,64,128]{2,1,0:T(8,128)}), f32[16,16,128]{2,1,0:T(8,128)}) %reduce-scatter.2.cloned.1.call-update) | async-done | bytes 131088 | tf_op jit(solution)/shard_map/reduce_scatter | solution.py:89
  285.5 1.7 fusion.51
  (66 shorter events, 1.2 us)
Async XLA Ops:
  6.5 2.1 copy-start
  28.9 19.2 %copy-start.11 = (s32[16,32]{1,0:T(8,128)S(1)}, s32[16,32]{1,0:T(8,128)}, u32[]{:S(2)}) copy-start(s32[16,32]{1,0:T(8,128)} %param.17) | copy-start | bytes 6148
  28.9 19.7 %copy-start.13 = (s32[16,3]{0,1:T(4,128)S(1)}, s32[16,3]{0,1:T(4,128)}, u32[]{:S(2)}) copy-start(s32[16,3]{0,1:T(4,128)} %param.16) | copy-start | bytes 580
  28.9 19.9 %copy-start.4 = (bf16[32,64,64]{2,1,0:T(8,128)(2,1)S(1)}, bf16[32,64,64]{2,1,0:T(8,128)(2,1)}, u32[]{:S(2)}) copy-start(bf16[32,64,64]{2,1,0:T(8,128)(2,1)} %param.20) | copy-start | bytes 786436
  28.9 169.5 %all-to-all-start = ((bf16[128,3,64,128]{3,2,1,0:T(8,128)(2,1)}), bf16[128,3,64,128]{3,2,1,0:T(8,128)(2,1)}, u32[]{:S(2)}, u32[]{:S(2)}) async-start(bf16[128,3,64,128]{3,2,1,0:T(8,128)(2,1)} %select_select_fusion), calls=%async_computation | async-start | bytes 12582912 | tf_op jit(solution)/shard_map/all_to_all | solution.py:42
  47.9 237.6 %reduce-scatter.2.cloned.1.call-start = ((), (), s32[]{:S(2)}) async-start(), calls=%async_computation.2 | async-start | bytes 655360 | tf_op jit(solution)/shard_map/reduce_scatter | solution.py:89
  50.4 3.6 %copy-start.14 = (s32[16,3]{0,1:T(4,128)S(1)}, s32[16,3]{0,1:T(4,128)}, u32[]{:S(2)}) copy-start(s32[16,3]{0,1:T(4,128)} %param.18) | copy-start | bytes 580
  50.4 4.0 %copy-start.16 = (f32[32]{0:T(128)S(1)}, f32[32]{0:T(128)}, u32[]{:S(2)}) copy-start(f32[32]{0:T(128)} %param.21) | copy-start | bytes 388
  50.4 4.0 %copy-start.17 = (f32[32]{0:T(128)S(1)}, f32[32]{0:T(128)}, u32[]{:S(2)}) copy-start(f32[32]{0:T(128)} %param.22) | copy-start | bytes 388
  52.0 162.0 %copy-start.1 = (bf16[32,128,128]{2,1,0:T(8,128)(2,1)}, bf16[32,128,128]{2,1,0:T(8,128)(2,1)S(1)}, u32[]{:S(2)}) copy-start(bf16[32,128,128]{2,1,0:T(8,128)(2,1)S(1)} %fusion.33) | copy-start | bytes 3145732
  203.4 3.3 %copy-start.9 = (bf16[128,64,128]{2,1,0:T(8,128)(2,1)S(1)}, bf16[128,64,128]{2,1,0:T(8,128)(2,1)}, u32[]{:S(2)}) copy-start(bf16[128,64,128]{2,1,0:T(8,128)(2,1)} %gather_fusion.5) | copy-start | bytes 6291460
  214.0 3.3 %copy-start.10 = (bf16[128,64,128]{2,1,0:T(8,128)(2,1)S(1)}, bf16[128,64,128]{2,1,0:T(8,128)(2,1)}, u32[]{:S(2)}) copy-start(bf16[128,64,128]{2,1,0:T(8,128)(2,1)} %gather_fusion.7) | copy-start | bytes 6291460
  224.7 8.5 %copy-start.5 = (bf16[32,64,64]{2,1,0:T(8,128)(2,1)S(1)}, bf16[32,64,64]{2,1,0:T(8,128)(2,1)}, u32[]{:S(2)}) copy-start(bf16[32,64,64]{2,1,0:T(8,128)(2,1)} %param.20) | copy-start | bytes 786436
  233.2 2.4 copy-start.3
  235.6 1.1 copy-start.6
  236.7 1.2 copy-start.2
  236.7 1.9 copy-start.8
  236.7 2.0 copy-start.21
  236.7 2.1 copy-start.22
  238.9 1.6 copy-start.7
  239.6 1.5 copy-start.19
  239.6 1.5 copy-start.20
  243.1 1.3 copy-start.12
  243.1 11.0 %copy-start.18 = (f32[128]{0:T(128)S(1)}, f32[128]{0:T(128)}, u32[]{:S(2)}) copy-start(f32[128]{0:T(128)} %param.23) | copy-start | bytes 1540
  243.1 11.2 %copy-start.15 = (bf16[64,64]{1,0:T(8,128)(2,1)S(1)}, bf16[64,64]{1,0:T(8,128)(2,1)}, u32[]{:S(2)}) copy-start(bf16[64,64]{1,0:T(8,128)(2,1)} %param.19) | copy-start | bytes 24580
Sparse Core Ops, SparseCore 0:
  244.5 41.0 reduce-scatter.1
where the time goes:
time: 295 us; the launch traced here: 294 us
  waiting for transfers between devices  174 us (59%)
  local copies, waits for them, and re-layouts  44.9 us (15%)
  starting transfers between devices  19.2 us (7%)
  matrix products  17.3 us (6%)
  other arithmetic  14.8 us (5%)
  between operations  13.8 us (5%)
  blocking collectives  9.71 us (3%)
    all_to_all x1, waiting for transfers between devices, on_device(): lax.all_to_all(picked, 'ado', split_axis=0, concat_axis=0, tiled=True)  144 us
    reduce_scatter x1, waiting for transfers between devices, on_device(): lax.psum_scatter(partial_value, 'grp', scatter_dimension=1, tiled=True)  30.8 us
    gather x4, local copies, waits for them, and re-layouts, on_device(): pulled = jnp.take(flat, places, axis=0)  19.9 us
    all_to_all x1, starting transfers between devices, on_device(): lax.all_to_all(picked, 'ado', split_axis=0, concat_axis=0, tiled=True)  19 us
    gather x1, local copies, waits for them, and re-layouts, on_device(): picked = jnp.take(store, jnp.maximum(slots, 0), axis=0)  13.3 us
    all_gather x1, blocking collectives, on_device(): whole = lax.all_gather(window_tier_states, 'grp', axis=1, tiled=True)  9.71 us
    dot_general x4, matrix products, on_device(): jnp.einsum('wmab,mbc->wac', pulled, wide, preferred_element_type=jnp.floa...  8.13 us
    dot_general x4, matrix products, on_device(): jnp.einsum('mab,wmbc->wac', maps, pulled, preferred_element_type=jnp.floa...  7.73 us
  transfers between devices with their start and end apart: 2, of which 2 were waited for; matrix products, arithmetic and copies ran while one was open for 2% of the time, Pallas kernels for 0%

commit v1 on v0

v1 whole, which is shorter than its diff:
```python
import jax
import jax.numpy as jnp
from jax import lax
from jax.experimental import pallas as pl
from jax.experimental.pallas import tpu as pltpu
from jax.sharding import PartitionSpec as P

STEP_WEIGHT = 0.5
F32 = jnp.float32
BF16 = jnp.bfloat16
VMEM = pl.BlockSpec(memory_space=pltpu.VMEM)
SMEM = pl.BlockSpec(memory_space=pltpu.SMEM)


def doubled(matrices):
    empty = jnp.zeros_like(matrices)
    upper_half = jnp.concatenate([matrices, empty], axis=-1)
    lower_half = jnp.concatenate([empty, matrices], axis=-1)
    return jnp.concatenate([upper_half, lower_half], axis=-2)


def rotate(parts):
    width = parts.shape[-1] // 2
    return jnp.concatenate([parts[..., width:], -parts[..., :width]], axis=-1)


def pick_kernel(slot_ref, store_ref, out_ref):
    base = pl.program_id(0) * out_ref.shape[0]
    for row in range(out_ref.shape[0]):
        out_ref[row] = store_ref[jnp.maximum(slot_ref[base + row], 0)]


def pick(slots, store, steps):
    total = slots.shape[0]
    block = total // steps
    return pl.pallas_call(
        pick_kernel,
        grid=(steps,),
        in_specs=[SMEM, pl.BlockSpec(store.shape, lambda i: (0, 0, 0))],
        out_specs=pl.BlockSpec((block,) + store.shape[1:], lambda i: (i, 0, 0)),
        out_shape=jax.ShapeDtypeStruct((total,) + store.shape[1:], store.dtype),
        compiler_params=pltpu.CompilerParams(vmem_limit_bytes=24 * 2**20),
        cost_estimate=pl.CostEstimate(flops=0, bytes_accessed=8 * 2**20, transcendentals=0),
    )(slots, store)


def terms_kernel(
    group_ref, up_ref, down_ref, tri_ref, re_ref, im_ref,
    flat_ref, left_ref, wide_ref, maps_ref, ham_ref, rho_ref,
    out_ref, tall, long,
):
    group = group_ref[0]
    windows, modes = up_ref.shape
    width = ham_ref.shape[0]

    def pair(step, carry):
        for j in range(2):
            w = step * 2 + j
            for k in range(modes):
                tile = flat_ref[up_ref[w, k]]
                tall[k * width:(k + 1) * width, j * 128:(j + 1) * 128] = tile
                long[j * width:(j + 1) * width, k * 128:(k + 1) * 128] = tile
        left = jnp.dot(left_ref[...], tall[...], preferred_element_type=F32)
        right = jnp.dot(long[...], wide_ref[...], preferred_element_type=F32)
        for j in range(2):
            w = step * 2 + j
            head = jnp.dot(ham_ref[...], rho_ref[w], preferred_element_type=F32)
            diff = left[:, j * 128:(j + 1) * 128] - right[j * width:(j + 1) * width] + head
            out_ref[w] = rotate(diff)
            for t in range(tri_ref.shape[0]):
                mode = tri_ref[t, w] - group * modes

                @pl.when((mode >= 0) & (mode < modes))
                def _():
                    state = flat_ref[down_ref[t, w]]
                    lower = jnp.dot(maps_ref[mode], state, preferred_element_type=F32)
                    start = pl.multiple_of(mode * 128, 128)
                    higher = jnp.dot(state, wide_ref[pl.ds(start, 128), :], preferred_element_type=F32)
                    out_ref[w] += re_ref[mode] * rotate(lower - higher) + im_ref[mode] * (lower + higher)
        return carry

    lax.fori_loop(0, windows // 2, pair, 0)


def on_device(
    states, send_slot, window_tier_states, modes_tri, use_up, use_down,
    hamiltonian, coupling, coup_re, coup_im, decay_rate,
):
    width = hamiltonian.shape[0]
    windows, share = window_tier_states.shape[:2]
    modes = coupling.shape[0]
    group = lax.axis_index("grp")
    slots = send_slot.reshape(-1)
    picked = pick(slots, states[0, 0], 8).reshape(send_slot.shape[2:] + states.shape[3:])
    received = lax.all_to_all(picked, "ado", split_axis=0, concat_axis=0, tiled=True)
    flat = received.reshape(-1, width, 2 * width)

    maps_wide = doubled(coupling).reshape(modes * 2 * width, 2 * width)
    maps_left = jnp.swapaxes(coupling, 0, 1).reshape(width, modes * width)
    ham_wide = doubled(hamiltonian)
    head_cols = lax.dynamic_slice_in_dim(hamiltonian, group * share, share, 1)
    right_part = jnp.einsum("wab,bc->wac", window_tier_states, ham_wide, preferred_element_type=F32)
    every_mode = jnp.arange(decay_rate.shape[0], dtype=jnp.int32)
    hits = modes_tri[:, :, None] == every_mode
    damping = jnp.sum(jnp.where(hits, decay_rate, 0.0), axis=(1, 2))
    own = rotate(right_part) + damping[:, None, None] * window_tier_states.astype(F32)

    partial_value = pl.pallas_call(
        terms_kernel,
        in_specs=[SMEM] * 6 + [VMEM] * 6,
        out_specs=VMEM,
        out_shape=jax.ShapeDtypeStruct((windows, width, 2 * width), F32),
        scratch_shapes=[
            pltpu.VMEM((modes * width, 256), BF16),
            pltpu.VMEM((2 * width, modes * 128), BF16),
        ],
        compiler_params=pltpu.CompilerParams(vmem_limit_bytes=32 * 2**20),
        cost_estimate=pl.CostEstimate(flops=2 * 10**9, bytes_accessed=10 * 2**20, transcendentals=0),
    )(
        jnp.reshape(group, (1,)).astype(jnp.int32), use_up, use_down.T, modes_tri.T, coup_re, coup_im,
        flat, maps_left, maps_wide, coupling, head_cols, window_tier_states,
    )
    blocks = partial_value.reshape(windows, width // share, share, 2 * width)
    count = width // share
    total = lax.dynamic_index_in_dim(blocks, group, 1, keepdims=False)
    for shift in (2, 1, 3):
        block = lax.dynamic_index_in_dim(blocks, lax.rem(group + shift, count), 1, keepdims=False)
        total = total + lax.ppermute(block, "grp", [(i, (i + shift) % count) for i in range(count)])
    return STEP_WEIGHT * (total - own)


def solution(mesh):
    in_specs = (
        P("grp", "ado", None, None, None),
        P("grp", "ado", None, None),
        P("ado", "grp", None),
        P("ado", None),
        P("ado", "grp"),
        P("ado", None),
        P(),
        P("grp", None, None),
        P("grp"),
        P("grp"),
        P(),
    )
    out_specs = P("ado", "grp", None)
    return jax.shard_map(
        on_device, mesh=mesh, in_specs=in_specs, out_specs=out_specs, check_vma=False
    )
```

time: 295 us -> 222 us (0.75)
  the two profiles are of different devices: /device:TPU:1 before, /device:TPU:30 now
where the time goes in v1:
time: 222 us; the launch traced here: 221 us
  waiting for transfers between devices  171 us (77%)
  starting transfers between devices  27.7 us (12%)
  Pallas kernels  14.5 us (7%)
  local copies, waits for them, and re-layouts  6.18 us (3%)
    all_to_all x1, waiting for transfers between devices, on_device(): lax.all_to_all(picked, 'ado', split_axis=0, concat_axis=0, tiled=True)  166 us
    all_to_all x1, starting transfers between devices, on_device(): lax.all_to_all(picked, 'ado', split_axis=0, concat_axis=0, tiled=True)  17.7 us
    pallas_call x1, Pallas kernels, on_device(): pl.pallas_call(terms_kernel, in_specs=[SMEM] * 6 + [VMEM] * 6, out_specs=...  13.1 us
    ppermute x3, starting transfers between devices, on_device(): lax.ppermute(block, 'grp', [(i, (i + shift) % count) for i in range(count)])  10 us
    ppermute x3, waiting for transfers between devices, on_device(): lax.ppermute(block, 'grp', [(i, (i + shift) % count) for i in range(count)])  5.53 us
    unnamed x23, local copies, waits for them, and re-layouts  5.06 us
  transfers between devices with their start and end apart: 4, of which 3 were waited for; matrix products, arithmetic and copies ran while one was open for 1% of the time, Pallas kernels for 0%

profile of v1, /device:TPU:30, one launch (start us, length us, event | category | flops | bytes accessed | tf_op | source)
XLA Modules:
  0.0 221.4 jit_solution(15412028319406910419)
XLA Ops:
  0.0 0.8 copy.17
  0.8 0.2 reshape.24.slot_ref
  1.0 0.0 copy-start.2
  1.0 1.6 copy-done.2
  2.6 1.4 shard_map.109
  3.9 0.0 copy-start
  4.0 2.6 %copy-done = bf16[384,64,128]{2,1,0:T(8,128)(2,1)} copy-done((bf16[384,64,128]{2,1,0:T(8,128)(2,1)}, bf16[384,64,128]{2,1,0:T(8,128)(2,1)S(1)}, u32[]{:S(2)}) %copy-start) | copy-done | bytes 6291480
  6.6 0.0 copy-start.1
  6.6 0.0 copy-start.9
  6.6 17.7 %all-to-all-start = ((bf16[128,3,64,128]{3,2,1,0:T(8,128)(2,1)}), bf16[128,3,64,128]{3,2,1,0:T(8,128)(2,1)}, u32[]{:S(2)}, u32[]{:S(2)}) async-start(bf16[128,3,64,128]{3,2,1,0:T(8,128)(2,1)} %bitcast.31), calls=%async_computation | async-start | bytes 12582912 | tf_op jit(solution)/shard_map/all_to_all | solution.py:95
  24.3 0.0 copy-start.3
  24.3 0.0 copy-start.4
  24.3 0.0 copy-start.5
  24.3 0.0 copy-start.6
  24.3 0.0 copy-start.7
  24.3 0.0 copy-start.8
  24.4 0.0 copy-done.1
  24.4 0.3 copy.18
  24.7 0.5 reshape.27.left_ref
  25.2 0.0 copy-done.9
  25.2 0.1 constant_dynamic-slice_fusion.ham_ref
  25.3 0.3 fusion.2
  25.6 0.0 copy-done.3
  25.6 0.2 convolution_bitcast_fusion
  25.8 165.7 %all-to-all-done = bf16[128,3,64,128]{3,2,1,0:T(8,128)(2,1)} async-done(((bf16[128,3,64,128]{3,2,1,0:T(8,128)(2,1)}), bf16[128,3,64,128]{3,2,1,0:T(8,128)(2,1)}, u32[]{:S(2)}, u32[]{:S(2)}) %all-to-all-start) | async-done | bytes 6291488 | tf_op jit(solution)/shard_map/all_to_all | solution.py:95
  191.5 0.0 copy-done.4
  191.5 0.0 copy-done.5
  191.6 0.0 copy-done.6
  191.6 0.0 copy-done.7
  191.6 0.0 copy-done.8
  191.6 0.0 copy-start.10
  191.6 13.1 %shard_map.110 = f32[16,64,128]{2,1,0:T(8,128)S(1)} custom-call(s32[1]{0:T(128)} %bitcast.group_ref, s32[16,32]{1,0:T(8,128)S(1)} %copy-done.4, s32[3,16]{1,0:T(4,128)S(1)} %bitcast.38, s32[3,16]{1,0:T(4,128)S(1)} %bitcast.37, f32[32]{0:T(128)S(1)} %copy-done.7, f32[32]{0:T(128)S(1)} %copy-done.8, bf16[384,64,128]{2,1,0:T(8,128)(2,1)} %bitcast.5.flat_ref, ...), custom_call_target="tpu_custom_call" | custom-call | flops 2000000000 | bytes 10485760 | tf_op jit(solution)/shard_map/pallas_call | solution.py:108
  204.7 4.2 %collective-permute-start = (f32[16,16,128]{2,1,0:T(8,128)S(1)}, f32[16,16,128]{2,1,0:T(8,128)S(1)}, u32[]{:S(2)}, u32[]{:S(2)}) collective-permute-start(f32[16,16,128]{2,1,0:T(8,128)S(1)} %get-tuple-element.5), channel_id=1, source_target_pairs={{0,256},{128,384},{256,0},{384,128},{1,257},{129,385},{257,1},{385... | collective-permute-start | bytes 393224 | tf_op jit(solution)/shard_map/ppermute | solution.py:128
  208.9 3.6 %collective-permute-start.1 = (f32[16,16,128]{2,1,0:T(8,128)S(1)}, f32[16,16,128]{2,1,0:T(8,128)S(1)}, u32[]{:S(2)}, u32[]{:S(2)}) collective-permute-start(f32[16,16,128]{2,1,0:T(8,128)S(1)} %get-tuple-element.7), channel_id=1, source_target_pairs={{0,128},{128,256},{256,384},{384,0},{1,129},{129,257},{257,385},{3... | collective-permute-start | bytes 393224 | tf_op jit(solution)/shard_map/ppermute | solution.py:128
  212.5 2.2 %collective-permute-start.2 = (f32[16,16,128]{2,1,0:T(8,128)S(1)}, f32[16,16,128]{2,1,0:T(8,128)S(1)}, u32[]{:S(2)}, u32[]{:S(2)}) collective-permute-start(f32[16,16,128]{2,1,0:T(8,128)S(1)} %get-tuple-element.6), channel_id=1, source_target_pairs={{0,384},{128,0},{256,128},{384,256},{1,385},{129,1},{257,129},{385... | collective-permute-start | bytes 393224 | tf_op jit(solution)/shard_map/ppermute | solution.py:128
  214.8 0.1 fusion.20
  214.9 0.0 copy-done.10
  214.9 0.2 select_reduce_fusion
  215.1 0.0 collective-permute-done
  215.1 0.7 collective-permute-done.1
  215.8 4.8 %collective-permute-done.2 = f32[16,16,128]{2,1,0:T(8,128)S(1)} collective-permute-done((f32[16,16,128]{2,1,0:T(8,128)S(1)}, f32[16,16,128]{2,1,0:T(8,128)S(1)}, u32[]{:S(2)}, u32[]{:S(2)}) %collective-permute-start.2) | collective-permute-done | bytes 131104 | tf_op jit(solution)/shard_map/ppermute | solution.py:128
  220.6 0.8 fusion.4
  (1 shorter events, 0.0 us)
Async XLA Ops:
  1.0 1.6 copy-start.2
  3.9 2.6 %copy-start = (bf16[384,64,128]{2,1,0:T(8,128)(2,1)}, bf16[384,64,128]{2,1,0:T(8,128)(2,1)S(1)}, u32[]{:S(2)}) copy-start(bf16[384,64,128]{2,1,0:T(8,128)(2,1)S(1)} %shard_map.109) | copy-start | bytes 18874372
  6.6 17.8 %copy-start.1 = (bf16[32,64,64]{2,1,0:T(8,128)(2,1)S(1)}, bf16[32,64,64]{2,1,0:T(8,128)(2,1)}, u32[]{:S(2)}) copy-start(bf16[32,64,64]{2,1,0:T(8,128)(2,1)} %maps_ref.1) | copy-start | bytes 786436
  6.6 18.6 %copy-start.9 = (bf16[64,64]{1,0:T(8,128)(2,1)S(1)}, bf16[64,64]{1,0:T(8,128)(2,1)}, u32[]{:S(2)}) copy-start(bf16[64,64]{1,0:T(8,128)(2,1)} %param.17) | copy-start | bytes 24580
  6.6 184.9 %all-to-all-start = ((bf16[128,3,64,128]{3,2,1,0:T(8,128)(2,1)}), bf16[128,3,64,128]{3,2,1,0:T(8,128)(2,1)}, u32[]{:S(2)}, u32[]{:S(2)}) async-start(bf16[128,3,64,128]{3,2,1,0:T(8,128)(2,1)} %bitcast.31), calls=%async_computation | async-start | bytes 12582912 | tf_op jit(solution)/shard_map/all_to_all | solution.py:95
  24.3 1.3 copy-start.3
  24.3 167.3 %copy-start.4 = (s32[16,32]{1,0:T(8,128)S(1)}, s32[16,32]{1,0:T(8,128)}, u32[]{:S(2)}) copy-start(s32[16,32]{1,0:T(8,128)} %up_ref.1) | copy-start | bytes 6148
  24.3 167.3 %copy-start.5 = (s32[16,3]{0,1:T(4,128)S(1)}, s32[16,3]{0,1:T(4,128)}, u32[]{:S(2)}) copy-start(s32[16,3]{0,1:T(4,128)} %param.14) | copy-start | bytes 580
  24.3 167.2 %copy-start.6 = (s32[16,3]{0,1:T(4,128)S(1)}, s32[16,3]{0,1:T(4,128)}, u32[]{:S(2)}) copy-start(s32[16,3]{0,1:T(4,128)} %param.16) | copy-start | bytes 580
  24.3 167.2 %copy-start.7 = (f32[32]{0:T(128)S(1)}, f32[32]{0:T(128)}, u32[]{:S(2)}) copy-start(f32[32]{0:T(128)} %re_ref.1) | copy-start | bytes 388
  24.3 167.2 %copy-start.8 = (f32[32]{0:T(128)S(1)}, f32[32]{0:T(128)}, u32[]{:S(2)}) copy-start(f32[32]{0:T(128)} %im_ref.1) | copy-start | bytes 388
  191.6 23.3 %copy-start.10 = (f32[128]{0:T(128)S(1)}, f32[128]{0:T(128)}, u32[]{:S(2)}) copy-start(f32[128]{0:T(128)} %param.21) | copy-start | bytes 1540
  204.7 10.3 %collective-permute-start = (f32[16,16,128]{2,1,0:T(8,128)S(1)}, f32[16,16,128]{2,1,0:T(8,128)S(1)}, u32[]{:S(2)}, u32[]{:S(2)}) collective-permute-start(f32[16,16,128]{2,1,0:T(8,128)S(1)} %get-tuple-element.5), channel_id=1, source_target_pairs={{0,256},{128,384},{256,0},{384,128},{1,257},{129,385},{257,1},{385... | collective-permute-start | bytes 393224 | tf_op jit(solution)/shard_map/ppermute | solution.py:128
  208.9 6.9 %collective-permute-start.1 = (f32[16,16,128]{2,1,0:T(8,128)S(1)}, f32[16,16,128]{2,1,0:T(8,128)S(1)}, u32[]{:S(2)}, u32[]{:S(2)}) collective-permute-start(f32[16,16,128]{2,1,0:T(8,128)S(1)} %get-tuple-element.7), channel_id=1, source_target_pairs={{0,128},{128,256},{256,384},{384,0},{1,129},{129,257},{257,385},{3... | collective-permute-start | bytes 393224 | tf_op jit(solution)/shard_map/ppermute | solution.py:128
  212.5 8.1 %collective-permute-start.2 = (f32[16,16,128]{2,1,0:T(8,128)S(1)}, f32[16,16,128]{2,1,0:T(8,128)S(1)}, u32[]{:S(2)}, u32[]{:S(2)}) collective-permute-start(f32[16,16,128]{2,1,0:T(8,128)S(1)} %get-tuple-element.6), channel_id=1, source_target_pairs={{0,384},{128,0},{256,128},{384,256},{1,385},{129,1},{257,129},{385... | collective-permute-start | bytes 393224 | tf_op jit(solution)/shard_map/ppermute | solution.py:128

commit v2 on v1

v2 whole, which is shorter than its diff:
```python
import jax
import jax.numpy as jnp
from jax import lax
from jax.experimental import pallas as pl
from jax.experimental.pallas import tpu as pltpu
from jax.sharding import PartitionSpec as P

STEP_WEIGHT = 0.5
F32 = jnp.float32
BF16 = jnp.bfloat16
LINK = jnp.float16
VMEM = pl.BlockSpec(memory_space=pltpu.VMEM)
SMEM = pl.BlockSpec(memory_space=pltpu.SMEM)


def doubled(matrices):
    empty = jnp.zeros_like(matrices)
    upper_half = jnp.concatenate([matrices, empty], axis=-1)
    lower_half = jnp.concatenate([empty, matrices], axis=-1)
    return jnp.concatenate([upper_half, lower_half], axis=-2)


def rotate(parts):
    width = parts.shape[-1] // 2
    return jnp.concatenate([parts[..., width:], -parts[..., :width]], axis=-1)

RINGS = 8
CAP = 3
LOT = 8
ROWS = 40
GRID = [(z, y, c) for z in range(RINGS) for y in range(RINGS) for c in range(2)]
COLLECT = [[z * 16 + y * 2 for z in range(RINGS)] for y in range(RINGS)] + [
    [z * 16 + y * 2 + 1 for y in range(RINGS)] for z in range(RINGS)
]
DELIVER = [[z * 16 + y * 2 for y in range(RINGS)] for z in range(RINGS)] + [
    [z * 16 + y * 2 + 1 for z in range(RINGS)] for y in range(RINGS)
]
SIBLING = [(i, i ^ 1) for i in range(2 * RINGS * RINGS)]


def pick_kernel(core_ref, own_slot, sib_slot, own_ref, sib_ref, out_ref):
    core = core_ref[0]
    target = pl.program_id(0)
    first = jnp.where(core == 0, target * 16, target * 2 + 1)
    step = jnp.where(core == 0, 2, 16)
    count = own_slot.shape[0] // CAP
    for kind, (slots, store) in enumerate(((own_slot, own_ref), (sib_slot, sib_ref))):
        for c in range(CAP):
            for r in range(RINGS):
                slot = slots[c * count + first + r * step]
                out_ref[0, kind * CAP * RINGS + c * RINGS + r] = store[jnp.maximum(slot, 0)]


def pick(core, own_slots, sib_slots, own, sib):
    tile = own.shape[1:]
    whole = pl.BlockSpec(own.shape, lambda i: (0, 0, 0))
    block = 2 * CAP * RINGS
    return pl.pallas_call(
        pick_kernel,
        grid=(RINGS,),
        in_specs=[SMEM, SMEM, SMEM, whole, whole],
        out_specs=pl.BlockSpec((1, block) + tile, lambda i: (i, 0, 0, 0)),
        out_shape=jax.ShapeDtypeStruct((RINGS, block) + tile, own.dtype),
        compiler_params=pltpu.CompilerParams(vmem_limit_bytes=24 * 2**20),
        cost_estimate=pl.CostEstimate(flops=0, bytes_accessed=10 * 2**20, transcendentals=0),
    )(core, own_slots, sib_slots, own, sib)


def terms_kernel(
    spot_ref, list_ref, re_ref, im_ref, flat_ref, wide_ref, ham_ref, rho_ref, out_ref,
):
    group, here = spot_ref[0], spot_ref[1]
    windows, share = rho_ref.shape[:2]
    width = ham_ref.shape[0]
    modes = wide_ref.shape[0] - 1
    blocks = width // share

    def add(r, w, value, fresh):
        for b in range(blocks):
            part = value[b * share:(b + 1) * share]
            index = lax.rem(b - group + blocks, blocks)
            if fresh:
                out_ref[index, r, w] = part
            else:
                out_ref[index, r, w] += part

    def lot(r, column, base):
        entries = [list_ref[r, base + n, column] for n in range(LOT)]
        maps = [lax.shift_right_logical(e, 9) for e in entries]
        tiles = [flat_ref[e & 511] for e in entries]
        rows = [
            wide_ref[maps[n], :width, :] + wide_ref[maps[n + 1], width:, :] for n in range(0, LOT, 2)
        ]
        left = jnp.dot(
            jnp.concatenate(rows, axis=1), jnp.concatenate(tiles, axis=0), preferred_element_type=F32
        )
        right = jnp.dot(
            jnp.concatenate(tiles, axis=1),
            jnp.concatenate([wide_ref[m] for m in maps], axis=0),
            preferred_element_type=F32,
        )
        return rotate(left - right)

    together = 4

    def step(index, carry):
        r = index // (windows // together)
        first = lax.rem(index, windows // together) * together
        for j in range(together):
            w = first + j
            add(r, w, lot(r, here * windows + w, 0), True)
        for j in range(together):
            w = first + j
            column = here * windows + w
            for base in range(LOT, modes, LOT):

                @pl.when(lax.shift_right_logical(list_ref[r, base, column], 9) < modes)
                def _():
                    add(r, w, lot(r, column, base), False)

            def lower(n, inner):
                entry = list_ref[r, modes + n, column]
                mode = lax.shift_right_logical(entry, 9)
                state = flat_ref[entry & 511]
                wide = wide_ref[mode]
                ahead = jnp.dot(wide[:width, :width], state, preferred_element_type=F32)
                after = jnp.dot(state, wide, preferred_element_type=F32)
                add(r, w, re_ref[mode] * rotate(ahead - after) + im_ref[mode] * (ahead + after), False)
                return inner

            lax.fori_loop(0, list_ref[r, modes + CAP, column], lower, 0)
        return carry

    lax.fori_loop(0, RINGS * (windows // together), step, 0)
    for w in range(windows):
        add(here, w, rotate(jnp.dot(ham_ref[...], rho_ref[w], preferred_element_type=F32)), False)


def use_lists(core, place, group, modes, modes_tri, use_up, use_down):
    windows = use_up.shape[0]

    def locate(places):
        owner = places // CAP
        z, y, c = owner // 16, (owner // 2) % RINGS, owner % 2
        collector = jnp.where(core == 0, y, z)
        source = jnp.where(core == 0, z, y)
        kind = jnp.where(c == core, 0, 1)
        row = ((source * 2 + kind) * CAP + places % CAP) * RINGS + place
        return collector, row

    def packed(collector, live, values, empty):
        count = values.shape[0]
        every = jnp.arange(RINGS, dtype=jnp.int32)[None, :, None]
        mask = ((collector[:, None, :] == every) & live[:, None, :]).reshape(count, RINGS * windows)
        spread = jnp.broadcast_to(values[:, None, :] - empty, (count, RINGS, windows)).reshape(count, -1)
        order = jnp.arange(count, dtype=jnp.int32)
        ranks = jnp.sum(
            jnp.where((order[:, None] > order[None, :])[:, :, None] & mask[None], 1, 0), axis=1
        )
        take = (order[:, None, None] == ranks[None]) & mask[None]
        return empty + jnp.sum(jnp.where(take, spread[None], 0), axis=1), jnp.sum(mask.astype(jnp.int32), axis=0)

    mode_ids = jnp.arange(modes, dtype=jnp.int32)[:, None]
    collector, row = locate(use_up.T)
    up, _ = packed(collector, jnp.ones(collector.shape, bool), mode_ids * 512 + row, modes * 512)
    collector, row = locate(use_down.T)
    local = modes_tri.T - group * modes
    live = (local >= 0) & (local < modes)
    down, count = packed(collector, live, local * 512 + row, 0)
    blank = jnp.zeros((ROWS - up.shape[0] - down.shape[0] - 1, up.shape[1]), jnp.int32)
    return jnp.concatenate([up, down, count[None], blank], axis=0)


def on_device(
    states, send_slot, window_tier_states, modes_tri, use_up, use_down,
    hamiltonian, coupling, coup_re, coup_im, decay_rate,
):
    width = hamiltonian.shape[0]
    windows, share = window_tier_states.shape[:2]
    modes = coupling.shape[0]
    group = lax.axis_index("grp")
    index = lax.axis_index("ado")
    core = index % 2
    place = jnp.where(core == 0, (index // 2) % RINGS, index // 16)

    slots = jnp.transpose(send_slot[0, 0]).reshape(-1)
    sib_store = lax.ppermute(states[0, 0], "ado", SIBLING)
    sib_slots = lax.ppermute(slots, "ado", SIBLING)
    lists = use_lists(core, place, group, modes, modes_tri, use_up, use_down)
    lists = lax.all_gather(lists, "ado", axis_index_groups=DELIVER, axis=0, tiled=False)
    picked = pick(jnp.reshape(core, (1,)).astype(jnp.int32), slots, sib_slots, states[0, 0], sib_store)
    received = lax.all_to_all(
        picked, "ado", split_axis=0, concat_axis=0, tiled=True, axis_index_groups=COLLECT
    )
    flat = received.reshape(-1, width, 2 * width)

    maps_wide = jnp.concatenate([doubled(coupling), jnp.zeros((1, 2 * width, 2 * width), BF16)], axis=0)
    ham_wide = doubled(hamiltonian)
    head_cols = lax.dynamic_slice_in_dim(hamiltonian, group * share, share, 1)
    right_part = jnp.einsum("wab,bc->wac", window_tier_states, ham_wide, preferred_element_type=F32)
    every_mode = jnp.arange(decay_rate.shape[0], dtype=jnp.int32)
    hits = modes_tri[:, :, None] == every_mode
    damping = jnp.sum(jnp.where(hits, decay_rate, 0.0), axis=(1, 2))
    own = rotate(right_part) + damping[:, None, None] * window_tier_states.astype(F32)

    count = width // share
    parts = pl.pallas_call(
        terms_kernel,
        in_specs=[SMEM] * 4 + [VMEM] * 4,
        out_specs=VMEM,
        out_shape=jax.ShapeDtypeStruct((count, RINGS, windows, share, 2 * width), F32),
        compiler_params=pltpu.CompilerParams(vmem_limit_bytes=32 * 2**20),
        cost_estimate=pl.CostEstimate(flops=2 * 10**9, bytes_accessed=10 * 2**20, transcendentals=0),
    )(
        jnp.stack([group, place]).astype(jnp.int32), lists, coup_re, coup_im,
        flat, maps_wide, head_cols, window_tier_states,
    )
    total = parts[0]
    for shift in (2, 1, 3):
        ring = [(i, (i + shift) % count) for i in range(count)]
        total = total + lax.ppermute(parts[shift].astype(LINK), "grp", ring).astype(F32)
    summed = lax.all_to_all(
        total.astype(LINK), "ado", split_axis=0, concat_axis=0, tiled=True, axis_index_groups=DELIVER
    )
    return STEP_WEIGHT * (jnp.sum(summed.astype(F32), axis=0) - own)


def solution(mesh):
    in_specs = (
        P("grp", "ado", None, None, None),
        P("grp", "ado", None, None),
        P("ado", "grp", None),
        P("ado", None),
        P("ado", "grp"),
        P("ado", None),
        P(),
        P("grp", None, None),
        P("grp"),
        P("grp"),
        P(),
    )
    out_specs = P("ado", "grp", None)
    return jax.shard_map(
        on_device, mesh=mesh, in_specs=in_specs, out_specs=out_specs, check_vma=False
    )
```

time: 222 us -> 176 us (0.79)
  the two profiles are of different devices: /device:TPU:30 before, /device:TPU:1 now
where the time goes in v2:
time: 176 us; the launch traced here: 175 us
  waiting for transfers between devices  67.8 us (39%)
  blocking collectives  35.7 us (20%)
  starting transfers between devices  31.4 us (18%)
  Pallas kernels  29.8 us (17%)
  local copies, waits for them, and re-layouts  6.2 us (4%)
  other arithmetic  3.77 us (2%)
    all_gather x1, blocking collectives, on_device(): lax.all_gather(lists, 'ado', axis_index_groups=DELIVER, axis=0, tiled=False)  35.7 us
    all_to_all x1, waiting for transfers between devices, on_device(): lax.all_to_all(picked, 'ado', split_axis=0, concat_axis=0, tiled=True, ax...  35.2 us
    pallas_call x1, Pallas kernels, on_device(): pl.pallas_call(terms_kernel, in_specs=[SMEM] * 4 + [VMEM] * 4, out_specs=...  28.4 us
    ppermute x3, waiting for transfers between devices, on_device(): lax.ppermute(parts[shift].astype(LINK), 'grp', ring).astype(F32)  19.6 us
    all_to_all x1, waiting for transfers between devices, on_device(): lax.all_to_all(total.astype(LINK), 'ado', split_axis=0, concat_axis=0, ti...  11.6 us
    ppermute x3, starting transfers between devices, on_device(): lax.ppermute(parts[shift].astype(LINK), 'grp', ring).astype(F32)  8.82 us
    ppermute x1, starting transfers between devices, on_device(): sib_store = lax.ppermute(states[0, 0], 'ado', SIBLING)  8.78 us
    all_to_all x1, starting transfers between devices, on_device(): lax.all_to_all(total.astype(LINK), 'ado', split_axis=0, concat_axis=0, ti...  6.98 us
  transfers between devices with their start and end apart: 7, of which 6 were waited for; matrix products, arithmetic and copies ran while one was open for 2% of the time, Pallas kernels for 0%

profile of v2, /device:TPU:1, one launch (start us, length us, event | category | flops | bytes accessed | tf_op | source)
XLA Modules:
  0.0 175.3 jit_solution(1629704015485468726)
XLA Ops:
  0.0 8.8 %collective-permute-start.1 = (bf16[128,64,128]{2,1,0:T(8,128)(2,1)}, bf16[128,64,128]{2,1,0:T(8,128)(2,1)S(1)}, u32[]{:S(2)}, u32[]{:S(2)}) collective-permute-start(bf16[128,64,128]{2,1,0:T(8,128)(2,1)} %bitcast.106), channel_id=1, source_target_pairs={{0,1},{1,0},{2,3},{3,2},{4,5},{5,4},{6,7},{7,6},{8,9},{9,8},{10,11... | collective-permute-start | bytes 6291464 | tf_op jit(solution)/shard_map/ppermute | solution.py:187
  8.8 0.7 copy.22
  9.5 1.9 %collective-permute-start = (s32[384]{0:T(512)S(1)}, s32[384]{0:T(512)S(1)}, u32[]{:S(2)}, u32[]{:S(2)}) collective-permute-start(s32[384]{0:T(512)S(1)} %bitcast.109), channel_id=1, source_target_pairs={{0,1},{1,0},{2,3},{3,2},{4,5},{5,4},{6,7},{7,6},{8,9},{9,8},{10,11... | collective-permute-start | bytes 4616 | tf_op jit(solution)/shard_map/ppermute | solution.py:188
  11.4 1.2 collective-permute-done.sib_slot
  12.6 0.2 collective-permute-done.1.sib_ref
  12.8 1.6 copy-done.1
  14.4 1.5 shard_map.109
  15.8 2.6 %copy-done = bf16[8,48,64,128]{3,2,1,0:T(8,128)(2,1)} copy-done((bf16[8,48,64,128]{3,2,1,0:T(8,128)(2,1)}, bf16[8,48,64,128]{3,2,1,0:T(8,128)(2,1)S(1)}, u32[]{:S(2)}) %copy-start) | copy-done | bytes 6291480
  18.5 4.9 %all-to-all-start = ((bf16[8,48,64,128]{3,2,1,0:T(8,128)(2,1)}), bf16[8,48,64,128]{3,2,1,0:T(8,128)(2,1)}, u32[]{:S(2)}, u32[]{:S(2)}) async-start(bf16[8,48,64,128]{3,2,1,0:T(8,128)(2,1)} %copy-done), calls=%async_computation | async-start | bytes 12582912 | tf_op jit(solution)/shard_map/all_to_all | solution.py:192
  23.5 0.1 copy.19
  23.6 0.1 eq.126
  23.7 0.1 bitcast_compare_fusion
  23.8 0.0 copy-start.7
  23.8 0.1 copy.18
  23.9 0.0 copy-start.3
  23.9 0.0 copy-start.4
  24.0 0.1 eq.135
  24.1 0.1 and.152
  24.2 0.1 broadcast_in_dim.104
  24.3 0.1 broadcast_in_dim.106
  24.3 0.1 pad.14.clone
  24.4 0.3 fusion.2
  24.7 0.1 concatenate.31.wide_ref
  24.9 0.1 select_reduce_fusion.4
  25.0 0.2 select_reduce_fusion.1
  25.2 0.1 select_reduce_fusion
  25.4 0.1 add_add_fusion
  25.5 35.7 %all-gather = s32[320,128]{1,0:T(8,128)S(1)} all-gather(s32[40,128]{1,0:T(8,128)S(1)} %add_add_fusion), channel_id=2, replica_groups={{0,2,4,6,8,10,12,14},{16,18,20,22,24,26,28,30},{32,34,36,38,40,42,44,46..., dimensions={0}, use_global_device_ids=true | all-gather | bytes 184320 | tf_op jit(solution)/shard_map/all_gather | solution.py:190
  61.1 0.1 pad_add_fusion.spot_ref
  61.2 0.1 constant_dynamic-slice_fusion.ham_ref
  61.3 35.2 %all-to-all-done = bf16[8,48,64,128]{3,2,1,0:T(8,128)(2,1)} async-done(((bf16[8,48,64,128]{3,2,1,0:T(8,128)(2,1)}), bf16[8,48,64,128]{3,2,1,0:T(8,128)(2,1)}, u32[]{:S(2)}, u32[]{:S(2)}) %all-to-all-start) | async-done | bytes 6291488 | tf_op jit(solution)/shard_map/all_to_all | solution.py:192
  96.5 28.4 %shard_map.110 = f32[4,8,16,16,128]{4,3,2,1,0:T(8,128)S(1)} custom-call(s32[2]{0:T(128)S(1)} %pad_add_fusion.spot_ref, s32[8,40,128]{2,1,0:T(8,128)S(1)} %bitcast.108, f32[32]{0:T(128)S(1)} %copy-done.3, f32[32]{0:T(128)S(1)} %copy-done.4, bf16[384,64,128]{2,1,0:T(8,128)(2,1)} %bitcast.18.flat_ref, bf16[33,128,128]{2,1,0:T(8,128)(2,1)S(1)} %concatenate.31.wide_ref, ...), custom_call_target="tpu_custom_call" | custom-call | flops 2000000000 | bytes 10485760 | tf_op jit(solution)/shard_map/pallas_call | solution.py:207
  124.9 0.4 convert.5
  125.3 0.4 slice_bitcast_fusion.3
  125.7 2.3 %collective-permute-start.2 = (f16[8,16,16,128]{3,2,1,0:T(8,128)(2,1)S(1)}, f16[8,16,16,128]{3,2,1,0:T(8,128)(2,1)S(1)}, u32[]{:S(2)}, u32[]{:S(2)}) collective-permute-start(f16[8,16,16,128]{3,2,1,0:T(8,128)(2,1)S(1)} %get-tuple-element.5), channel_id=1, source_target_pairs={{0,256},{128,384},{256,0},{384,128},{1,257},{129,385},{257,1},{385... | collective-permute-start | bytes 1572872 | tf_op jit(solution)/shard_map/ppermute | solution.py:221
  128.1 3.8 %collective-permute-start.3 = (f16[8,16,16,128]{3,2,1,0:T(8,128)(2,1)S(1)}, f16[8,16,16,128]{3,2,1,0:T(8,128)(2,1)S(1)}, u32[]{:S(2)}, u32[]{:S(2)}) collective-permute-start(f16[8,16,16,128]{3,2,1,0:T(8,128)(2,1)S(1)} %get-tuple-element.7), channel_id=1, source_target_pairs={{0,128},{128,256},{256,384},{384,0},{1,129},{129,257},{257,385},{3... | collective-permute-start | bytes 1572872 | tf_op jit(solution)/shard_map/ppermute | solution.py:221
  131.9 0.0 copy-start.10
  131.9 2.7 %collective-permute-start.4 = (f16[8,16,16,128]{3,2,1,0:T(8,128)(2,1)S(1)}, f16[8,16,16,128]{3,2,1,0:T(8,128)(2,1)S(1)}, u32[]{:S(2)}, u32[]{:S(2)}) collective-permute-start(f16[8,16,16,128]{3,2,1,0:T(8,128)(2,1)S(1)} %get-tuple-element.6), channel_id=1, source_target_pairs={{0,384},{128,0},{256,128},{384,256},{1,385},{129,1},{257,129},{385... | collective-permute-start | bytes 1572872 | tf_op jit(solution)/shard_map/ppermute | solution.py:221
  134.6 5.5 %collective-permute-done.2 = f16[8,16,16,128]{3,2,1,0:T(8,128)(2,1)S(1)} collective-permute-done((f16[8,16,16,128]{3,2,1,0:T(8,128)(2,1)S(1)}, f16[8,16,16,128]{3,2,1,0:T(8,128)(2,1)S(1)}, u32[]{:S(2)}, u32[]{:S(2)}) %collective-permute-start.2) | collective-permute-done | bytes 524320 | tf_op jit(solution)/shard_map/ppermute | solution.py:221
  140.1 14.1 %collective-permute-done.3 = f16[8,16,16,128]{3,2,1,0:T(8,128)(2,1)S(1)} collective-permute-done((f16[8,16,16,128]{3,2,1,0:T(8,128)(2,1)S(1)}, f16[8,16,16,128]{3,2,1,0:T(8,128)(2,1)S(1)}, u32[]{:S(2)}, u32[]{:S(2)}) %collective-permute-start.3) | collective-permute-done | bytes 524320 | tf_op jit(solution)/shard_map/ppermute | solution.py:221
  154.2 1.1 fusion.6
  155.3 7.0 %all-to-all-start.1 = ((f16[8,16,16,128]{3,2,1,0:T(8,128)(2,1)}), f16[8,16,16,128]{3,2,1,0:T(8,128)(2,1)S(1)}, u32[]{:S(2)}, u32[]{:S(2)}) async-start(f16[8,16,16,128]{3,2,1,0:T(8,128)(2,1)} %fusion.6), calls=%async_computation.1 | async-start | bytes 1048576 | tf_op jit(solution)/shard_map/all_to_all | solution.py:222
  162.3 0.2 select_reduce_fusion.2
  162.4 0.2 convolution_bitcast_fusion
  162.7 0.1 fusion.49
  162.8 11.6 %all-to-all-done.1 = f16[8,16,16,128]{3,2,1,0:T(8,128)(2,1)S(1)} async-done(((f16[8,16,16,128]{3,2,1,0:T(8,128)(2,1)}), f16[8,16,16,128]{3,2,1,0:T(8,128)(2,1)S(1)}, u32[]{:S(2)}, u32[]{:S(2)}) %all-to-all-start.1) | async-done | bytes 524320 | tf_op jit(solution)/shard_map/all_to_all | solution.py:222
  174.4 0.1 convert_reduce_fusion
  174.5 0.8 fusion.9
  (33 shorter events, 0.2 us)
Async XLA Ops:
  0.0 12.8 %collective-permute-start.1 = (bf16[128,64,128]{2,1,0:T(8,128)(2,1)}, bf16[128,64,128]{2,1,0:T(8,128)(2,1)S(1)}, u32[]{:S(2)}, u32[]{:S(2)}) collective-permute-start(bf16[128,64,128]{2,1,0:T(8,128)(2,1)} %bitcast.106), channel_id=1, source_target_pairs={{0,1},{1,0},{2,3},{3,2},{4,5},{5,4},{6,7},{7,6},{8,9},{9,8},{10,11... | collective-permute-start | bytes 6291464 | tf_op jit(solution)/shard_map/ppermute | solution.py:187
  9.5 3.1 %collective-permute-start = (s32[384]{0:T(512)S(1)}, s32[384]{0:T(512)S(1)}, u32[]{:S(2)}, u32[]{:S(2)}) collective-permute-start(s32[384]{0:T(512)S(1)} %bitcast.109), channel_id=1, source_target_pairs={{0,1},{1,0},{2,3},{3,2},{4,5},{5,4},{6,7},{7,6},{8,9},{9,8},{10,11... | collective-permute-start | bytes 4616 | tf_op jit(solution)/shard_map/ppermute | solution.py:188
  12.8 1.6 copy-start.1
  15.8 2.7 %copy-start = (bf16[8,48,64,128]{3,2,1,0:T(8,128)(2,1)}, bf16[8,48,64,128]{3,2,1,0:T(8,128)(2,1)S(1)}, u32[]{:S(2)}) copy-start(bf16[8,48,64,128]{3,2,1,0:T(8,128)(2,1)S(1)} %shard_map.109) | copy-start | bytes 18874372
  18.5 5.0 %copy-start.8 = (s32[16,32]{1,0:T(8,128)S(1)}, s32[16,32]{1,0:T(8,128)}, u32[]{:S(2)}) copy-start(s32[16,32]{1,0:T(8,128)} %param.15) | copy-start | bytes 6148
  18.5 5.4 %copy-start.6 = (s32[16,3]{0,1:T(4,128)S(1)}, s32[16,3]{0,1:T(4,128)}, u32[]{:S(2)}) copy-start(s32[16,3]{0,1:T(4,128)} %param.14) | copy-start | bytes 580
  18.5 5.4 %copy-start.9 = (s32[16,3]{0,1:T(4,128)S(1)}, s32[16,3]{0,1:T(4,128)}, u32[]{:S(2)}) copy-start(s32[16,3]{0,1:T(4,128)} %param.16) | copy-start | bytes 580
  18.5 5.9 %copy-start.5 = (bf16[32,64,64]{2,1,0:T(8,128)(2,1)S(1)}, bf16[32,64,64]{2,1,0:T(8,128)(2,1)}, u32[]{:S(2)}) copy-start(bf16[32,64,64]{2,1,0:T(8,128)(2,1)} %param.18) | copy-start | bytes 786436
  18.5 78.0 %all-to-all-start = ((bf16[8,48,64,128]{3,2,1,0:T(8,128)(2,1)}), bf16[8,48,64,128]{3,2,1,0:T(8,128)(2,1)}, u32[]{:S(2)}, u32[]{:S(2)}) async-start(bf16[8,48,64,128]{3,2,1,0:T(8,128)(2,1)} %copy-done), calls=%async_computation | async-start | bytes 12582912 | tf_op jit(solution)/shard_map/all_to_all | solution.py:192
  23.8 37.5 %copy-start.7 = (bf16[64,64]{1,0:T(8,128)(2,1)S(1)}, bf16[64,64]{1,0:T(8,128)(2,1)}, u32[]{:S(2)}) copy-start(bf16[64,64]{1,0:T(8,128)(2,1)} %param.17) | copy-start | bytes 24580
  23.9 72.6 %copy-start.2 = (bf16[16,16,128]{2,1,0:T(8,128)(2,1)S(1)}, bf16[16,16,128]{2,1,0:T(8,128)(2,1)}, u32[]{:S(2)}) copy-start(bf16[16,16,128]{2,1,0:T(8,128)(2,1)} %rho_ref.1) | copy-start | bytes 196612
  23.9 72.6 %copy-start.3 = (f32[32]{0:T(128)S(1)}, f32[32]{0:T(128)}, u32[]{:S(2)}) copy-start(f32[32]{0:T(128)} %re_ref.1) | copy-start | bytes 388
  23.9 72.6 %copy-start.4 = (f32[32]{0:T(128)S(1)}, f32[32]{0:T(128)}, u32[]{:S(2)}) copy-start(f32[32]{0:T(128)} %im_ref.1) | copy-start | bytes 388
  125.7 14.4 %collective-permute-start.2 = (f16[8,16,16,128]{3,2,1,0:T(8,128)(2,1)S(1)}, f16[8,16,16,128]{3,2,1,0:T(8,128)(2,1)S(1)}, u32[]{:S(2)}, u32[]{:S(2)}) collective-permute-start(f16[8,16,16,128]{3,2,1,0:T(8,128)(2,1)S(1)} %get-tuple-element.5), channel_id=1, source_target_pairs={{0,256},{128,384},{256,0},{384,128},{1,257},{129,385},{257,1},{385... | collective-permute-start | bytes 1572872 | tf_op jit(solution)/shard_map/ppermute | solution.py:221
  128.1 26.1 %collective-permute-start.3 = (f16[8,16,16,128]{3,2,1,0:T(8,128)(2,1)S(1)}, f16[8,16,16,128]{3,2,1,0:T(8,128)(2,1)S(1)}, u32[]{:S(2)}, u32[]{:S(2)}) collective-permute-start(f16[8,16,16,128]{3,2,1,0:T(8,128)(2,1)S(1)} %get-tuple-element.7), channel_id=1, source_target_pairs={{0,128},{128,256},{256,384},{384,0},{1,129},{129,257},{257,385},{3... | collective-permute-start | bytes 1572872 | tf_op jit(solution)/shard_map/ppermute | solution.py:221
  131.9 30.4 %copy-start.10 = (f32[128]{0:T(128)S(1)}, f32[128]{0:T(128)}, u32[]{:S(2)}) copy-start(f32[128]{0:T(128)} %param.21) | copy-start | bytes 1540
  131.9 22.3 %collective-permute-start.4 = (f16[8,16,16,128]{3,2,1,0:T(8,128)(2,1)S(1)}, f16[8,16,16,128]{3,2,1,0:T(8,128)(2,1)S(1)}, u32[]{:S(2)}, u32[]{:S(2)}) collective-permute-start(f16[8,16,16,128]{3,2,1,0:T(8,128)(2,1)S(1)} %get-tuple-element.6), channel_id=1, source_target_pairs={{0,384},{128,0},{256,128},{384,256},{1,385},{129,1},{257,129},{385... | collective-permute-start | bytes 1572872 | tf_op jit(solution)/shard_map/ppermute | solution.py:221
  155.3 19.1 %all-to-all-start.1 = ((f16[8,16,16,128]{3,2,1,0:T(8,128)(2,1)}), f16[8,16,16,128]{3,2,1,0:T(8,128)(2,1)S(1)}, u32[]{:S(2)}, u32[]{:S(2)}) async-start(f16[8,16,16,128]{3,2,1,0:T(8,128)(2,1)} %fusion.6), calls=%async_computation.1 | async-start | bytes 1048576 | tf_op jit(solution)/shard_map/all_to_all | solution.py:222

commit v3 on v1

v3 whole, which is shorter than its diff:
```python
import functools

import jax
import jax.numpy as jnp
from jax import lax
from jax.experimental import pallas as pl
from jax.experimental.pallas import tpu as pltpu
from jax.sharding import PartitionSpec as P

STEP_WEIGHT = 0.5
F32 = jnp.float32
BF16 = jnp.bfloat16
LINK = jnp.float16
VMEM = pl.BlockSpec(memory_space=pltpu.VMEM)
SMEM = pl.BlockSpec(memory_space=pltpu.SMEM)


def doubled(matrices):
    empty = jnp.zeros_like(matrices)
    upper_half = jnp.concatenate([matrices, empty], axis=-1)
    lower_half = jnp.concatenate([empty, matrices], axis=-1)
    return jnp.concatenate([upper_half, lower_half], axis=-2)


def rotate(parts):
    width = parts.shape[-1] // 2
    return jnp.concatenate([parts[..., width:], -parts[..., :width]], axis=-1)

RINGS = 8
CAP = 3
LOT = 4
SPAN = 2 * CAP * RINGS
FAR = ((4, 0), (3, -1), (-3, 1))
NEAR = ((0, 0), (1, 1), (2, 2), (-1, -1), (-2, -2))
SIBLING = [(i, i ^ 1) for i in range(2 * RINGS * RINGS)]


def device(core, along, across):
    along, across = along % RINGS, across % RINGS
    return along * 16 + across * 2 if core == 0 else across * 16 + along * 2 + 1


def onward(step):
    return [
        (device(c, a, b), device(c, a + step, b)) for c in range(2) for a in range(RINGS) for b in range(RINGS)
    ]


DELIVER = [[device(c, a, b) for b in range(RINGS)] for c in range(2) for a in range(RINGS)]
LISTENERS = [
    [device(c, a + far, b) for far in (0, 4) for b in range(RINGS)] for c in range(2) for a in range(RINGS // 2)
]


def pick_kernel(spot_ref, own_slot, sib_slot, own_ref, sib_ref, *out_refs):
    core, along = spot_ref[0], spot_ref[1]
    far = jnp.where(core == 0, 16, 2)
    near = jnp.where(core == 0, 2, 16)
    count = own_slot.shape[0] // CAP
    for (ahead, _), out_ref in zip(FAR + NEAR, out_refs, strict=True):
        first = lax.rem(along + ahead + RINGS, RINGS) * far + core
        for kind, (slots, store) in enumerate(((own_slot, own_ref), (sib_slot, sib_ref))):
            for c in range(CAP):
                for r in range(RINGS):
                    slot = slots[c * count + first + r * near]
                    out_ref[kind * CAP * RINGS + c * RINGS + r] = store[jnp.maximum(slot, 0)]


def pick(spot, own_slots, sib_slots, own, sib):
    shape = jax.ShapeDtypeStruct((SPAN,) + own.shape[1:], own.dtype)
    return pl.pallas_call(
        pick_kernel,
        in_specs=[SMEM, SMEM, SMEM, VMEM, VMEM],
        out_specs=[VMEM] * len(FAR + NEAR),
        out_shape=[shape] * len(FAR + NEAR),
        compiler_params=pltpu.CompilerParams(vmem_limit_bytes=24 * 2**20),
        cost_estimate=pl.CostEstimate(flops=0, bytes_accessed=10 * 2**20, transcendentals=0),
    )(spot, own_slots, sib_slots, own, sib)


def terms_kernel(sources, modes, windows, spot_ref, list_ref, re_ref, im_ref, *refs):
    flat_refs = refs[:sources]
    wide_ref, ham_ref, rho_ref, out_ref, flat, acc = refs[sources:]
    group, here = spot_ref[0], spot_ref[1]
    share = rho_ref.shape[1]
    width = ham_ref.shape[0]
    pairs = RINGS * windows
    blocks = width // share
    downs, extra, counts = modes, modes + CAP, modes + CAP + modes // LOT + CAP

    def gather(row, carry):
        for n, ref in enumerate(flat_refs):
            flat[n * SPAN + row] = ref[row]
        return carry

    lax.fori_loop(0, SPAN, gather, 0, unroll=8)

    def lot(pair, base):
        entries = [list_ref[base + n, pair] for n in range(LOT)]
        maps = [lax.shift_right_logical(e, 9) for e in entries]
        tiles = [flat[e & 511] for e in entries]
        rows = [
            wide_ref[maps[n], :width, :] + wide_ref[maps[n + 1], width:, :] for n in range(0, LOT, 2)
        ]
        left = jnp.dot(
            jnp.concatenate(rows, axis=1), jnp.concatenate(tiles, axis=0), preferred_element_type=F32
        )
        right = jnp.dot(
            jnp.concatenate(tiles, axis=1),
            jnp.concatenate([wide_ref[m] for m in maps], axis=0),
            preferred_element_type=F32,
        )
        return rotate(left - right)

    together = 8

    def first(index, carry):
        for j in range(together):
            pair = index * together + j
            acc[pair] = lot(pair, 0)
        return carry

    lax.fori_loop(0, pairs // together, first, 0)

    def listed(level, work):
        def some(index, carry):
            found = [list_ref[extra + level, index * 4 + j] for j in range(4)]
            values = [work(jnp.minimum(pair, pairs - 1)) for pair in found]
            for pair, value in zip(found, values, strict=True):
                acc[pair] += value
            return carry

        lax.fori_loop(0, lax.shift_right_logical(list_ref[counts, level] + 3, 2), some, 0)

    def more(level, carry):
        listed(level, lambda pair: lot(pair, level * LOT))
        return carry

    lax.fori_loop(1, modes // LOT, more, 0)

    def lower(t, carry):
        def work(pair):
            entry = list_ref[downs + t, pair]
            mode = lax.shift_right_logical(entry, 9)
            state = flat[entry & 511]
            wide = wide_ref[mode]
            ahead = jnp.dot(wide[:width, :width], state, preferred_element_type=F32)
            after = jnp.dot(state, wide, preferred_element_type=F32)
            return re_ref[mode] * rotate(ahead - after) + im_ref[mode] * (ahead + after)

        listed(modes // LOT + t, work)
        return carry

    lax.fori_loop(0, CAP, lower, 0)

    if sources == len(NEAR):

        def local(w, carry):
            acc[here * windows + w] += rotate(
                jnp.dot(ham_ref[...], rho_ref[w], preferred_element_type=F32)
            )
            return carry

        lax.fori_loop(0, windows, local, 0)

    def leave(r, carry):
        for w in range(windows):
            value = acc[r * windows + w]
            for b in range(blocks):
                out_ref[lax.rem(b - group + blocks, blocks), r, w] = value[b * share:(b + 1) * share]
        return carry

    lax.fori_loop(0, RINGS, leave, 0)


def terms(spot, lists, coup_re, coup_im, pieces, maps_wide, head_cols, rho):
    modes = maps_wide.shape[0] - 1
    windows, share, lanes = rho.shape
    width = head_cols.shape[0]
    return pl.pallas_call(
        functools.partial(terms_kernel, len(pieces), modes, windows),
        in_specs=[SMEM] * 4 + [VMEM] * (len(pieces) + 3),
        out_specs=VMEM,
        out_shape=jax.ShapeDtypeStruct((width // share, RINGS, windows, share, lanes), F32),
        scratch_shapes=[
            pltpu.VMEM((len(pieces) * SPAN, width, lanes), BF16),
            pltpu.VMEM((RINGS * windows + 1, width, lanes), F32),
        ],
        compiler_params=pltpu.CompilerParams(vmem_limit_bytes=28 * 2**20),
        cost_estimate=pl.CostEstimate(flops=10**9, bytes_accessed=10 * 2**20, transcendentals=0),
    )(spot, lists, coup_re, coup_im, *pieces, maps_wide, head_cols, rho)


def use_lists(steps, target, core, along, across, group, modes, heard):
    half = (along // 4 + target // 4) % 2
    heard = lax.dynamic_index_in_dim(heard.reshape((2, RINGS) + heard.shape[1:]), half, 0, keepdims=False)
    windows = heard.shape[-1]
    pairs = RINGS * windows
    heard = jnp.transpose(heard, (1, 0, 2)).reshape(-1, pairs)
    receiver = jnp.arange(pairs, dtype=jnp.int32) // windows

    def locate(places):
        owner = places // CAP
        z, y, c = owner // 16, (owner // 2) % RINGS, owner % 2
        off = (jnp.where(core == 0, z, y) - along) % RINGS
        source = jnp.full_like(off, -1)
        for n, (_, step) in enumerate(steps):
            source = jnp.where(off == -step % RINGS, n, source)
        mine = (jnp.where(core == 0, y, z) == across) & (source >= 0)
        kind = jnp.where(c == core, 0, 1)
        return mine, ((source * 2 + kind) * CAP + places % CAP) * RINGS + receiver

    mine, row = locate(heard[:modes])
    ids = jnp.arange(modes, dtype=jnp.int32)
    below = (ids[:, None] > ids[None, :]).astype(F32)
    rank = jnp.dot(below, mine.astype(F32), preferred_element_type=F32).astype(jnp.int32)
    count = jnp.sum(mine.astype(jnp.int32), axis=0)
    value = ids[:, None] * 512 + row - modes * 512
    hit = mine[None] & (rank[None] == ids[:, None, None])
    up = modes * 512 + jnp.sum(jnp.where(hit, value[None], 0), axis=1)

    mine, row = locate(heard[modes:modes + CAP])
    local = heard[modes + CAP:modes + 2 * CAP] - group * modes
    live = mine & (local >= 0) & (local < modes)
    down = jnp.where(live, local * 512 + row, 0)

    levels = jnp.arange(modes // LOT, dtype=jnp.int32) * LOT
    flags = jnp.concatenate([count[None, :] > levels[:, None], live], axis=0)
    lanes = jnp.arange(pairs, dtype=jnp.int32)
    ahead = (lanes[:, None] < lanes[None, :]).astype(F32)
    order = jnp.dot(flags.astype(F32), ahead, preferred_element_type=F32).astype(jnp.int32)
    hit = flags[:, None, :] & (order[:, None, :] == lanes[None, :, None])
    listed = pairs + jnp.sum(jnp.where(hit, lanes - pairs, 0), axis=2)
    totals = jnp.sum(flags.astype(jnp.int32), axis=1)
    totals = jnp.pad(totals, (0, pairs - totals.shape[0]))[None]
    return jnp.concatenate([up, down, listed, totals], axis=0)


def over_groups(parts):
    count = parts.shape[0]
    total = parts[0]
    for shift in (2, 1, 3):
        ring = [(i, (i + shift) % count) for i in range(count)]
        total = total + lax.ppermute(parts[shift].astype(LINK), "grp", ring).astype(F32)
    return total


def on_device(
    states, send_slot, window_tier_states, modes_tri, use_up, use_down,
    hamiltonian, coupling, coup_re, coup_im, decay_rate,
):
    width = hamiltonian.shape[0]
    share = window_tier_states.shape[1]
    modes = coupling.shape[0]
    group = lax.axis_index("grp").astype(jnp.int32)
    index = lax.axis_index("ado").astype(jnp.int32)
    core, z, y = index & 1, index >> 4, (index >> 1) & 7
    along = jnp.where(core == 0, z, y)
    across = jnp.where(core == 0, y, z)

    slots = jnp.transpose(send_slot[0, 0]).reshape(-1)
    sib_store = lax.ppermute(states[0, 0], "ado", SIBLING)
    sib_slots = lax.ppermute(slots, "ado", SIBLING)
    said = jnp.concatenate([use_up.T, use_down.T, modes_tri.T], axis=0)
    heard = lax.all_gather(said, "ado", axis_index_groups=LISTENERS, axis=0, tiled=False)
    slots, heard = lax.optimization_barrier((slots, heard))
    picked = pick(jnp.stack([core, along]), slots, sib_slots, states[0, 0], sib_store)

    def send(steps, blocks):
        return [
            block if step == 0 else lax.ppermute(block, "ado", onward(step))
            for (_, step), block in zip(steps, blocks, strict=True)
        ]

    far_states = send(FAR, picked[:len(FAR)])
    near_states = send(NEAR, picked[len(FAR):])
    where = (core, along, across, group, modes, heard)
    far_lists = use_lists(FAR, 4, *where)
    near_lists = use_lists(NEAR, 0, *where)

    maps_wide = jnp.concatenate([doubled(coupling), jnp.zeros((1, 2 * width, 2 * width), BF16)], axis=0)
    head_cols = lax.dynamic_slice_in_dim(hamiltonian, group * share, share, 1)
    spot = jnp.stack([group, across])
    shared = (maps_wide, head_cols, window_tier_states)
    far = over_groups(terms(spot, far_lists, coup_re, coup_im, far_states, *shared))
    far = lax.ppermute(far.astype(LINK), "ado", onward(4))
    near = over_groups(terms(spot, near_lists, coup_re, coup_im, near_states, *shared))
    summed = lax.all_to_all(
        (near + far.astype(F32)).astype(LINK), "ado", split_axis=0, concat_axis=0, tiled=True,
        axis_index_groups=DELIVER,
    )

    ham_wide = doubled(hamiltonian)
    right_part = jnp.einsum("wab,bc->wac", window_tier_states, ham_wide, preferred_element_type=F32)
    every_mode = jnp.arange(decay_rate.shape[0], dtype=jnp.int32)
    hits = modes_tri[:, :, None] == every_mode
    damping = jnp.sum(jnp.where(hits, decay_rate, 0.0), axis=(1, 2))
    own = rotate(right_part) + damping[:, None, None] * window_tier_states.astype(F32)
    return STEP_WEIGHT * (jnp.sum(summed.astype(F32), axis=0) - own)


def solution(mesh):
    in_specs = (
        P("grp", "ado", None, None, None),
        P("grp", "ado", None, None),
        P("ado", "grp", None),
        P("ado", None),
        P("ado", "grp"),
        P("ado", None),
        P(),
        P("grp", None, None),
        P("grp"),
        P("grp"),
        P(),
    )
    out_specs = P("ado", "grp", None)
    return jax.shard_map(
        on_device, mesh=mesh, in_specs=in_specs, out_specs=out_specs, check_vma=False
    )
```

time: 222 us -> 190 us (0.86)
  the two profiles are of different devices: /device:TPU:30 before, /device:TPU:2 now
where the time goes in v3:
time: 190 us
  blocking collectives  58.2 us (31%)
  starting transfers between devices  56 us (29%)
  waiting for transfers between devices  33.7 us (18%)
  Pallas kernels  25.9 us (14%)
  other arithmetic  8.67 us (5%)
  local copies, waits for them, and re-layouts  5.73 us (3%)
    all_gather x1, blocking collectives, on_device(): lax.all_gather(said, 'ado', axis_index_groups=LISTENERS, axis=0, tiled=Fa...  58.2 us
    pallas_call x2, Pallas kernels, terms(): pl.pallas_call(functools.partial(terms_kernel, len(pieces), modes, window...  23.6 us
    ppermute x6, starting transfers between devices, over_groups(): lax.ppermute(parts[shift].astype(LINK), 'grp', ring).astype(F32)  20.6 us
    ppermute x6, starting transfers between devices, send(): lax.ppermute(block, 'ado', onward(step))  19.6 us
    all_to_all x1, waiting for transfers between devices, on_device(): lax.all_to_all((near + far.astype(F32)).astype(LINK), 'ado', split_axis=0...  12.7 us
    ppermute x1, waiting for transfers between devices, on_device(): far = lax.ppermute(far.astype(LINK), 'ado', onward(4))  12.5 us
    ppermute x1, starting transfers between devices, on_device(): far = lax.ppermute(far.astype(LINK), 'ado', onward(4))  8 us
    ppermute x6, waiting for transfers between devices, send(): lax.ppermute(block, 'ado', onward(step))  4.72 us
  transfers between devices with their start and end apart: 16, of which 5 were waited for; matrix products, arithmetic and copies ran while one was open for 7% of the time, Pallas kernels for 12%

profile of v3, /device:TPU:2, one launch (start us, length us, event | category | flops | bytes accessed | tf_op | source)
XLA Modules:
  0.0 189.6 jit_solution(12514596690991723344)
XLA Ops:
  0.0 0.7 copy.91
  0.7 1.9 %collective-permute-start = (s32[384]{0:T(512)S(1)}, s32[384]{0:T(512)S(1)}, u32[]{:S(2)}, u32[]{:S(2)}) collective-permute-start(s32[384]{0:T(512)S(1)} %bitcast.150), channel_id=1, source_target_pairs={{0,1},{1,0},{2,3},{3,2},{4,5},{5,4},{6,7},{7,6},{8,9},{9,8},{10,11... | collective-permute-start | bytes 4616 | tf_op jit(solution)/shard_map/ppermute | solution.py:263
  2.6 2.4 %collective-permute-start.1 = (bf16[128,64,128]{2,1,0:T(8,128)(2,1)}, bf16[128,64,128]{2,1,0:T(8,128)(2,1)}, u32[]{:S(2)}, u32[]{:S(2)}) collective-permute-start(bf16[128,64,128]{2,1,0:T(8,128)(2,1)} %bitcast.148), channel_id=1, source_target_pairs={{0,1},{1,0},{2,3},{3,2},{4,5},{5,4},{6,7},{7,6},{8,9},{9,8},{10,11... | collective-permute-start | bytes 6291464 | tf_op jit(solution)/shard_map/ppermute | solution.py:262
  5.1 0.8 copy.74
  5.9 0.8 copy.73
  6.6 0.8 add_bitcast_fusion
  7.4 58.2 %all-gather.1 = s32[16,38,16]{1,2,0:T(8,128)S(1)} all-gather(s32[1,38,16]{1,2,0:T(8,128)S(1)} %add_bitcast_fusion), channel_id=2, replica_groups={{0,2,4,6,8,10,12,14,64,66,68,70,72,74,76,78},{16,18,20,22,24,26,28,30,8..., dimensions={0}, use_global_device_ids=true | all-gather | bytes 41344 | tf_op jit(solution)/shard_map/all_gather | solution.py:265
  65.7 0.1 copy.88
  67.0 0.8 slice_divide_fusion
  68.7 0.2 fusion.51
  68.9 0.4 fusion.49
  69.7 0.1 convolution_convert_fusion.2
  70.0 0.1 convolution_convert_fusion
  70.1 0.2 fusion.50
  70.4 0.1 convolution_convert_fusion.1
  70.7 1.5 fusion.2
  72.3 0.5 select_reduce_fusion
  73.3 2.3 %shard_map.109 = (bf16[48,64,128]{2,1,0:T(8,128)(2,1)S(1)}, bf16[48,64,128]{2,1,0:T(8,128)(2,1)S(1)}, bf16[48,64,128]{2,1,0:T(8,128)(2,1)S(1)}, bf16[48,64,128]{...) custom-call(s32[2]{0:T(128)S(1)} %pad_add_fusion.5.spot_ref, ...), custom_call_target="tpu_custom_call" | custom-call | bytes 10485760 | tf_op jit(solution)/shard_map/pallas_call | solution.py:71
  75.5 1.9 %collective-permute-start.9 = (bf16[48,64,128]{2,1,0:T(8,128)(2,1)S(1)}, bf16[48,64,128]{2,1,0:T(8,128)(2,1)S(1)}, u32[]{:S(2)}, u32[]{:S(2)}) collective-permute-start(bf16[48,64,128]{2,1,0:T(8,128)(2,1)S(1)} %get-tuple-element.23), channel_id=1, source_target_pairs={{0,112},{2,114},{4,116},{6,118},{8,120},{10,122},{12,124},{14,126}... | collective-permute-start | bytes 2359304 | tf_op jit(solution)/shard_map/ppermute | solution.py:271
  77.5 3.9 %collective-permute-start.10 = (bf16[48,64,128]{2,1,0:T(8,128)(2,1)S(1)}, bf16[48,64,128]{2,1,0:T(8,128)(2,1)S(1)}, u32[]{:S(2)}, u32[]{:S(2)}) collective-permute-start(bf16[48,64,128]{2,1,0:T(8,128)(2,1)S(1)} %get-tuple-element.24), channel_id=1, source_target_pairs={{0,16},{2,18},{4,20},{6,22},{8,24},{10,26},{12,28},{14,30},{16,32}... | collective-permute-start | bytes 2359304 | tf_op jit(solution)/shard_map/ppermute | solution.py:271
  81.6 2.9 %collective-permute-start.2 = (bf16[48,64,128]{2,1,0:T(8,128)(2,1)S(1)}, bf16[48,64,128]{2,1,0:T(8,128)(2,1)S(1)}, u32[]{:S(2)}, u32[]{:S(2)}) collective-permute-start(bf16[48,64,128]{2,1,0:T(8,128)(2,1)S(1)} %get-tuple-element.18), channel_id=1, source_target_pairs={{0,16},{2,18},{4,20},{6,22},{8,24},{10,26},{12,28},{14,30},{16,32}... | collective-permute-start | bytes 2359304 | tf_op jit(solution)/shard_map/ppermute | solution.py:271
  84.6 5.5 %collective-permute-start.3 = (bf16[48,64,128]{2,1,0:T(8,128)(2,1)S(1)}, bf16[48,64,128]{2,1,0:T(8,128)(2,1)S(1)}, u32[]{:S(2)}, u32[]{:S(2)}) collective-permute-start(bf16[48,64,128]{2,1,0:T(8,128)(2,1)S(1)} %get-tuple-element.19), channel_id=1, source_target_pairs={{0,32},{2,34},{4,36},{6,38},{8,40},{10,42},{12,44},{14,46},{16,48}... | collective-permute-start | bytes 2359304 | tf_op jit(solution)/shard_map/ppermute | solution.py:271
  90.1 2.8 %collective-permute-start.4 = (bf16[48,64,128]{2,1,0:T(8,128)(2,1)S(1)}, bf16[48,64,128]{2,1,0:T(8,128)(2,1)S(1)}, u32[]{:S(2)}, u32[]{:S(2)}) collective-permute-start(bf16[48,64,128]{2,1,0:T(8,128)(2,1)S(1)} %get-tuple-element.20), channel_id=1, source_target_pairs={{0,112},{2,114},{4,116},{6,118},{8,120},{10,122},{12,124},{14,126}... | collective-permute-start | bytes 2359304 | tf_op jit(solution)/shard_map/ppermute | solution.py:271
  92.9 2.5 %collective-permute-start.5 = (bf16[48,64,128]{2,1,0:T(8,128)(2,1)S(1)}, bf16[48,64,128]{2,1,0:T(8,128)(2,1)S(1)}, u32[]{:S(2)}, u32[]{:S(2)}) collective-permute-start(bf16[48,64,128]{2,1,0:T(8,128)(2,1)S(1)} %get-tuple-element.21), channel_id=1, source_target_pairs={{0,96},{2,98},{4,100},{6,102},{8,104},{10,106},{12,108},{14,110},{... | collective-permute-start | bytes 2359304 | tf_op jit(solution)/shard_map/ppermute | solution.py:271
  95.5 9.3 %shard_map.111 = f32[4,8,16,16,128]{4,3,2,1,0:T(8,128)S(1)} custom-call(s32[2]{0:T(128)S(1)} %pad_add_fusion.4.spot_ref, s32[47,128]{1,0:T(8,128)S(1)} %pad_add_fusion.1.list_ref, f32[32]{0:T(128)S(1)} %copy-done.2, f32[32]{0:T(128)S(1)} %copy-done.3, bf16[48,64,128]{2,1,0:T(8,128)(2,1)S(1)} %get-tuple-element.22.refs_0_, ...), custom_call_target="tpu_custom_call" | custom-call | flops 1000000000 | bytes 10485760 | tf_op jit(solution)/shard_map/pallas_call | solution.py:180
  104.8 0.4 convert.11
  105.3 0.4 slice_bitcast_fusion.4
  105.7 2.5 %collective-permute-start.13 = (f16[8,16,16,128]{3,2,1,0:T(8,128)(2,1)S(1)}, f16[8,16,16,128]{3,2,1,0:T(8,128)(2,1)S(1)}, u32[]{:S(2)}, u32[]{:S(2)}) collective-permute-start(f16[8,16,16,128]{3,2,1,0:T(8,128)(2,1)S(1)} %get-tuple-element.39), channel_id=1, source_target_pairs={{0,384},{128,0},{256,128},{384,256},{1,385},{129,1},{257,129},{385... | collective-permute-start | bytes 1572872 | tf_op jit(solution)/shard_map/ppermute | solution.py:244
  108.2 3.4 %collective-permute-start.12 = (f16[8,16,16,128]{3,2,1,0:T(8,128)(2,1)S(1)}, f16[8,16,16,128]{3,2,1,0:T(8,128)(2,1)S(1)}, u32[]{:S(2)}, u32[]{:S(2)}) collective-permute-start(f16[8,16,16,128]{3,2,1,0:T(8,128)(2,1)S(1)} %get-tuple-element.40), channel_id=1, source_target_pairs={{0,128},{128,256},{256,384},{384,0},{1,129},{129,257},{257,385},{3... | collective-permute-start | bytes 1572872 | tf_op jit(solution)/shard_map/ppermute | solution.py:244
  111.5 3.8 %collective-permute-done.3.refs_2_ = bf16[48,64,128]{2,1,0:T(8,128)(2,1)S(1)} collective-permute-done((bf16[48,64,128]{2,1,0:T(8,128)(2,1)S(1)}, bf16[48,64,128]{2,1,0:T(8,128)(2,1)S(1)}, u32[]{:S(2)}, u32[]{:S(2)}) %collective-permute-start.3) | collective-permute-done | bytes 786464 | tf_op jit(solution)/shard_map/ppermute | solution.py:271
  115.4 4.0 %collective-permute-start.11 = (f16[8,16,16,128]{3,2,1,0:T(8,128)(2,1)S(1)}, f16[8,16,16,128]{3,2,1,0:T(8,128)(2,1)S(1)}, u32[]{:S(2)}, u32[]{:S(2)}) collective-permute-start(f16[8,16,16,128]{3,2,1,0:T(8,128)(2,1)S(1)} %get-tuple-element.38), channel_id=1, source_target_pairs={{0,256},{128,384},{256,0},{384,128},{1,257},{129,385},{257,1},{385... | collective-permute-start | bytes 1572872 | tf_op jit(solution)/shard_map/ppermute | solution.py:244
  119.4 0.9 collective-permute-done.5.refs_4_
  120.3 14.3 %shard_map.110 = f32[4,8,16,16,128]{4,3,2,1,0:T(8,128)S(1)} custom-call(s32[2]{0:T(128)S(1)} %pad_add_fusion.4.spot_ref, s32[47,128]{1,0:T(8,128)S(1)} %pad_add_fusion.list_ref, f32[32]{0:T(128)S(1)} %copy-done.2, f32[32]{0:T(128)S(1)} %copy-done.3, bf16[48,64,128]{2,1,0:T(8,128)(2,1)S(1)} %get-tuple-element.17.refs_0_, ...), custom_call_target="tpu_custom_call" | custom-call | flops 1000000000 | bytes 10485760 | tf_op jit(solution)/shard_map/pallas_call | solution.py:180
  134.6 0.4 convert.10
  135.0 0.4 slice_bitcast_fusion.7
  135.5 1.9 %collective-permute-start.8 = (f16[8,16,16,128]{3,2,1,0:T(8,128)(2,1)S(1)}, f16[8,16,16,128]{3,2,1,0:T(8,128)(2,1)S(1)}, u32[]{:S(2)}, u32[]{:S(2)}) collective-permute-start(f16[8,16,16,128]{3,2,1,0:T(8,128)(2,1)S(1)} %get-tuple-element.36), channel_id=1, source_target_pairs={{0,384},{128,0},{256,128},{384,256},{1,385},{129,1},{257,129},{385... | collective-permute-start | bytes 1572872 | tf_op jit(solution)/shard_map/ppermute | solution.py:244
  137.4 3.9 %collective-permute-start.7 = (f16[8,16,16,128]{3,2,1,0:T(8,128)(2,1)S(1)}, f16[8,16,16,128]{3,2,1,0:T(8,128)(2,1)S(1)}, u32[]{:S(2)}, u32[]{:S(2)}) collective-permute-start(f16[8,16,16,128]{3,2,1,0:T(8,128)(2,1)S(1)} %get-tuple-element.37), channel_id=1, source_target_pairs={{0,128},{128,256},{256,384},{384,0},{1,129},{129,257},{257,385},{3... | collective-permute-start | bytes 1572872 | tf_op jit(solution)/shard_map/ppermute | solution.py:244
  141.4 4.9 %collective-permute-start.6 = (f16[8,16,16,128]{3,2,1,0:T(8,128)(2,1)S(1)}, f16[8,16,16,128]{3,2,1,0:T(8,128)(2,1)S(1)}, u32[]{:S(2)}, u32[]{:S(2)}) collective-permute-start(f16[8,16,16,128]{3,2,1,0:T(8,128)(2,1)S(1)} %get-tuple-element.35), channel_id=1, source_target_pairs={{0,256},{128,384},{256,0},{384,128},{1,257},{129,385},{257,1},{385... | collective-permute-start | bytes 1572872 | tf_op jit(solution)/shard_map/ppermute | solution.py:244
  146.3 0.3 fusion.6
  146.6 8.0 %collective-permute-start.14 = (f16[8,16,16,128]{3,2,1,0:T(8,128)(2,1)S(1)}, f16[8,16,16,128]{3,2,1,0:T(8,128)(2,1)S(1)}, u32[]{:S(2)}, u32[]{:S(2)}) collective-permute-start(f16[8,16,16,128]{3,2,1,0:T(8,128)(2,1)S(1)} %fusion.6), channel_id=1, source_target_pairs={{0,64},{2,66},{4,68},{6,70},{8,72},{10,74},{12,76},{14,78},{16,80}... | collective-permute-start | bytes 1572872 | tf_op jit(solution)/shard_map/ppermute | solution.py:286
  154.6 3.7 %collective-permute-done.6 = f16[8,16,16,128]{3,2,1,0:T(8,128)(2,1)S(1)} collective-permute-done((f16[8,16,16,128]{3,2,1,0:T(8,128)(2,1)S(1)}, f16[8,16,16,128]{3,2,1,0:T(8,128)(2,1)S(1)}, u32[]{:S(2)}, u32[]{:S(2)}) %collective-permute-start.6) | collective-permute-done | bytes 524320 | tf_op jit(solution)/shard_map/ppermute | solution.py:244
  158.4 12.5 %collective-permute-done.14 = f16[8,16,16,128]{3,2,1,0:T(8,128)(2,1)S(1)} collective-permute-done((f16[8,16,16,128]{3,2,1,0:T(8,128)(2,1)S(1)}, f16[8,16,16,128]{3,2,1,0:T(8,128)(2,1)S(1)}, u32[]{:S(2)}, u32[]{:S(2)}) %collective-permute-start.14) | collective-permute-done | bytes 524320 | tf_op jit(solution)/shard_map/ppermute | solution.py:286
  170.9 1.2 fusion.11
  172.0 3.5 %all-to-all-start = ((f16[8,16,16,128]{3,2,1,0:T(8,128)(2,1)}), f16[8,16,16,128]{3,2,1,0:T(8,128)(2,1)S(1)}, u32[]{:S(2)}, u32[]{:S(2)}) async-start(f16[8,16,16,128]{3,2,1,0:T(8,128)(2,1)} %fusion.11), calls=%async_computation | async-start | bytes 1048576 | tf_op jit(solution)/shard_map/all_to_all | solution.py:288
  175.6 0.2 select_reduce_fusion.4
  175.7 0.2 convolution_bitcast_fusion
  176.1 12.7 %all-to-all-done = f16[8,16,16,128]{3,2,1,0:T(8,128)(2,1)S(1)} async-done(((f16[8,16,16,128]{3,2,1,0:T(8,128)(2,1)}), f16[8,16,16,128]{3,2,1,0:T(8,128)(2,1)S(1)}, u32[]{:S(2)}, u32[]{:S(2)}) %all-to-all-start) | async-done | bytes 524320 | tf_op jit(solution)/shard_map/all_to_all | solution.py:288
  188.8 0.8 fusion.25
  (80 shorter events, 3.8 us)
Async XLA Ops:
  0.0 70.5 %copy-start.4 = (bf16[64,64]{1,0:T(8,128)(2,1)S(1)}, bf16[64,64]{1,0:T(8,128)(2,1)}, u32[]{:S(2)}) copy-start(bf16[64,64]{1,0:T(8,128)(2,1)} %param.17) | copy-start | bytes 24580
  0.7 72.5 %collective-permute-start = (s32[384]{0:T(512)S(1)}, s32[384]{0:T(512)S(1)}, u32[]{:S(2)}, u32[]{:S(2)}) collective-permute-start(s32[384]{0:T(512)S(1)} %bitcast.150), channel_id=1, source_target_pairs={{0,1},{1,0},{2,3},{3,2},{4,5},{5,4},{6,7},{7,6},{8,9},{9,8},{10,11... | collective-permute-start | bytes 4616 | tf_op jit(solution)/shard_map/ppermute | solution.py:263
  2.6 70.6 %collective-permute-start.1 = (bf16[128,64,128]{2,1,0:T(8,128)(2,1)}, bf16[128,64,128]{2,1,0:T(8,128)(2,1)}, u32[]{:S(2)}, u32[]{:S(2)}) collective-permute-start(bf16[128,64,128]{2,1,0:T(8,128)(2,1)} %bitcast.148), channel_id=1, source_target_pairs={{0,1},{1,0},{2,3},{3,2},{4,5},{5,4},{6,7},{7,6},{8,9},{9,8},{10,11... | collective-permute-start | bytes 6291464 | tf_op jit(solution)/shard_map/ppermute | solution.py:262
  70.0 3.2 %copy-start = (bf16[1,1,128,64,128]{4,3,2,1,0:T(8,128)(2,1)S(1)}, bf16[1,1,128,64,128]{4,3,2,1,0:T(8,128)(2,1)}, u32[]{:S(2)}) copy-start(bf16[1,1,128,64,128]{4,3,2,1,0:T(8,128)(2,1)} %param.11) | copy-start | bytes 6291460
  73.2 22.3 %copy-start.1 = (bf16[16,16,128]{2,1,0:T(8,128)(2,1)S(1)}, bf16[16,16,128]{2,1,0:T(8,128)(2,1)}, u32[]{:S(2)}) copy-start(bf16[16,16,128]{2,1,0:T(8,128)(2,1)} %refs_5_.1) | copy-start | bytes 196612
  73.2 22.3 %copy-start.2 = (f32[32]{0:T(128)S(1)}, f32[32]{0:T(128)}, u32[]{:S(2)}) copy-start(f32[32]{0:T(128)} %re_ref.3) | copy-start | bytes 388
  73.2 22.3 %copy-start.3 = (f32[32]{0:T(128)S(1)}, f32[32]{0:T(128)}, u32[]{:S(2)}) copy-start(f32[32]{0:T(128)} %im_ref.3) | copy-start | bytes 388
  75.5 17.4 %collective-permute-start.9 = (bf16[48,64,128]{2,1,0:T(8,128)(2,1)S(1)}, bf16[48,64,128]{2,1,0:T(8,128)(2,1)S(1)}, u32[]{:S(2)}, u32[]{:S(2)}) collective-permute-start(bf16[48,64,128]{2,1,0:T(8,128)(2,1)S(1)} %get-tuple-element.23), channel_id=1, source_target_pairs={{0,112},{2,114},{4,116},{6,118},{8,120},{10,122},{12,124},{14,126}... | collective-permute-start | bytes 2359304 | tf_op jit(solution)/shard_map/ppermute | solution.py:271
  77.5 18.0 %collective-permute-start.10 = (bf16[48,64,128]{2,1,0:T(8,128)(2,1)S(1)}, bf16[48,64,128]{2,1,0:T(8,128)(2,1)S(1)}, u32[]{:S(2)}, u32[]{:S(2)}) collective-permute-start(bf16[48,64,128]{2,1,0:T(8,128)(2,1)S(1)} %get-tuple-element.24), channel_id=1, source_target_pairs={{0,16},{2,18},{4,20},{6,22},{8,24},{10,26},{12,28},{14,30},{16,32}... | collective-permute-start | bytes 2359304 | tf_op jit(solution)/shard_map/ppermute | solution.py:271
  81.6 26.5 %collective-permute-start.2 = (bf16[48,64,128]{2,1,0:T(8,128)(2,1)S(1)}, bf16[48,64,128]{2,1,0:T(8,128)(2,1)S(1)}, u32[]{:S(2)}, u32[]{:S(2)}) collective-permute-start(bf16[48,64,128]{2,1,0:T(8,128)(2,1)S(1)} %get-tuple-element.18), channel_id=1, source_target_pairs={{0,16},{2,18},{4,20},{6,22},{8,24},{10,26},{12,28},{14,30},{16,32}... | collective-permute-start | bytes 2359304 | tf_op jit(solution)/shard_map/ppermute | solution.py:271
  84.6 30.8 %collective-permute-start.3 = (bf16[48,64,128]{2,1,0:T(8,128)(2,1)S(1)}, bf16[48,64,128]{2,1,0:T(8,128)(2,1)S(1)}, u32[]{:S(2)}, u32[]{:S(2)}) collective-permute-start(bf16[48,64,128]{2,1,0:T(8,128)(2,1)S(1)} %get-tuple-element.19), channel_id=1, source_target_pairs={{0,32},{2,34},{4,36},{6,38},{8,40},{10,42},{12,44},{14,46},{16,48}... | collective-permute-start | bytes 2359304 | tf_op jit(solution)/shard_map/ppermute | solution.py:271
  90.1 29.3 %collective-permute-start.4 = (bf16[48,64,128]{2,1,0:T(8,128)(2,1)S(1)}, bf16[48,64,128]{2,1,0:T(8,128)(2,1)S(1)}, u32[]{:S(2)}, u32[]{:S(2)}) collective-permute-start(bf16[48,64,128]{2,1,0:T(8,128)(2,1)S(1)} %get-tuple-element.20), channel_id=1, source_target_pairs={{0,112},{2,114},{4,116},{6,118},{8,120},{10,122},{12,124},{14,126}... | collective-permute-start | bytes 2359304 | tf_op jit(solution)/shard_map/ppermute | solution.py:271
  92.9 27.4 %collective-permute-start.5 = (bf16[48,64,128]{2,1,0:T(8,128)(2,1)S(1)}, bf16[48,64,128]{2,1,0:T(8,128)(2,1)S(1)}, u32[]{:S(2)}, u32[]{:S(2)}) collective-permute-start(bf16[48,64,128]{2,1,0:T(8,128)(2,1)S(1)} %get-tuple-element.21), channel_id=1, source_target_pairs={{0,96},{2,98},{4,100},{6,102},{8,104},{10,106},{12,108},{14,110},{... | collective-permute-start | bytes 2359304 | tf_op jit(solution)/shard_map/ppermute | solution.py:271
  105.7 35.7 %collective-permute-start.13 = (f16[8,16,16,128]{3,2,1,0:T(8,128)(2,1)S(1)}, f16[8,16,16,128]{3,2,1,0:T(8,128)(2,1)S(1)}, u32[]{:S(2)}, u32[]{:S(2)}) collective-permute-start(f16[8,16,16,128]{3,2,1,0:T(8,128)(2,1)S(1)} %get-tuple-element.39), channel_id=1, source_target_pairs={{0,384},{128,0},{256,128},{384,256},{1,385},{129,1},{257,129},{385... | collective-permute-start | bytes 1572872 | tf_op jit(solution)/shard_map/ppermute | solution.py:244
  108.2 38.1 %collective-permute-start.12 = (f16[8,16,16,128]{3,2,1,0:T(8,128)(2,1)S(1)}, f16[8,16,16,128]{3,2,1,0:T(8,128)(2,1)S(1)}, u32[]{:S(2)}, u32[]{:S(2)}) collective-permute-start(f16[8,16,16,128]{3,2,1,0:T(8,128)(2,1)S(1)} %get-tuple-element.40), channel_id=1, source_target_pairs={{0,128},{128,256},{256,384},{384,0},{1,129},{129,257},{257,385},{3... | collective-permute-start | bytes 1572872 | tf_op jit(solution)/shard_map/ppermute | solution.py:244
  115.4 30.9 %collective-permute-start.11 = (f16[8,16,16,128]{3,2,1,0:T(8,128)(2,1)S(1)}, f16[8,16,16,128]{3,2,1,0:T(8,128)(2,1)S(1)}, u32[]{:S(2)}, u32[]{:S(2)}) collective-permute-start(f16[8,16,16,128]{3,2,1,0:T(8,128)(2,1)S(1)} %get-tuple-element.38), channel_id=1, source_target_pairs={{0,256},{128,384},{256,0},{384,128},{1,257},{129,385},{257,1},{385... | collective-permute-start | bytes 1572872 | tf_op jit(solution)/shard_map/ppermute | solution.py:244
  135.5 19.1 %collective-permute-start.8 = (f16[8,16,16,128]{3,2,1,0:T(8,128)(2,1)S(1)}, f16[8,16,16,128]{3,2,1,0:T(8,128)(2,1)S(1)}, u32[]{:S(2)}, u32[]{:S(2)}) collective-permute-start(f16[8,16,16,128]{3,2,1,0:T(8,128)(2,1)S(1)} %get-tuple-element.36), channel_id=1, source_target_pairs={{0,384},{128,0},{256,128},{384,256},{1,385},{129,1},{257,129},{385... | collective-permute-start | bytes 1572872 | tf_op jit(solution)/shard_map/ppermute | solution.py:244
  137.4 17.2 %collective-permute-start.7 = (f16[8,16,16,128]{3,2,1,0:T(8,128)(2,1)S(1)}, f16[8,16,16,128]{3,2,1,0:T(8,128)(2,1)S(1)}, u32[]{:S(2)}, u32[]{:S(2)}) collective-permute-start(f16[8,16,16,128]{3,2,1,0:T(8,128)(2,1)S(1)} %get-tuple-element.37), channel_id=1, source_target_pairs={{0,128},{128,256},{256,384},{384,0},{1,129},{129,257},{257,385},{3... | collective-permute-start | bytes 1572872 | tf_op jit(solution)/shard_map/ppermute | solution.py:244
  141.4 17.0 %collective-permute-start.6 = (f16[8,16,16,128]{3,2,1,0:T(8,128)(2,1)S(1)}, f16[8,16,16,128]{3,2,1,0:T(8,128)(2,1)S(1)}, u32[]{:S(2)}, u32[]{:S(2)}) collective-permute-start(f16[8,16,16,128]{3,2,1,0:T(8,128)(2,1)S(1)} %get-tuple-element.35), channel_id=1, source_target_pairs={{0,256},{128,384},{256,0},{384,128},{1,257},{129,385},{257,1},{385... | collective-permute-start | bytes 1572872 | tf_op jit(solution)/shard_map/ppermute | solution.py:244
  146.6 29.0 %copy-start.5 = (s32[16,3]{0,1:T(4,128)S(1)}, s32[16,3]{0,1:T(4,128)}, u32[]{:S(2)}) copy-start(s32[16,3]{0,1:T(4,128)} %param.14) | copy-start | bytes 580
  146.6 29.0 %copy-start.6 = (f32[128]{0:T(128)S(1)}, f32[128]{0:T(128)}, u32[]{:S(2)}) copy-start(f32[128]{0:T(128)} %param.21) | copy-start | bytes 1540
  146.6 24.3 %collective-permute-start.14 = (f16[8,16,16,128]{3,2,1,0:T(8,128)(2,1)S(1)}, f16[8,16,16,128]{3,2,1,0:T(8,128)(2,1)S(1)}, u32[]{:S(2)}, u32[]{:S(2)}) collective-permute-start(f16[8,16,16,128]{3,2,1,0:T(8,128)(2,1)S(1)} %fusion.6), channel_id=1, source_target_pairs={{0,64},{2,66},{4,68},{6,70},{8,72},{10,74},{12,76},{14,78},{16,80}... | collective-permute-start | bytes 1572872 | tf_op jit(solution)/shard_map/ppermute | solution.py:286
  172.0 16.7 %all-to-all-start = ((f16[8,16,16,128]{3,2,1,0:T(8,128)(2,1)}), f16[8,16,16,128]{3,2,1,0:T(8,128)(2,1)S(1)}, u32[]{:S(2)}, u32[]{:S(2)}) async-start(f16[8,16,16,128]{3,2,1,0:T(8,128)(2,1)} %fusion.11), calls=%async_computation | async-start | bytes 1048576 | tf_op jit(solution)/shard_map/all_to_all | solution.py:288

commit v4 on v3

--- a/solution.py
+++ b/solution.py
@@ -262,8 +262,10 @@
     sib_store = lax.ppermute(states[0, 0], "ado", SIBLING)
     sib_slots = lax.ppermute(slots, "ado", SIBLING)
     said = jnp.concatenate([use_up.T, use_down.T, modes_tri.T], axis=0)
-    heard = lax.all_gather(said, "ado", axis_index_groups=LISTENERS, axis=0, tiled=False)
-    slots, heard = lax.optimization_barrier((slots, heard))
+    said = jnp.broadcast_to(said, (2 * RINGS,) + said.shape)
+    heard = lax.all_to_all(
+        said, "ado", split_axis=0, concat_axis=0, tiled=True, axis_index_groups=LISTENERS
+    )
     picked = pick(jnp.stack([core, along]), slots, sib_slots, states[0, 0], sib_store)
 
     def send(steps, blocks):

time: 190 us -> 186 us (0.979)
  the two profiles are of different devices: /device:TPU:2 before, /device:TPU:64 now
where the time goes in v4:
time: 186 us; the launch traced here: 184 us
  starting transfers between devices  71.6 us (38%)
  waiting for transfers between devices  38.8 us (21%)
  local copies, waits for them, and re-layouts  27.3 us (15%)
  Pallas kernels  25.5 us (14%)
  other arithmetic  19.2 us (10%)
    pallas_call x2, Pallas kernels, terms(): pl.pallas_call(functools.partial(terms_kernel, len(pieces), modes, window...  23.3 us
    ppermute x6, starting transfers between devices, over_groups(): lax.ppermute(parts[shift].astype(LINK), 'grp', ring).astype(F32)  21.6 us
    ppermute x6, starting transfers between devices, send(): lax.ppermute(block, 'ado', onward(step))  19.6 us
    all_to_all x1, starting transfers between devices, on_device(): lax.all_to_all(said, 'ado', split_axis=0, concat_axis=0, tiled=True, axis...  14.8 us
    all_to_all x1, waiting for transfers between devices, on_device(): lax.all_to_all((near + far.astype(F32)).astype(LINK), 'ado', split_axis=0...  12.8 us
    ppermute x6, waiting for transfers between devices, over_groups(): lax.ppermute(parts[shift].astype(LINK), 'grp', ring).astype(F32)  10.6 us
    ppermute x6, waiting for transfers between devices, send(): lax.ppermute(block, 'ado', onward(step))  8 us
    all_to_all x1, starting transfers between devices, on_device(): lax.all_to_all((near + far.astype(F32)).astype(LINK), 'ado', split_axis=0...  7.19 us
  transfers between devices with their start and end apart: 17, of which 6 were waited for; matrix products, arithmetic and copies ran while one was open for 23% of the time, Pallas kernels for 13%

profile of v4, /device:TPU:64, one launch (start us, length us, event | category | flops | bytes accessed | tf_op | source)
XLA Modules:
  0.0 183.8 jit_solution(8539604059540347769)
XLA Ops:
  3.1 14.8 %all-to-all-start = ((s32[16,1,608]{2,1,0:T(1,128)}), s32[16,1,608]{2,1,0:T(1,128)S(1)}, u32[]{:S(2)}, u32[]{:S(2)}) async-start(s32[16,1,608]{2,1,0:T(1,128)} %reshape.378), calls=%async_computation | async-start | bytes 81920 | tf_op jit(solution)/shard_map/all_to_all | solution.py:266
  18.5 1.9 %collective-permute-start = (s32[384]{0:T(512)S(1)}, s32[384]{0:T(512)S(1)}, u32[]{:S(2)}, u32[]{:S(2)}) collective-permute-start(s32[384]{0:T(512)S(1)} %bitcast.151), channel_id=1, source_target_pairs={{0,1},{1,0},{2,3},{3,2},{4,5},{5,4},{6,7},{7,6},{8,9},{9,8},{10,11... | collective-permute-start | bytes 4616 | tf_op jit(solution)/shard_map/ppermute | solution.py:263
  20.4 2.4 %collective-permute-start.1 = (bf16[128,64,128]{2,1,0:T(8,128)(2,1)}, bf16[128,64,128]{2,1,0:T(8,128)(2,1)}, u32[]{:S(2)}, u32[]{:S(2)}) collective-permute-start(bf16[128,64,128]{2,1,0:T(8,128)(2,1)} %bitcast.149), channel_id=1, source_target_pairs={{0,1},{1,0},{2,3},{3,2},{4,5},{5,4},{6,7},{7,6},{8,9},{9,8},{10,11... | collective-permute-start | bytes 6291464 | tf_op jit(solution)/shard_map/ppermute | solution.py:262
  25.1 1.5 fusion.2
  26.9 3.3 %all-to-all-done = s32[16,1,608]{2,1,0:T(1,128)S(1)} async-done(((s32[16,1,608]{2,1,0:T(1,128)}), s32[16,1,608]{2,1,0:T(1,128)S(1)}, u32[]{:S(2)}, u32[]{:S(2)}) %all-to-all-start) | async-done | bytes 38944 | tf_op jit(solution)/shard_map/all_to_all | solution.py:266
  32.4 1.0 copy.55
  33.4 2.1 %slice_divide_fusion = (s32[32,8,16]{2,1,0:T(8,128)}, s32[32,8,16]{2,1,0:T(8,128)}, s32[8,16]{1,0:T(8,128)}, pred[32,8,16]{2,1,0:T(8,128)(4,1)}, s32[8,16]{1,0:T...) fusion(s32[38,8,16]{2,1,0:T(8,128)S(1)} %bitcast.153, s32[]{:T(128)} %select_n.527, ...), kind=kLoop, calls=%fused_computation.96 | loop fusion | flops 581376 | bytes 107529 | tf_op jit(solution)/shard_map/jit(floor_divide)/div | solution.py:203
  36.2 1.6 copy.63
  37.8 1.6 copy.64
  39.4 0.9 copy.62
  40.3 1.6 copy.58
  41.9 1.6 copy.57
  43.5 0.9 copy.56
  44.4 2.0 %fusion.49 = (s32[32,128]{0,1:T(8,128)}, s32[32,128]{0,1:T(8,128)}) fusion(s32[32,8,16]{0,2,1:T(8,128)} %copy.63, s32[128]{0:T(128)} %and_select_fusion, s32[]{:T(128)} %and.403, s32[32]{0:T(128)} %iota_multiply_fusion.1, s32[]{:T(128)} %select_n.527, pred[]{:T(512)S(6)} %eq.298, s32[32,8,16]{0,2,1:T(8,128)} %copy.64, pred[32,8,16]{0,2,1:T(8,128)(4,1)S(1)} %copy.62, ...), kind=kLoop, calls=%fused_computation.149 | loop fusion | flops 647168 | bytes 107145 | tf_op jit(solution)/shard_map/sub | solution.py:218
  47.0 0.8 mul.130
  47.8 0.8 rem.585
  48.6 0.8 div.206
  51.6 0.8 mul.120
  52.4 0.8 rem.503
  54.7 0.8 div.182
  57.8 0.9 copy.66
  58.7 1.1 fusion.51
  61.8 1.1 select_reduce_fusion
  62.9 1.1 fusion.50
  64.2 0.9 copy.60
  65.4 2.3 %shard_map.109 = (bf16[48,64,128]{2,1,0:T(8,128)(2,1)S(1)}, bf16[48,64,128]{2,1,0:T(8,128)(2,1)S(1)}, bf16[48,64,128]{2,1,0:T(8,128)(2,1)S(1)}, bf16[48,64,128]{...) custom-call(s32[2]{0:T(128)S(1)} %pad_add_fusion.6.spot_ref, ...), custom_call_target="tpu_custom_call" | custom-call | bytes 10485760 | tf_op jit(solution)/shard_map/pallas_call | solution.py:71
  67.7 2.5 %collective-permute-start.9 = (bf16[48,64,128]{2,1,0:T(8,128)(2,1)S(1)}, bf16[48,64,128]{2,1,0:T(8,128)(2,1)S(1)}, u32[]{:S(2)}, u32[]{:S(2)}) collective-permute-start(bf16[48,64,128]{2,1,0:T(8,128)(2,1)S(1)} %get-tuple-element.19), channel_id=1, source_target_pairs={{0,112},{2,114},{4,116},{6,118},{8,120},{10,122},{12,124},{14,126}... | collective-permute-start | bytes 2359304 | tf_op jit(solution)/shard_map/ppermute | solution.py:273
  70.2 3.4 %collective-permute-start.10 = (bf16[48,64,128]{2,1,0:T(8,128)(2,1)S(1)}, bf16[48,64,128]{2,1,0:T(8,128)(2,1)S(1)}, u32[]{:S(2)}, u32[]{:S(2)}) collective-permute-start(bf16[48,64,128]{2,1,0:T(8,128)(2,1)S(1)} %get-tuple-element.20), channel_id=1, source_target_pairs={{0,16},{2,18},{4,20},{6,22},{8,24},{10,26},{12,28},{14,30},{16,32}... | collective-permute-start | bytes 2359304 | tf_op jit(solution)/shard_map/ppermute | solution.py:273
  73.7 3.4 %collective-permute-start.2 = (bf16[48,64,128]{2,1,0:T(8,128)(2,1)S(1)}, bf16[48,64,128]{2,1,0:T(8,128)(2,1)S(1)}, u32[]{:S(2)}, u32[]{:S(2)}) collective-permute-start(bf16[48,64,128]{2,1,0:T(8,128)(2,1)S(1)} %get-tuple-element.14), channel_id=1, source_target_pairs={{0,16},{2,18},{4,20},{6,22},{8,24},{10,26},{12,28},{14,30},{16,32}... | collective-permute-start | bytes 2359304 | tf_op jit(solution)/shard_map/ppermute | solution.py:273
  77.1 4.0 %collective-permute-start.3 = (bf16[48,64,128]{2,1,0:T(8,128)(2,1)S(1)}, bf16[48,64,128]{2,1,0:T(8,128)(2,1)S(1)}, u32[]{:S(2)}, u32[]{:S(2)}) collective-permute-start(bf16[48,64,128]{2,1,0:T(8,128)(2,1)S(1)} %get-tuple-element.15), channel_id=1, source_target_pairs={{0,32},{2,34},{4,36},{6,38},{8,40},{10,42},{12,44},{14,46},{16,48}... | collective-permute-start | bytes 2359304 | tf_op jit(solution)/shard_map/ppermute | solution.py:273
  81.2 3.9 %collective-permute-start.4 = (bf16[48,64,128]{2,1,0:T(8,128)(2,1)S(1)}, bf16[48,64,128]{2,1,0:T(8,128)(2,1)S(1)}, u32[]{:S(2)}, u32[]{:S(2)}) collective-permute-start(bf16[48,64,128]{2,1,0:T(8,128)(2,1)S(1)} %get-tuple-element.16), channel_id=1, source_target_pairs={{0,112},{2,114},{4,116},{6,118},{8,120},{10,122},{12,124},{14,126}... | collective-permute-start | bytes 2359304 | tf_op jit(solution)/shard_map/ppermute | solution.py:273
  85.1 2.5 %collective-permute-start.5 = (bf16[48,64,128]{2,1,0:T(8,128)(2,1)S(1)}, bf16[48,64,128]{2,1,0:T(8,128)(2,1)S(1)}, u32[]{:S(2)}, u32[]{:S(2)}) collective-permute-start(bf16[48,64,128]{2,1,0:T(8,128)(2,1)S(1)} %get-tuple-element.17), channel_id=1, source_target_pairs={{0,96},{2,98},{4,100},{6,102},{8,104},{10,106},{12,108},{14,110},{... | collective-permute-start | bytes 2359304 | tf_op jit(solution)/shard_map/ppermute | solution.py:273
  87.6 9.8 %shard_map.111 = f32[4,8,16,16,128]{4,3,2,1,0:T(8,128)S(1)} custom-call(s32[2]{0:T(128)S(1)} %pad_add_fusion.5.spot_ref, s32[47,128]{1,0:T(8,128)S(1)} %pad_add_fusion.1.list_ref, f32[32]{0:T(128)S(1)} %copy-done.2, f32[32]{0:T(128)S(1)} %copy-done.3, bf16[48,64,128]{2,1,0:T(8,128)(2,1)S(1)} %get-tuple-element.18.refs_0_, ...), custom_call_target="tpu_custom_call" | custom-call | flops 1000000000 | bytes 10485760 | tf_op jit(solution)/shard_map/pallas_call | solution.py:180
  98.3 4.4 %collective-permute-start.13 = (f16[8,16,16,128]{3,2,1,0:T(8,128)(2,1)S(1)}, f16[8,16,16,128]{3,2,1,0:T(8,128)(2,1)S(1)}, u32[]{:S(2)}, u32[]{:S(2)}) collective-permute-start(f16[8,16,16,128]{3,2,1,0:T(8,128)(2,1)S(1)} %get-tuple-element.35), channel_id=1, source_target_pairs={{0,384},{128,0},{256,128},{384,256},{1,385},{129,1},{257,129},{385... | collective-permute-start | bytes 1572872 | tf_op jit(solution)/shard_map/ppermute | solution.py:244
  102.7 1.9 %collective-permute-start.12 = (f16[8,16,16,128]{3,2,1,0:T(8,128)(2,1)S(1)}, f16[8,16,16,128]{3,2,1,0:T(8,128)(2,1)S(1)}, u32[]{:S(2)}, u32[]{:S(2)}) collective-permute-start(f16[8,16,16,128]{3,2,1,0:T(8,128)(2,1)S(1)} %get-tuple-element.36), channel_id=1, source_target_pairs={{0,128},{128,256},{256,384},{384,0},{1,129},{129,257},{257,385},{3... | collective-permute-start | bytes 1572872 | tf_op jit(solution)/shard_map/ppermute | solution.py:244
  104.6 8.0 %collective-permute-done.3.refs_2_ = bf16[48,64,128]{2,1,0:T(8,128)(2,1)S(1)} collective-permute-done((bf16[48,64,128]{2,1,0:T(8,128)(2,1)S(1)}, bf16[48,64,128]{2,1,0:T(8,128)(2,1)S(1)}, u32[]{:S(2)}, u32[]{:S(2)}) %collective-permute-start.3) | collective-permute-done | bytes 786464 | tf_op jit(solution)/shard_map/ppermute | solution.py:273
  112.6 4.9 %collective-permute-start.11 = (f16[8,16,16,128]{3,2,1,0:T(8,128)(2,1)S(1)}, f16[8,16,16,128]{3,2,1,0:T(8,128)(2,1)S(1)}, u32[]{:S(2)}, u32[]{:S(2)}) collective-permute-start(f16[8,16,16,128]{3,2,1,0:T(8,128)(2,1)S(1)} %get-tuple-element.34), channel_id=1, source_target_pairs={{0,256},{128,384},{256,0},{384,128},{1,257},{129,385},{257,1},{385... | collective-permute-start | bytes 1572872 | tf_op jit(solution)/shard_map/ppermute | solution.py:244
  117.5 13.5 %shard_map.110 = f32[4,8,16,16,128]{4,3,2,1,0:T(8,128)S(1)} custom-call(s32[2]{0:T(128)S(1)} %pad_add_fusion.5.spot_ref, s32[47,128]{1,0:T(8,128)S(1)} %pad_add_fusion.list_ref, f32[32]{0:T(128)S(1)} %copy-done.2, f32[32]{0:T(128)S(1)} %copy-done.3, bf16[48,64,128]{2,1,0:T(8,128)(2,1)S(1)} %get-tuple-element.13.refs_0_, ...), custom_call_target="tpu_custom_call" | custom-call | flops 1000000000 | bytes 10485760 | tf_op jit(solution)/shard_map/pallas_call | solution.py:180
  131.7 3.1 %collective-permute-start.8 = (f16[8,16,16,128]{3,2,1,0:T(8,128)(2,1)S(1)}, f16[8,16,16,128]{3,2,1,0:T(8,128)(2,1)S(1)}, u32[]{:S(2)}, u32[]{:S(2)}) collective-permute-start(f16[8,16,16,128]{3,2,1,0:T(8,128)(2,1)S(1)} %get-tuple-element.32), channel_id=1, source_target_pairs={{0,384},{128,0},{256,128},{384,256},{1,385},{129,1},{257,129},{385... | collective-permute-start | bytes 1572872 | tf_op jit(solution)/shard_map/ppermute | solution.py:244
  134.8 3.4 %collective-permute-start.7 = (f16[8,16,16,128]{3,2,1,0:T(8,128)(2,1)S(1)}, f16[8,16,16,128]{3,2,1,0:T(8,128)(2,1)S(1)}, u32[]{:S(2)}, u32[]{:S(2)}) collective-permute-start(f16[8,16,16,128]{3,2,1,0:T(8,128)(2,1)S(1)} %get-tuple-element.33), channel_id=1, source_target_pairs={{0,128},{128,256},{256,384},{384,0},{1,129},{129,257},{257,385},{3... | collective-permute-start | bytes 1572872 | tf_op jit(solution)/shard_map/ppermute | solution.py:244
  138.2 4.0 %collective-permute-start.6 = (f16[8,16,16,128]{3,2,1,0:T(8,128)(2,1)S(1)}, f16[8,16,16,128]{3,2,1,0:T(8,128)(2,1)S(1)}, u32[]{:S(2)}, u32[]{:S(2)}) collective-permute-start(f16[8,16,16,128]{3,2,1,0:T(8,128)(2,1)S(1)} %get-tuple-element.31), channel_id=1, source_target_pairs={{0,256},{128,384},{256,0},{384,128},{1,257},{129,385},{257,1},{385... | collective-permute-start | bytes 1572872 | tf_op jit(solution)/shard_map/ppermute | solution.py:244
  142.5 4.1 %collective-permute-start.14 = (f16[8,16,16,128]{3,2,1,0:T(8,128)(2,1)S(1)}, f16[8,16,16,128]{3,2,1,0:T(8,128)(2,1)S(1)}, u32[]{:S(2)}, u32[]{:S(2)}) collective-permute-start(f16[8,16,16,128]{3,2,1,0:T(8,128)(2,1)S(1)} %fusion.6), channel_id=1, source_target_pairs={{0,64},{2,66},{4,68},{6,70},{8,72},{10,74},{12,76},{14,78},{16,80}... | collective-permute-start | bytes 1572872 | tf_op jit(solution)/shard_map/ppermute | solution.py:288
  146.6 1.9 %collective-permute-done.8 = f16[8,16,16,128]{3,2,1,0:T(8,128)(2,1)S(1)} collective-permute-done((f16[8,16,16,128]{3,2,1,0:T(8,128)(2,1)S(1)}, f16[8,16,16,128]{3,2,1,0:T(8,128)(2,1)S(1)}, u32[]{:S(2)}, u32[]{:S(2)}) %collective-permute-start.8) | collective-permute-done | bytes 524320 | tf_op jit(solution)/shard_map/ppermute | solution.py:244
  148.5 8.7 %collective-permute-done.7 = f16[8,16,16,128]{3,2,1,0:T(8,128)(2,1)S(1)} collective-permute-done((f16[8,16,16,128]{3,2,1,0:T(8,128)(2,1)S(1)}, f16[8,16,16,128]{3,2,1,0:T(8,128)(2,1)S(1)}, u32[]{:S(2)}, u32[]{:S(2)}) %collective-permute-start.7) | collective-permute-done | bytes 524320 | tf_op jit(solution)/shard_map/ppermute | solution.py:244
  157.3 4.1 %collective-permute-done.14 = f16[8,16,16,128]{3,2,1,0:T(8,128)(2,1)S(1)} collective-permute-done((f16[8,16,16,128]{3,2,1,0:T(8,128)(2,1)S(1)}, f16[8,16,16,128]{3,2,1,0:T(8,128)(2,1)S(1)}, u32[]{:S(2)}, u32[]{:S(2)}) %collective-permute-start.14) | collective-permute-done | bytes 524320 | tf_op jit(solution)/shard_map/ppermute | solution.py:288
  161.3 1.2 fusion.11
  162.5 7.2 %all-to-all-start.1 = ((f16[8,16,16,128]{3,2,1,0:T(8,128)(2,1)}), f16[8,16,16,128]{3,2,1,0:T(8,128)(2,1)S(1)}, u32[]{:S(2)}, u32[]{:S(2)}) async-start(f16[8,16,16,128]{3,2,1,0:T(8,128)(2,1)} %fusion.11), calls=%async_computation.1 | async-start | bytes 1048576 | tf_op jit(solution)/shard_map/all_to_all | solution.py:290
  170.2 12.8 %all-to-all-done.1 = f16[8,16,16,128]{3,2,1,0:T(8,128)(2,1)S(1)} async-done(((f16[8,16,16,128]{3,2,1,0:T(8,128)(2,1)}), f16[8,16,16,128]{3,2,1,0:T(8,128)(2,1)S(1)}, u32[]{:S(2)}, u32[]{:S(2)}) %all-to-all-start.1) | async-done | bytes 524320 | tf_op jit(solution)/shard_map/all_to_all | solution.py:290
  (88 shorter events, 21.6 us)
Async XLA Ops:
  2.3 24.5 %copy-start.4 = (bf16[64,64]{1,0:T(8,128)(2,1)S(1)}, bf16[64,64]{1,0:T(8,128)(2,1)}, u32[]{:S(2)}) copy-start(bf16[64,64]{1,0:T(8,128)(2,1)} %param.17) | copy-start | bytes 24580
  3.1 27.2 %all-to-all-start = ((s32[16,1,608]{2,1,0:T(1,128)}), s32[16,1,608]{2,1,0:T(1,128)S(1)}, u32[]{:S(2)}, u32[]{:S(2)}) async-start(s32[16,1,608]{2,1,0:T(1,128)} %reshape.378), calls=%async_computation | async-start | bytes 81920 | tf_op jit(solution)/shard_map/all_to_all | solution.py:266
  18.5 46.9 %collective-permute-start = (s32[384]{0:T(512)S(1)}, s32[384]{0:T(512)S(1)}, u32[]{:S(2)}, u32[]{:S(2)}) collective-permute-start(s32[384]{0:T(512)S(1)} %bitcast.151), channel_id=1, source_target_pairs={{0,1},{1,0},{2,3},{3,2},{4,5},{5,4},{6,7},{7,6},{8,9},{9,8},{10,11... | collective-permute-start | bytes 4616 | tf_op jit(solution)/shard_map/ppermute | solution.py:263
  20.4 45.0 %collective-permute-start.1 = (bf16[128,64,128]{2,1,0:T(8,128)(2,1)}, bf16[128,64,128]{2,1,0:T(8,128)(2,1)}, u32[]{:S(2)}, u32[]{:S(2)}) collective-permute-start(bf16[128,64,128]{2,1,0:T(8,128)(2,1)} %bitcast.149), channel_id=1, source_target_pairs={{0,1},{1,0},{2,3},{3,2},{4,5},{5,4},{6,7},{7,6},{8,9},{9,8},{10,11... | collective-permute-start | bytes 6291464 | tf_op jit(solution)/shard_map/ppermute | solution.py:262
  31.5 33.9 %copy-start = (bf16[1,1,128,64,128]{4,3,2,1,0:T(8,128)(2,1)S(1)}, bf16[1,1,128,64,128]{4,3,2,1,0:T(8,128)(2,1)}, u32[]{:S(2)}) copy-start(bf16[1,1,128,64,128]{4,3,2,1,0:T(8,128)(2,1)} %param.11) | copy-start | bytes 6291460
  65.3 22.3 %copy-start.1 = (bf16[16,16,128]{2,1,0:T(8,128)(2,1)S(1)}, bf16[16,16,128]{2,1,0:T(8,128)(2,1)}, u32[]{:S(2)}) copy-start(bf16[16,16,128]{2,1,0:T(8,128)(2,1)} %refs_5_.1) | copy-start | bytes 196612
  65.4 22.3 %copy-start.2 = (f32[32]{0:T(128)S(1)}, f32[32]{0:T(128)}, u32[]{:S(2)}) copy-start(f32[32]{0:T(128)} %re_ref.3) | copy-start | bytes 388
  65.4 22.3 %copy-start.3 = (f32[32]{0:T(128)S(1)}, f32[32]{0:T(128)}, u32[]{:S(2)}) copy-start(f32[32]{0:T(128)} %im_ref.3) | copy-start | bytes 388
  67.7 17.4 %collective-permute-start.9 = (bf16[48,64,128]{2,1,0:T(8,128)(2,1)S(1)}, bf16[48,64,128]{2,1,0:T(8,128)(2,1)S(1)}, u32[]{:S(2)}, u32[]{:S(2)}) collective-permute-start(bf16[48,64,128]{2,1,0:T(8,128)(2,1)S(1)} %get-tuple-element.19), channel_id=1, source_target_pairs={{0,112},{2,114},{4,116},{6,118},{8,120},{10,122},{12,124},{14,126}... | collective-permute-start | bytes 2359304 | tf_op jit(solution)/shard_map/ppermute | solution.py:273
  70.2 17.4 %collective-permute-start.10 = (bf16[48,64,128]{2,1,0:T(8,128)(2,1)S(1)}, bf16[48,64,128]{2,1,0:T(8,128)(2,1)S(1)}, u32[]{:S(2)}, u32[]{:S(2)}) collective-permute-start(bf16[48,64,128]{2,1,0:T(8,128)(2,1)S(1)} %get-tuple-element.20), channel_id=1, source_target_pairs={{0,16},{2,18},{4,20},{6,22},{8,24},{10,26},{12,28},{14,30},{16,32}... | collective-permute-start | bytes 2359304 | tf_op jit(solution)/shard_map/ppermute | solution.py:273
  73.7 28.9 %collective-permute-start.2 = (bf16[48,64,128]{2,1,0:T(8,128)(2,1)S(1)}, bf16[48,64,128]{2,1,0:T(8,128)(2,1)S(1)}, u32[]{:S(2)}, u32[]{:S(2)}) collective-permute-start(bf16[48,64,128]{2,1,0:T(8,128)(2,1)S(1)} %get-tuple-element.14), channel_id=1, source_target_pairs={{0,16},{2,18},{4,20},{6,22},{8,24},{10,26},{12,28},{14,30},{16,32}... | collective-permute-start | bytes 2359304 | tf_op jit(solution)/shard_map/ppermute | solution.py:273
  77.1 35.4 %collective-permute-start.3 = (bf16[48,64,128]{2,1,0:T(8,128)(2,1)S(1)}, bf16[48,64,128]{2,1,0:T(8,128)(2,1)S(1)}, u32[]{:S(2)}, u32[]{:S(2)}) collective-permute-start(bf16[48,64,128]{2,1,0:T(8,128)(2,1)S(1)} %get-tuple-element.15), channel_id=1, source_target_pairs={{0,32},{2,34},{4,36},{6,38},{8,40},{10,42},{12,44},{14,46},{16,48}... | collective-permute-start | bytes 2359304 | tf_op jit(solution)/shard_map/ppermute | solution.py:273
  81.2 36.3 %collective-permute-start.4 = (bf16[48,64,128]{2,1,0:T(8,128)(2,1)S(1)}, bf16[48,64,128]{2,1,0:T(8,128)(2,1)S(1)}, u32[]{:S(2)}, u32[]{:S(2)}) collective-permute-start(bf16[48,64,128]{2,1,0:T(8,128)(2,1)S(1)} %get-tuple-element.16), channel_id=1, source_target_pairs={{0,112},{2,114},{4,116},{6,118},{8,120},{10,122},{12,124},{14,126}... | collective-permute-start | bytes 2359304 | tf_op jit(solution)/shard_map/ppermute | solution.py:273
  85.1 32.4 %collective-permute-start.5 = (bf16[48,64,128]{2,1,0:T(8,128)(2,1)S(1)}, bf16[48,64,128]{2,1,0:T(8,128)(2,1)S(1)}, u32[]{:S(2)}, u32[]{:S(2)}) collective-permute-start(bf16[48,64,128]{2,1,0:T(8,128)(2,1)S(1)} %get-tuple-element.17), channel_id=1, source_target_pairs={{0,96},{2,98},{4,100},{6,102},{8,104},{10,106},{12,108},{14,110},{... | collective-permute-start | bytes 2359304 | tf_op jit(solution)/shard_map/ppermute | solution.py:273
  98.3 39.9 %collective-permute-start.13 = (f16[8,16,16,128]{3,2,1,0:T(8,128)(2,1)S(1)}, f16[8,16,16,128]{3,2,1,0:T(8,128)(2,1)S(1)}, u32[]{:S(2)}, u32[]{:S(2)}) collective-permute-start(f16[8,16,16,128]{3,2,1,0:T(8,128)(2,1)S(1)} %get-tuple-element.35), channel_id=1, source_target_pairs={{0,384},{128,0},{256,128},{384,256},{1,385},{129,1},{257,129},{385... | collective-permute-start | bytes 1572872 | tf_op jit(solution)/shard_map/ppermute | solution.py:244
  102.7 39.5 %collective-permute-start.12 = (f16[8,16,16,128]{3,2,1,0:T(8,128)(2,1)S(1)}, f16[8,16,16,128]{3,2,1,0:T(8,128)(2,1)S(1)}, u32[]{:S(2)}, u32[]{:S(2)}) collective-permute-start(f16[8,16,16,128]{3,2,1,0:T(8,128)(2,1)S(1)} %get-tuple-element.36), channel_id=1, source_target_pairs={{0,128},{128,256},{256,384},{384,0},{1,129},{129,257},{257,385},{3... | collective-permute-start | bytes 1572872 | tf_op jit(solution)/shard_map/ppermute | solution.py:244
  112.6 29.6 %collective-permute-start.11 = (f16[8,16,16,128]{3,2,1,0:T(8,128)(2,1)S(1)}, f16[8,16,16,128]{3,2,1,0:T(8,128)(2,1)S(1)}, u32[]{:S(2)}, u32[]{:S(2)}) collective-permute-start(f16[8,16,16,128]{3,2,1,0:T(8,128)(2,1)S(1)} %get-tuple-element.34), channel_id=1, source_target_pairs={{0,256},{128,384},{256,0},{384,128},{1,257},{129,385},{257,1},{385... | collective-permute-start | bytes 1572872 | tf_op jit(solution)/shard_map/ppermute | solution.py:244
  131.7 16.8 %collective-permute-start.8 = (f16[8,16,16,128]{3,2,1,0:T(8,128)(2,1)S(1)}, f16[8,16,16,128]{3,2,1,0:T(8,128)(2,1)S(1)}, u32[]{:S(2)}, u32[]{:S(2)}) collective-permute-start(f16[8,16,16,128]{3,2,1,0:T(8,128)(2,1)S(1)} %get-tuple-element.32), channel_id=1, source_target_pairs={{0,384},{128,0},{256,128},{384,256},{1,385},{129,1},{257,129},{385... | collective-permute-start | bytes 1572872 | tf_op jit(solution)/shard_map/ppermute | solution.py:244
  134.8 22.5 %collective-permute-start.7 = (f16[8,16,16,128]{3,2,1,0:T(8,128)(2,1)S(1)}, f16[8,16,16,128]{3,2,1,0:T(8,128)(2,1)S(1)}, u32[]{:S(2)}, u32[]{:S(2)}) collective-permute-start(f16[8,16,16,128]{3,2,1,0:T(8,128)(2,1)S(1)} %get-tuple-element.33), channel_id=1, source_target_pairs={{0,128},{128,256},{256,384},{384,0},{1,129},{129,257},{257,385},{3... | collective-permute-start | bytes 1572872 | tf_op jit(solution)/shard_map/ppermute | solution.py:244
  138.2 19.1 %collective-permute-start.6 = (f16[8,16,16,128]{3,2,1,0:T(8,128)(2,1)S(1)}, f16[8,16,16,128]{3,2,1,0:T(8,128)(2,1)S(1)}, u32[]{:S(2)}, u32[]{:S(2)}) collective-permute-start(f16[8,16,16,128]{3,2,1,0:T(8,128)(2,1)S(1)} %get-tuple-element.31), channel_id=1, source_target_pairs={{0,256},{128,384},{256,0},{384,128},{1,257},{129,385},{257,1},{385... | collective-permute-start | bytes 1572872 | tf_op jit(solution)/shard_map/ppermute | solution.py:244
  142.5 27.2 %copy-start.6 = (s32[16,3]{0,1:T(4,128)S(1)}, s32[16,3]{0,1:T(4,128)}, u32[]{:S(2)}) copy-start(s32[16,3]{0,1:T(4,128)} %param.14) | copy-start | bytes 580
  142.5 27.2 %copy-start.7 = (f32[128]{0:T(128)S(1)}, f32[128]{0:T(128)}, u32[]{:S(2)}) copy-start(f32[128]{0:T(128)} %param.21) | copy-start | bytes 1540
  142.5 27.4 %copy-start.5 = (bf16[64,64]{1,0:T(8,128)(2,1)S(1)}, bf16[64,64]{1,0:T(8,128)(2,1)}, u32[]{:S(2)}) copy-start(bf16[64,64]{1,0:T(8,128)(2,1)} %param.17) | copy-start | bytes 24580
  142.5 18.8 %collective-permute-start.14 = (f16[8,16,16,128]{3,2,1,0:T(8,128)(2,1)S(1)}, f16[8,16,16,128]{3,2,1,0:T(8,128)(2,1)S(1)}, u32[]{:S(2)}, u32[]{:S(2)}) collective-permute-start(f16[8,16,16,128]{3,2,1,0:T(8,128)(2,1)S(1)} %fusion.6), channel_id=1, source_target_pairs={{0,64},{2,66},{4,68},{6,70},{8,72},{10,74},{12,76},{14,78},{16,80}... | collective-permute-start | bytes 1572872 | tf_op jit(solution)/shard_map/ppermute | solution.py:288
  162.5 20.5 %all-to-all-start.1 = ((f16[8,16,16,128]{3,2,1,0:T(8,128)(2,1)}), f16[8,16,16,128]{3,2,1,0:T(8,128)(2,1)S(1)}, u32[]{:S(2)}, u32[]{:S(2)}) async-start(f16[8,16,16,128]{3,2,1,0:T(8,128)(2,1)} %fusion.11), calls=%async_computation.1 | async-start | bytes 1048576 | tf_op jit(solution)/shard_map/all_to_all | solution.py:290

commit v5 on v4

--- a/solution.py
+++ b/solution.py
@@ -47,11 +47,6 @@
 
 
 DELIVER = [[device(c, a, b) for b in range(RINGS)] for c in range(2) for a in range(RINGS)]
-LISTENERS = [
-    [device(c, a + far, b) for far in (0, 4) for b in range(RINGS)] for c in range(2) for a in range(RINGS // 2)
-]
-
-
 def pick_kernel(spot_ref, own_slot, sib_slot, own_ref, sib_ref, *out_refs):
     core, along = spot_ref[0], spot_ref[1]
     far = jnp.where(core == 0, 16, 2)
@@ -78,15 +73,17 @@
     )(spot, own_slots, sib_slots, own, sib)
 
 
-def terms_kernel(sources, modes, windows, spot_ref, list_ref, re_ref, im_ref, *refs):
+def terms_kernel(sources, modes, windows, part, spot_ref, list_ref, re_ref, im_ref, *refs):
     flat_refs = refs[:sources]
     wide_ref, ham_ref, rho_ref, out_ref, flat, acc = refs[sources:]
-    group, here = spot_ref[0], spot_ref[1]
+    here = spot_ref[2]
     share = rho_ref.shape[1]
     width = ham_ref.shape[0]
     pairs = RINGS * windows
     blocks = width // share
-    downs, extra, counts = modes, modes + CAP, modes + CAP + modes // LOT + CAP
+    begin, end, slot = part
+    levels = modes // LOT + CAP
+    downs, extra, counts = modes, modes + CAP + slot * levels, list_ref.shape[0] - 1
 
     def gather(row, carry):
         for n, ref in enumerate(flat_refs):
@@ -120,7 +117,7 @@
             acc[pair] = lot(pair, 0)
         return carry
 
-    lax.fori_loop(0, pairs // together, first, 0)
+    lax.fori_loop(begin * windows // together, end * windows // together, first, 0)
 
     def listed(level, work):
         def some(index, carry):
@@ -130,7 +127,7 @@
                 acc[pair] += value
             return carry
 
-        lax.fori_loop(0, lax.shift_right_logical(list_ref[counts, level] + 3, 2), some, 0)
+        lax.fori_loop(0, lax.shift_right_logical(list_ref[counts, slot * levels + level] + 3, 2), some, 0)
 
     def more(level, carry):
         listed(level, lambda pair: lot(pair, level * LOT))
@@ -161,27 +158,27 @@
             )
             return carry
 
-        lax.fori_loop(0, windows, local, 0)
+        lax.fori_loop(0, jnp.where((here >= begin) & (here < end), windows, 0), local, 0)
 
     def leave(r, carry):
         for w in range(windows):
             value = acc[r * windows + w]
             for b in range(blocks):
-                out_ref[lax.rem(b - group + blocks, blocks), r, w] = value[b * share:(b + 1) * share]
-        return carry
-
-    lax.fori_loop(0, RINGS, leave, 0)
-
-
-def terms(spot, lists, coup_re, coup_im, pieces, maps_wide, head_cols, rho):
+                out_ref[b, r - begin, w] = value[b * share:(b + 1) * share]
+        return carry
+
+    lax.fori_loop(begin, end, leave, 0)
+
+
+def terms(part, spot, lists, coup_re, coup_im, pieces, maps_wide, head_cols, rho):
     modes = maps_wide.shape[0] - 1
     windows, share, lanes = rho.shape
     width = head_cols.shape[0]
     return pl.pallas_call(
-        functools.partial(terms_kernel, len(pieces), modes, windows),
+        functools.partial(terms_kernel, len(pieces), modes, windows, part),
         in_specs=[SMEM] * 4 + [VMEM] * (len(pieces) + 3),
         out_specs=VMEM,
-        out_shape=jax.ShapeDtypeStruct((width // share, RINGS, windows, share, lanes), F32),
+        out_shape=jax.ShapeDtypeStruct((width // share, part[1] - part[0], windows, share, lanes), F32),
         scratch_shapes=[
             pltpu.VMEM((len(pieces) * SPAN, width, lanes), BF16),
             pltpu.VMEM((RINGS * windows + 1, width, lanes), F32),
@@ -191,58 +188,86 @@
     )(spot, lists, coup_re, coup_im, *pieces, maps_wide, head_cols, rho)
 
 
-def use_lists(steps, target, core, along, across, group, modes, heard):
-    half = (along // 4 + target // 4) % 2
-    heard = lax.dynamic_index_in_dim(heard.reshape((2, RINGS) + heard.shape[1:]), half, 0, keepdims=False)
-    windows = heard.shape[-1]
-    pairs = RINGS * windows
-    heard = jnp.transpose(heard, (1, 0, 2)).reshape(-1, pairs)
-    receiver = jnp.arange(pairs, dtype=jnp.int32) // windows
+def lists_kernel(steps, parts, modes, spot_ref, heard_ref, out_ref):
+    core, along, across, group = spot_ref[0], spot_ref[1], spot_ref[2], spot_ref[3]
+    pairs = heard_ref.shape[1]
+    windows = pairs // RINGS
 
     def locate(places):
-        owner = places // CAP
-        z, y, c = owner // 16, (owner // 2) % RINGS, owner % 2
-        off = (jnp.where(core == 0, z, y) - along) % RINGS
+        owner = lax.shift_right_logical(places * 171, 9)
+        z, y, c = lax.shift_right_logical(owner, 4), lax.shift_right_logical(owner, 1) & 7, owner & 1
+        off = (jnp.where(core == 0, z, y) - along) & (RINGS - 1)
         source = jnp.full_like(off, -1)
         for n, (_, step) in enumerate(steps):
             source = jnp.where(off == -step % RINGS, n, source)
         mine = (jnp.where(core == 0, y, z) == across) & (source >= 0)
         kind = jnp.where(c == core, 0, 1)
-        return mine, ((source * 2 + kind) * CAP + places % CAP) * RINGS + receiver
-
-    mine, row = locate(heard[:modes])
-    ids = jnp.arange(modes, dtype=jnp.int32)
-    below = (ids[:, None] > ids[None, :]).astype(F32)
-    rank = jnp.dot(below, mine.astype(F32), preferred_element_type=F32).astype(jnp.int32)
-    count = jnp.sum(mine.astype(jnp.int32), axis=0)
-    value = ids[:, None] * 512 + row - modes * 512
-    hit = mine[None] & (rank[None] == ids[:, None, None])
-    up = modes * 512 + jnp.sum(jnp.where(hit, value[None], 0), axis=1)
-
-    mine, row = locate(heard[modes:modes + CAP])
-    local = heard[modes + CAP:modes + 2 * CAP] - group * modes
+        lanes = lax.broadcasted_iota(jnp.int32, places.shape, 1)
+        receiver = lax.shift_right_logical(lanes, windows.bit_length() - 1)
+        return mine, ((source * 2 + kind) * CAP + places - owner * CAP) * RINGS + receiver
+
+    def square(n, axis):
+        return lax.broadcasted_iota(jnp.int32, (n, n), axis)
+
+    def ones(mask):
+        return jnp.where(mask, 1.0, 0.0)
+
+    mine, row = locate(heard_ref[:modes])
+    ids = lax.broadcasted_iota(jnp.int32, mine.shape, 0)
+    below = ones(square(modes, 0) > square(modes, 1))
+    rank = jnp.dot(below, ones(mine), preferred_element_type=F32).astype(jnp.int32)
+    rank = jnp.where(mine, rank, -1)
+    count = jnp.sum(ones(mine), axis=0, keepdims=True)
+    value = (ids * 512 + row - modes * 512).astype(F32)
+    for n in range(modes):
+        found = jnp.sum(jnp.where(rank == n, value, 0.0), axis=0, keepdims=True)
+        out_ref[n:n + 1] = found.astype(jnp.int32) + modes * 512
+
+    mine, row = locate(heard_ref[modes:modes + CAP])
+    local = heard_ref[modes + CAP:modes + 2 * CAP] - group * modes
     live = mine & (local >= 0) & (local < modes)
-    down = jnp.where(live, local * 512 + row, 0)
-
-    levels = jnp.arange(modes // LOT, dtype=jnp.int32) * LOT
-    flags = jnp.concatenate([count[None, :] > levels[:, None], live], axis=0)
-    lanes = jnp.arange(pairs, dtype=jnp.int32)
-    ahead = (lanes[:, None] < lanes[None, :]).astype(F32)
-    order = jnp.dot(flags.astype(F32), ahead, preferred_element_type=F32).astype(jnp.int32)
-    hit = flags[:, None, :] & (order[:, None, :] == lanes[None, :, None])
-    listed = pairs + jnp.sum(jnp.where(hit, lanes - pairs, 0), axis=2)
-    totals = jnp.sum(flags.astype(jnp.int32), axis=1)
-    totals = jnp.pad(totals, (0, pairs - totals.shape[0]))[None]
-    return jnp.concatenate([up, down, listed, totals], axis=0)
+    out_ref[modes:modes + CAP] = jnp.where(live, local * 512 + row, 0)
+
+    first = lax.broadcasted_iota(jnp.int32, (1, pairs), 1)
+    flags = []
+    for begin, end in parts:
+        inside = (first >= begin * windows) & (first < end * windows)
+        for n in range(modes // LOT):
+            flags.append(ones(inside & (count > n * LOT)))
+        for t in range(CAP):
+            flags.append(ones(inside & live[t:t + 1]))
+    total = len(flags)
+    flags = jnp.concatenate(flags + [jnp.zeros((pairs - total, pairs), F32)], axis=0)
+    turned = (((1,), (1,)), ((), ()))
+    down, over = square(pairs, 0), square(pairs, 1)
+    chosen = lax.dot_general(ones(down == over), flags, turned, preferred_element_type=F32)
+    order = lax.dot_general(ones(down > over), flags, turned, preferred_element_type=F32)
+    order = jnp.where(chosen > 0.5, order, -1.0)
+    numbers = (down - pairs).astype(F32)
+    lanes = over.astype(F32)
+    for n in range(total):
+        found = jnp.sum(jnp.where(order[:, n:n + 1] == lanes, numbers, 0.0), axis=0, keepdims=True)
+        out_ref[modes + CAP + n:modes + CAP + n + 1] = found.astype(jnp.int32) + pairs
+    sums = lax.dot_general(jnp.ones((8, pairs), F32), flags, turned, preferred_element_type=F32)
+    last = out_ref.shape[0] - 1
+    out_ref[last:last + 1] = sums[:1].astype(jnp.int32)
+
+
+def use_lists(steps, parts, modes, spot, heard):
+    rows = modes + CAP + len(parts) * (modes // LOT + CAP) + 1
+    return pl.pallas_call(
+        functools.partial(lists_kernel, steps, parts, modes),
+        in_specs=[SMEM, VMEM],
+        out_specs=VMEM,
+        out_shape=jax.ShapeDtypeStruct((rows + -rows % 8, heard.shape[1]), jnp.int32),
+        compiler_params=pltpu.CompilerParams(vmem_limit_bytes=8 * 2**20),
+        cost_estimate=pl.CostEstimate(flops=10**7, bytes_accessed=2**17, transcendentals=0),
+    )(spot, heard)
 
 
 def over_groups(parts):
-    count = parts.shape[0]
-    total = parts[0]
-    for shift in (2, 1, 3):
-        ring = [(i, (i + shift) % count) for i in range(count)]
-        total = total + lax.ppermute(parts[shift].astype(LINK), "grp", ring).astype(F32)
-    return total
+    parts = lax.all_to_all(parts.astype(LINK), "grp", split_axis=0, concat_axis=0, tiled=True)
+    return jnp.sum(parts.astype(F32), axis=0)
 
 
 def on_device(
@@ -250,7 +275,7 @@
     hamiltonian, coupling, coup_re, coup_im, decay_rate,
 ):
     width = hamiltonian.shape[0]
-    share = window_tier_states.shape[1]
+    windows, share = window_tier_states.shape[:2]
     modes = coupling.shape[0]
     group = lax.axis_index("grp").astype(jnp.int32)
     index = lax.axis_index("ado").astype(jnp.int32)
@@ -258,15 +283,22 @@
     along = jnp.where(core == 0, z, y)
     across = jnp.where(core == 0, y, z)
 
+    spot = jnp.stack([core, along, across, group])
+
     slots = jnp.transpose(send_slot[0, 0]).reshape(-1)
     sib_store = lax.ppermute(states[0, 0], "ado", SIBLING)
     sib_slots = lax.ppermute(slots, "ado", SIBLING)
-    said = jnp.concatenate([use_up.T, use_down.T, modes_tri.T], axis=0)
-    said = jnp.broadcast_to(said, (2 * RINGS,) + said.shape)
+    said = jnp.concatenate([use_up.T, use_down.T, modes_tri.T, jnp.zeros_like(use_down.T)[:2]], axis=0)
+    lane = jnp.arange(RINGS * windows, dtype=jnp.int32) // windows
+    said = jnp.where(lane == across, jnp.tile(said, (1, RINGS)), 0)
     heard = lax.all_to_all(
-        said, "ado", split_axis=0, concat_axis=0, tiled=True, axis_index_groups=LISTENERS
+        jnp.broadcast_to(said, (RINGS,) + said.shape), "ado", split_axis=0, concat_axis=0, tiled=True,
+        axis_index_groups=DELIVER,
     )
-    picked = pick(jnp.stack([core, along]), slots, sib_slots, states[0, 0], sib_store)
+    heard = jnp.sum(heard, axis=0)
+    heard_far = lax.ppermute(heard, "ado", onward(4))
+    picked = pick(spot, slots, sib_slots, states[0, 0], sib_store)
+    heard, heard_far, picked = lax.optimization_barrier((heard, heard_far, picked))
 
     def send(steps, blocks):
         return [
@@ -276,20 +308,22 @@
 
     far_states = send(FAR, picked[:len(FAR)])
     near_states = send(NEAR, picked[len(FAR):])
-    where = (core, along, across, group, modes, heard)
-    far_lists = use_lists(FAR, 4, *where)
-    near_lists = use_lists(NEAR, 0, *where)
+    half = RINGS // 2
+    far_lists = use_lists(FAR, ((0, RINGS),), modes, spot, heard_far)
+    near_lists = use_lists(NEAR, ((0, half), (half, RINGS)), modes, spot, heard)
 
     maps_wide = jnp.concatenate([doubled(coupling), jnp.zeros((1, 2 * width, 2 * width), BF16)], axis=0)
     head_cols = lax.dynamic_slice_in_dim(hamiltonian, group * share, share, 1)
-    spot = jnp.stack([group, across])
     shared = (maps_wide, head_cols, window_tier_states)
-    far = over_groups(terms(spot, far_lists, coup_re, coup_im, far_states, *shared))
+    far = over_groups(terms((0, RINGS, 0), spot, far_lists, coup_re, coup_im, far_states, *shared))
     far = lax.ppermute(far.astype(LINK), "ado", onward(4))
-    near = over_groups(terms(spot, near_lists, coup_re, coup_im, near_states, *shared))
+    near = [
+        over_groups(terms(part, spot, near_lists, coup_re, coup_im, near_states, *shared))
+        for part in ((0, half, 0), (half, RINGS, 1))
+    ]
     summed = lax.all_to_all(
-        (near + far.astype(F32)).astype(LINK), "ado", split_axis=0, concat_axis=0, tiled=True,
-        axis_index_groups=DELIVER,
+        (jnp.concatenate(near, axis=0) + far.astype(F32)).astype(LINK), "ado", split_axis=0, concat_axis=0,
+        tiled=True, axis_index_groups=DELIVER,
     )
 
     ham_wide = doubled(hamiltonian)

time: 186 us -> 190 us (1.022)
  the two profiles are of different devices: /device:TPU:64 before, /device:TPU:130 now
where the time goes in v5:
time: 190 us; the launch traced here: 189 us
  starting transfers between devices  73.6 us (39%)
  waiting for transfers between devices  49 us (26%)
  Pallas kernels  32.4 us (17%)
  local copies, waits for them, and re-layouts  22.1 us (12%)
  other arithmetic  11.3 us (6%)
    pallas_call x3, Pallas kernels, terms(): pl.pallas_call(functools.partial(terms_kernel, len(pieces), modes, window...  27.4 us
    unnamed x60, local copies, waits for them, and re-layouts  20.4 us
    ppermute x6, starting transfers between devices, send(): lax.ppermute(block, 'ado', onward(step))  19.6 us
    ppermute x6, waiting for transfers between devices, send(): lax.ppermute(block, 'ado', onward(step))  14.2 us
    all_to_all x3, starting transfers between devices, over_groups(): lax.all_to_all(parts.astype(LINK), 'grp', split_axis=0, concat_axis=0, ti...  13.9 us
    all_to_all x1, waiting for transfers between devices, on_device(): lax.all_to_all((jnp.concatenate(near, axis=0) + far.astype(F32)).astype(L...  12.8 us
    ppermute x1, waiting for transfers between devices, on_device(): far = lax.ppermute(far.astype(LINK), 'ado', onward(4))  10.7 us
    all_to_all x1, starting transfers between devices, on_device(): lax.all_to_all((jnp.concatenate(near, axis=0) + far.astype(F32)).astype(L...  10.5 us
  transfers between devices with their start and end apart: 15, of which 5 were waited for; matrix products, arithmetic and copies ran while one was open for 7% of the time, Pallas kernels for 17%

profile of v5, /device:TPU:130, one launch (start us, length us, event | category | flops | bytes accessed | tf_op | source)
XLA Modules:
  0.0 189.0 jit_solution(17138998630749670444)
XLA Ops:
  0.0 1.9 %collective-permute-start.2 = (bf16[128,64,128]{2,1,0:T(8,128)(2,1)}, bf16[128,64,128]{2,1,0:T(8,128)(2,1)S(1)}, u32[]{:S(2)}, u32[]{:S(2)}) collective-permute-start(bf16[128,64,128]{2,1,0:T(8,128)(2,1)} %bitcast.23), channel_id=1, source_target_pairs={{0,1},{1,0},{2,3},{3,2},{4,5},{5,4},{6,7},{7,6},{8,9},{9,8},{10,11... | collective-permute-start | bytes 6291464 | tf_op jit(solution)/shard_map/ppermute | solution.py:289
  1.9 0.8 copy.20
  2.7 0.8 copy.21
  3.5 0.8 add_add_fusion
  4.5 0.7 broadcast_in_dim.27
  5.1 7.1 %all-to-all-start = ((s32[8,40,128]{2,1,0:T(8,128)}), s32[8,40,128]{2,1,0:T(8,128)S(1)}, u32[]{:S(2)}, u32[]{:S(2)}) async-start(s32[8,40,128]{2,1,0:T(8,128)} %broadcast_in_dim.27), calls=%async_computation | async-start | bytes 327680 | tf_op jit(solution)/shard_map/all_to_all | solution.py:294
  12.2 0.7 copy.25
  12.9 3.8 %collective-permute-start.1 = (s32[384]{0:T(512)S(1)}, s32[384]{0:T(512)S(1)}, u32[]{:S(2)}, u32[]{:S(2)}) collective-permute-start(s32[384]{0:T(512)S(1)} %bitcast.25), channel_id=1, source_target_pairs={{0,1},{1,0},{2,3},{3,2},{4,5},{5,4},{6,7},{7,6},{8,9},{9,8},{10,11... | collective-permute-start | bytes 4616 | tf_op jit(solution)/shard_map/ppermute | solution.py:290
  16.7 4.9 %all-to-all-done = s32[8,40,128]{2,1,0:T(8,128)S(1)} async-done(((s32[8,40,128]{2,1,0:T(8,128)}), s32[8,40,128]{2,1,0:T(8,128)S(1)}, u32[]{:S(2)}, u32[]{:S(2)}) %all-to-all-start) | async-done | bytes 163872 | tf_op jit(solution)/shard_map/all_to_all | solution.py:294
  21.7 9.1 %collective-permute-start = (s32[40,128]{1,0:T(8,128)S(1)}, s32[40,128]{1,0:T(8,128)S(1)}, u32[]{:S(2)}, u32[]{:S(2)}) collective-permute-start(s32[40,128]{1,0:T(8,128)S(1)} %reduce_sum.54.heard_ref), channel_id=1, source_target_pairs={{0,64},{2,66},{4,68},{6,70},{8,72},{10,74},{12,76},{14,78},{16,80}... | collective-permute-start | bytes 61448 | tf_op jit(solution)/shard_map/ppermute | solution.py:299
  31.5 1.4 copy-done.1
  32.9 1.6 copy-done
  34.5 1.6 copy-done.2
  36.1 2.7 %shard_map.109 = (bf16[48,64,128]{2,1,0:T(8,128)(2,1)S(1)}, bf16[48,64,128]{2,1,0:T(8,128)(2,1)S(1)}, bf16[48,64,128]{2,1,0:T(8,128)(2,1)S(1)}, bf16[48,64,128]{...) custom-call(s32[4]{0:T(128)S(1)} %pad_add_fusion.spot_ref, ...), custom_call_target="tpu_custom_call" | custom-call | bytes 10485760 | tf_op jit(solution)/shard_map/pallas_call | solution.py:66
  38.7 0.9 copy-done.4
  40.2 0.9 copy-done.22
  41.1 0.9 copy-done.23
  42.6 3.4 %collective-permute-start.3 = (bf16[48,64,128]{2,1,0:T(8,128)(2,1)}, bf16[48,64,128]{2,1,0:T(8,128)(2,1)S(1)}, u32[]{:S(2)}, u32[]{:S(2)}) collective-permute-start(bf16[48,64,128]{2,1,0:T(8,128)(2,1)} %get-tuple-element.33), channel_id=1, source_target_pairs={{0,16},{2,18},{4,20},{6,22},{8,24},{10,26},{12,28},{14,30},{16,32}... | collective-permute-start | bytes 2359304 | tf_op jit(solution)/shard_map/ppermute | solution.py:305
  46.0 1.9 %collective-permute-start.4 = (bf16[48,64,128]{2,1,0:T(8,128)(2,1)}, bf16[48,64,128]{2,1,0:T(8,128)(2,1)S(1)}, u32[]{:S(2)}, u32[]{:S(2)}) collective-permute-start(bf16[48,64,128]{2,1,0:T(8,128)(2,1)} %get-tuple-element.34), channel_id=1, source_target_pairs={{0,32},{2,34},{4,36},{6,38},{8,40},{10,42},{12,44},{14,46},{16,48}... | collective-permute-start | bytes 2359304 | tf_op jit(solution)/shard_map/ppermute | solution.py:305
  47.9 3.4 %collective-permute-start.5 = (bf16[48,64,128]{2,1,0:T(8,128)(2,1)}, bf16[48,64,128]{2,1,0:T(8,128)(2,1)}, u32[]{:S(2)}, u32[]{:S(2)}) collective-permute-start(bf16[48,64,128]{2,1,0:T(8,128)(2,1)} %get-tuple-element.35), channel_id=1, source_target_pairs={{0,112},{2,114},{4,116},{6,118},{8,120},{10,122},{12,124},{14,126}... | collective-permute-start | bytes 2359304 | tf_op jit(solution)/shard_map/ppermute | solution.py:305
  51.3 5.1 %collective-permute-start.6 = (bf16[48,64,128]{2,1,0:T(8,128)(2,1)}, bf16[48,64,128]{2,1,0:T(8,128)(2,1)}, u32[]{:S(2)}, u32[]{:S(2)}) collective-permute-start(bf16[48,64,128]{2,1,0:T(8,128)(2,1)} %get-tuple-element.36), channel_id=1, source_target_pairs={{0,96},{2,98},{4,100},{6,102},{8,104},{10,106},{12,108},{14,110},{... | collective-permute-start | bytes 2359304 | tf_op jit(solution)/shard_map/ppermute | solution.py:305
  57.0 2.5 %collective-permute-start.7 = (bf16[48,64,128]{2,1,0:T(8,128)(2,1)}, bf16[48,64,128]{2,1,0:T(8,128)(2,1)}, u32[]{:S(2)}, u32[]{:S(2)}) collective-permute-start(bf16[48,64,128]{2,1,0:T(8,128)(2,1)} %copy-done.23), channel_id=1, source_target_pairs={{0,112},{2,114},{4,116},{6,118},{8,120},{10,122},{12,124},{14,126}... | collective-permute-start | bytes 2359304 | tf_op jit(solution)/shard_map/ppermute | solution.py:305
  59.4 0.7 copy-done.7
  60.8 1.3 shard_map.110.list_ref
  62.1 3.4 %collective-permute-start.8 = (bf16[48,64,128]{2,1,0:T(8,128)(2,1)}, bf16[48,64,128]{2,1,0:T(8,128)(2,1)}, u32[]{:S(2)}, u32[]{:S(2)}) collective-permute-start(bf16[48,64,128]{2,1,0:T(8,128)(2,1)} %copy-done.22), channel_id=1, source_target_pairs={{0,16},{2,18},{4,20},{6,22},{8,24},{10,26},{12,28},{14,30},{16,32}... | collective-permute-start | bytes 2359304 | tf_op jit(solution)/shard_map/ppermute | solution.py:305
  65.5 14.2 %collective-permute-done.6.refs_4_ = bf16[48,64,128]{2,1,0:T(8,128)(2,1)} collective-permute-done((bf16[48,64,128]{2,1,0:T(8,128)(2,1)}, bf16[48,64,128]{2,1,0:T(8,128)(2,1)}, u32[]{:S(2)}, u32[]{:S(2)}) %collective-permute-start.6) | collective-permute-done | bytes 786464 | tf_op jit(solution)/shard_map/ppermute | solution.py:305
  79.8 0.7 copy-done.10
  81.7 7.1 %shard_map.112 = f32[4,4,16,16,128]{4,3,2,1,0:T(8,128)S(1)} custom-call(s32[4]{0:T(128)S(1)} %copy-done.10, s32[64,128]{1,0:T(8,128)S(1)} %shard_map.110.list_ref, f32[32]{0:T(128)S(1)} %copy-done.16, f32[32]{0:T(128)S(1)} %copy-done.19, bf16[48,64,128]{2,1,0:T(8,128)(2,1)S(1)} %get-tuple-element.32.refs_0_, ...), custom_call_target="tpu_custom_call" | custom-call | flops 1000000000 | bytes 10485760 | tf_op jit(solution)/shard_map/pallas_call | solution.py:177
  88.9 1.2 convert_element_type.35
  90.0 4.5 %all-to-all-start.2 = ((f16[4,4,16,16,128]{4,3,2,1,0:T(8,128)(2,1)}), f16[4,4,16,16,128]{4,3,2,1,0:T(8,128)(2,1)}, u32[]{:S(2)}, u32[]{:S(2)}) async-start(f16[4,4,16,16,128]{4,3,2,1,0:T(8,128)(2,1)} %convert_element_type.35), calls=%async_computation.2 | async-start | bytes 2097152 | tf_op jit(solution)/shard_map/all_to_all | solution.py:269
  95.2 0.7 copy-done.15
  95.9 1.1 shard_map.113.list_ref
  97.0 1.1 copy-done.5
  100.2 10.3 %shard_map.114 = f32[4,8,16,16,128]{4,3,2,1,0:T(8,128)S(1)} custom-call(s32[4]{0:T(128)S(1)} %copy-done.12, s32[48,128]{1,0:T(8,128)S(1)} %shard_map.113.list_ref, f32[32]{0:T(128)S(1)} %copy-done.17, f32[32]{0:T(128)S(1)} %copy-done.20, bf16[48,64,128]{2,1,0:T(8,128)(2,1)S(1)} %copy-done.5, bf16[48,64,128]{2,1,0:T(8,128)(2,1)} %collective-permute-done.7.refs_1_, ...), custom_call_target="tpu_custom_call" | custom-call | flops 1000000000 | bytes 10485760 | tf_op jit(solution)/shard_map/pallas_call | solution.py:177
  110.5 1.8 convert_element_type.37
  112.2 4.5 %all-to-all-start.3 = ((f16[4,8,16,16,128]{4,3,2,1,0:T(8,128)(2,1)}), f16[4,8,16,16,128]{4,3,2,1,0:T(8,128)(2,1)}, u32[]{:S(2)}, u32[]{:S(2)}) async-start(f16[4,8,16,16,128]{4,3,2,1,0:T(8,128)(2,1)} %convert_element_type.37), calls=%async_computation.3 | async-start | bytes 4194304 | tf_op jit(solution)/shard_map/all_to_all | solution.py:269
  118.7 10.0 %shard_map.111 = f32[4,4,16,16,128]{4,3,2,1,0:T(8,128)S(1)} custom-call(s32[4]{0:T(128)S(1)} %copy-done.13, s32[64,128]{1,0:T(8,128)S(1)} %shard_map.110.list_ref, f32[32]{0:T(128)S(1)} %copy-done.18, f32[32]{0:T(128)S(1)} %copy-done.21, bf16[48,64,128]{2,1,0:T(8,128)(2,1)S(1)} %get-tuple-element.32.refs_0_, ...), custom_call_target="tpu_custom_call" | custom-call | flops 1000000000 | bytes 10485760 | tf_op jit(solution)/shard_map/pallas_call | solution.py:177
  128.7 1.2 convert_element_type.33
  129.9 6.4 %all-to-all-done.3 = f16[4,8,16,16,128]{4,3,2,1,0:T(8,128)(2,1)} async-done(((f16[4,8,16,16,128]{4,3,2,1,0:T(8,128)(2,1)}), f16[4,8,16,16,128]{4,3,2,1,0:T(8,128)(2,1)}, u32[]{:S(2)}, u32[]{:S(2)}) %all-to-all-start.3) | async-done | bytes 2097184 | tf_op jit(solution)/shard_map/all_to_all | solution.py:269
  136.3 4.9 %all-to-all-start.1 = ((f16[4,4,16,16,128]{4,3,2,1,0:T(8,128)(2,1)}), f16[4,4,16,16,128]{4,3,2,1,0:T(8,128)(2,1)S(1)}, u32[]{:S(2)}, u32[]{:S(2)}) async-start(f16[4,4,16,16,128]{4,3,2,1,0:T(8,128)(2,1)} %convert_element_type.33), calls=%async_computation.1 | async-start | bytes 2097152 | tf_op jit(solution)/shard_map/all_to_all | solution.py:269
  141.2 2.2 %convert_reduce_fusion = f32[8,16,16,128]{3,2,1,0:T(8,128)S(1)} fusion(f16[4,8,16,16,128]{4,3,2,1,0:T(8,128)(2,1)} %all-to-all-done.3), kind=kLoop, calls=%fused_computation | loop fusion | flops 1835008 | bytes 3145728 | tf_op jit(solution)/shard_map/reduce_sum | solution.py:270
  143.4 7.6 %collective-permute-start.9 = (f16[8,16,16,128]{3,2,1,0:T(8,128)(2,1)S(1)}, f16[8,16,16,128]{3,2,1,0:T(8,128)(2,1)S(1)}, u32[]{:S(2)}, u32[]{:S(2)}) collective-permute-start(f16[8,16,16,128]{3,2,1,0:T(8,128)(2,1)S(1)} %convert_element_type.39), channel_id=1, source_target_pairs={{0,64},{2,66},{4,68},{6,70},{8,72},{10,74},{12,76},{14,78},{16,80}... | collective-permute-start | bytes 1572872 | tf_op jit(solution)/shard_map/ppermute | solution.py:319
  151.1 1.4 convert_reduce_fusion.1
  152.7 10.7 %collective-permute-done.9 = f16[8,16,16,128]{3,2,1,0:T(8,128)(2,1)S(1)} collective-permute-done((f16[8,16,16,128]{3,2,1,0:T(8,128)(2,1)S(1)}, f16[8,16,16,128]{3,2,1,0:T(8,128)(2,1)S(1)}, u32[]{:S(2)}, u32[]{:S(2)}) %collective-permute-start.9) | collective-permute-done | bytes 524320 | tf_op jit(solution)/shard_map/ppermute | solution.py:319
  163.4 0.9 fusion.3
  164.3 10.5 %all-to-all-start.4 = ((f16[8,16,16,128]{3,2,1,0:T(8,128)(2,1)}), f16[8,16,16,128]{3,2,1,0:T(8,128)(2,1)S(1)}, u32[]{:S(2)}, u32[]{:S(2)}) async-start(f16[8,16,16,128]{3,2,1,0:T(8,128)(2,1)} %fusion.3), calls=%async_computation.4 | async-start | bytes 1048576 | tf_op jit(solution)/shard_map/all_to_all | solution.py:324
  175.4 12.8 %all-to-all-done.4 = f16[8,16,16,128]{3,2,1,0:T(8,128)(2,1)S(1)} async-done(((f16[8,16,16,128]{3,2,1,0:T(8,128)(2,1)}), f16[8,16,16,128]{3,2,1,0:T(8,128)(2,1)S(1)}, u32[]{:S(2)}, u32[]{:S(2)}) %all-to-all-start.4) | async-done | bytes 524320 | tf_op jit(solution)/shard_map/all_to_all | solution.py:324
  188.2 0.8 fusion.5
  (74 shorter events, 10.1 us)
Async XLA Ops:
  0.0 31.5 %collective-permute-start.2 = (bf16[128,64,128]{2,1,0:T(8,128)(2,1)}, bf16[128,64,128]{2,1,0:T(8,128)(2,1)S(1)}, u32[]{:S(2)}, u32[]{:S(2)}) collective-permute-start(bf16[128,64,128]{2,1,0:T(8,128)(2,1)} %bitcast.23), channel_id=1, source_target_pairs={{0,1},{1,0},{2,3},{3,2},{4,5},{5,4},{6,7},{7,6},{8,9},{9,8},{10,11... | collective-permute-start | bytes 6291464 | tf_op jit(solution)/shard_map/ppermute | solution.py:289
  5.1 16.5 %all-to-all-start = ((s32[8,40,128]{2,1,0:T(8,128)}), s32[8,40,128]{2,1,0:T(8,128)S(1)}, u32[]{:S(2)}, u32[]{:S(2)}) async-start(s32[8,40,128]{2,1,0:T(8,128)} %broadcast_in_dim.27), calls=%async_computation | async-start | bytes 327680 | tf_op jit(solution)/shard_map/all_to_all | solution.py:294
  12.9 18.6 %collective-permute-start.1 = (s32[384]{0:T(512)S(1)}, s32[384]{0:T(512)S(1)}, u32[]{:S(2)}, u32[]{:S(2)}) collective-permute-start(s32[384]{0:T(512)S(1)} %bitcast.25), channel_id=1, source_target_pairs={{0,1},{1,0},{2,3},{3,2},{4,5},{5,4},{6,7},{7,6},{8,9},{9,8},{10,11... | collective-permute-start | bytes 4616 | tf_op jit(solution)/shard_map/ppermute | solution.py:290
  21.7 20.3 %collective-permute-start = (s32[40,128]{1,0:T(8,128)S(1)}, s32[40,128]{1,0:T(8,128)S(1)}, u32[]{:S(2)}, u32[]{:S(2)}) collective-permute-start(s32[40,128]{1,0:T(8,128)S(1)} %reduce_sum.54.heard_ref), channel_id=1, source_target_pairs={{0,64},{2,66},{4,68},{6,70},{8,72},{10,74},{12,76},{14,78},{16,80}... | collective-permute-start | bytes 61448 | tf_op jit(solution)/shard_map/ppermute | solution.py:299
  30.8 0.6 copy-start.6
  31.5 1.4 copy-start.1
  32.9 1.6 copy-start
  34.5 1.6 copy-start.2
  36.1 20.4 %copy-start.24 = (bf16[32,64,64]{2,1,0:T(8,128)(2,1)S(1)}, bf16[32,64,64]{2,1,0:T(8,128)(2,1)}, u32[]{:S(2)}) copy-start(bf16[32,64,64]{2,1,0:T(8,128)(2,1)} %param.18) | copy-start | bytes 786436
  38.7 0.9 copy-start.4
  39.6 0.6 copy-start.8
  40.2 0.9 copy-start.22
  41.1 0.9 copy-start.23
  42.0 14.9 %copy-start.25 = (bf16[64,64]{1,0:T(8,128)(2,1)S(1)}, bf16[64,64]{1,0:T(8,128)(2,1)}, u32[]{:S(2)}) copy-start(bf16[64,64]{1,0:T(8,128)(2,1)} %param.17) | copy-start | bytes 24580
  42.0 37.8 %copy-start.3 = (bf16[16,16,128]{2,1,0:T(8,128)(2,1)S(1)}, bf16[16,16,128]{2,1,0:T(8,128)(2,1)}, u32[]{:S(2)}) copy-start(bf16[16,16,128]{2,1,0:T(8,128)(2,1)} %refs_5_.1) | copy-start | bytes 196612
  42.0 0.6 copy-start.14
  42.6 19.5 %collective-permute-start.3 = (bf16[48,64,128]{2,1,0:T(8,128)(2,1)}, bf16[48,64,128]{2,1,0:T(8,128)(2,1)S(1)}, u32[]{:S(2)}, u32[]{:S(2)}) collective-permute-start(bf16[48,64,128]{2,1,0:T(8,128)(2,1)} %get-tuple-element.33), channel_id=1, source_target_pairs={{0,16},{2,18},{4,20},{6,22},{8,24},{10,26},{12,28},{14,30},{16,32}... | collective-permute-start | bytes 2359304 | tf_op jit(solution)/shard_map/ppermute | solution.py:305
  46.0 19.5 %collective-permute-start.4 = (bf16[48,64,128]{2,1,0:T(8,128)(2,1)}, bf16[48,64,128]{2,1,0:T(8,128)(2,1)S(1)}, u32[]{:S(2)}, u32[]{:S(2)}) collective-permute-start(bf16[48,64,128]{2,1,0:T(8,128)(2,1)} %get-tuple-element.34), channel_id=1, source_target_pairs={{0,32},{2,34},{4,36},{6,38},{8,40},{10,42},{12,44},{14,46},{16,48}... | collective-permute-start | bytes 2359304 | tf_op jit(solution)/shard_map/ppermute | solution.py:305
  47.9 17.6 %collective-permute-start.5 = (bf16[48,64,128]{2,1,0:T(8,128)(2,1)}, bf16[48,64,128]{2,1,0:T(8,128)(2,1)}, u32[]{:S(2)}, u32[]{:S(2)}) collective-permute-start(bf16[48,64,128]{2,1,0:T(8,128)(2,1)} %get-tuple-element.35), channel_id=1, source_target_pairs={{0,112},{2,114},{4,116},{6,118},{8,120},{10,122},{12,124},{14,126}... | collective-permute-start | bytes 2359304 | tf_op jit(solution)/shard_map/ppermute | solution.py:305
  51.3 28.4 %collective-permute-start.6 = (bf16[48,64,128]{2,1,0:T(8,128)(2,1)}, bf16[48,64,128]{2,1,0:T(8,128)(2,1)}, u32[]{:S(2)}, u32[]{:S(2)}) collective-permute-start(bf16[48,64,128]{2,1,0:T(8,128)(2,1)} %get-tuple-element.36), channel_id=1, source_target_pairs={{0,96},{2,98},{4,100},{6,102},{8,104},{10,106},{12,108},{14,110},{... | collective-permute-start | bytes 2359304 | tf_op jit(solution)/shard_map/ppermute | solution.py:305
  57.0 40.1 %collective-permute-start.7 = (bf16[48,64,128]{2,1,0:T(8,128)(2,1)}, bf16[48,64,128]{2,1,0:T(8,128)(2,1)}, u32[]{:S(2)}, u32[]{:S(2)}) collective-permute-start(bf16[48,64,128]{2,1,0:T(8,128)(2,1)} %copy-done.23), channel_id=1, source_target_pairs={{0,112},{2,114},{4,116},{6,118},{8,120},{10,122},{12,124},{14,126}... | collective-permute-start | bytes 2359304 | tf_op jit(solution)/shard_map/ppermute | solution.py:305
  59.4 0.7 copy-start.7
  60.1 0.7 copy-start.9
  62.1 34.9 %collective-permute-start.8 = (bf16[48,64,128]{2,1,0:T(8,128)(2,1)}, bf16[48,64,128]{2,1,0:T(8,128)(2,1)}, u32[]{:S(2)}, u32[]{:S(2)}) collective-permute-start(bf16[48,64,128]{2,1,0:T(8,128)(2,1)} %copy-done.22), channel_id=1, source_target_pairs={{0,16},{2,18},{4,20},{6,22},{8,24},{10,26},{12,28},{14,30},{16,32}... | collective-permute-start | bytes 2359304 | tf_op jit(solution)/shard_map/ppermute | solution.py:305
  79.8 0.7 copy-start.10
  80.4 0.7 copy-start.16
  81.1 0.7 copy-start.19
  90.0 22.2 %all-to-all-start.2 = ((f16[4,4,16,16,128]{4,3,2,1,0:T(8,128)(2,1)}), f16[4,4,16,16,128]{4,3,2,1,0:T(8,128)(2,1)}, u32[]{:S(2)}, u32[]{:S(2)}) async-start(f16[4,4,16,16,128]{4,3,2,1,0:T(8,128)(2,1)} %convert_element_type.35), calls=%async_computation.2 | async-start | bytes 2097152 | tf_op jit(solution)/shard_map/all_to_all | solution.py:269
  94.5 0.7 copy-start.11
  95.2 0.7 copy-start.15
  97.0 1.1 copy-start.5
  98.2 0.7 copy-start.12
  98.8 0.7 copy-start.17
  99.5 0.7 copy-start.20
  112.2 24.0 %all-to-all-start.3 = ((f16[4,8,16,16,128]{4,3,2,1,0:T(8,128)(2,1)}), f16[4,8,16,16,128]{4,3,2,1,0:T(8,128)(2,1)}, u32[]{:S(2)}, u32[]{:S(2)}) async-start(f16[4,8,16,16,128]{4,3,2,1,0:T(8,128)(2,1)} %convert_element_type.37), calls=%async_computation.3 | async-start | bytes 4194304 | tf_op jit(solution)/shard_map/all_to_all | solution.py:269
  116.8 0.7 copy-start.13
  117.4 0.7 copy-start.18
  118.1 0.7 copy-start.21
  136.3 16.3 %all-to-all-start.1 = ((f16[4,4,16,16,128]{4,3,2,1,0:T(8,128)(2,1)}), f16[4,4,16,16,128]{4,3,2,1,0:T(8,128)(2,1)S(1)}, u32[]{:S(2)}, u32[]{:S(2)}) async-start(f16[4,4,16,16,128]{4,3,2,1,0:T(8,128)(2,1)} %convert_element_type.33), calls=%async_computation.1 | async-start | bytes 2097152 | tf_op jit(solution)/shard_map/all_to_all | solution.py:269
  143.4 19.9 %collective-permute-start.9 = (f16[8,16,16,128]{3,2,1,0:T(8,128)(2,1)S(1)}, f16[8,16,16,128]{3,2,1,0:T(8,128)(2,1)S(1)}, u32[]{:S(2)}, u32[]{:S(2)}) collective-permute-start(f16[8,16,16,128]{3,2,1,0:T(8,128)(2,1)S(1)} %convert_element_type.39), channel_id=1, source_target_pairs={{0,64},{2,66},{4,68},{6,70},{8,72},{10,74},{12,76},{14,78},{16,80}... | collective-permute-start | bytes 1572872 | tf_op jit(solution)/shard_map/ppermute | solution.py:319
  152.5 22.3 %copy-start.27 = (s32[16,3]{0,1:T(4,128)S(1)}, s32[16,3]{0,1:T(4,128)}, u32[]{:S(2)}) copy-start(s32[16,3]{0,1:T(4,128)} %param.14) | copy-start | bytes 580
  152.5 22.3 %copy-start.28 = (f32[128]{0:T(128)S(1)}, f32[128]{0:T(128)}, u32[]{:S(2)}) copy-start(f32[128]{0:T(128)} %param.21) | copy-start | bytes 1540
  152.5 22.5 %copy-start.26 = (bf16[64,64]{1,0:T(8,128)(2,1)S(1)}, bf16[64,64]{1,0:T(8,128)(2,1)}, u32[]{:S(2)}) copy-start(bf16[64,64]{1,0:T(8,128)(2,1)} %param.17) | copy-start | bytes 24580
  164.3 23.8 %all-to-all-start.4 = ((f16[8,16,16,128]{3,2,1,0:T(8,128)(2,1)}), f16[8,16,16,128]{3,2,1,0:T(8,128)(2,1)S(1)}, u32[]{:S(2)}, u32[]{:S(2)}) async-start(f16[8,16,16,128]{3,2,1,0:T(8,128)(2,1)} %fusion.3), calls=%async_computation.4 | async-start | bytes 1048576 | tf_op jit(solution)/shard_map/all_to_all | solution.py:324

commit v6 on v5

--- a/solution.py
+++ b/solution.py
@@ -47,14 +47,19 @@
 
 
 DELIVER = [[device(c, a, b) for b in range(RINGS)] for c in range(2) for a in range(RINGS)]
-def pick_kernel(spot_ref, own_slot, sib_slot, own_ref, sib_ref, *out_refs):
+def pick_kernel(spot_ref, own_slot, sib_slot, own_ref, sib_hbm, *refs):
+    out_refs, (sib_ref, sem) = refs[:-2], refs[-2:]
+    copy = pltpu.make_async_copy(sib_hbm, sib_ref, sem)
+    copy.start()
     core, along = spot_ref[0], spot_ref[1]
     far = jnp.where(core == 0, 16, 2)
     near = jnp.where(core == 0, 2, 16)
     count = own_slot.shape[0] // CAP
-    for (ahead, _), out_ref in zip(FAR + NEAR, out_refs, strict=True):
-        first = lax.rem(along + ahead + RINGS, RINGS) * far + core
-        for kind, (slots, store) in enumerate(((own_slot, own_ref), (sib_slot, sib_ref))):
+    for kind, (slots, store) in enumerate(((own_slot, own_ref), (sib_slot, sib_ref))):
+        if kind == 1:
+            copy.wait()
+        for (ahead, _), out_ref in zip(FAR + NEAR, out_refs, strict=True):
+            first = lax.rem(along + ahead + RINGS, RINGS) * far + core
             for c in range(CAP):
                 for r in range(RINGS):
                     slot = slots[c * count + first + r * near]
@@ -65,9 +70,10 @@
     shape = jax.ShapeDtypeStruct((SPAN,) + own.shape[1:], own.dtype)
     return pl.pallas_call(
         pick_kernel,
-        in_specs=[SMEM, SMEM, SMEM, VMEM, VMEM],
+        in_specs=[SMEM, SMEM, SMEM, VMEM, pl.BlockSpec(memory_space=pl.ANY)],
         out_specs=[VMEM] * len(FAR + NEAR),
         out_shape=[shape] * len(FAR + NEAR),
+        scratch_shapes=[pltpu.VMEM(own.shape, own.dtype), pltpu.SemaphoreType.DMA],
         compiler_params=pltpu.CompilerParams(vmem_limit_bytes=24 * 2**20),
         cost_estimate=pl.CostEstimate(flops=0, bytes_accessed=10 * 2**20, transcendentals=0),
     )(spot, own_slots, sib_slots, own, sib)
@@ -75,8 +81,9 @@
 
 def terms_kernel(sources, modes, windows, part, spot_ref, list_ref, re_ref, im_ref, *refs):
     flat_refs = refs[:sources]
-    wide_ref, ham_ref, rho_ref, out_ref, flat, acc = refs[sources:]
-    here = spot_ref[2]
+    wide_ref, ham_ref, rho_ref = refs[sources:sources + 3]
+    out_refs, (flat, acc) = refs[sources + 3:-2], refs[-2:]
+    here, group = spot_ref[2], spot_ref[3]
     share = rho_ref.shape[1]
     width = ham_ref.shape[0]
     pairs = RINGS * windows
@@ -162,9 +169,9 @@
 
     def leave(r, carry):
         for w in range(windows):
-            value = acc[r * windows + w]
-            for b in range(blocks):
-                out_ref[b, r - begin, w] = value[b * share:(b + 1) * share]
+            for shift, out_ref in enumerate(out_refs):
+                block = lax.rem(group + shift, blocks) * share
+                out_ref[r - begin, w] = acc[r * windows + w, pl.ds(pl.multiple_of(block, share), share), :]
         return carry
 
     lax.fori_loop(begin, end, leave, 0)
@@ -177,8 +184,8 @@
     return pl.pallas_call(
         functools.partial(terms_kernel, len(pieces), modes, windows, part),
         in_specs=[SMEM] * 4 + [VMEM] * (len(pieces) + 3),
-        out_specs=VMEM,
-        out_shape=jax.ShapeDtypeStruct((width // share, part[1] - part[0], windows, share, lanes), F32),
+        out_specs=[VMEM] * (width // share),
+        out_shape=[jax.ShapeDtypeStruct((part[1] - part[0], windows, share, lanes), F32)] * (width // share),
         scratch_shapes=[
             pltpu.VMEM((len(pieces) * SPAN, width, lanes), BF16),
             pltpu.VMEM((RINGS * windows + 1, width, lanes), F32),
@@ -188,7 +195,7 @@
     )(spot, lists, coup_re, coup_im, *pieces, maps_wide, head_cols, rho)
 
 
-def lists_kernel(steps, parts, modes, spot_ref, heard_ref, out_ref):
+def lists_of(steps, parts, modes, spot_ref, heard_ref, out_ref):
     core, along, across, group = spot_ref[0], spot_ref[1], spot_ref[2], spot_ref[3]
     pairs = heard_ref.shape[1]
     windows = pairs // RINGS
@@ -253,21 +260,65 @@
     out_ref[last:last + 1] = sums[:1].astype(jnp.int32)
 
 
-def use_lists(steps, parts, modes, spot, heard):
-    rows = modes + CAP + len(parts) * (modes // LOT + CAP) + 1
+def lists_kernel(kinds, modes, spot_ref, *refs):
+    for (steps, parts), heard_ref, out_ref in zip(kinds, refs[:len(kinds)], refs[len(kinds):], strict=True):
+        lists_of(steps, parts, modes, spot_ref, heard_ref, out_ref)
+
+
+def use_lists(kinds, modes, spot, heard):
+    rows = [modes + CAP + len(parts) * (modes // LOT + CAP) + 1 for _, parts in kinds]
     return pl.pallas_call(
-        functools.partial(lists_kernel, steps, parts, modes),
-        in_specs=[SMEM, VMEM],
+        functools.partial(lists_kernel, kinds, modes),
+        in_specs=[SMEM] + [VMEM] * len(kinds),
+        out_specs=[VMEM] * len(kinds),
+        out_shape=[jax.ShapeDtypeStruct((n + -n % 8, heard[0].shape[1]), jnp.int32) for n in rows],
+        compiler_params=pltpu.CompilerParams(vmem_limit_bytes=8 * 2**20),
+        cost_estimate=pl.CostEstimate(flops=10**7, bytes_accessed=2**18, transcendentals=0),
+    )(spot, *heard)
+
+
+def say_kernel(spot_ref, up_ref, down_ref, tri_ref, out_ref):
+    windows, modes = up_ref.shape
+    shape = (windows, out_ref.shape[2])
+    lanes = lax.broadcasted_iota(jnp.int32, shape, 1)
+    row = lax.broadcasted_iota(jnp.int32, shape, 0)
+    place = jnp.where(lanes == spot_ref[2] * windows + row, 1.0, 0.0)
+
+    def put(values, axis):
+        def half(part):
+            return lax.dot_general(
+                part.astype(F32), place, (((axis,), (0,)), ((), ())), preferred_element_type=F32
+            )
+
+        high = lax.shift_right_logical(values, 5)
+        return (half(high) * 32.0 + half(values & 31)).astype(jnp.int32)
+
+    up, down, tri = put(up_ref[...], 0), put(down_ref[...], 1), put(tri_ref[...], 1)
+    spare = jnp.zeros((out_ref.shape[1] - modes - 2 * CAP, shape[1]), jnp.int32)
+    whole = jnp.concatenate([up, down, tri, spare], axis=0)
+    for n in range(out_ref.shape[0]):
+        out_ref[n] = whole
+
+
+def say(spot, use_up, use_down, modes_tri):
+    windows, modes = use_up.shape
+    rows = modes + 2 * CAP
+    return pl.pallas_call(
+        say_kernel,
+        in_specs=[SMEM, VMEM, VMEM, VMEM],
         out_specs=VMEM,
-        out_shape=jax.ShapeDtypeStruct((rows + -rows % 8, heard.shape[1]), jnp.int32),
-        compiler_params=pltpu.CompilerParams(vmem_limit_bytes=8 * 2**20),
-        cost_estimate=pl.CostEstimate(flops=10**7, bytes_accessed=2**17, transcendentals=0),
-    )(spot, heard)
+        out_shape=jax.ShapeDtypeStruct((RINGS, rows + -rows % 8, RINGS * windows), jnp.int32),
+        cost_estimate=pl.CostEstimate(flops=10**6, bytes_accessed=2**18, transcendentals=0),
+    )(spot, use_up, use_down.T, modes_tri.T)
 
 
 def over_groups(parts):
-    parts = lax.all_to_all(parts.astype(LINK), "grp", split_axis=0, concat_axis=0, tiled=True)
-    return jnp.sum(parts.astype(F32), axis=0)
+    count = len(parts)
+    total = parts[0]
+    for shift in (2, 1, 3):
+        ring = [(i, (i + shift) % count) for i in range(count)]
+        total = total + lax.ppermute(parts[shift].astype(LINK), "grp", ring).astype(F32)
+    return total
 
 
 def on_device(
@@ -288,17 +339,13 @@
     slots = jnp.transpose(send_slot[0, 0]).reshape(-1)
     sib_store = lax.ppermute(states[0, 0], "ado", SIBLING)
     sib_slots = lax.ppermute(slots, "ado", SIBLING)
-    said = jnp.concatenate([use_up.T, use_down.T, modes_tri.T, jnp.zeros_like(use_down.T)[:2]], axis=0)
-    lane = jnp.arange(RINGS * windows, dtype=jnp.int32) // windows
-    said = jnp.where(lane == across, jnp.tile(said, (1, RINGS)), 0)
+    said, slots = lax.optimization_barrier((say(spot, use_up, use_down, modes_tri), slots))
     heard = lax.all_to_all(
-        jnp.broadcast_to(said, (RINGS,) + said.shape), "ado", split_axis=0, concat_axis=0, tiled=True,
-        axis_index_groups=DELIVER,
+        said, "ado", split_axis=0, concat_axis=0, tiled=True, axis_index_groups=DELIVER
     )
     heard = jnp.sum(heard, axis=0)
     heard_far = lax.ppermute(heard, "ado", onward(4))
     picked = pick(spot, slots, sib_slots, states[0, 0], sib_store)
-    heard, heard_far, picked = lax.optimization_barrier((heard, heard_far, picked))
 
     def send(steps, blocks):
         return [
@@ -309,18 +356,22 @@
     far_states = send(FAR, picked[:len(FAR)])
     near_states = send(NEAR, picked[len(FAR):])
     half = RINGS // 2
-    far_lists = use_lists(FAR, ((0, RINGS),), modes, spot, heard_far)
-    near_lists = use_lists(NEAR, ((0, half), (half, RINGS)), modes, spot, heard)
+    held, heard_far, heard = lax.optimization_barrier((picked[0], heard_far, heard))
+    far_states[0] = held
+    kinds = ((FAR, ((0, RINGS),)), (NEAR, ((0, half), (half, RINGS))))
+    far_lists, near_lists = use_lists(kinds, modes, spot, (heard_far, heard))
 
     maps_wide = jnp.concatenate([doubled(coupling), jnp.zeros((1, 2 * width, 2 * width), BF16)], axis=0)
     head_cols = lax.dynamic_slice_in_dim(hamiltonian, group * share, share, 1)
     shared = (maps_wide, head_cols, window_tier_states)
-    far = over_groups(terms((0, RINGS, 0), spot, far_lists, coup_re, coup_im, far_states, *shared))
+    far = terms((0, RINGS, 0), spot, far_lists, coup_re, coup_im, far_states, *shared)
+    far, near_lists = lax.optimization_barrier((far, near_lists))
+    far = over_groups(far)
     far = lax.ppermute(far.astype(LINK), "ado", onward(4))
-    near = [
-        over_groups(terms(part, spot, near_lists, coup_re, coup_im, near_states, *shared))
-        for part in ((0, half, 0), (half, RINGS, 1))
-    ]
+    first = terms((0, half, 0), spot, near_lists, coup_re, coup_im, near_states, *shared)
+    first, near_lists = lax.optimization_barrier((first, near_lists))
+    second = terms((half, RINGS, 1), spot, near_lists, coup_re, coup_im, near_states, *shared)
+    near = [over_groups(first), over_groups(second)]
     summed = lax.all_to_all(
         (jnp.concatenate(near, axis=0) + far.astype(F32)).astype(LINK), "ado", split_axis=0, concat_axis=0,
         tiled=True, axis_index_groups=DELIVER,

time: 190 us -> 181 us (0.953)
  the two profiles are of different devices: /device:TPU:130 before, /device:TPU:64 now
where the time goes in v6:
time: 181 us; the launch traced here: 180 us
  starting transfers between devices  86.9 us (48%)
  Pallas kernels  32.7 us (18%)
  waiting for transfers between devices  30.7 us (17%)
  blocking collectives  17.6 us (10%)
  local copies, waits for them, and re-layouts  5.87 us (3%)
  other arithmetic  5.29 us (3%)
    ppermute x9, starting transfers between devices, over_groups(): lax.ppermute(parts[shift].astype(LINK), 'grp', ring).astype(F32)  31.8 us
    ppermute x6, starting transfers between devices, send(): lax.ppermute(block, 'ado', onward(step))  29.5 us
    pallas_call x3, Pallas kernels, terms(): pl.pallas_call(functools.partial(terms_kernel, len(pieces), modes, window...  26.5 us
    all_to_all x1, blocking collectives, on_device(): lax.all_to_all(said, 'ado', split_axis=0, concat_axis=0, tiled=True, axis...  17.6 us
    all_to_all x1, waiting for transfers between devices, on_device(): lax.all_to_all((jnp.concatenate(near, axis=0) + far.astype(F32)).astype(L...  12.8 us
    ppermute x1, waiting for transfers between devices, on_device(): far = lax.ppermute(far.astype(LINK), 'ado', onward(4))  11.2 us
    all_to_all x1, starting transfers between devices, on_device(): lax.all_to_all((jnp.concatenate(near, axis=0) + far.astype(F32)).astype(L...  10.4 us
    unnamed x29, local copies, waits for them, and re-layouts  5.66 us
  transfers between devices with their start and end apart: 20, of which 4 were waited for; matrix products, arithmetic and copies ran while one was open for 3% of the time, Pallas kernels for 16%

profile of v6, /device:TPU:64, one launch (start us, length us, event | category | flops | bytes accessed | tf_op | source)
XLA Modules:
  0.0 179.8 jit_solution(8738147080439925907)
XLA Ops:
  0.0 1.9 %collective-permute-start.1 = (bf16[128,64,128]{2,1,0:T(8,128)(2,1)}, bf16[128,64,128]{2,1,0:T(8,128)(2,1)S(1)}, u32[]{:S(2)}, u32[]{:S(2)}) collective-permute-start(bf16[128,64,128]{2,1,0:T(8,128)(2,1)} %bitcast.20), channel_id=1, source_target_pairs={{0,1},{1,0},{2,3},{3,2},{4,5},{5,4},{6,7},{7,6},{8,9},{9,8},{10,11... | collective-permute-start | bytes 6291464 | tf_op jit(solution)/shard_map/ppermute | solution.py:340
  1.9 0.7 copy.15
  2.6 2.4 %collective-permute-start = (s32[384]{0:T(512)S(1)}, s32[384]{0:T(512)S(1)}, u32[]{:S(2)}, u32[]{:S(2)}) collective-permute-start(s32[384]{0:T(512)S(1)} %bitcast.22), channel_id=1, source_target_pairs={{0,1},{1,0},{2,3},{3,2},{4,5},{5,4},{6,7},{7,6},{8,9},{9,8},{10,11... | collective-permute-start | bytes 4616 | tf_op jit(solution)/shard_map/ppermute | solution.py:341
  5.0 0.7 pad_add_fusion.spot_ref
  5.7 1.7 shard_map.109
  7.3 1.6 copy-done
  8.9 0.7 copy-done.2
  9.6 3.0 %shard_map.110 = (bf16[48,64,128]{2,1,0:T(8,128)(2,1)S(1)}, bf16[48,64,128]{2,1,0:T(8,128)(2,1)}, bf16[48,64,128]{2,1,0:T(8,128)(2,1)}, bf16[48,64,128]{2,1,0:T(...) custom-call(s32[4]{0:T(128)S(1)} %copy-done.2, ...), custom_call_target="tpu_custom_call" | custom-call | bytes 10485760 | tf_op jit(solution)/shard_map/pallas_call | solution.py:71
  12.6 0.9 copy-done.6
  13.5 0.9 copy-done.7
  14.4 0.9 copy-done.8
  15.3 6.9 %collective-permute-start.3 = (bf16[48,64,128]{2,1,0:T(8,128)(2,1)}, bf16[48,64,128]{2,1,0:T(8,128)(2,1)}, u32[]{:S(2)}, u32[]{:S(2)}) collective-permute-start(bf16[48,64,128]{2,1,0:T(8,128)(2,1)} %get-tuple-element.49), channel_id=1, source_target_pairs={{0,112},{2,114},{4,116},{6,118},{8,120},{10,122},{12,124},{14,126}... | collective-permute-start | bytes 2359304 | tf_op jit(solution)/shard_map/ppermute | solution.py:352
  22.2 1.9 %collective-permute-start.4 = (bf16[48,64,128]{2,1,0:T(8,128)(2,1)}, bf16[48,64,128]{2,1,0:T(8,128)(2,1)}, u32[]{:S(2)}, u32[]{:S(2)}) collective-permute-start(bf16[48,64,128]{2,1,0:T(8,128)(2,1)} %get-tuple-element.50), channel_id=1, source_target_pairs={{0,16},{2,18},{4,20},{6,22},{8,24},{10,26},{12,28},{14,30},{16,32}... | collective-permute-start | bytes 2359304 | tf_op jit(solution)/shard_map/ppermute | solution.py:352
  24.2 1.9 %collective-permute-start.5 = (bf16[48,64,128]{2,1,0:T(8,128)(2,1)}, bf16[48,64,128]{2,1,0:T(8,128)(2,1)S(1)}, u32[]{:S(2)}, u32[]{:S(2)}) collective-permute-start(bf16[48,64,128]{2,1,0:T(8,128)(2,1)} %get-tuple-element.58), channel_id=1, source_target_pairs={{0,16},{2,18},{4,20},{6,22},{8,24},{10,26},{12,28},{14,30},{16,32}... | collective-permute-start | bytes 2359304 | tf_op jit(solution)/shard_map/ppermute | solution.py:352
  26.1 6.8 %collective-permute-start.6 = (bf16[48,64,128]{2,1,0:T(8,128)(2,1)}, bf16[48,64,128]{2,1,0:T(8,128)(2,1)S(1)}, u32[]{:S(2)}, u32[]{:S(2)}) collective-permute-start(bf16[48,64,128]{2,1,0:T(8,128)(2,1)} %get-tuple-element.59), channel_id=1, source_target_pairs={{0,32},{2,34},{4,36},{6,38},{8,40},{10,42},{12,44},{14,46},{16,48}... | collective-permute-start | bytes 2359304 | tf_op jit(solution)/shard_map/ppermute | solution.py:352
  32.9 17.6 %all_to_all.10 = s32[8,40,128]{2,1,0:T(8,128)S(1)} all-to-all(s32[8,40,128]{2,1,0:T(8,128)S(1)} %copy-done.10), channel_id=1, replica_groups={{0,2,4,6,8,10,12,14},{16,18,20,22,24,26,28,30},{32,34,36,38,40,42,44,46..., dimensions={0} | all-to-all | bytes 327680 | tf_op jit(solution)/shard_map/all_to_all | solution.py:343
  50.5 5.5 %collective-permute-start.2 = (s32[40,128]{1,0:T(8,128)S(1)}, s32[40,128]{1,0:T(8,128)S(1)}, u32[]{:S(2)}, u32[]{:S(2)}) collective-permute-start(s32[40,128]{1,0:T(8,128)S(1)} %reduce_sum.27.refs_1_), channel_id=1, source_target_pairs={{0,64},{2,66},{4,68},{6,70},{8,72},{10,74},{12,76},{14,78},{16,80}... | collective-permute-start | bytes 61448 | tf_op jit(solution)/shard_map/ppermute | solution.py:347
  56.1 4.1 %collective-permute-done.2.refs_0_ = s32[40,128]{1,0:T(8,128)S(1)} collective-permute-done((s32[40,128]{1,0:T(8,128)S(1)}, s32[40,128]{1,0:T(8,128)S(1)}, u32[]{:S(2)}, u32[]{:S(2)}) %collective-permute-start.2) | collective-permute-done | bytes 20512 | tf_op jit(solution)/shard_map/ppermute | solution.py:347
  60.1 9.9 %collective-permute-start.7 = (bf16[48,64,128]{2,1,0:T(8,128)(2,1)}, bf16[48,64,128]{2,1,0:T(8,128)(2,1)S(1)}, u32[]{:S(2)}, u32[]{:S(2)}) collective-permute-start(bf16[48,64,128]{2,1,0:T(8,128)(2,1)} %copy-done.7), channel_id=1, source_target_pairs={{0,112},{2,114},{4,116},{6,118},{8,120},{10,122},{12,124},{14,126}... | collective-permute-start | bytes 2359304 | tf_op jit(solution)/shard_map/ppermute | solution.py:352
  70.0 2.1 %collective-permute-start.8 = (bf16[48,64,128]{2,1,0:T(8,128)(2,1)}, bf16[48,64,128]{2,1,0:T(8,128)(2,1)}, u32[]{:S(2)}, u32[]{:S(2)}) collective-permute-start(bf16[48,64,128]{2,1,0:T(8,128)(2,1)} %copy-done.6), channel_id=1, source_target_pairs={{0,96},{2,98},{4,100},{6,102},{8,104},{10,106},{12,108},{14,110},{... | collective-permute-start | bytes 2359304 | tf_op jit(solution)/shard_map/ppermute | solution.py:352
  72.1 1.6 fusion.2
  73.7 0.1 concatenate.30.refs_3_.refs_5_
  73.9 1.5 shard_map.111
  75.5 10.1 %shard_map.112 = (f32[8,16,16,128]{3,2,1,0:T(8,128)S(1)}, f32[8,16,16,128]{3,2,1,0:T(8,128)S(1)}, f32[8,16,16,128]{3,2,1,0:T(8,128)S(1)}, f32[8,16,16,128]{3,2,1,0:T(8,128)S(1)}) custom-call(s32[4]{0:T(128)S(1)} %copy-done.3, s32[48,128]{1,0:T(8,128)S(1)} %get-tuple-element.47.list_ref, f32[32]{0:T(128)S(1)} %copy-done.4, f32[32]{0:T(128)S(1)} %copy-done.5, ...), custom_call_target="tpu_custom_call" | custom-call | flops 1000000000 | bytes 10485760 | tf_op jit(solution)/shard_map/pallas_call | solution.py:184
  85.7 3.3 %collective-permute-start.15 = (f16[8,16,16,128]{3,2,1,0:T(8,128)(2,1)S(1)}, f16[8,16,16,128]{3,2,1,0:T(8,128)(2,1)S(1)}, u32[]{:S(2)}, u32[]{:S(2)}) collective-permute-start(f16[8,16,16,128]{3,2,1,0:T(8,128)(2,1)S(1)} %convert_element_type.81), channel_id=1, source_target_pairs={{0,256},{128,384},{256,0},{384,128},{1,257},{129,385},{257,1},{385... | collective-permute-start | bytes 1572872 | tf_op jit(solution)/shard_map/ppermute | solution.py:320
  89.1 2.2 %collective-permute-start.16 = (f16[8,16,16,128]{3,2,1,0:T(8,128)(2,1)S(1)}, f16[8,16,16,128]{3,2,1,0:T(8,128)(2,1)S(1)}, u32[]{:S(2)}, u32[]{:S(2)}) collective-permute-start(f16[8,16,16,128]{3,2,1,0:T(8,128)(2,1)S(1)} %convert_element_type.83), channel_id=1, source_target_pairs={{0,128},{128,256},{256,384},{384,0},{1,129},{129,257},{257,385},{3... | collective-permute-start | bytes 1572872 | tf_op jit(solution)/shard_map/ppermute | solution.py:320
  91.4 4.9 %collective-permute-start.17 = (f16[8,16,16,128]{3,2,1,0:T(8,128)(2,1)S(1)}, f16[8,16,16,128]{3,2,1,0:T(8,128)(2,1)S(1)}, u32[]{:S(2)}, u32[]{:S(2)}) collective-permute-start(f16[8,16,16,128]{3,2,1,0:T(8,128)(2,1)S(1)} %convert_element_type.85), channel_id=1, source_target_pairs={{0,384},{128,0},{256,128},{384,256},{1,385},{129,1},{257,129},{385... | collective-permute-start | bytes 1572872 | tf_op jit(solution)/shard_map/ppermute | solution.py:320
  96.2 2.7 %collective-permute-done.8.refs_4_ = bf16[48,64,128]{2,1,0:T(8,128)(2,1)} collective-permute-done((bf16[48,64,128]{2,1,0:T(8,128)(2,1)}, bf16[48,64,128]{2,1,0:T(8,128)(2,1)}, u32[]{:S(2)}, u32[]{:S(2)}) %collective-permute-start.8) | collective-permute-done | bytes 786464 | tf_op jit(solution)/shard_map/ppermute | solution.py:352
  98.9 9.8 %shard_map.113 = (f32[4,16,16,128]{3,2,1,0:T(8,128)S(1)}, f32[4,16,16,128]{3,2,1,0:T(8,128)S(1)}, f32[4,16,16,128]{3,2,1,0:T(8,128)S(1)}, f32[4,16,16,128]{3,2,1,0:T(8,128)S(1)}) custom-call(s32[4]{0:T(128)S(1)} %copy-done.3, s32[64,128]{1,0:T(8,128)S(1)} %get-tuple-element.70.list_ref, f32[32]{0:T(128)S(1)} %copy-done.4, f32[32]{0:T(128)S(1)} %copy-done.5, ...), custom_call_target="tpu_custom_call" | custom-call | flops 1000000000 | bytes 10485760 | tf_op jit(solution)/shard_map/pallas_call | solution.py:184
  108.8 2.0 %collective-permute-start.10 = (f16[4,16,16,128]{3,2,1,0:T(8,128)(2,1)S(1)}, f16[4,16,16,128]{3,2,1,0:T(8,128)(2,1)S(1)}, u32[]{:S(2)}, u32[]{:S(2)}) collective-permute-start(f16[4,16,16,128]{3,2,1,0:T(8,128)(2,1)S(1)} %convert_element_type.71), channel_id=1, source_target_pairs={{0,128},{128,256},{256,384},{384,0},{1,129},{129,257},{257,385},{3... | collective-permute-start | bytes 786440 | tf_op jit(solution)/shard_map/ppermute | solution.py:320
  110.8 5.1 %collective-permute-start.11 = (f16[4,16,16,128]{3,2,1,0:T(8,128)(2,1)S(1)}, f16[4,16,16,128]{3,2,1,0:T(8,128)(2,1)S(1)}, u32[]{:S(2)}, u32[]{:S(2)}) collective-permute-start(f16[4,16,16,128]{3,2,1,0:T(8,128)(2,1)S(1)} %convert_element_type.73), channel_id=1, source_target_pairs={{0,384},{128,0},{256,128},{384,256},{1,385},{129,1},{257,129},{385... | collective-permute-start | bytes 786440 | tf_op jit(solution)/shard_map/ppermute | solution.py:320
  116.0 6.6 %shard_map.114 = (f32[4,16,16,128]{3,2,1,0:T(8,128)S(1)}, f32[4,16,16,128]{3,2,1,0:T(8,128)S(1)}, f32[4,16,16,128]{3,2,1,0:T(8,128)S(1)}, f32[4,16,16,128]{3,2,1,0:T(8,128)S(1)}) custom-call(s32[4]{0:T(128)S(1)} %copy-done.3, s32[64,128]{1,0:T(8,128)S(1)} %get-tuple-element.70.list_ref, f32[32]{0:T(128)S(1)} %copy-done.4, f32[32]{0:T(128)S(1)} %copy-done.5, ...), custom_call_target="tpu_custom_call" | custom-call | flops 1000000000 | bytes 10485760 | tf_op jit(solution)/shard_map/pallas_call | solution.py:184
  122.7 1.9 %collective-permute-start.9 = (f16[4,16,16,128]{3,2,1,0:T(8,128)(2,1)S(1)}, f16[4,16,16,128]{3,2,1,0:T(8,128)(2,1)S(1)}, u32[]{:S(2)}, u32[]{:S(2)}) collective-permute-start(f16[4,16,16,128]{3,2,1,0:T(8,128)(2,1)S(1)} %convert_element_type.69), channel_id=1, source_target_pairs={{0,256},{128,384},{256,0},{384,128},{1,257},{129,385},{257,1},{385... | collective-permute-start | bytes 786440 | tf_op jit(solution)/shard_map/ppermute | solution.py:320
  124.6 5.4 %collective-permute-start.12 = (f16[4,16,16,128]{3,2,1,0:T(8,128)(2,1)S(1)}, f16[4,16,16,128]{3,2,1,0:T(8,128)(2,1)S(1)}, u32[]{:S(2)}, u32[]{:S(2)}) collective-permute-start(f16[4,16,16,128]{3,2,1,0:T(8,128)(2,1)S(1)} %convert_element_type.75), channel_id=1, source_target_pairs={{0,256},{128,384},{256,0},{384,128},{1,257},{129,385},{257,1},{385... | collective-permute-start | bytes 786440 | tf_op jit(solution)/shard_map/ppermute | solution.py:320
  130.1 1.9 %collective-permute-start.13 = (f16[4,16,16,128]{3,2,1,0:T(8,128)(2,1)S(1)}, f16[4,16,16,128]{3,2,1,0:T(8,128)(2,1)S(1)}, u32[]{:S(2)}, u32[]{:S(2)}) collective-permute-start(f16[4,16,16,128]{3,2,1,0:T(8,128)(2,1)S(1)} %convert_element_type.77), channel_id=1, source_target_pairs={{0,128},{128,256},{256,384},{384,0},{1,129},{129,257},{257,385},{3... | collective-permute-start | bytes 786440 | tf_op jit(solution)/shard_map/ppermute | solution.py:320
  132.0 0.3 add_convert_fusion
  132.3 5.1 %collective-permute-start.14 = (f16[4,16,16,128]{3,2,1,0:T(8,128)(2,1)S(1)}, f16[4,16,16,128]{3,2,1,0:T(8,128)(2,1)S(1)}, u32[]{:S(2)}, u32[]{:S(2)}) collective-permute-start(f16[4,16,16,128]{3,2,1,0:T(8,128)(2,1)S(1)} %convert_element_type.79), channel_id=1, source_target_pairs={{0,384},{128,0},{256,128},{384,256},{1,385},{129,1},{257,129},{385... | collective-permute-start | bytes 786440 | tf_op jit(solution)/shard_map/ppermute | solution.py:320
  137.4 5.4 %collective-permute-start.18 = (f16[8,16,16,128]{3,2,1,0:T(8,128)(2,1)S(1)}, f16[8,16,16,128]{3,2,1,0:T(8,128)(2,1)S(1)}, u32[]{:S(2)}, u32[]{:S(2)}) collective-permute-start(f16[8,16,16,128]{3,2,1,0:T(8,128)(2,1)S(1)} %add_convert_fusion), channel_id=1, source_target_pairs={{0,64},{2,66},{4,68},{6,70},{8,72},{10,74},{12,76},{14,78},{16,80}... | collective-permute-start | bytes 1572872 | tf_op jit(solution)/shard_map/ppermute | solution.py:370
  142.9 0.1 convert_add_fusion.1
  143.0 0.1 convert_add_fusion
  143.1 11.2 %collective-permute-done.18 = f16[8,16,16,128]{3,2,1,0:T(8,128)(2,1)S(1)} collective-permute-done((f16[8,16,16,128]{3,2,1,0:T(8,128)(2,1)S(1)}, f16[8,16,16,128]{3,2,1,0:T(8,128)(2,1)S(1)}, u32[]{:S(2)}, u32[]{:S(2)}) %collective-permute-start.18) | collective-permute-done | bytes 524320 | tf_op jit(solution)/shard_map/ppermute | solution.py:370
  154.3 0.9 fusion.3
  155.3 10.4 %all-to-all-start.1 = ((f16[8,16,16,128]{3,2,1,0:T(8,128)(2,1)}), f16[8,16,16,128]{3,2,1,0:T(8,128)(2,1)S(1)}, u32[]{:S(2)}, u32[]{:S(2)}) async-start(f16[8,16,16,128]{3,2,1,0:T(8,128)(2,1)} %fusion.3), calls=%async_computation.1 | async-start | bytes 1048576 | tf_op jit(solution)/shard_map/all_to_all | solution.py:375
  165.7 0.2 select_reduce_fusion
  165.9 0.2 convolution_bitcast_fusion
  166.1 0.1 fusion.19
  166.2 12.8 %all-to-all-done.1 = f16[8,16,16,128]{3,2,1,0:T(8,128)(2,1)S(1)} async-done(((f16[8,16,16,128]{3,2,1,0:T(8,128)(2,1)}), f16[8,16,16,128]{3,2,1,0:T(8,128)(2,1)S(1)}, u32[]{:S(2)}, u32[]{:S(2)}) %all-to-all-start.1) | async-done | bytes 524320 | tf_op jit(solution)/shard_map/all_to_all | solution.py:375
  179.0 0.8 fusion.5
  (51 shorter events, 0.7 us)
Async XLA Ops:
  0.0 7.3 %collective-permute-start.1 = (bf16[128,64,128]{2,1,0:T(8,128)(2,1)}, bf16[128,64,128]{2,1,0:T(8,128)(2,1)S(1)}, u32[]{:S(2)}, u32[]{:S(2)}) collective-permute-start(bf16[128,64,128]{2,1,0:T(8,128)(2,1)} %bitcast.20), channel_id=1, source_target_pairs={{0,1},{1,0},{2,3},{3,2},{4,5},{5,4},{6,7},{7,6},{8,9},{9,8},{10,11... | collective-permute-start | bytes 6291464 | tf_op jit(solution)/shard_map/ppermute | solution.py:340
  2.6 4.7 %collective-permute-start = (s32[384]{0:T(512)S(1)}, s32[384]{0:T(512)S(1)}, u32[]{:S(2)}, u32[]{:S(2)}) collective-permute-start(s32[384]{0:T(512)S(1)} %bitcast.22), channel_id=1, source_target_pairs={{0,1},{1,0},{2,3},{3,2},{4,5},{5,4},{6,7},{7,6},{8,9},{9,8},{10,11... | collective-permute-start | bytes 4616 | tf_op jit(solution)/shard_map/ppermute | solution.py:341
  7.3 1.6 copy-start
  8.9 0.7 copy-start.2
  9.6 23.3 %copy-start.10 = (s32[8,40,128]{2,1,0:T(8,128)S(1)}, s32[8,40,128]{2,1,0:T(8,128)}, u32[]{:S(2)}) copy-start(s32[8,40,128]{2,1,0:T(8,128)} %shard_map.109) | copy-start | bytes 491524
  12.6 0.9 copy-start.6
  13.5 0.9 copy-start.7
  14.4 0.9 copy-start.8
  15.3 54.7 %collective-permute-start.3 = (bf16[48,64,128]{2,1,0:T(8,128)(2,1)}, bf16[48,64,128]{2,1,0:T(8,128)(2,1)}, u32[]{:S(2)}, u32[]{:S(2)}) collective-permute-start(bf16[48,64,128]{2,1,0:T(8,128)(2,1)} %get-tuple-element.49), channel_id=1, source_target_pairs={{0,112},{2,114},{4,116},{6,118},{8,120},{10,122},{12,124},{14,126}... | collective-permute-start | bytes 2359304 | tf_op jit(solution)/shard_map/ppermute | solution.py:352
  22.2 53.2 %collective-permute-start.4 = (bf16[48,64,128]{2,1,0:T(8,128)(2,1)}, bf16[48,64,128]{2,1,0:T(8,128)(2,1)}, u32[]{:S(2)}, u32[]{:S(2)}) collective-permute-start(bf16[48,64,128]{2,1,0:T(8,128)(2,1)} %get-tuple-element.50), channel_id=1, source_target_pairs={{0,16},{2,18},{4,20},{6,22},{8,24},{10,26},{12,28},{14,30},{16,32}... | collective-permute-start | bytes 2359304 | tf_op jit(solution)/shard_map/ppermute | solution.py:352
  24.2 65.0 %collective-permute-start.5 = (bf16[48,64,128]{2,1,0:T(8,128)(2,1)}, bf16[48,64,128]{2,1,0:T(8,128)(2,1)S(1)}, u32[]{:S(2)}, u32[]{:S(2)}) collective-permute-start(bf16[48,64,128]{2,1,0:T(8,128)(2,1)} %get-tuple-element.58), channel_id=1, source_target_pairs={{0,16},{2,18},{4,20},{6,22},{8,24},{10,26},{12,28},{14,30},{16,32}... | collective-permute-start | bytes 2359304 | tf_op jit(solution)/shard_map/ppermute | solution.py:352
  26.1 47.7 %copy-start.11 = (bf16[64,64]{1,0:T(8,128)(2,1)S(1)}, bf16[64,64]{1,0:T(8,128)(2,1)}, u32[]{:S(2)}) copy-start(bf16[64,64]{1,0:T(8,128)(2,1)} %param.17) | copy-start | bytes 24580
  26.1 47.8 %copy-start.3 = (s32[4]{0:T(128)S(1)}, s32[4]{0:T(128)}, u32[]{:S(2)}) copy-start(s32[4]{0:T(128)} %pad_add_fusion.spot_ref) | copy-start | bytes 52
  26.1 49.3 %copy-start.1 = (bf16[16,16,128]{2,1,0:T(8,128)(2,1)S(1)}, bf16[16,16,128]{2,1,0:T(8,128)(2,1)}, u32[]{:S(2)}) copy-start(bf16[16,16,128]{2,1,0:T(8,128)(2,1)} %refs_7_.3) | copy-start | bytes 196612
  26.1 49.3 %copy-start.4 = (f32[32]{0:T(128)S(1)}, f32[32]{0:T(128)}, u32[]{:S(2)}) copy-start(f32[32]{0:T(128)} %re_ref.5) | copy-start | bytes 388
  26.1 49.3 %copy-start.5 = (f32[32]{0:T(128)S(1)}, f32[32]{0:T(128)}, u32[]{:S(2)}) copy-start(f32[32]{0:T(128)} %im_ref.5) | copy-start | bytes 388
  26.1 65.2 %collective-permute-start.6 = (bf16[48,64,128]{2,1,0:T(8,128)(2,1)}, bf16[48,64,128]{2,1,0:T(8,128)(2,1)S(1)}, u32[]{:S(2)}, u32[]{:S(2)}) collective-permute-start(bf16[48,64,128]{2,1,0:T(8,128)(2,1)} %get-tuple-element.59), channel_id=1, source_target_pairs={{0,32},{2,34},{4,36},{6,38},{8,40},{10,42},{12,44},{14,46},{16,48}... | collective-permute-start | bytes 2359304 | tf_op jit(solution)/shard_map/ppermute | solution.py:352
  50.5 9.6 %collective-permute-start.2 = (s32[40,128]{1,0:T(8,128)S(1)}, s32[40,128]{1,0:T(8,128)S(1)}, u32[]{:S(2)}, u32[]{:S(2)}) collective-permute-start(s32[40,128]{1,0:T(8,128)S(1)} %reduce_sum.27.refs_1_), channel_id=1, source_target_pairs={{0,64},{2,66},{4,68},{6,70},{8,72},{10,74},{12,76},{14,78},{16,80}... | collective-permute-start | bytes 61448 | tf_op jit(solution)/shard_map/ppermute | solution.py:347
  60.1 36.1 %collective-permute-start.7 = (bf16[48,64,128]{2,1,0:T(8,128)(2,1)}, bf16[48,64,128]{2,1,0:T(8,128)(2,1)S(1)}, u32[]{:S(2)}, u32[]{:S(2)}) collective-permute-start(bf16[48,64,128]{2,1,0:T(8,128)(2,1)} %copy-done.7), channel_id=1, source_target_pairs={{0,112},{2,114},{4,116},{6,118},{8,120},{10,122},{12,124},{14,126}... | collective-permute-start | bytes 2359304 | tf_op jit(solution)/shard_map/ppermute | solution.py:352
  70.0 28.9 %collective-permute-start.8 = (bf16[48,64,128]{2,1,0:T(8,128)(2,1)}, bf16[48,64,128]{2,1,0:T(8,128)(2,1)}, u32[]{:S(2)}, u32[]{:S(2)}) collective-permute-start(bf16[48,64,128]{2,1,0:T(8,128)(2,1)} %copy-done.6), channel_id=1, source_target_pairs={{0,96},{2,98},{4,100},{6,102},{8,104},{10,106},{12,108},{14,110},{... | collective-permute-start | bytes 2359304 | tf_op jit(solution)/shard_map/ppermute | solution.py:352
  72.1 3.4 %copy-start.9 = (bf16[48,64,128]{2,1,0:T(8,128)(2,1)S(1)}, bf16[48,64,128]{2,1,0:T(8,128)(2,1)}, u32[]{:S(2)}) copy-start(bf16[48,64,128]{2,1,0:T(8,128)(2,1)} %copy-done.8) | copy-start | bytes 2359300
  85.7 37.0 %collective-permute-start.15 = (f16[8,16,16,128]{3,2,1,0:T(8,128)(2,1)S(1)}, f16[8,16,16,128]{3,2,1,0:T(8,128)(2,1)S(1)}, u32[]{:S(2)}, u32[]{:S(2)}) collective-permute-start(f16[8,16,16,128]{3,2,1,0:T(8,128)(2,1)S(1)} %convert_element_type.81), channel_id=1, source_target_pairs={{0,256},{128,384},{256,0},{384,128},{1,257},{129,385},{257,1},{385... | collective-permute-start | bytes 1572872 | tf_op jit(solution)/shard_map/ppermute | solution.py:320
  89.1 35.5 %collective-permute-start.16 = (f16[8,16,16,128]{3,2,1,0:T(8,128)(2,1)S(1)}, f16[8,16,16,128]{3,2,1,0:T(8,128)(2,1)S(1)}, u32[]{:S(2)}, u32[]{:S(2)}) collective-permute-start(f16[8,16,16,128]{3,2,1,0:T(8,128)(2,1)S(1)} %convert_element_type.83), channel_id=1, source_target_pairs={{0,128},{128,256},{256,384},{384,0},{1,129},{129,257},{257,385},{3... | collective-permute-start | bytes 1572872 | tf_op jit(solution)/shard_map/ppermute | solution.py:320
  91.4 38.7 %collective-permute-start.17 = (f16[8,16,16,128]{3,2,1,0:T(8,128)(2,1)S(1)}, f16[8,16,16,128]{3,2,1,0:T(8,128)(2,1)S(1)}, u32[]{:S(2)}, u32[]{:S(2)}) collective-permute-start(f16[8,16,16,128]{3,2,1,0:T(8,128)(2,1)S(1)} %convert_element_type.85), channel_id=1, source_target_pairs={{0,384},{128,0},{256,128},{384,256},{1,385},{129,1},{257,129},{385... | collective-permute-start | bytes 1572872 | tf_op jit(solution)/shard_map/ppermute | solution.py:320
  108.8 23.5 %collective-permute-start.10 = (f16[4,16,16,128]{3,2,1,0:T(8,128)(2,1)S(1)}, f16[4,16,16,128]{3,2,1,0:T(8,128)(2,1)S(1)}, u32[]{:S(2)}, u32[]{:S(2)}) collective-permute-start(f16[4,16,16,128]{3,2,1,0:T(8,128)(2,1)S(1)} %convert_element_type.71), channel_id=1, source_target_pairs={{0,128},{128,256},{256,384},{384,0},{1,129},{129,257},{257,385},{3... | collective-permute-start | bytes 786440 | tf_op jit(solution)/shard_map/ppermute | solution.py:320
  110.8 26.6 %collective-permute-start.11 = (f16[4,16,16,128]{3,2,1,0:T(8,128)(2,1)S(1)}, f16[4,16,16,128]{3,2,1,0:T(8,128)(2,1)S(1)}, u32[]{:S(2)}, u32[]{:S(2)}) collective-permute-start(f16[4,16,16,128]{3,2,1,0:T(8,128)(2,1)S(1)} %convert_element_type.73), channel_id=1, source_target_pairs={{0,384},{128,0},{256,128},{384,256},{1,385},{129,1},{257,129},{385... | collective-permute-start | bytes 786440 | tf_op jit(solution)/shard_map/ppermute | solution.py:320
  122.7 20.2 %collective-permute-start.9 = (f16[4,16,16,128]{3,2,1,0:T(8,128)(2,1)S(1)}, f16[4,16,16,128]{3,2,1,0:T(8,128)(2,1)S(1)}, u32[]{:S(2)}, u32[]{:S(2)}) collective-permute-start(f16[4,16,16,128]{3,2,1,0:T(8,128)(2,1)S(1)} %convert_element_type.69), channel_id=1, source_target_pairs={{0,256},{128,384},{256,0},{384,128},{1,257},{129,385},{257,1},{385... | collective-permute-start | bytes 786440 | tf_op jit(solution)/shard_map/ppermute | solution.py:320
  124.6 18.4 %collective-permute-start.12 = (f16[4,16,16,128]{3,2,1,0:T(8,128)(2,1)S(1)}, f16[4,16,16,128]{3,2,1,0:T(8,128)(2,1)S(1)}, u32[]{:S(2)}, u32[]{:S(2)}) collective-permute-start(f16[4,16,16,128]{3,2,1,0:T(8,128)(2,1)S(1)} %convert_element_type.75), channel_id=1, source_target_pairs={{0,256},{128,384},{256,0},{384,128},{1,257},{129,385},{257,1},{385... | collective-permute-start | bytes 786440 | tf_op jit(solution)/shard_map/ppermute | solution.py:320
  130.1 12.9 %collective-permute-start.13 = (f16[4,16,16,128]{3,2,1,0:T(8,128)(2,1)S(1)}, f16[4,16,16,128]{3,2,1,0:T(8,128)(2,1)S(1)}, u32[]{:S(2)}, u32[]{:S(2)}) collective-permute-start(f16[4,16,16,128]{3,2,1,0:T(8,128)(2,1)S(1)} %convert_element_type.77), channel_id=1, source_target_pairs={{0,128},{128,256},{256,384},{384,0},{1,129},{129,257},{257,385},{3... | collective-permute-start | bytes 786440 | tf_op jit(solution)/shard_map/ppermute | solution.py:320
  132.3 10.7 %collective-permute-start.14 = (f16[4,16,16,128]{3,2,1,0:T(8,128)(2,1)S(1)}, f16[4,16,16,128]{3,2,1,0:T(8,128)(2,1)S(1)}, u32[]{:S(2)}, u32[]{:S(2)}) collective-permute-start(f16[4,16,16,128]{3,2,1,0:T(8,128)(2,1)S(1)} %convert_element_type.79), channel_id=1, source_target_pairs={{0,384},{128,0},{256,128},{384,256},{1,385},{129,1},{257,129},{385... | collective-permute-start | bytes 786440 | tf_op jit(solution)/shard_map/ppermute | solution.py:320
  137.4 16.9 %collective-permute-start.18 = (f16[8,16,16,128]{3,2,1,0:T(8,128)(2,1)S(1)}, f16[8,16,16,128]{3,2,1,0:T(8,128)(2,1)S(1)}, u32[]{:S(2)}, u32[]{:S(2)}) collective-permute-start(f16[8,16,16,128]{3,2,1,0:T(8,128)(2,1)S(1)} %add_convert_fusion), channel_id=1, source_target_pairs={{0,64},{2,66},{4,68},{6,70},{8,72},{10,74},{12,76},{14,78},{16,80}... | collective-permute-start | bytes 1572872 | tf_op jit(solution)/shard_map/ppermute | solution.py:370
  143.0 22.7 %copy-start.12 = (s32[16,3]{0,1:T(4,128)S(1)}, s32[16,3]{0,1:T(4,128)}, u32[]{:S(2)}) copy-start(s32[16,3]{0,1:T(4,128)} %param.14) | copy-start | bytes 580
  143.0 22.7 %copy-start.13 = (f32[128]{0:T(128)S(1)}, f32[128]{0:T(128)}, u32[]{:S(2)}) copy-start(f32[128]{0:T(128)} %param.21) | copy-start | bytes 1540
  155.3 23.7 %all-to-all-start.1 = ((f16[8,16,16,128]{3,2,1,0:T(8,128)(2,1)}), f16[8,16,16,128]{3,2,1,0:T(8,128)(2,1)S(1)}, u32[]{:S(2)}, u32[]{:S(2)}) async-start(f16[8,16,16,128]{3,2,1,0:T(8,128)(2,1)} %fusion.3), calls=%async_computation.1 | async-start | bytes 1048576 | tf_op jit(solution)/shard_map/all_to_all | solution.py:375

commit v7 on v6

--- a/solution.py
+++ b/solution.py
@@ -339,11 +339,11 @@
     slots = jnp.transpose(send_slot[0, 0]).reshape(-1)
     sib_store = lax.ppermute(states[0, 0], "ado", SIBLING)
     sib_slots = lax.ppermute(slots, "ado", SIBLING)
-    said, slots = lax.optimization_barrier((say(spot, use_up, use_down, modes_tri), slots))
     heard = lax.all_to_all(
-        said, "ado", split_axis=0, concat_axis=0, tiled=True, axis_index_groups=DELIVER
+        say(spot, use_up, use_down, modes_tri), "ado", split_axis=0, concat_axis=0, tiled=True,
+        axis_index_groups=DELIVER,
     )
-    heard = jnp.sum(heard, axis=0)
+    heard, slots = lax.optimization_barrier((jnp.sum(heard, axis=0), slots))
     heard_far = lax.ppermute(heard, "ado", onward(4))
     picked = pick(spot, slots, sib_slots, states[0, 0], sib_store)
 

time: 181 us -> 192 us (1.061)
  starting transfers between devices: 86.9 us -> 111 us
  blocking collectives: 17.6 us -> 0 us
  waiting for transfers between devices: 30.7 us -> 35.8 us
    all_to_all x1 -> x0, blocking collectives: 17.6 us -> none  [on_device(): lax.all_to_all(said, 'ado', split_axis=0, concat_axis=0, tiled=True, axis...]
    ppermute x6, starting transfers between devices: 29.5 us -> 43.7 us  [send(): lax.ppermute(block, 'ado', onward(step))]
    all_to_all x0 -> x1, starting transfers between devices: none -> 7.1 us  [on_device(): lax.all_to_all(say(spot, use_up, use_down, modes_tri), 'ado', split_axis=...]
    all_to_all x0 -> x1, waiting for transfers between devices: none -> 4.04 us  [on_device(): lax.all_to_all(say(spot, use_up, use_down, modes_tri), 'ado', split_axis=...]
    all_to_all x1, starting transfers between devices: 10.4 us -> 7 us  [on_device(): lax.all_to_all((jnp.concatenate(near, axis=0) + far.astype(F32)).astype(L...]
    ppermute x9, starting transfers between devices: 31.8 us -> 34.4 us  [over_groups(): lax.ppermute(parts[shift].astype(LINK), 'grp', ring).astype(F32)]
    ppermute x1, waiting for transfers between devices: 11.2 us -> 13.7 us  [on_device(): far = lax.ppermute(far.astype(LINK), 'ado', onward(4))]
    ppermute x1, starting transfers between devices: 2.39 us -> 4.7 us  [on_device(): sib_slots = lax.ppermute(slots, 'ado', SIBLING)]
  transfers between devices with their start and end apart: 20 -> 21, of which waited for: 4 -> 5; matrix products, arithmetic and copies ran while one was open for 3% -> 2% of each run, Pallas kernels for 16% -> 15%
where the time goes in v7:
time: 192 us; the launch traced here: 190 us
  starting transfers between devices  111 us (58%)
  waiting for transfers between devices  35.8 us (19%)
  Pallas kernels  32.3 us (17%)
  other arithmetic  5.28 us (3%)
  local copies, waits for them, and re-layouts  4.92 us (3%)
    ppermute x6, starting transfers between devices, send(): lax.ppermute(block, 'ado', onward(step))  43.7 us
    ppermute x9, starting transfers between devices, over_groups(): lax.ppermute(parts[shift].astype(LINK), 'grp', ring).astype(F32)  34.4 us
    pallas_call x3, Pallas kernels, terms(): pl.pallas_call(functools.partial(terms_kernel, len(pieces), modes, window...  25.9 us
    ppermute x1, waiting for transfers between devices, on_device(): far = lax.ppermute(far.astype(LINK), 'ado', onward(4))  13.7 us
    all_to_all x1, waiting for transfers between devices, on_device(): lax.all_to_all((jnp.concatenate(near, axis=0) + far.astype(F32)).astype(L...  12.8 us
    all_to_all x1, starting transfers between devices, on_device(): lax.all_to_all(say(spot, use_up, use_down, modes_tri), 'ado', split_axis=...  7.1 us
    all_to_all x1, starting transfers between devices, on_device(): lax.all_to_all((jnp.concatenate(near, axis=0) + far.astype(F32)).astype(L...  7 us
    ppermute x1, starting transfers between devices, on_device(): far = lax.ppermute(far.astype(LINK), 'ado', onward(4))  6.7 us
  transfers between devices with their start and end apart: 21, of which 5 were waited for; matrix products, arithmetic and copies ran while one was open for 2% of the time, Pallas kernels for 15%

profile of v7, /device:TPU:64, one launch (start us, length us, event | category | flops | bytes accessed | tf_op | source)
XLA Modules:
  0.0 190.5 jit_solution(17736106498260996077)
XLA Ops:
  0.0 1.9 %collective-permute-start.1 = (bf16[128,64,128]{2,1,0:T(8,128)(2,1)}, bf16[128,64,128]{2,1,0:T(8,128)(2,1)S(1)}, u32[]{:S(2)}, u32[]{:S(2)}) collective-permute-start(bf16[128,64,128]{2,1,0:T(8,128)(2,1)} %bitcast.20), channel_id=1, source_target_pairs={{0,1},{1,0},{2,3},{3,2},{4,5},{5,4},{6,7},{7,6},{8,9},{9,8},{10,11... | collective-permute-start | bytes 6291464 | tf_op jit(solution)/shard_map/ppermute | solution.py:340
  1.9 0.6 pad_add_fusion.spot_ref
  2.5 1.7 shard_map.109
  4.2 7.1 %all-to-all-start = ((s32[8,40,128]{2,1,0:T(8,128)}), s32[8,40,128]{2,1,0:T(8,128)S(1)}, u32[]{:S(2)}, u32[]{:S(2)}) async-start(s32[8,40,128]{2,1,0:T(8,128)} %shard_map.109), calls=%async_computation | async-start | bytes 327680 | tf_op jit(solution)/shard_map/all_to_all | solution.py:342
  11.3 0.7 copy.15
  12.0 4.7 %collective-permute-start = (s32[384]{0:T(512)S(1)}, s32[384]{0:T(512)S(1)}, u32[]{:S(2)}, u32[]{:S(2)}) collective-permute-start(s32[384]{0:T(512)S(1)} %bitcast.22), channel_id=1, source_target_pairs={{0,1},{1,0},{2,3},{3,2},{4,5},{5,4},{6,7},{7,6},{8,9},{9,8},{10,11... | collective-permute-start | bytes 4616 | tf_op jit(solution)/shard_map/ppermute | solution.py:341
  16.7 4.0 %all-to-all-done = s32[8,40,128]{2,1,0:T(8,128)S(1)} async-done(((s32[8,40,128]{2,1,0:T(8,128)}), s32[8,40,128]{2,1,0:T(8,128)S(1)}, u32[]{:S(2)}, u32[]{:S(2)}) %all-to-all-start) | async-done | bytes 163872 | tf_op jit(solution)/shard_map/all_to_all | solution.py:342
  20.8 1.6 copy-done
  22.4 0.6 copy-done.2
  23.0 3.2 %shard_map.110 = (bf16[48,64,128]{2,1,0:T(8,128)(2,1)S(1)}, bf16[48,64,128]{2,1,0:T(8,128)(2,1)S(1)}, bf16[48,64,128]{2,1,0:T(8,128)(2,1)}, bf16[48,64,128]{2,1,...) custom-call(s32[4]{0:T(128)S(1)} %copy-done.2, ...), custom_call_target="tpu_custom_call" | custom-call | bytes 10485760 | tf_op jit(solution)/shard_map/pallas_call | solution.py:71
  26.2 0.9 copy-done.6
  27.2 3.3 %collective-permute-start.3 = (bf16[48,64,128]{2,1,0:T(8,128)(2,1)S(1)}, bf16[48,64,128]{2,1,0:T(8,128)(2,1)S(1)}, u32[]{:S(2)}, u32[]{:S(2)}) collective-permute-start(bf16[48,64,128]{2,1,0:T(8,128)(2,1)S(1)} %get-tuple-element.49), channel_id=1, source_target_pairs={{0,112},{2,114},{4,116},{6,118},{8,120},{10,122},{12,124},{14,126}... | collective-permute-start | bytes 2359304 | tf_op jit(solution)/shard_map/ppermute | solution.py:352
  30.4 3.1 %collective-permute-start.4 = (bf16[48,64,128]{2,1,0:T(8,128)(2,1)}, bf16[48,64,128]{2,1,0:T(8,128)(2,1)}, u32[]{:S(2)}, u32[]{:S(2)}) collective-permute-start(bf16[48,64,128]{2,1,0:T(8,128)(2,1)} %get-tuple-element.50), channel_id=1, source_target_pairs={{0,16},{2,18},{4,20},{6,22},{8,24},{10,26},{12,28},{14,30},{16,32}... | collective-permute-start | bytes 2359304 | tf_op jit(solution)/shard_map/ppermute | solution.py:352
  33.5 4.3 %collective-permute-start.5 = (bf16[48,64,128]{2,1,0:T(8,128)(2,1)}, bf16[48,64,128]{2,1,0:T(8,128)(2,1)S(1)}, u32[]{:S(2)}, u32[]{:S(2)}) collective-permute-start(bf16[48,64,128]{2,1,0:T(8,128)(2,1)} %get-tuple-element.58), channel_id=1, source_target_pairs={{0,16},{2,18},{4,20},{6,22},{8,24},{10,26},{12,28},{14,30},{16,32}... | collective-permute-start | bytes 2359304 | tf_op jit(solution)/shard_map/ppermute | solution.py:352
  37.8 6.9 %collective-permute-start.6 = (bf16[48,64,128]{2,1,0:T(8,128)(2,1)}, bf16[48,64,128]{2,1,0:T(8,128)(2,1)S(1)}, u32[]{:S(2)}, u32[]{:S(2)}) collective-permute-start(bf16[48,64,128]{2,1,0:T(8,128)(2,1)} %get-tuple-element.59), channel_id=1, source_target_pairs={{0,32},{2,34},{4,36},{6,38},{8,40},{10,42},{12,44},{14,46},{16,48}... | collective-permute-start | bytes 2359304 | tf_op jit(solution)/shard_map/ppermute | solution.py:352
  44.7 5.9 %collective-permute-start.2 = (s32[40,128]{1,0:T(8,128)S(1)}, s32[40,128]{1,0:T(8,128)S(1)}, u32[]{:S(2)}, u32[]{:S(2)}) collective-permute-start(s32[40,128]{1,0:T(8,128)S(1)} %reduce_sum.27.refs_1_), channel_id=1, source_target_pairs={{0,64},{2,66},{4,68},{6,70},{8,72},{10,74},{12,76},{14,78},{16,80}... | collective-permute-start | bytes 61448 | tf_op jit(solution)/shard_map/ppermute | solution.py:347
  50.6 3.7 %collective-permute-done.2.refs_0_ = s32[40,128]{1,0:T(8,128)S(1)} collective-permute-done((s32[40,128]{1,0:T(8,128)S(1)}, s32[40,128]{1,0:T(8,128)S(1)}, u32[]{:S(2)}, u32[]{:S(2)}) %collective-permute-start.2) | collective-permute-done | bytes 20512 | tf_op jit(solution)/shard_map/ppermute | solution.py:347
  54.3 23.3 %collective-permute-start.7 = (bf16[48,64,128]{2,1,0:T(8,128)(2,1)}, bf16[48,64,128]{2,1,0:T(8,128)(2,1)S(1)}, u32[]{:S(2)}, u32[]{:S(2)}) collective-permute-start(bf16[48,64,128]{2,1,0:T(8,128)(2,1)} %get-tuple-element.60), channel_id=1, source_target_pairs={{0,112},{2,114},{4,116},{6,118},{8,120},{10,122},{12,124},{14,126}... | collective-permute-start | bytes 2359304 | tf_op jit(solution)/shard_map/ppermute | solution.py:352
  77.6 0.9 copy-done.8
  78.5 2.9 %collective-permute-start.8 = (bf16[48,64,128]{2,1,0:T(8,128)(2,1)}, bf16[48,64,128]{2,1,0:T(8,128)(2,1)}, u32[]{:S(2)}, u32[]{:S(2)}) collective-permute-start(bf16[48,64,128]{2,1,0:T(8,128)(2,1)} %get-tuple-element.61), channel_id=1, source_target_pairs={{0,96},{2,98},{4,100},{6,102},{8,104},{10,106},{12,108},{14,110},{... | collective-permute-start | bytes 2359304 | tf_op jit(solution)/shard_map/ppermute | solution.py:352
  81.4 1.6 fusion.2
  83.1 0.1 concatenate.30.refs_3_.refs_5_
  83.3 1.5 shard_map.111
  84.9 9.5 %shard_map.112 = (f32[8,16,16,128]{3,2,1,0:T(8,128)S(1)}, f32[8,16,16,128]{3,2,1,0:T(8,128)S(1)}, f32[8,16,16,128]{3,2,1,0:T(8,128)S(1)}, f32[8,16,16,128]{3,2,1,0:T(8,128)S(1)}) custom-call(s32[4]{0:T(128)S(1)} %copy-done.3, s32[48,128]{1,0:T(8,128)S(1)} %get-tuple-element.47.list_ref, f32[32]{0:T(128)S(1)} %copy-done.4, f32[32]{0:T(128)S(1)} %copy-done.5, ...), custom_call_target="tpu_custom_call" | custom-call | flops 1000000000 | bytes 10485760 | tf_op jit(solution)/shard_map/pallas_call | solution.py:184
  94.5 5.9 %collective-permute-start.15 = (f16[8,16,16,128]{3,2,1,0:T(8,128)(2,1)S(1)}, f16[8,16,16,128]{3,2,1,0:T(8,128)(2,1)S(1)}, u32[]{:S(2)}, u32[]{:S(2)}) collective-permute-start(f16[8,16,16,128]{3,2,1,0:T(8,128)(2,1)S(1)} %convert_element_type.81), channel_id=1, source_target_pairs={{0,256},{128,384},{256,0},{384,128},{1,257},{129,385},{257,1},{385... | collective-permute-start | bytes 1572872 | tf_op jit(solution)/shard_map/ppermute | solution.py:320
  100.5 1.9 %collective-permute-start.16 = (f16[8,16,16,128]{3,2,1,0:T(8,128)(2,1)S(1)}, f16[8,16,16,128]{3,2,1,0:T(8,128)(2,1)S(1)}, u32[]{:S(2)}, u32[]{:S(2)}) collective-permute-start(f16[8,16,16,128]{3,2,1,0:T(8,128)(2,1)S(1)} %convert_element_type.83), channel_id=1, source_target_pairs={{0,128},{128,256},{256,384},{384,0},{1,129},{129,257},{257,385},{3... | collective-permute-start | bytes 1572872 | tf_op jit(solution)/shard_map/ppermute | solution.py:320
  102.5 5.1 %collective-permute-start.17 = (f16[8,16,16,128]{3,2,1,0:T(8,128)(2,1)S(1)}, f16[8,16,16,128]{3,2,1,0:T(8,128)(2,1)S(1)}, u32[]{:S(2)}, u32[]{:S(2)}) collective-permute-start(f16[8,16,16,128]{3,2,1,0:T(8,128)(2,1)S(1)} %convert_element_type.85), channel_id=1, source_target_pairs={{0,384},{128,0},{256,128},{384,256},{1,385},{129,1},{257,129},{385... | collective-permute-start | bytes 1572872 | tf_op jit(solution)/shard_map/ppermute | solution.py:320
  107.6 1.6 collective-permute-done.8.refs_4_
  109.2 10.5 %shard_map.113 = (f32[4,16,16,128]{3,2,1,0:T(8,128)S(1)}, f32[4,16,16,128]{3,2,1,0:T(8,128)S(1)}, f32[4,16,16,128]{3,2,1,0:T(8,128)S(1)}, f32[4,16,16,128]{3,2,1,0:T(8,128)S(1)}) custom-call(s32[4]{0:T(128)S(1)} %copy-done.3, s32[64,128]{1,0:T(8,128)S(1)} %get-tuple-element.70.list_ref, f32[32]{0:T(128)S(1)} %copy-done.4, f32[32]{0:T(128)S(1)} %copy-done.5, ...), custom_call_target="tpu_custom_call" | custom-call | flops 1000000000 | bytes 10485760 | tf_op jit(solution)/shard_map/pallas_call | solution.py:184
  119.7 2.1 %collective-permute-start.10 = (f16[4,16,16,128]{3,2,1,0:T(8,128)(2,1)S(1)}, f16[4,16,16,128]{3,2,1,0:T(8,128)(2,1)S(1)}, u32[]{:S(2)}, u32[]{:S(2)}) collective-permute-start(f16[4,16,16,128]{3,2,1,0:T(8,128)(2,1)S(1)} %convert_element_type.71), channel_id=1, source_target_pairs={{0,128},{128,256},{256,384},{384,0},{1,129},{129,257},{257,385},{3... | collective-permute-start | bytes 786440 | tf_op jit(solution)/shard_map/ppermute | solution.py:320
  121.8 5.0 %collective-permute-start.11 = (f16[4,16,16,128]{3,2,1,0:T(8,128)(2,1)S(1)}, f16[4,16,16,128]{3,2,1,0:T(8,128)(2,1)S(1)}, u32[]{:S(2)}, u32[]{:S(2)}) collective-permute-start(f16[4,16,16,128]{3,2,1,0:T(8,128)(2,1)S(1)} %convert_element_type.73), channel_id=1, source_target_pairs={{0,384},{128,0},{256,128},{384,256},{1,385},{129,1},{257,129},{385... | collective-permute-start | bytes 786440 | tf_op jit(solution)/shard_map/ppermute | solution.py:320
  126.8 5.9 %shard_map.114 = (f32[4,16,16,128]{3,2,1,0:T(8,128)S(1)}, f32[4,16,16,128]{3,2,1,0:T(8,128)S(1)}, f32[4,16,16,128]{3,2,1,0:T(8,128)S(1)}, f32[4,16,16,128]{3,2,1,0:T(8,128)S(1)}) custom-call(s32[4]{0:T(128)S(1)} %copy-done.3, s32[64,128]{1,0:T(8,128)S(1)} %get-tuple-element.70.list_ref, f32[32]{0:T(128)S(1)} %copy-done.4, f32[32]{0:T(128)S(1)} %copy-done.5, ...), custom_call_target="tpu_custom_call" | custom-call | flops 1000000000 | bytes 10485760 | tf_op jit(solution)/shard_map/pallas_call | solution.py:184
  132.9 3.3 %collective-permute-start.9 = (f16[4,16,16,128]{3,2,1,0:T(8,128)(2,1)S(1)}, f16[4,16,16,128]{3,2,1,0:T(8,128)(2,1)S(1)}, u32[]{:S(2)}, u32[]{:S(2)}) collective-permute-start(f16[4,16,16,128]{3,2,1,0:T(8,128)(2,1)S(1)} %convert_element_type.69), channel_id=1, source_target_pairs={{0,256},{128,384},{256,0},{384,128},{1,257},{129,385},{257,1},{385... | collective-permute-start | bytes 786440 | tf_op jit(solution)/shard_map/ppermute | solution.py:320
  136.3 4.0 %collective-permute-start.12 = (f16[4,16,16,128]{3,2,1,0:T(8,128)(2,1)S(1)}, f16[4,16,16,128]{3,2,1,0:T(8,128)(2,1)S(1)}, u32[]{:S(2)}, u32[]{:S(2)}) collective-permute-start(f16[4,16,16,128]{3,2,1,0:T(8,128)(2,1)S(1)} %convert_element_type.75), channel_id=1, source_target_pairs={{0,256},{128,384},{256,0},{384,128},{1,257},{129,385},{257,1},{385... | collective-permute-start | bytes 786440 | tf_op jit(solution)/shard_map/ppermute | solution.py:320
  140.3 1.9 %collective-permute-start.13 = (f16[4,16,16,128]{3,2,1,0:T(8,128)(2,1)S(1)}, f16[4,16,16,128]{3,2,1,0:T(8,128)(2,1)S(1)}, u32[]{:S(2)}, u32[]{:S(2)}) collective-permute-start(f16[4,16,16,128]{3,2,1,0:T(8,128)(2,1)S(1)} %convert_element_type.77), channel_id=1, source_target_pairs={{0,128},{128,256},{256,384},{384,0},{1,129},{129,257},{257,385},{3... | collective-permute-start | bytes 786440 | tf_op jit(solution)/shard_map/ppermute | solution.py:320
  142.3 0.3 add_convert_fusion
  142.6 5.1 %collective-permute-start.14 = (f16[4,16,16,128]{3,2,1,0:T(8,128)(2,1)S(1)}, f16[4,16,16,128]{3,2,1,0:T(8,128)(2,1)S(1)}, u32[]{:S(2)}, u32[]{:S(2)}) collective-permute-start(f16[4,16,16,128]{3,2,1,0:T(8,128)(2,1)S(1)} %convert_element_type.79), channel_id=1, source_target_pairs={{0,384},{128,0},{256,128},{384,256},{1,385},{129,1},{257,129},{385... | collective-permute-start | bytes 786440 | tf_op jit(solution)/shard_map/ppermute | solution.py:320
  147.7 6.7 %collective-permute-start.18 = (f16[8,16,16,128]{3,2,1,0:T(8,128)(2,1)S(1)}, f16[8,16,16,128]{3,2,1,0:T(8,128)(2,1)S(1)}, u32[]{:S(2)}, u32[]{:S(2)}) collective-permute-start(f16[8,16,16,128]{3,2,1,0:T(8,128)(2,1)S(1)} %add_convert_fusion), channel_id=1, source_target_pairs={{0,64},{2,66},{4,68},{6,70},{8,72},{10,74},{12,76},{14,78},{16,80}... | collective-permute-start | bytes 1572872 | tf_op jit(solution)/shard_map/ppermute | solution.py:370
  154.4 0.1 convert_add_fusion.1
  154.6 0.1 convert_add_fusion
  154.7 13.7 %collective-permute-done.18 = f16[8,16,16,128]{3,2,1,0:T(8,128)(2,1)S(1)} collective-permute-done((f16[8,16,16,128]{3,2,1,0:T(8,128)(2,1)S(1)}, f16[8,16,16,128]{3,2,1,0:T(8,128)(2,1)S(1)}, u32[]{:S(2)}, u32[]{:S(2)}) %collective-permute-start.18) | collective-permute-done | bytes 524320 | tf_op jit(solution)/shard_map/ppermute | solution.py:370
  168.4 0.9 fusion.3
  169.3 7.0 %all-to-all-start.1 = ((f16[8,16,16,128]{3,2,1,0:T(8,128)(2,1)}), f16[8,16,16,128]{3,2,1,0:T(8,128)(2,1)S(1)}, u32[]{:S(2)}, u32[]{:S(2)}) async-start(f16[8,16,16,128]{3,2,1,0:T(8,128)(2,1)} %fusion.3), calls=%async_computation.1 | async-start | bytes 1048576 | tf_op jit(solution)/shard_map/all_to_all | solution.py:375
  176.4 0.2 select_reduce_fusion
  176.5 0.2 convolution_bitcast_fusion
  176.8 0.1 fusion.19
  176.9 12.8 %all-to-all-done.1 = f16[8,16,16,128]{3,2,1,0:T(8,128)(2,1)S(1)} async-done(((f16[8,16,16,128]{3,2,1,0:T(8,128)(2,1)}), f16[8,16,16,128]{3,2,1,0:T(8,128)(2,1)S(1)}, u32[]{:S(2)}, u32[]{:S(2)}) %all-to-all-start.1) | async-done | bytes 524320 | tf_op jit(solution)/shard_map/all_to_all | solution.py:375
  189.7 0.8 fusion.5
  (50 shorter events, 0.7 us)
Async XLA Ops:
  0.0 20.8 %collective-permute-start.1 = (bf16[128,64,128]{2,1,0:T(8,128)(2,1)}, bf16[128,64,128]{2,1,0:T(8,128)(2,1)S(1)}, u32[]{:S(2)}, u32[]{:S(2)}) collective-permute-start(bf16[128,64,128]{2,1,0:T(8,128)(2,1)} %bitcast.20), channel_id=1, source_target_pairs={{0,1},{1,0},{2,3},{3,2},{4,5},{5,4},{6,7},{7,6},{8,9},{9,8},{10,11... | collective-permute-start | bytes 6291464 | tf_op jit(solution)/shard_map/ppermute | solution.py:340
  4.2 16.5 %all-to-all-start = ((s32[8,40,128]{2,1,0:T(8,128)}), s32[8,40,128]{2,1,0:T(8,128)S(1)}, u32[]{:S(2)}, u32[]{:S(2)}) async-start(s32[8,40,128]{2,1,0:T(8,128)} %shard_map.109), calls=%async_computation | async-start | bytes 327680 | tf_op jit(solution)/shard_map/all_to_all | solution.py:342
  12.0 8.8 %collective-permute-start = (s32[384]{0:T(512)S(1)}, s32[384]{0:T(512)S(1)}, u32[]{:S(2)}, u32[]{:S(2)}) collective-permute-start(s32[384]{0:T(512)S(1)} %bitcast.22), channel_id=1, source_target_pairs={{0,1},{1,0},{2,3},{3,2},{4,5},{5,4},{6,7},{7,6},{8,9},{9,8},{10,11... | collective-permute-start | bytes 4616 | tf_op jit(solution)/shard_map/ppermute | solution.py:341
  20.8 1.6 copy-start
  22.4 0.6 copy-start.2
  26.2 0.9 copy-start.6
  27.1 56.1 %copy-start.10 = (bf16[64,64]{1,0:T(8,128)(2,1)S(1)}, bf16[64,64]{1,0:T(8,128)(2,1)}, u32[]{:S(2)}) copy-start(bf16[64,64]{1,0:T(8,128)(2,1)} %param.17) | copy-start | bytes 24580
  27.1 56.2 %copy-start.3 = (s32[4]{0:T(128)S(1)}, s32[4]{0:T(128)}, u32[]{:S(2)}) copy-start(s32[4]{0:T(128)} %pad_add_fusion.spot_ref) | copy-start | bytes 52
  27.1 57.7 %copy-start.1 = (bf16[16,16,128]{2,1,0:T(8,128)(2,1)S(1)}, bf16[16,16,128]{2,1,0:T(8,128)(2,1)}, u32[]{:S(2)}) copy-start(bf16[16,16,128]{2,1,0:T(8,128)(2,1)} %refs_7_.3) | copy-start | bytes 196612
  27.1 57.7 %copy-start.4 = (f32[32]{0:T(128)S(1)}, f32[32]{0:T(128)}, u32[]{:S(2)}) copy-start(f32[32]{0:T(128)} %re_ref.5) | copy-start | bytes 388
  27.1 57.7 %copy-start.5 = (f32[32]{0:T(128)S(1)}, f32[32]{0:T(128)}, u32[]{:S(2)}) copy-start(f32[32]{0:T(128)} %im_ref.5) | copy-start | bytes 388
  27.2 50.5 %collective-permute-start.3 = (bf16[48,64,128]{2,1,0:T(8,128)(2,1)S(1)}, bf16[48,64,128]{2,1,0:T(8,128)(2,1)S(1)}, u32[]{:S(2)}, u32[]{:S(2)}) collective-permute-start(bf16[48,64,128]{2,1,0:T(8,128)(2,1)S(1)} %get-tuple-element.49), channel_id=1, source_target_pairs={{0,112},{2,114},{4,116},{6,118},{8,120},{10,122},{12,124},{14,126}... | collective-permute-start | bytes 2359304 | tf_op jit(solution)/shard_map/ppermute | solution.py:352
  30.4 54.4 %collective-permute-start.4 = (bf16[48,64,128]{2,1,0:T(8,128)(2,1)}, bf16[48,64,128]{2,1,0:T(8,128)(2,1)}, u32[]{:S(2)}, u32[]{:S(2)}) collective-permute-start(bf16[48,64,128]{2,1,0:T(8,128)(2,1)} %get-tuple-element.50), channel_id=1, source_target_pairs={{0,16},{2,18},{4,20},{6,22},{8,24},{10,26},{12,28},{14,30},{16,32}... | collective-permute-start | bytes 2359304 | tf_op jit(solution)/shard_map/ppermute | solution.py:352
  33.5 67.0 %collective-permute-start.5 = (bf16[48,64,128]{2,1,0:T(8,128)(2,1)}, bf16[48,64,128]{2,1,0:T(8,128)(2,1)S(1)}, u32[]{:S(2)}, u32[]{:S(2)}) collective-permute-start(bf16[48,64,128]{2,1,0:T(8,128)(2,1)} %get-tuple-element.58), channel_id=1, source_target_pairs={{0,16},{2,18},{4,20},{6,22},{8,24},{10,26},{12,28},{14,30},{16,32}... | collective-permute-start | bytes 2359304 | tf_op jit(solution)/shard_map/ppermute | solution.py:352
  37.8 64.7 %collective-permute-start.6 = (bf16[48,64,128]{2,1,0:T(8,128)(2,1)}, bf16[48,64,128]{2,1,0:T(8,128)(2,1)S(1)}, u32[]{:S(2)}, u32[]{:S(2)}) collective-permute-start(bf16[48,64,128]{2,1,0:T(8,128)(2,1)} %get-tuple-element.59), channel_id=1, source_target_pairs={{0,32},{2,34},{4,36},{6,38},{8,40},{10,42},{12,44},{14,46},{16,48}... | collective-permute-start | bytes 2359304 | tf_op jit(solution)/shard_map/ppermute | solution.py:352
  44.7 9.6 %collective-permute-start.2 = (s32[40,128]{1,0:T(8,128)S(1)}, s32[40,128]{1,0:T(8,128)S(1)}, u32[]{:S(2)}, u32[]{:S(2)}) collective-permute-start(s32[40,128]{1,0:T(8,128)S(1)} %reduce_sum.27.refs_1_), channel_id=1, source_target_pairs={{0,64},{2,66},{4,68},{6,70},{8,72},{10,74},{12,76},{14,78},{16,80}... | collective-permute-start | bytes 61448 | tf_op jit(solution)/shard_map/ppermute | solution.py:347
  54.3 53.3 %collective-permute-start.7 = (bf16[48,64,128]{2,1,0:T(8,128)(2,1)}, bf16[48,64,128]{2,1,0:T(8,128)(2,1)S(1)}, u32[]{:S(2)}, u32[]{:S(2)}) collective-permute-start(bf16[48,64,128]{2,1,0:T(8,128)(2,1)} %get-tuple-element.60), channel_id=1, source_target_pairs={{0,112},{2,114},{4,116},{6,118},{8,120},{10,122},{12,124},{14,126}... | collective-permute-start | bytes 2359304 | tf_op jit(solution)/shard_map/ppermute | solution.py:352
  77.6 0.9 copy-start.8
  78.5 30.7 %collective-permute-start.8 = (bf16[48,64,128]{2,1,0:T(8,128)(2,1)}, bf16[48,64,128]{2,1,0:T(8,128)(2,1)}, u32[]{:S(2)}, u32[]{:S(2)}) collective-permute-start(bf16[48,64,128]{2,1,0:T(8,128)(2,1)} %get-tuple-element.61), channel_id=1, source_target_pairs={{0,96},{2,98},{4,100},{6,102},{8,104},{10,106},{12,108},{14,110},{... | collective-permute-start | bytes 2359304 | tf_op jit(solution)/shard_map/ppermute | solution.py:352
  81.4 3.4 %copy-start.7 = (bf16[48,64,128]{2,1,0:T(8,128)(2,1)S(1)}, bf16[48,64,128]{2,1,0:T(8,128)(2,1)}, u32[]{:S(2)}) copy-start(bf16[48,64,128]{2,1,0:T(8,128)(2,1)} %copy-done.6) | copy-start | bytes 2359300
  81.4 3.4 %copy-start.9 = (bf16[48,64,128]{2,1,0:T(8,128)(2,1)S(1)}, bf16[48,64,128]{2,1,0:T(8,128)(2,1)}, u32[]{:S(2)}) copy-start(bf16[48,64,128]{2,1,0:T(8,128)(2,1)} %copy-done.8) | copy-start | bytes 2359300
  94.5 38.5 %collective-permute-start.15 = (f16[8,16,16,128]{3,2,1,0:T(8,128)(2,1)S(1)}, f16[8,16,16,128]{3,2,1,0:T(8,128)(2,1)S(1)}, u32[]{:S(2)}, u32[]{:S(2)}) collective-permute-start(f16[8,16,16,128]{3,2,1,0:T(8,128)(2,1)S(1)} %convert_element_type.81), channel_id=1, source_target_pairs={{0,256},{128,384},{256,0},{384,128},{1,257},{129,385},{257,1},{385... | collective-permute-start | bytes 1572872 | tf_op jit(solution)/shard_map/ppermute | solution.py:320
  100.5 35.8 %collective-permute-start.16 = (f16[8,16,16,128]{3,2,1,0:T(8,128)(2,1)S(1)}, f16[8,16,16,128]{3,2,1,0:T(8,128)(2,1)S(1)}, u32[]{:S(2)}, u32[]{:S(2)}) collective-permute-start(f16[8,16,16,128]{3,2,1,0:T(8,128)(2,1)S(1)} %convert_element_type.83), channel_id=1, source_target_pairs={{0,128},{128,256},{256,384},{384,0},{1,129},{129,257},{257,385},{3... | collective-permute-start | bytes 1572872 | tf_op jit(solution)/shard_map/ppermute | solution.py:320
  102.5 37.9 %collective-permute-start.17 = (f16[8,16,16,128]{3,2,1,0:T(8,128)(2,1)S(1)}, f16[8,16,16,128]{3,2,1,0:T(8,128)(2,1)S(1)}, u32[]{:S(2)}, u32[]{:S(2)}) collective-permute-start(f16[8,16,16,128]{3,2,1,0:T(8,128)(2,1)S(1)} %convert_element_type.85), channel_id=1, source_target_pairs={{0,384},{128,0},{256,128},{384,256},{1,385},{129,1},{257,129},{385... | collective-permute-start | bytes 1572872 | tf_op jit(solution)/shard_map/ppermute | solution.py:320
  119.7 22.9 %collective-permute-start.10 = (f16[4,16,16,128]{3,2,1,0:T(8,128)(2,1)S(1)}, f16[4,16,16,128]{3,2,1,0:T(8,128)(2,1)S(1)}, u32[]{:S(2)}, u32[]{:S(2)}) collective-permute-start(f16[4,16,16,128]{3,2,1,0:T(8,128)(2,1)S(1)} %convert_element_type.71), channel_id=1, source_target_pairs={{0,128},{128,256},{256,384},{384,0},{1,129},{129,257},{257,385},{3... | collective-permute-start | bytes 786440 | tf_op jit(solution)/shard_map/ppermute | solution.py:320
  121.8 25.9 %collective-permute-start.11 = (f16[4,16,16,128]{3,2,1,0:T(8,128)(2,1)S(1)}, f16[4,16,16,128]{3,2,1,0:T(8,128)(2,1)S(1)}, u32[]{:S(2)}, u32[]{:S(2)}) collective-permute-start(f16[4,16,16,128]{3,2,1,0:T(8,128)(2,1)S(1)} %convert_element_type.73), channel_id=1, source_target_pairs={{0,384},{128,0},{256,128},{384,256},{1,385},{129,1},{257,129},{385... | collective-permute-start | bytes 786440 | tf_op jit(solution)/shard_map/ppermute | solution.py:320
  132.9 21.5 %collective-permute-start.9 = (f16[4,16,16,128]{3,2,1,0:T(8,128)(2,1)S(1)}, f16[4,16,16,128]{3,2,1,0:T(8,128)(2,1)S(1)}, u32[]{:S(2)}, u32[]{:S(2)}) collective-permute-start(f16[4,16,16,128]{3,2,1,0:T(8,128)(2,1)S(1)} %convert_element_type.69), channel_id=1, source_target_pairs={{0,256},{128,384},{256,0},{384,128},{1,257},{129,385},{257,1},{385... | collective-permute-start | bytes 786440 | tf_op jit(solution)/shard_map/ppermute | solution.py:320
  136.3 18.3 %collective-permute-start.12 = (f16[4,16,16,128]{3,2,1,0:T(8,128)(2,1)S(1)}, f16[4,16,16,128]{3,2,1,0:T(8,128)(2,1)S(1)}, u32[]{:S(2)}, u32[]{:S(2)}) collective-permute-start(f16[4,16,16,128]{3,2,1,0:T(8,128)(2,1)S(1)} %convert_element_type.75), channel_id=1, source_target_pairs={{0,256},{128,384},{256,0},{384,128},{1,257},{129,385},{257,1},{385... | collective-permute-start | bytes 786440 | tf_op jit(solution)/shard_map/ppermute | solution.py:320
  140.3 14.2 %collective-permute-start.13 = (f16[4,16,16,128]{3,2,1,0:T(8,128)(2,1)S(1)}, f16[4,16,16,128]{3,2,1,0:T(8,128)(2,1)S(1)}, u32[]{:S(2)}, u32[]{:S(2)}) collective-permute-start(f16[4,16,16,128]{3,2,1,0:T(8,128)(2,1)S(1)} %convert_element_type.77), channel_id=1, source_target_pairs={{0,128},{128,256},{256,384},{384,0},{1,129},{129,257},{257,385},{3... | collective-permute-start | bytes 786440 | tf_op jit(solution)/shard_map/ppermute | solution.py:320
  142.6 12.0 %collective-permute-start.14 = (f16[4,16,16,128]{3,2,1,0:T(8,128)(2,1)S(1)}, f16[4,16,16,128]{3,2,1,0:T(8,128)(2,1)S(1)}, u32[]{:S(2)}, u32[]{:S(2)}) collective-permute-start(f16[4,16,16,128]{3,2,1,0:T(8,128)(2,1)S(1)} %convert_element_type.79), channel_id=1, source_target_pairs={{0,384},{128,0},{256,128},{384,256},{1,385},{129,1},{257,129},{385... | collective-permute-start | bytes 786440 | tf_op jit(solution)/shard_map/ppermute | solution.py:320
  147.7 20.7 %collective-permute-start.18 = (f16[8,16,16,128]{3,2,1,0:T(8,128)(2,1)S(1)}, f16[8,16,16,128]{3,2,1,0:T(8,128)(2,1)S(1)}, u32[]{:S(2)}, u32[]{:S(2)}) collective-permute-start(f16[8,16,16,128]{3,2,1,0:T(8,128)(2,1)S(1)} %add_convert_fusion), channel_id=1, source_target_pairs={{0,64},{2,66},{4,68},{6,70},{8,72},{10,74},{12,76},{14,78},{16,80}... | collective-permute-start | bytes 1572872 | tf_op jit(solution)/shard_map/ppermute | solution.py:370
  154.6 21.8 %copy-start.11 = (s32[16,3]{0,1:T(4,128)S(1)}, s32[16,3]{0,1:T(4,128)}, u32[]{:S(2)}) copy-start(s32[16,3]{0,1:T(4,128)} %param.14) | copy-start | bytes 580
  154.6 21.8 %copy-start.12 = (f32[128]{0:T(128)S(1)}, f32[128]{0:T(128)}, u32[]{:S(2)}) copy-start(f32[128]{0:T(128)} %param.21) | copy-start | bytes 1540
  169.3 20.3 %all-to-all-start.1 = ((f16[8,16,16,128]{3,2,1,0:T(8,128)(2,1)}), f16[8,16,16,128]{3,2,1,0:T(8,128)(2,1)S(1)}, u32[]{:S(2)}, u32[]{:S(2)}) async-start(f16[8,16,16,128]{3,2,1,0:T(8,128)(2,1)} %fusion.3), calls=%async_computation.1 | async-start | bytes 1048576 | tf_op jit(solution)/shard_map/all_to_all | solution.py:375

commit v8 on v7

--- a/solution.py
+++ b/solution.py
@@ -47,6 +47,11 @@
 
 
 DELIVER = [[device(c, a, b) for b in range(RINGS)] for c in range(2) for a in range(RINGS)]
+LISTENERS = [
+    [device(c, a + far, b) for far in (0, 4) for b in range(RINGS)] for c in range(2) for a in range(RINGS // 2)
+]
+
+
 def pick_kernel(spot_ref, own_slot, sib_slot, own_ref, sib_hbm, *refs):
     out_refs, (sib_ref, sem) = refs[:-2], refs[-2:]
     copy = pltpu.make_async_copy(sib_hbm, sib_ref, sem)
@@ -116,7 +121,7 @@
         )
         return rotate(left - right)
 
-    together = 8
+    together = 16
 
     def first(index, carry):
         for j in range(together):
@@ -159,13 +164,10 @@
 
     if sources == len(NEAR):
 
-        def local(w, carry):
+        for w in range(windows):
             acc[here * windows + w] += rotate(
                 jnp.dot(ham_ref[...], rho_ref[w], preferred_element_type=F32)
             )
-            return carry
-
-        lax.fori_loop(0, jnp.where((here >= begin) & (here < end), windows, 0), local, 0)
 
     def leave(r, carry):
         for w in range(windows):
@@ -260,21 +262,26 @@
     out_ref[last:last + 1] = sums[:1].astype(jnp.int32)
 
 
-def lists_kernel(kinds, modes, spot_ref, *refs):
-    for (steps, parts), heard_ref, out_ref in zip(kinds, refs[:len(kinds)], refs[len(kinds):], strict=True):
-        lists_of(steps, parts, modes, spot_ref, heard_ref, out_ref)
+def lists_kernel(kinds, modes, spot_ref, heard_ref, *refs):
+    out_refs, sum_ref = refs[:-1], refs[-1]
+    half = lax.shift_right_logical(spot_ref[1], 2)
+    for (steps, parts, far), out_ref in zip(kinds, out_refs, strict=True):
+        begin = (half ^ far) * RINGS
+        sum_ref[...] = sum(heard_ref[begin + r] for r in range(RINGS))
+        lists_of(steps, parts, modes, spot_ref, sum_ref, out_ref)
 
 
 def use_lists(kinds, modes, spot, heard):
-    rows = [modes + CAP + len(parts) * (modes // LOT + CAP) + 1 for _, parts in kinds]
+    rows = [modes + CAP + len(parts) * (modes // LOT + CAP) + 1 for _, parts, _ in kinds]
     return pl.pallas_call(
         functools.partial(lists_kernel, kinds, modes),
-        in_specs=[SMEM] + [VMEM] * len(kinds),
+        in_specs=[SMEM, VMEM],
         out_specs=[VMEM] * len(kinds),
-        out_shape=[jax.ShapeDtypeStruct((n + -n % 8, heard[0].shape[1]), jnp.int32) for n in rows],
+        out_shape=[jax.ShapeDtypeStruct((n + -n % 8, heard.shape[2]), jnp.int32) for n in rows],
+        scratch_shapes=[pltpu.VMEM(heard.shape[1:], jnp.int32)],
         compiler_params=pltpu.CompilerParams(vmem_limit_bytes=8 * 2**20),
         cost_estimate=pl.CostEstimate(flops=10**7, bytes_accessed=2**18, transcendentals=0),
-    )(spot, *heard)
+    )(spot, heard)
 
 
 def say_kernel(spot_ref, up_ref, down_ref, tri_ref, out_ref):
@@ -307,7 +314,7 @@
         say_kernel,
         in_specs=[SMEM, VMEM, VMEM, VMEM],
         out_specs=VMEM,
-        out_shape=jax.ShapeDtypeStruct((RINGS, rows + -rows % 8, RINGS * windows), jnp.int32),
+        out_shape=jax.ShapeDtypeStruct((2 * RINGS, rows + -rows % 8, RINGS * windows), jnp.int32),
         cost_estimate=pl.CostEstimate(flops=10**6, bytes_accessed=2**18, transcendentals=0),
     )(spot, use_up, use_down.T, modes_tri.T)
 
@@ -341,10 +348,9 @@
     sib_slots = lax.ppermute(slots, "ado", SIBLING)
     heard = lax.all_to_all(
         say(spot, use_up, use_down, modes_tri), "ado", split_axis=0, concat_axis=0, tiled=True,
-        axis_index_groups=DELIVER,
+        axis_index_groups=LISTENERS,
     )
-    heard, slots = lax.optimization_barrier((jnp.sum(heard, axis=0), slots))
-    heard_far = lax.ppermute(heard, "ado", onward(4))
+    heard, slots = lax.optimization_barrier((heard, slots))
     picked = pick(spot, slots, sib_slots, states[0, 0], sib_store)
 
     def send(steps, blocks):
@@ -355,11 +361,10 @@
 
     far_states = send(FAR, picked[:len(FAR)])
     near_states = send(NEAR, picked[len(FAR):])
-    half = RINGS // 2
-    held, heard_far, heard = lax.optimization_barrier((picked[0], heard_far, heard))
+    held, heard = lax.optimization_barrier((picked[0], heard))
     far_states[0] = held
-    kinds = ((FAR, ((0, RINGS),)), (NEAR, ((0, half), (half, RINGS))))
-    far_lists, near_lists = use_lists(kinds, modes, spot, (heard_far, heard))
+    kinds = ((FAR, ((0, RINGS),), 1), (NEAR, ((0, RINGS),), 0))
+    far_lists, near_lists = use_lists(kinds, modes, spot, heard)
 
     maps_wide = jnp.concatenate([doubled(coupling), jnp.zeros((1, 2 * width, 2 * width), BF16)], axis=0)
     head_cols = lax.dynamic_slice_in_dim(hamiltonian, group * share, share, 1)
@@ -368,12 +373,9 @@
     far, near_lists = lax.optimization_barrier((far, near_lists))
     far = over_groups(far)
     far = lax.ppermute(far.astype(LINK), "ado", onward(4))
-    first = terms((0, half, 0), spot, near_lists, coup_re, coup_im, near_states, *shared)
-    first, near_lists = lax.optimization_barrier((first, near_lists))
-    second = terms((half, RINGS, 1), spot, near_lists, coup_re, coup_im, near_states, *shared)
-    near = [over_groups(first), over_groups(second)]
+    near = over_groups(terms((0, RINGS, 0), spot, near_lists, coup_re, coup_im, near_states, *shared))
     summed = lax.all_to_all(
-        (jnp.concatenate(near, axis=0) + far.astype(F32)).astype(LINK), "ado", split_axis=0, concat_axis=0,
+        (near + far.astype(F32)).astype(LINK), "ado", split_axis=0, concat_axis=0,
         tiled=True, axis_index_groups=DELIVER,
     )
 

time: 192 us -> 152 us (0.79)
  the two profiles are of different devices: /device:TPU:64 before, /device:TPU:2 now
where the time goes in v8:
time: 152 us; the launch traced here: 151 us
  starting transfers between devices  66.9 us (44%)
  waiting for transfers between devices  46.6 us (31%)
  Pallas kernels  24.7 us (16%)
  local copies, waits for them, and re-layouts  7.18 us (5%)
  other arithmetic  5.16 us (3%)
    ppermute x6, starting transfers between devices, over_groups(): lax.ppermute(parts[shift].astype(LINK), 'grp', ring).astype(F32)  21.3 us
    ppermute x6, starting transfers between devices, send(): lax.ppermute(block, 'ado', onward(step))  19.8 us
    pallas_call x2, Pallas kernels, terms(): pl.pallas_call(functools.partial(terms_kernel, len(pieces), modes, window...  18.5 us
    all_to_all x1, starting transfers between devices, on_device(): lax.all_to_all(say(spot, use_up, use_down, modes_tri), 'ado', split_axis=...  15.6 us
    all_to_all x1, waiting for transfers between devices, on_device(): lax.all_to_all(say(spot, use_up, use_down, modes_tri), 'ado', split_axis=...  14.5 us
    all_to_all x1, waiting for transfers between devices, on_device(): lax.all_to_all((near + far.astype(F32)).astype(LINK), 'ado', split_axis=0...  12.7 us
    ppermute x6, waiting for transfers between devices, over_groups(): lax.ppermute(parts[shift].astype(LINK), 'grp', ring).astype(F32)  9.61 us
    ppermute x1, waiting for transfers between devices, on_device(): far = lax.ppermute(far.astype(LINK), 'ado', onward(4))  8.31 us
  transfers between devices with their start and end apart: 17, of which 5 were waited for; matrix products, arithmetic and copies ran while one was open for 3% of the time, Pallas kernels for 14%

profile of v8, /device:TPU:2, one launch (start us, length us, event | category | flops | bytes accessed | tf_op | source)
XLA Modules:
  0.0 151.2 jit_solution(9453920167308548719)
XLA Ops:
  0.0 1.9 %collective-permute-start.1 = (bf16[128,64,128]{2,1,0:T(8,128)(2,1)}, bf16[128,64,128]{2,1,0:T(8,128)(2,1)S(1)}, u32[]{:S(2)}, u32[]{:S(2)}) collective-permute-start(bf16[128,64,128]{2,1,0:T(8,128)(2,1)} %bitcast.20), channel_id=1, source_target_pairs={{0,1},{1,0},{2,3},{3,2},{4,5},{5,4},{6,7},{7,6},{8,9},{9,8},{10,11... | collective-permute-start | bytes 6291464 | tf_op jit(solution)/shard_map/ppermute | solution.py:347
  1.9 0.6 pad_add_fusion.spot_ref
  2.5 1.7 %shard_map.109 = s32[16,40,128]{2,1,0:T(8,128)} custom-call(s32[4]{0:T(128)} %pad_add_fusion.spot_ref, s32[16,32]{1,0:T(8,128)} %up_ref.1, s32[3,16]{1,0:T(4,128)} %bitcast.25, s32[3,16]{1,0:T(4,128)} %bitcast.24), custom_call_target="tpu_custom_call" | custom-call | flops 1000000 | bytes 262144 | tf_op jit(solution)/shard_map/pallas_call | solution.py:313
  4.3 15.6 %all-to-all-start = ((s32[16,40,128]{2,1,0:T(8,128)}), s32[16,40,128]{2,1,0:T(8,128)S(1)}, u32[]{:S(2)}, u32[]{:S(2)}) async-start(s32[16,40,128]{2,1,0:T(8,128)} %shard_map.109), calls=%async_computation | async-start | bytes 655360 | tf_op jit(solution)/shard_map/all_to_all | solution.py:349
  19.9 0.7 copy.15
  20.6 2.1 %collective-permute-start = (s32[384]{0:T(512)S(1)}, s32[384]{0:T(512)S(1)}, u32[]{:S(2)}, u32[]{:S(2)}) collective-permute-start(s32[384]{0:T(512)S(1)} %bitcast.22), channel_id=1, source_target_pairs={{0,1},{1,0},{2,3},{3,2},{4,5},{5,4},{6,7},{7,6},{8,9},{9,8},{10,11... | collective-permute-start | bytes 4616 | tf_op jit(solution)/shard_map/ppermute | solution.py:348
  22.8 14.5 %all-to-all-done.heard_ref = s32[16,40,128]{2,1,0:T(8,128)S(1)} async-done(((s32[16,40,128]{2,1,0:T(8,128)}), s32[16,40,128]{2,1,0:T(8,128)S(1)}, u32[]{:S(2)}, u32[]{:S(2)}) %all-to-all-start) | async-done | bytes 327712 | tf_op jit(solution)/shard_map/all_to_all | solution.py:349
  37.2 1.6 %copy-done = bf16[1,1,128,64,128]{4,3,2,1,0:T(8,128)(2,1)S(1)} copy-done((bf16[1,1,128,64,128]{4,3,2,1,0:T(8,128)(2,1)S(1)}, bf16[1,1,128,64,128]{4,3,2,1,0:T(8,128)(2,1)}, u32[]{:S(2)}) %copy-start) | copy-done | bytes 2097176
  38.8 0.6 copy-done.2
  39.4 3.2 %shard_map.110 = (bf16[48,64,128]{2,1,0:T(8,128)(2,1)S(1)}, bf16[48,64,128]{2,1,0:T(8,128)(2,1)S(1)}, bf16[48,64,128]{2,1,0:T(8,128)(2,1)}, bf16[48,64,128]{2,1,...) custom-call(s32[4]{0:T(128)S(1)} %copy-done.2, ...), custom_call_target="tpu_custom_call" | custom-call | bytes 10485760 | tf_op jit(solution)/shard_map/pallas_call | solution.py:76
  42.7 0.9 copy-done.6
  43.6 2.5 %collective-permute-start.2 = (bf16[48,64,128]{2,1,0:T(8,128)(2,1)S(1)}, bf16[48,64,128]{2,1,0:T(8,128)(2,1)S(1)}, u32[]{:S(2)}, u32[]{:S(2)}) collective-permute-start(bf16[48,64,128]{2,1,0:T(8,128)(2,1)S(1)} %get-tuple-element.38), channel_id=1, source_target_pairs={{0,112},{2,114},{4,116},{6,118},{8,120},{10,122},{12,124},{14,126}... | collective-permute-start | bytes 2359304 | tf_op jit(solution)/shard_map/ppermute | solution.py:358
  46.0 3.5 %collective-permute-start.3 = (bf16[48,64,128]{2,1,0:T(8,128)(2,1)}, bf16[48,64,128]{2,1,0:T(8,128)(2,1)}, u32[]{:S(2)}, u32[]{:S(2)}) collective-permute-start(bf16[48,64,128]{2,1,0:T(8,128)(2,1)} %get-tuple-element.39), channel_id=1, source_target_pairs={{0,16},{2,18},{4,20},{6,22},{8,24},{10,26},{12,28},{14,30},{16,32}... | collective-permute-start | bytes 2359304 | tf_op jit(solution)/shard_map/ppermute | solution.py:358
  49.5 2.3 %collective-permute-start.4 = (bf16[48,64,128]{2,1,0:T(8,128)(2,1)}, bf16[48,64,128]{2,1,0:T(8,128)(2,1)S(1)}, u32[]{:S(2)}, u32[]{:S(2)}) collective-permute-start(bf16[48,64,128]{2,1,0:T(8,128)(2,1)} %get-tuple-element.47), channel_id=1, source_target_pairs={{0,16},{2,18},{4,20},{6,22},{8,24},{10,26},{12,28},{14,30},{16,32}... | collective-permute-start | bytes 2359304 | tf_op jit(solution)/shard_map/ppermute | solution.py:358
  51.9 3.2 %collective-permute-start.5 = (bf16[48,64,128]{2,1,0:T(8,128)(2,1)}, bf16[48,64,128]{2,1,0:T(8,128)(2,1)}, u32[]{:S(2)}, u32[]{:S(2)}) collective-permute-start(bf16[48,64,128]{2,1,0:T(8,128)(2,1)} %get-tuple-element.48), channel_id=1, source_target_pairs={{0,32},{2,34},{4,36},{6,38},{8,40},{10,42},{12,44},{14,46},{16,48}... | collective-permute-start | bytes 2359304 | tf_op jit(solution)/shard_map/ppermute | solution.py:358
  55.1 3.7 %collective-permute-start.6 = (bf16[48,64,128]{2,1,0:T(8,128)(2,1)}, bf16[48,64,128]{2,1,0:T(8,128)(2,1)}, u32[]{:S(2)}, u32[]{:S(2)}) collective-permute-start(bf16[48,64,128]{2,1,0:T(8,128)(2,1)} %get-tuple-element.49), channel_id=1, source_target_pairs={{0,112},{2,114},{4,116},{6,118},{8,120},{10,122},{12,124},{14,126}... | collective-permute-start | bytes 2359304 | tf_op jit(solution)/shard_map/ppermute | solution.py:358
  58.8 0.9 copy-done.8
  59.8 4.5 %collective-permute-start.7 = (bf16[48,64,128]{2,1,0:T(8,128)(2,1)}, bf16[48,64,128]{2,1,0:T(8,128)(2,1)}, u32[]{:S(2)}, u32[]{:S(2)}) collective-permute-start(bf16[48,64,128]{2,1,0:T(8,128)(2,1)} %get-tuple-element.50), channel_id=1, source_target_pairs={{0,96},{2,98},{4,100},{6,102},{8,104},{10,106},{12,108},{14,110},{... | collective-permute-start | bytes 2359304 | tf_op jit(solution)/shard_map/ppermute | solution.py:358
  64.3 1.5 %fusion.2 = bf16[32,128,128]{2,1,0:T(8,128)(2,1)S(1)} fusion(bf16[32,64,64]{2,1,0:T(8,128)(2,1)} %param.18), kind=kLoop, calls=%fused_computation.5 | loop fusion | flops 4194304 | bytes 1310720 | tf_op jit(solution)/shard_map/concatenate | solution.py:22
  65.9 0.1 concatenate.27.refs_3_.refs_5_
  66.0 0.1 constant_dynamic-slice_fusion.refs_4_.refs_6_
  66.1 1.3 shard_map.111
  67.4 1.1 copy-done.7
  68.6 1.1 copy-done.9
  69.7 8.5 %shard_map.112 = (f32[8,16,16,128]{3,2,1,0:T(8,128)S(1)}, f32[8,16,16,128]{3,2,1,0:T(8,128)S(1)}, f32[8,16,16,128]{3,2,1,0:T(8,128)S(1)}, f32[8,16,16,128]{3,2,1,0:T(8,128)S(1)}) custom-call(s32[4]{0:T(128)S(1)} %copy-done.3, s32[48,128]{1,0:T(8,128)S(1)} %get-tuple-element.36.list_ref, f32[32]{0:T(128)S(1)} %copy-done.4, f32[32]{0:T(128)S(1)} %copy-done.5, ...), custom_call_target="tpu_custom_call" | custom-call | flops 1000000000 | bytes 10485760 | tf_op jit(solution)/shard_map/pallas_call | solution.py:186
  78.2 0.1 convert_element_type.61
  78.3 2.4 %collective-permute-start.13 = (f16[8,16,16,128]{3,2,1,0:T(8,128)(2,1)S(1)}, f16[8,16,16,128]{3,2,1,0:T(8,128)(2,1)S(1)}, u32[]{:S(2)}, u32[]{:S(2)}) collective-permute-start(f16[8,16,16,128]{3,2,1,0:T(8,128)(2,1)S(1)} %convert_element_type.61), channel_id=1, source_target_pairs={{0,384},{128,0},{256,128},{384,256},{1,385},{129,1},{257,129},{385... | collective-permute-start | bytes 1572872 | tf_op jit(solution)/shard_map/ppermute | solution.py:327
  80.8 0.1 convert_element_type.59
  80.9 3.4 %collective-permute-start.12 = (f16[8,16,16,128]{3,2,1,0:T(8,128)(2,1)S(1)}, f16[8,16,16,128]{3,2,1,0:T(8,128)(2,1)S(1)}, u32[]{:S(2)}, u32[]{:S(2)}) collective-permute-start(f16[8,16,16,128]{3,2,1,0:T(8,128)(2,1)S(1)} %convert_element_type.59), channel_id=1, source_target_pairs={{0,128},{128,256},{256,384},{384,0},{1,129},{129,257},{257,385},{3... | collective-permute-start | bytes 1572872 | tf_op jit(solution)/shard_map/ppermute | solution.py:327
  84.3 1.5 %collective-permute-done.5.refs_2_ = bf16[48,64,128]{2,1,0:T(8,128)(2,1)} collective-permute-done((bf16[48,64,128]{2,1,0:T(8,128)(2,1)}, bf16[48,64,128]{2,1,0:T(8,128)(2,1)}, u32[]{:S(2)}, u32[]{:S(2)}) %collective-permute-start.5) | collective-permute-done | bytes 786464 | tf_op jit(solution)/shard_map/ppermute | solution.py:358
  85.9 4.0 %collective-permute-start.11 = (f16[8,16,16,128]{3,2,1,0:T(8,128)(2,1)S(1)}, f16[8,16,16,128]{3,2,1,0:T(8,128)(2,1)S(1)}, u32[]{:S(2)}, u32[]{:S(2)}) collective-permute-start(f16[8,16,16,128]{3,2,1,0:T(8,128)(2,1)S(1)} %convert_element_type.57), channel_id=1, source_target_pairs={{0,256},{128,384},{256,0},{384,128},{1,257},{129,385},{257,1},{385... | collective-permute-start | bytes 1572872 | tf_op jit(solution)/shard_map/ppermute | solution.py:327
  89.9 10.0 %shard_map.113 = (f32[8,16,16,128]{3,2,1,0:T(8,128)S(1)}, f32[8,16,16,128]{3,2,1,0:T(8,128)S(1)}, f32[8,16,16,128]{3,2,1,0:T(8,128)S(1)}, f32[8,16,16,128]{3,2,1,0:T(8,128)S(1)}) custom-call(s32[4]{0:T(128)S(1)} %copy-done.3, s32[48,128]{1,0:T(8,128)S(1)} %get-tuple-element.45.list_ref, f32[32]{0:T(128)S(1)} %copy-done.4, f32[32]{0:T(128)S(1)} %copy-done.5, ...), custom_call_target="tpu_custom_call" | custom-call | flops 1000000000 | bytes 10485760 | tf_op jit(solution)/shard_map/pallas_call | solution.py:186
  99.9 0.1 convert_element_type.55
  100.0 3.4 %collective-permute-start.10 = (f16[8,16,16,128]{3,2,1,0:T(8,128)(2,1)S(1)}, f16[8,16,16,128]{3,2,1,0:T(8,128)(2,1)S(1)}, u32[]{:S(2)}, u32[]{:S(2)}) collective-permute-start(f16[8,16,16,128]{3,2,1,0:T(8,128)(2,1)S(1)} %convert_element_type.55), channel_id=1, source_target_pairs={{0,384},{128,0},{256,128},{384,256},{1,385},{129,1},{257,129},{385... | collective-permute-start | bytes 1572872 | tf_op jit(solution)/shard_map/ppermute | solution.py:327
  103.5 2.4 %collective-permute-start.9 = (f16[8,16,16,128]{3,2,1,0:T(8,128)(2,1)S(1)}, f16[8,16,16,128]{3,2,1,0:T(8,128)(2,1)S(1)}, u32[]{:S(2)}, u32[]{:S(2)}) collective-permute-start(f16[8,16,16,128]{3,2,1,0:T(8,128)(2,1)S(1)} %convert_element_type.53), channel_id=1, source_target_pairs={{0,128},{128,256},{256,384},{384,0},{1,129},{129,257},{257,385},{3... | collective-permute-start | bytes 1572872 | tf_op jit(solution)/shard_map/ppermute | solution.py:327
  105.9 0.1 convert_element_type.51
  106.0 5.6 %collective-permute-start.8 = (f16[8,16,16,128]{3,2,1,0:T(8,128)(2,1)S(1)}, f16[8,16,16,128]{3,2,1,0:T(8,128)(2,1)S(1)}, u32[]{:S(2)}, u32[]{:S(2)}) collective-permute-start(f16[8,16,16,128]{3,2,1,0:T(8,128)(2,1)S(1)} %convert_element_type.51), channel_id=1, source_target_pairs={{0,256},{128,384},{256,0},{384,128},{1,257},{129,385},{257,1},{385... | collective-permute-start | bytes 1572872 | tf_op jit(solution)/shard_map/ppermute | solution.py:327
  111.6 0.3 add_convert_fusion.1
  111.9 2.7 %collective-permute-start.14 = (f16[8,16,16,128]{3,2,1,0:T(8,128)(2,1)S(1)}, f16[8,16,16,128]{3,2,1,0:T(8,128)(2,1)S(1)}, u32[]{:S(2)}, u32[]{:S(2)}) collective-permute-start(f16[8,16,16,128]{3,2,1,0:T(8,128)(2,1)S(1)} %add_convert_fusion.1), channel_id=1, source_target_pairs={{0,64},{2,66},{4,68},{6,70},{8,72},{10,74},{12,76},{14,78},{16,80}... | collective-permute-start | bytes 1572872 | tf_op jit(solution)/shard_map/ppermute | solution.py:375
  114.6 9.6 %collective-permute-done.10 = f16[8,16,16,128]{3,2,1,0:T(8,128)(2,1)S(1)} collective-permute-done((f16[8,16,16,128]{3,2,1,0:T(8,128)(2,1)S(1)}, f16[8,16,16,128]{3,2,1,0:T(8,128)(2,1)S(1)}, u32[]{:S(2)}, u32[]{:S(2)}) %collective-permute-start.10) | collective-permute-done | bytes 524320 | tf_op jit(solution)/shard_map/ppermute | solution.py:327
  124.2 8.3 %collective-permute-done.14 = f16[8,16,16,128]{3,2,1,0:T(8,128)(2,1)S(1)} collective-permute-done((f16[8,16,16,128]{3,2,1,0:T(8,128)(2,1)S(1)}, f16[8,16,16,128]{3,2,1,0:T(8,128)(2,1)S(1)}, u32[]{:S(2)}, u32[]{:S(2)}) %collective-permute-start.14) | collective-permute-done | bytes 524320 | tf_op jit(solution)/shard_map/ppermute | solution.py:375
  132.5 1.2 add_convert_fusion
  133.7 3.5 %all-to-all-start.1 = ((f16[8,16,16,128]{3,2,1,0:T(8,128)(2,1)}), f16[8,16,16,128]{3,2,1,0:T(8,128)(2,1)S(1)}, u32[]{:S(2)}, u32[]{:S(2)}) async-start(f16[8,16,16,128]{3,2,1,0:T(8,128)(2,1)} %add_convert_fusion), calls=%async_computation.1 | async-start | bytes 1048576 | tf_op jit(solution)/shard_map/all_to_all | solution.py:377
  137.2 0.2 select_reduce_fusion
  137.4 0.2 convolution_bitcast_fusion
  137.6 0.1 fusion.18
  137.7 12.7 %all-to-all-done.1 = f16[8,16,16,128]{3,2,1,0:T(8,128)(2,1)S(1)} async-done(((f16[8,16,16,128]{3,2,1,0:T(8,128)(2,1)}), f16[8,16,16,128]{3,2,1,0:T(8,128)(2,1)S(1)}, u32[]{:S(2)}, u32[]{:S(2)}) %all-to-all-start.1) | async-done | bytes 524320 | tf_op jit(solution)/shard_map/all_to_all | solution.py:377
  150.4 0.8 fusion.4
  (35 shorter events, 0.3 us)
Async XLA Ops:
  0.0 37.2 %collective-permute-start.1 = (bf16[128,64,128]{2,1,0:T(8,128)(2,1)}, bf16[128,64,128]{2,1,0:T(8,128)(2,1)S(1)}, u32[]{:S(2)}, u32[]{:S(2)}) collective-permute-start(bf16[128,64,128]{2,1,0:T(8,128)(2,1)} %bitcast.20), channel_id=1, source_target_pairs={{0,1},{1,0},{2,3},{3,2},{4,5},{5,4},{6,7},{7,6},{8,9},{9,8},{10,11... | collective-permute-start | bytes 6291464 | tf_op jit(solution)/shard_map/ppermute | solution.py:347
  4.3 33.0 %all-to-all-start = ((s32[16,40,128]{2,1,0:T(8,128)}), s32[16,40,128]{2,1,0:T(8,128)S(1)}, u32[]{:S(2)}, u32[]{:S(2)}) async-start(s32[16,40,128]{2,1,0:T(8,128)} %shard_map.109), calls=%async_computation | async-start | bytes 655360 | tf_op jit(solution)/shard_map/all_to_all | solution.py:349
  20.6 16.6 %collective-permute-start = (s32[384]{0:T(512)S(1)}, s32[384]{0:T(512)S(1)}, u32[]{:S(2)}, u32[]{:S(2)}) collective-permute-start(s32[384]{0:T(512)S(1)} %bitcast.22), channel_id=1, source_target_pairs={{0,1},{1,0},{2,3},{3,2},{4,5},{5,4},{6,7},{7,6},{8,9},{9,8},{10,11... | collective-permute-start | bytes 4616 | tf_op jit(solution)/shard_map/ppermute | solution.py:348
  37.2 1.6 %copy-start = (bf16[1,1,128,64,128]{4,3,2,1,0:T(8,128)(2,1)S(1)}, bf16[1,1,128,64,128]{4,3,2,1,0:T(8,128)(2,1)}, u32[]{:S(2)}) copy-start(bf16[1,1,128,64,128]{4,3,2,1,0:T(8,128)(2,1)} %param.11) | copy-start | bytes 6291460
  38.8 0.6 copy-start.2
  42.6 0.9 copy-start.6
  43.5 22.5 %copy-start.10 = (bf16[64,64]{1,0:T(8,128)(2,1)S(1)}, bf16[64,64]{1,0:T(8,128)(2,1)}, u32[]{:S(2)}) copy-start(bf16[64,64]{1,0:T(8,128)(2,1)} %param.17) | copy-start | bytes 24580
  43.5 22.5 %copy-start.3 = (s32[4]{0:T(128)S(1)}, s32[4]{0:T(128)}, u32[]{:S(2)}) copy-start(s32[4]{0:T(128)} %pad_add_fusion.spot_ref) | copy-start | bytes 52
  43.5 23.9 %copy-start.1 = (bf16[16,16,128]{2,1,0:T(8,128)(2,1)S(1)}, bf16[16,16,128]{2,1,0:T(8,128)(2,1)}, u32[]{:S(2)}) copy-start(bf16[16,16,128]{2,1,0:T(8,128)(2,1)} %refs_7_.1) | copy-start | bytes 196612
  43.5 23.9 %copy-start.4 = (f32[32]{0:T(128)S(1)}, f32[32]{0:T(128)}, u32[]{:S(2)}) copy-start(f32[32]{0:T(128)} %re_ref.3) | copy-start | bytes 388
  43.5 23.9 %copy-start.5 = (f32[32]{0:T(128)S(1)}, f32[32]{0:T(128)}, u32[]{:S(2)}) copy-start(f32[32]{0:T(128)} %im_ref.3) | copy-start | bytes 388
  43.6 15.3 %collective-permute-start.2 = (bf16[48,64,128]{2,1,0:T(8,128)(2,1)S(1)}, bf16[48,64,128]{2,1,0:T(8,128)(2,1)S(1)}, u32[]{:S(2)}, u32[]{:S(2)}) collective-permute-start(bf16[48,64,128]{2,1,0:T(8,128)(2,1)S(1)} %get-tuple-element.38), channel_id=1, source_target_pairs={{0,112},{2,114},{4,116},{6,118},{8,120},{10,122},{12,124},{14,126}... | collective-permute-start | bytes 2359304 | tf_op jit(solution)/shard_map/ppermute | solution.py:358
  46.0 21.4 %collective-permute-start.3 = (bf16[48,64,128]{2,1,0:T(8,128)(2,1)}, bf16[48,64,128]{2,1,0:T(8,128)(2,1)}, u32[]{:S(2)}, u32[]{:S(2)}) collective-permute-start(bf16[48,64,128]{2,1,0:T(8,128)(2,1)} %get-tuple-element.39), channel_id=1, source_target_pairs={{0,16},{2,18},{4,20},{6,22},{8,24},{10,26},{12,28},{14,30},{16,32}... | collective-permute-start | bytes 2359304 | tf_op jit(solution)/shard_map/ppermute | solution.py:358
  49.5 31.4 %collective-permute-start.4 = (bf16[48,64,128]{2,1,0:T(8,128)(2,1)}, bf16[48,64,128]{2,1,0:T(8,128)(2,1)S(1)}, u32[]{:S(2)}, u32[]{:S(2)}) collective-permute-start(bf16[48,64,128]{2,1,0:T(8,128)(2,1)} %get-tuple-element.47), channel_id=1, source_target_pairs={{0,16},{2,18},{4,20},{6,22},{8,24},{10,26},{12,28},{14,30},{16,32}... | collective-permute-start | bytes 2359304 | tf_op jit(solution)/shard_map/ppermute | solution.py:358
  51.9 34.0 %collective-permute-start.5 = (bf16[48,64,128]{2,1,0:T(8,128)(2,1)}, bf16[48,64,128]{2,1,0:T(8,128)(2,1)}, u32[]{:S(2)}, u32[]{:S(2)}) collective-permute-start(bf16[48,64,128]{2,1,0:T(8,128)(2,1)} %get-tuple-element.48), channel_id=1, source_target_pairs={{0,32},{2,34},{4,36},{6,38},{8,40},{10,42},{12,44},{14,46},{16,48}... | collective-permute-start | bytes 2359304 | tf_op jit(solution)/shard_map/ppermute | solution.py:358
  55.1 34.8 %collective-permute-start.6 = (bf16[48,64,128]{2,1,0:T(8,128)(2,1)}, bf16[48,64,128]{2,1,0:T(8,128)(2,1)}, u32[]{:S(2)}, u32[]{:S(2)}) collective-permute-start(bf16[48,64,128]{2,1,0:T(8,128)(2,1)} %get-tuple-element.49), channel_id=1, source_target_pairs={{0,112},{2,114},{4,116},{6,118},{8,120},{10,122},{12,124},{14,126}... | collective-permute-start | bytes 2359304 | tf_op jit(solution)/shard_map/ppermute | solution.py:358
  58.8 0.9 copy-start.8
  59.8 30.1 %collective-permute-start.7 = (bf16[48,64,128]{2,1,0:T(8,128)(2,1)}, bf16[48,64,128]{2,1,0:T(8,128)(2,1)}, u32[]{:S(2)}, u32[]{:S(2)}) collective-permute-start(bf16[48,64,128]{2,1,0:T(8,128)(2,1)} %get-tuple-element.50), channel_id=1, source_target_pairs={{0,96},{2,98},{4,100},{6,102},{8,104},{10,106},{12,108},{14,110},{... | collective-permute-start | bytes 2359304 | tf_op jit(solution)/shard_map/ppermute | solution.py:358
  67.4 1.1 copy-start.7
  68.6 1.1 copy-start.9
  78.3 27.7 %collective-permute-start.13 = (f16[8,16,16,128]{3,2,1,0:T(8,128)(2,1)S(1)}, f16[8,16,16,128]{3,2,1,0:T(8,128)(2,1)S(1)}, u32[]{:S(2)}, u32[]{:S(2)}) collective-permute-start(f16[8,16,16,128]{3,2,1,0:T(8,128)(2,1)S(1)} %convert_element_type.61), channel_id=1, source_target_pairs={{0,384},{128,0},{256,128},{384,256},{1,385},{129,1},{257,129},{385... | collective-permute-start | bytes 1572872 | tf_op jit(solution)/shard_map/ppermute | solution.py:327
  80.9 30.6 %collective-permute-start.12 = (f16[8,16,16,128]{3,2,1,0:T(8,128)(2,1)S(1)}, f16[8,16,16,128]{3,2,1,0:T(8,128)(2,1)S(1)}, u32[]{:S(2)}, u32[]{:S(2)}) collective-permute-start(f16[8,16,16,128]{3,2,1,0:T(8,128)(2,1)S(1)} %convert_element_type.59), channel_id=1, source_target_pairs={{0,128},{128,256},{256,384},{384,0},{1,129},{129,257},{257,385},{3... | collective-permute-start | bytes 1572872 | tf_op jit(solution)/shard_map/ppermute | solution.py:327
  85.9 25.7 %collective-permute-start.11 = (f16[8,16,16,128]{3,2,1,0:T(8,128)(2,1)S(1)}, f16[8,16,16,128]{3,2,1,0:T(8,128)(2,1)S(1)}, u32[]{:S(2)}, u32[]{:S(2)}) collective-permute-start(f16[8,16,16,128]{3,2,1,0:T(8,128)(2,1)S(1)} %convert_element_type.57), channel_id=1, source_target_pairs={{0,256},{128,384},{256,0},{384,128},{1,257},{129,385},{257,1},{385... | collective-permute-start | bytes 1572872 | tf_op jit(solution)/shard_map/ppermute | solution.py:327
  100.0 24.2 %collective-permute-start.10 = (f16[8,16,16,128]{3,2,1,0:T(8,128)(2,1)S(1)}, f16[8,16,16,128]{3,2,1,0:T(8,128)(2,1)S(1)}, u32[]{:S(2)}, u32[]{:S(2)}) collective-permute-start(f16[8,16,16,128]{3,2,1,0:T(8,128)(2,1)S(1)} %convert_element_type.55), channel_id=1, source_target_pairs={{0,384},{128,0},{256,128},{384,256},{1,385},{129,1},{257,129},{385... | collective-permute-start | bytes 1572872 | tf_op jit(solution)/shard_map/ppermute | solution.py:327
  103.5 20.7 %collective-permute-start.9 = (f16[8,16,16,128]{3,2,1,0:T(8,128)(2,1)S(1)}, f16[8,16,16,128]{3,2,1,0:T(8,128)(2,1)S(1)}, u32[]{:S(2)}, u32[]{:S(2)}) collective-permute-start(f16[8,16,16,128]{3,2,1,0:T(8,128)(2,1)S(1)} %convert_element_type.53), channel_id=1, source_target_pairs={{0,128},{128,256},{256,384},{384,0},{1,129},{129,257},{257,385},{3... | collective-permute-start | bytes 1572872 | tf_op jit(solution)/shard_map/ppermute | solution.py:327
  106.0 18.2 %collective-permute-start.8 = (f16[8,16,16,128]{3,2,1,0:T(8,128)(2,1)S(1)}, f16[8,16,16,128]{3,2,1,0:T(8,128)(2,1)S(1)}, u32[]{:S(2)}, u32[]{:S(2)}) collective-permute-start(f16[8,16,16,128]{3,2,1,0:T(8,128)(2,1)S(1)} %convert_element_type.51), channel_id=1, source_target_pairs={{0,256},{128,384},{256,0},{384,128},{1,257},{129,385},{257,1},{385... | collective-permute-start | bytes 1572872 | tf_op jit(solution)/shard_map/ppermute | solution.py:327
  111.9 20.6 %collective-permute-start.14 = (f16[8,16,16,128]{3,2,1,0:T(8,128)(2,1)S(1)}, f16[8,16,16,128]{3,2,1,0:T(8,128)(2,1)S(1)}, u32[]{:S(2)}, u32[]{:S(2)}) collective-permute-start(f16[8,16,16,128]{3,2,1,0:T(8,128)(2,1)S(1)} %add_convert_fusion.1), channel_id=1, source_target_pairs={{0,64},{2,66},{4,68},{6,70},{8,72},{10,74},{12,76},{14,78},{16,80}... | collective-permute-start | bytes 1572872 | tf_op jit(solution)/shard_map/ppermute | solution.py:375
  132.5 4.7 %copy-start.11 = (s32[16,3]{0,1:T(4,128)S(1)}, s32[16,3]{0,1:T(4,128)}, u32[]{:S(2)}) copy-start(s32[16,3]{0,1:T(4,128)} %param.14) | copy-start | bytes 580
  132.5 4.7 %copy-start.12 = (f32[128]{0:T(128)S(1)}, f32[128]{0:T(128)}, u32[]{:S(2)}) copy-start(f32[128]{0:T(128)} %param.21) | copy-start | bytes 1540
  133.7 16.7 %all-to-all-start.1 = ((f16[8,16,16,128]{3,2,1,0:T(8,128)(2,1)}), f16[8,16,16,128]{3,2,1,0:T(8,128)(2,1)S(1)}, u32[]{:S(2)}, u32[]{:S(2)}) async-start(f16[8,16,16,128]{3,2,1,0:T(8,128)(2,1)} %add_convert_fusion), calls=%async_computation.1 | async-start | bytes 1048576 | tf_op jit(solution)/shard_map/all_to_all | solution.py:377

commit v9 on v8

--- a/solution.py
+++ b/solution.py
@@ -47,9 +47,6 @@
 
 
 DELIVER = [[device(c, a, b) for b in range(RINGS)] for c in range(2) for a in range(RINGS)]
-LISTENERS = [
-    [device(c, a + far, b) for far in (0, 4) for b in range(RINGS)] for c in range(2) for a in range(RINGS // 2)
-]
 
 
 def pick_kernel(spot_ref, own_slot, sib_slot, own_ref, sib_hbm, *refs):
@@ -87,7 +84,7 @@
 def terms_kernel(sources, modes, windows, part, spot_ref, list_ref, re_ref, im_ref, *refs):
     flat_refs = refs[:sources]
     wide_ref, ham_ref, rho_ref = refs[sources:sources + 3]
-    out_refs, (flat, acc) = refs[sources + 3:-2], refs[-2:]
+    out_refs, (flat, acc, sems) = refs[sources + 3:-3], refs[-3:]
     here, group = spot_ref[2], spot_ref[3]
     share = rho_ref.shape[1]
     width = ham_ref.shape[0]
@@ -97,12 +94,13 @@
     levels = modes // LOT + CAP
     downs, extra, counts = modes, modes + CAP + slot * levels, list_ref.shape[0] - 1
 
-    def gather(row, carry):
-        for n, ref in enumerate(flat_refs):
-            flat[n * SPAN + row] = ref[row]
-        return carry
-
-    lax.fori_loop(0, SPAN, gather, 0, unroll=8)
+    copies = [
+        pltpu.make_async_copy(ref, flat.at[pl.ds(n * SPAN, SPAN)], sems.at[n]) for n, ref in enumerate(flat_refs)
+    ]
+    for copy in copies:
+        copy.start()
+    for copy in copies:
+        copy.wait()
 
     def lot(pair, base):
         entries = [list_ref[base + n, pair] for n in range(LOT)]
@@ -185,12 +183,13 @@
     width = head_cols.shape[0]
     return pl.pallas_call(
         functools.partial(terms_kernel, len(pieces), modes, windows, part),
-        in_specs=[SMEM] * 4 + [VMEM] * (len(pieces) + 3),
+        in_specs=[SMEM] * 4 + [pl.BlockSpec(memory_space=pl.ANY)] * len(pieces) + [VMEM] * 3,
         out_specs=[VMEM] * (width // share),
         out_shape=[jax.ShapeDtypeStruct((part[1] - part[0], windows, share, lanes), F32)] * (width // share),
         scratch_shapes=[
             pltpu.VMEM((len(pieces) * SPAN, width, lanes), BF16),
             pltpu.VMEM((RINGS * windows + 1, width, lanes), F32),
+            pltpu.SemaphoreType.DMA((len(pieces),)),
         ],
         compiler_params=pltpu.CompilerParams(vmem_limit_bytes=28 * 2**20),
         cost_estimate=pl.CostEstimate(flops=10**9, bytes_accessed=10 * 2**20, transcendentals=0),
@@ -264,10 +263,9 @@
 
 def lists_kernel(kinds, modes, spot_ref, heard_ref, *refs):
     out_refs, sum_ref = refs[:-1], refs[-1]
-    half = lax.shift_right_logical(spot_ref[1], 2)
+    rows = sum_ref.shape[0]
     for (steps, parts, far), out_ref in zip(kinds, out_refs, strict=True):
-        begin = (half ^ far) * RINGS
-        sum_ref[...] = sum(heard_ref[begin + r] for r in range(RINGS))
+        sum_ref[...] = sum(heard_ref[r, far * rows:(far + 1) * rows] for r in range(RINGS))
         lists_of(steps, parts, modes, spot_ref, sum_ref, out_ref)
 
 
@@ -278,7 +276,7 @@
         in_specs=[SMEM, VMEM],
         out_specs=[VMEM] * len(kinds),
         out_shape=[jax.ShapeDtypeStruct((n + -n % 8, heard.shape[2]), jnp.int32) for n in rows],
-        scratch_shapes=[pltpu.VMEM(heard.shape[1:], jnp.int32)],
+        scratch_shapes=[pltpu.VMEM((heard.shape[1] // 2, heard.shape[2]), jnp.int32)],
         compiler_params=pltpu.CompilerParams(vmem_limit_bytes=8 * 2**20),
         cost_estimate=pl.CostEstimate(flops=10**7, bytes_accessed=2**18, transcendentals=0),
     )(spot, heard)
@@ -286,7 +284,7 @@
 
 def say_kernel(spot_ref, up_ref, down_ref, tri_ref, out_ref):
     windows, modes = up_ref.shape
-    shape = (windows, out_ref.shape[2])
+    shape = (windows, out_ref.shape[1])
     lanes = lax.broadcasted_iota(jnp.int32, shape, 1)
     row = lax.broadcasted_iota(jnp.int32, shape, 0)
     place = jnp.where(lanes == spot_ref[2] * windows + row, 1.0, 0.0)
@@ -301,10 +299,9 @@
         return (half(high) * 32.0 + half(values & 31)).astype(jnp.int32)
 
     up, down, tri = put(up_ref[...], 0), put(down_ref[...], 1), put(tri_ref[...], 1)
-    spare = jnp.zeros((out_ref.shape[1] - modes - 2 * CAP, shape[1]), jnp.int32)
+    spare = jnp.zeros((out_ref.shape[0] - modes - 2 * CAP, shape[1]), jnp.int32)
     whole = jnp.concatenate([up, down, tri, spare], axis=0)
-    for n in range(out_ref.shape[0]):
-        out_ref[n] = whole
+    out_ref[...] = whole
 
 
 def say(spot, use_up, use_down, modes_tri):
@@ -314,7 +311,7 @@
         say_kernel,
         in_specs=[SMEM, VMEM, VMEM, VMEM],
         out_specs=VMEM,
-        out_shape=jax.ShapeDtypeStruct((2 * RINGS, rows + -rows % 8, RINGS * windows), jnp.int32),
+        out_shape=jax.ShapeDtypeStruct((rows + -rows % 8, RINGS * windows), jnp.int32),
         cost_estimate=pl.CostEstimate(flops=10**6, bytes_accessed=2**18, transcendentals=0),
     )(spot, use_up, use_down.T, modes_tri.T)
 
@@ -346,12 +343,17 @@
     slots = jnp.transpose(send_slot[0, 0]).reshape(-1)
     sib_store = lax.ppermute(states[0, 0], "ado", SIBLING)
     sib_slots = lax.ppermute(slots, "ado", SIBLING)
+    said = say(spot, use_up, use_down, modes_tri)
+    said = jnp.concatenate([said, lax.ppermute(said, "ado", onward(4))], axis=0)
     heard = lax.all_to_all(
-        say(spot, use_up, use_down, modes_tri), "ado", split_axis=0, concat_axis=0, tiled=True,
-        axis_index_groups=LISTENERS,
+        jnp.broadcast_to(said, (RINGS,) + said.shape), "ado", split_axis=0, concat_axis=0, tiled=True,
+        axis_index_groups=DELIVER,
     )
-    heard, slots = lax.optimization_barrier((heard, slots))
     picked = pick(spot, slots, sib_slots, states[0, 0], sib_store)
+    maps_wide = jnp.concatenate([doubled(coupling), jnp.zeros((1, 2 * width, 2 * width), BF16)], axis=0)
+    head_cols = lax.dynamic_slice_in_dim(hamiltonian, group * share, share, 1)
+    shared = (maps_wide, head_cols, window_tier_states)
+    picked, heard, shared = lax.optimization_barrier((picked, heard, shared))
 
     def send(steps, blocks):
         return [
@@ -361,14 +363,9 @@
 
     far_states = send(FAR, picked[:len(FAR)])
     near_states = send(NEAR, picked[len(FAR):])
-    held, heard = lax.optimization_barrier((picked[0], heard))
-    far_states[0] = held
     kinds = ((FAR, ((0, RINGS),), 1), (NEAR, ((0, RINGS),), 0))
     far_lists, near_lists = use_lists(kinds, modes, spot, heard)
 
-    maps_wide = jnp.concatenate([doubled(coupling), jnp.zeros((1, 2 * width, 2 * width), BF16)], axis=0)
-    head_cols = lax.dynamic_slice_in_dim(hamiltonian, group * share, share, 1)
-    shared = (maps_wide, head_cols, window_tier_states)
     far = terms((0, RINGS, 0), spot, far_lists, coup_re, coup_im, far_states, *shared)
     far, near_lists = lax.optimization_barrier((far, near_lists))
     far = over_groups(far)

time: 152 us -> 156 us (1.026)
  the two profiles are of different devices: /device:TPU:2 before, /device:TPU:66 now
where the time goes in v9:
time: 156 us; the launch traced here: 155 us
  starting transfers between devices  76 us (49%)
  waiting for transfers between devices  37.8 us (24%)
  Pallas kernels  23.6 us (15%)
  local copies, waits for them, and re-layouts  10.7 us (7%)
  other arithmetic  5.89 us (4%)
    ppermute x6, starting transfers between devices, send(): lax.ppermute(block, 'ado', onward(step))  23.1 us
    ppermute x6, starting transfers between devices, over_groups(): lax.ppermute(parts[shift].astype(LINK), 'grp', ring).astype(F32)  19.7 us
    pallas_call x2, Pallas kernels, terms(): pl.pallas_call(functools.partial(terms_kernel, len(pieces), modes, window...  18.2 us
    all_to_all x1, waiting for transfers between devices, on_device(): lax.all_to_all((near + far.astype(F32)).astype(LINK), 'ado', split_axis=0...  12.8 us
    ppermute x1, starting transfers between devices, on_device(): said = jnp.concatenate([said, lax.ppermute(said, 'ado', onward(4))], axis=0)  10 us
    unnamed x41, local copies, waits for them, and re-layouts  9.79 us
    all_to_all x1, starting transfers between devices, on_device(): lax.all_to_all((near + far.astype(F32)).astype(LINK), 'ado', split_axis=0...  8.77 us
    ppermute x6, waiting for transfers between devices, over_groups(): lax.ppermute(parts[shift].astype(LINK), 'grp', ring).astype(F32)  8.34 us
  transfers between devices with their start and end apart: 18, of which 5 were waited for; matrix products, arithmetic and copies ran while one was open for 4% of the time, Pallas kernels for 15%

profile of v9, /device:TPU:66, one launch (start us, length us, event | category | flops | bytes accessed | tf_op | source)
XLA Modules:
  0.0 154.8 jit_solution(4928519338520958672)
XLA Ops:
  0.0 2.0 %collective-permute-start.1 = (bf16[128,64,128]{2,1,0:T(8,128)(2,1)}, bf16[128,64,128]{2,1,0:T(8,128)(2,1)}, u32[]{:S(2)}, u32[]{:S(2)}) collective-permute-start(bf16[128,64,128]{2,1,0:T(8,128)(2,1)} %bitcast.20), channel_id=1, source_target_pairs={{0,1},{1,0},{2,3},{3,2},{4,5},{5,4},{6,7},{7,6},{8,9},{9,8},{10,11... | collective-permute-start | bytes 6291464 | tf_op jit(solution)/shard_map/ppermute | solution.py:344
  2.1 0.6 pad_add_fusion.1.spot_ref
  2.7 1.6 %shard_map.110 = s32[40,128]{1,0:T(8,128)} custom-call(s32[4]{0:T(128)} %pad_add_fusion.1.spot_ref, s32[16,32]{1,0:T(8,128)} %up_ref.1, s32[3,16]{1,0:T(4,128)} %bitcast.25, s32[3,16]{1,0:T(4,128)} %bitcast.24), custom_call_target="tpu_custom_call" | custom-call | flops 1000000 | bytes 262144 | tf_op jit(solution)/shard_map/pallas_call | solution.py:310
  4.3 10.0 %collective-permute-start.2 = (s32[40,128]{1,0:T(8,128)}, s32[40,128]{1,0:T(8,128)S(1)}, u32[]{:S(2)}, u32[]{:S(2)}) collective-permute-start(s32[40,128]{1,0:T(8,128)} %shard_map.110), channel_id=1, source_target_pairs={{0,64},{2,66},{4,68},{6,70},{8,72},{10,74},{12,76},{14,78},{16,80}... | collective-permute-start | bytes 61448 | tf_op jit(solution)/shard_map/ppermute | solution.py:347
  14.3 2.0 %collective-permute-done.2 = s32[40,128]{1,0:T(8,128)S(1)} collective-permute-done((s32[40,128]{1,0:T(8,128)}, s32[40,128]{1,0:T(8,128)S(1)}, u32[]{:S(2)}, u32[]{:S(2)}) %collective-permute-start.2) | collective-permute-done | bytes 20512 | tf_op jit(solution)/shard_map/ppermute | solution.py:347
  16.2 0.7 pad_add_fusion
  17.0 0.8 broadcast_in_dim.10
  17.7 7.2 %all-to-all-start = ((s32[8,80,128]{2,1,0:T(8,128)}), s32[8,80,128]{2,1,0:T(8,128)S(1)}, u32[]{:S(2)}, u32[]{:S(2)}) async-start(s32[8,80,128]{2,1,0:T(8,128)} %broadcast_in_dim.10), calls=%async_computation | async-start | bytes 655360 | tf_op jit(solution)/shard_map/all_to_all | solution.py:348
  25.0 0.7 copy.15
  25.7 1.9 %collective-permute-start = (s32[384]{0:T(512)S(1)}, s32[384]{0:T(512)S(1)}, u32[]{:S(2)}, u32[]{:S(2)}) collective-permute-start(s32[384]{0:T(512)S(1)} %bitcast.22), channel_id=1, source_target_pairs={{0,1},{1,0},{2,3},{3,2},{4,5},{5,4},{6,7},{7,6},{8,9},{9,8},{10,11... | collective-permute-start | bytes 4616 | tf_op jit(solution)/shard_map/ppermute | solution.py:345
  27.6 1.5 fusion.2
  29.4 2.5 %shard_map.109 = (bf16[48,64,128]{2,1,0:T(8,128)(2,1)S(1)}, bf16[48,64,128]{2,1,0:T(8,128)(2,1)S(1)}, bf16[48,64,128]{2,1,0:T(8,128)(2,1)S(1)}, bf16[48,64,128]{...) custom-call(s32[4]{0:T(128)S(1)} %copy-done.5, ...), custom_call_target="tpu_custom_call" | custom-call | bytes 10485760 | tf_op jit(solution)/shard_map/pallas_call | solution.py:73
  31.9 0.9 copy-done.1
  32.8 0.9 copy-done.8
  33.7 0.9 copy-done.9
  34.5 0.9 copy-done.10
  35.4 0.9 copy-done.11
  36.3 0.9 copy-done.12
  37.2 0.9 copy-done.14
  38.1 0.9 copy-done.15
  39.0 2.5 %collective-permute-start.3 = (bf16[48,64,128]{2,1,0:T(8,128)(2,1)}, bf16[48,64,128]{2,1,0:T(8,128)(2,1)S(1)}, u32[]{:S(2)}, u32[]{:S(2)}) collective-permute-start(bf16[48,64,128]{2,1,0:T(8,128)(2,1)} %copy-done.15), channel_id=1, source_target_pairs={{0,112},{2,114},{4,116},{6,118},{8,120},{10,122},{12,124},{14,126}... | collective-permute-start | bytes 2359304 | tf_op jit(solution)/shard_map/ppermute | solution.py:360
  41.5 3.4 %collective-permute-start.4 = (bf16[48,64,128]{2,1,0:T(8,128)(2,1)}, bf16[48,64,128]{2,1,0:T(8,128)(2,1)S(1)}, u32[]{:S(2)}, u32[]{:S(2)}) collective-permute-start(bf16[48,64,128]{2,1,0:T(8,128)(2,1)} %copy-done.14), channel_id=1, source_target_pairs={{0,16},{2,18},{4,20},{6,22},{8,24},{10,26},{12,28},{14,30},{16,32}... | collective-permute-start | bytes 2359304 | tf_op jit(solution)/shard_map/ppermute | solution.py:360
  44.8 3.6 %collective-permute-start.5 = (bf16[48,64,128]{2,1,0:T(8,128)(2,1)}, bf16[48,64,128]{2,1,0:T(8,128)(2,1)S(1)}, u32[]{:S(2)}, u32[]{:S(2)}) collective-permute-start(bf16[48,64,128]{2,1,0:T(8,128)(2,1)} %copy-done.11), channel_id=1, source_target_pairs={{0,16},{2,18},{4,20},{6,22},{8,24},{10,26},{12,28},{14,30},{16,32}... | collective-permute-start | bytes 2359304 | tf_op jit(solution)/shard_map/ppermute | solution.py:360
  48.4 5.8 %collective-permute-start.6 = (bf16[48,64,128]{2,1,0:T(8,128)(2,1)}, bf16[48,64,128]{2,1,0:T(8,128)(2,1)S(1)}, u32[]{:S(2)}, u32[]{:S(2)}) collective-permute-start(bf16[48,64,128]{2,1,0:T(8,128)(2,1)} %copy-done.10), channel_id=1, source_target_pairs={{0,32},{2,34},{4,36},{6,38},{8,40},{10,42},{12,44},{14,46},{16,48}... | collective-permute-start | bytes 2359304 | tf_op jit(solution)/shard_map/ppermute | solution.py:360
  54.3 1.9 %collective-permute-start.7 = (bf16[48,64,128]{2,1,0:T(8,128)(2,1)}, bf16[48,64,128]{2,1,0:T(8,128)(2,1)S(1)}, u32[]{:S(2)}, u32[]{:S(2)}) collective-permute-start(bf16[48,64,128]{2,1,0:T(8,128)(2,1)} %copy-done.9), channel_id=1, source_target_pairs={{0,112},{2,114},{4,116},{6,118},{8,120},{10,122},{12,124},{14,126}... | collective-permute-start | bytes 2359304 | tf_op jit(solution)/shard_map/ppermute | solution.py:360
  56.2 5.9 %collective-permute-start.8 = (bf16[48,64,128]{2,1,0:T(8,128)(2,1)}, bf16[48,64,128]{2,1,0:T(8,128)(2,1)S(1)}, u32[]{:S(2)}, u32[]{:S(2)}) collective-permute-start(bf16[48,64,128]{2,1,0:T(8,128)(2,1)} %copy-done.8), channel_id=1, source_target_pairs={{0,96},{2,98},{4,100},{6,102},{8,104},{10,106},{12,108},{14,110},{... | collective-permute-start | bytes 2359304 | tf_op jit(solution)/shard_map/ppermute | solution.py:360
  62.1 1.3 shard_map.111
  63.5 0.8 copy-done.3
  64.3 1.1 copy-done.13
  65.4 7.9 %shard_map.112 = (f32[8,16,16,128]{3,2,1,0:T(8,128)S(1)}, f32[8,16,16,128]{3,2,1,0:T(8,128)S(1)}, f32[8,16,16,128]{3,2,1,0:T(8,128)S(1)}, f32[8,16,16,128]{3,2,1,0:T(8,128)S(1)}) custom-call(s32[4]{0:T(128)S(1)} %copy-done.5, s32[48,128]{1,0:T(8,128)S(1)} %get-tuple-element.49.list_ref, f32[32]{0:T(128)S(1)} %copy-done.6, f32[32]{0:T(128)S(1)} %copy-done.7, ...), custom_call_target="tpu_custom_call" | custom-call | flops 1000000000 | bytes 10485760 | tf_op jit(solution)/shard_map/pallas_call | solution.py:184
  73.5 2.6 %collective-permute-start.14 = (f16[8,16,16,128]{3,2,1,0:T(8,128)(2,1)S(1)}, f16[8,16,16,128]{3,2,1,0:T(8,128)(2,1)S(1)}, u32[]{:S(2)}, u32[]{:S(2)}) collective-permute-start(f16[8,16,16,128]{3,2,1,0:T(8,128)(2,1)S(1)} %convert_element_type.61), channel_id=1, source_target_pairs={{0,384},{128,0},{256,128},{384,256},{1,385},{129,1},{257,129},{385... | collective-permute-start | bytes 1572872 | tf_op jit(solution)/shard_map/ppermute | solution.py:324
  76.2 3.4 %collective-permute-start.13 = (f16[8,16,16,128]{3,2,1,0:T(8,128)(2,1)S(1)}, f16[8,16,16,128]{3,2,1,0:T(8,128)(2,1)S(1)}, u32[]{:S(2)}, u32[]{:S(2)}) collective-permute-start(f16[8,16,16,128]{3,2,1,0:T(8,128)(2,1)S(1)} %convert_element_type.59), channel_id=1, source_target_pairs={{0,128},{128,256},{256,384},{384,0},{1,129},{129,257},{257,385},{3... | collective-permute-start | bytes 1572872 | tf_op jit(solution)/shard_map/ppermute | solution.py:324
  79.6 7.8 %collective-permute-done.6.refs_2_ = bf16[48,64,128]{2,1,0:T(8,128)(2,1)S(1)} collective-permute-done((bf16[48,64,128]{2,1,0:T(8,128)(2,1)}, bf16[48,64,128]{2,1,0:T(8,128)(2,1)S(1)}, u32[]{:S(2)}, u32[]{:S(2)}) %collective-permute-start.6) | collective-permute-done | bytes 786464 | tf_op jit(solution)/shard_map/ppermute | solution.py:360
  87.4 4.0 %collective-permute-start.12 = (f16[8,16,16,128]{3,2,1,0:T(8,128)(2,1)S(1)}, f16[8,16,16,128]{3,2,1,0:T(8,128)(2,1)S(1)}, u32[]{:S(2)}, u32[]{:S(2)}) collective-permute-start(f16[8,16,16,128]{3,2,1,0:T(8,128)(2,1)S(1)} %convert_element_type.57), channel_id=1, source_target_pairs={{0,256},{128,384},{256,0},{384,128},{1,257},{129,385},{257,1},{385... | collective-permute-start | bytes 1572872 | tf_op jit(solution)/shard_map/ppermute | solution.py:324
  91.5 10.2 %shard_map.113 = (f32[8,16,16,128]{3,2,1,0:T(8,128)S(1)}, f32[8,16,16,128]{3,2,1,0:T(8,128)S(1)}, f32[8,16,16,128]{3,2,1,0:T(8,128)S(1)}, f32[8,16,16,128]{3,2,1,0:T(8,128)S(1)}) custom-call(s32[4]{0:T(128)S(1)} %copy-done.5, s32[48,128]{1,0:T(8,128)S(1)} %get-tuple-element.61.list_ref, f32[32]{0:T(128)S(1)} %copy-done.6, f32[32]{0:T(128)S(1)} %copy-done.7, ...), custom_call_target="tpu_custom_call" | custom-call | flops 1000000000 | bytes 10485760 | tf_op jit(solution)/shard_map/pallas_call | solution.py:184
  101.8 2.6 %collective-permute-start.11 = (f16[8,16,16,128]{3,2,1,0:T(8,128)(2,1)S(1)}, f16[8,16,16,128]{3,2,1,0:T(8,128)(2,1)S(1)}, u32[]{:S(2)}, u32[]{:S(2)}) collective-permute-start(f16[8,16,16,128]{3,2,1,0:T(8,128)(2,1)S(1)} %convert_element_type.55), channel_id=1, source_target_pairs={{0,384},{128,0},{256,128},{384,256},{1,385},{129,1},{257,129},{385... | collective-permute-start | bytes 1572872 | tf_op jit(solution)/shard_map/ppermute | solution.py:324
  104.5 3.2 %collective-permute-start.10 = (f16[8,16,16,128]{3,2,1,0:T(8,128)(2,1)S(1)}, f16[8,16,16,128]{3,2,1,0:T(8,128)(2,1)S(1)}, u32[]{:S(2)}, u32[]{:S(2)}) collective-permute-start(f16[8,16,16,128]{3,2,1,0:T(8,128)(2,1)S(1)} %convert_element_type.53), channel_id=1, source_target_pairs={{0,128},{128,256},{256,384},{384,0},{1,129},{129,257},{257,385},{3... | collective-permute-start | bytes 1572872 | tf_op jit(solution)/shard_map/ppermute | solution.py:324
  107.8 3.8 %collective-permute-start.9 = (f16[8,16,16,128]{3,2,1,0:T(8,128)(2,1)S(1)}, f16[8,16,16,128]{3,2,1,0:T(8,128)(2,1)S(1)}, u32[]{:S(2)}, u32[]{:S(2)}) collective-permute-start(f16[8,16,16,128]{3,2,1,0:T(8,128)(2,1)S(1)} %convert_element_type.51), channel_id=1, source_target_pairs={{0,256},{128,384},{256,0},{384,128},{1,257},{129,385},{257,1},{385... | collective-permute-start | bytes 1572872 | tf_op jit(solution)/shard_map/ppermute | solution.py:324
  111.7 0.3 add_convert_fusion.1
  112.0 3.3 %collective-permute-start.15 = (f16[8,16,16,128]{3,2,1,0:T(8,128)(2,1)S(1)}, f16[8,16,16,128]{3,2,1,0:T(8,128)(2,1)S(1)}, u32[]{:S(2)}, u32[]{:S(2)}) collective-permute-start(f16[8,16,16,128]{3,2,1,0:T(8,128)(2,1)S(1)} %add_convert_fusion.1), channel_id=1, source_target_pairs={{0,64},{2,66},{4,68},{6,70},{8,72},{10,74},{12,76},{14,78},{16,80}... | collective-permute-start | bytes 1572872 | tf_op jit(solution)/shard_map/ppermute | solution.py:372
  115.3 8.3 %collective-permute-done.11 = f16[8,16,16,128]{3,2,1,0:T(8,128)(2,1)S(1)} collective-permute-done((f16[8,16,16,128]{3,2,1,0:T(8,128)(2,1)S(1)}, f16[8,16,16,128]{3,2,1,0:T(8,128)(2,1)S(1)}, u32[]{:S(2)}, u32[]{:S(2)}) %collective-permute-start.11) | collective-permute-done | bytes 524320 | tf_op jit(solution)/shard_map/ppermute | solution.py:324
  123.7 7.0 %collective-permute-done.15 = f16[8,16,16,128]{3,2,1,0:T(8,128)(2,1)S(1)} collective-permute-done((f16[8,16,16,128]{3,2,1,0:T(8,128)(2,1)S(1)}, f16[8,16,16,128]{3,2,1,0:T(8,128)(2,1)S(1)}, u32[]{:S(2)}, u32[]{:S(2)}) %collective-permute-start.15) | collective-permute-done | bytes 524320 | tf_op jit(solution)/shard_map/ppermute | solution.py:372
  130.7 1.2 add_convert_fusion
  131.8 8.8 %all-to-all-start.1 = ((f16[8,16,16,128]{3,2,1,0:T(8,128)(2,1)}), f16[8,16,16,128]{3,2,1,0:T(8,128)(2,1)S(1)}, u32[]{:S(2)}, u32[]{:S(2)}) async-start(f16[8,16,16,128]{3,2,1,0:T(8,128)(2,1)} %add_convert_fusion), calls=%async_computation.1 | async-start | bytes 1048576 | tf_op jit(solution)/shard_map/all_to_all | solution.py:374
  140.6 0.2 select_reduce_fusion
  140.8 0.2 convolution_bitcast_fusion
  141.1 12.8 %all-to-all-done.1 = f16[8,16,16,128]{3,2,1,0:T(8,128)(2,1)S(1)} async-done(((f16[8,16,16,128]{3,2,1,0:T(8,128)(2,1)}), f16[8,16,16,128]{3,2,1,0:T(8,128)(2,1)S(1)}, u32[]{:S(2)}, u32[]{:S(2)}) %all-to-all-start.1) | async-done | bytes 524320 | tf_op jit(solution)/shard_map/all_to_all | solution.py:374
  154.0 0.8 fusion.4
  (53 shorter events, 0.9 us)
Async XLA Ops:
  0.0 29.1 %copy-start.16 = (bf16[64,64]{1,0:T(8,128)(2,1)S(1)}, bf16[64,64]{1,0:T(8,128)(2,1)}, u32[]{:S(2)}) copy-start(bf16[64,64]{1,0:T(8,128)(2,1)} %param.17) | copy-start | bytes 24580
  0.0 29.3 %collective-permute-start.1 = (bf16[128,64,128]{2,1,0:T(8,128)(2,1)}, bf16[128,64,128]{2,1,0:T(8,128)(2,1)}, u32[]{:S(2)}, u32[]{:S(2)}) collective-permute-start(bf16[128,64,128]{2,1,0:T(8,128)(2,1)} %bitcast.20), channel_id=1, source_target_pairs={{0,1},{1,0},{2,3},{3,2},{4,5},{5,4},{6,7},{7,6},{8,9},{9,8},{10,11... | collective-permute-start | bytes 6291464 | tf_op jit(solution)/shard_map/ppermute | solution.py:344
  4.3 12.0 %collective-permute-start.2 = (s32[40,128]{1,0:T(8,128)}, s32[40,128]{1,0:T(8,128)S(1)}, u32[]{:S(2)}, u32[]{:S(2)}) collective-permute-start(s32[40,128]{1,0:T(8,128)} %shard_map.110), channel_id=1, source_target_pairs={{0,64},{2,66},{4,68},{6,70},{8,72},{10,74},{12,76},{14,78},{16,80}... | collective-permute-start | bytes 61448 | tf_op jit(solution)/shard_map/ppermute | solution.py:347
  17.7 11.6 %copy-start = (bf16[1,1,128,64,128]{4,3,2,1,0:T(8,128)(2,1)S(1)}, bf16[1,1,128,64,128]{4,3,2,1,0:T(8,128)(2,1)}, u32[]{:S(2)}) copy-start(bf16[1,1,128,64,128]{4,3,2,1,0:T(8,128)(2,1)} %param.11) | copy-start | bytes 6291460
  17.7 11.6 %copy-start.5 = (s32[4]{0:T(128)S(1)}, s32[4]{0:T(128)}, u32[]{:S(2)}) copy-start(s32[4]{0:T(128)} %pad_add_fusion.1.spot_ref) | copy-start | bytes 52
  17.7 21.2 %all-to-all-start = ((s32[8,80,128]{2,1,0:T(8,128)}), s32[8,80,128]{2,1,0:T(8,128)S(1)}, u32[]{:S(2)}, u32[]{:S(2)}) async-start(s32[8,80,128]{2,1,0:T(8,128)} %broadcast_in_dim.10), calls=%async_computation | async-start | bytes 655360 | tf_op jit(solution)/shard_map/all_to_all | solution.py:348
  25.7 3.7 %collective-permute-start = (s32[384]{0:T(512)S(1)}, s32[384]{0:T(512)S(1)}, u32[]{:S(2)}, u32[]{:S(2)}) collective-permute-start(s32[384]{0:T(512)S(1)} %bitcast.22), channel_id=1, source_target_pairs={{0,1},{1,0},{2,3},{3,2},{4,5},{5,4},{6,7},{7,6},{8,9},{9,8},{10,11... | collective-permute-start | bytes 4616 | tf_op jit(solution)/shard_map/ppermute | solution.py:345
  29.3 34.1 %copy-start.6 = (f32[32]{0:T(128)S(1)}, f32[32]{0:T(128)}, u32[]{:S(2)}) copy-start(f32[32]{0:T(128)} %re_ref.3) | copy-start | bytes 388
  29.3 34.1 %copy-start.7 = (f32[32]{0:T(128)S(1)}, f32[32]{0:T(128)}, u32[]{:S(2)}) copy-start(f32[32]{0:T(128)} %im_ref.3) | copy-start | bytes 388
  31.9 0.9 copy-start.1
  32.8 0.9 copy-start.8
  33.7 0.9 copy-start.9
  34.5 0.9 copy-start.10
  35.4 0.9 copy-start.11
  36.3 0.9 copy-start.12
  37.2 0.9 copy-start.14
  38.1 0.9 copy-start.15
  39.0 17.2 %collective-permute-start.3 = (bf16[48,64,128]{2,1,0:T(8,128)(2,1)}, bf16[48,64,128]{2,1,0:T(8,128)(2,1)S(1)}, u32[]{:S(2)}, u32[]{:S(2)}) collective-permute-start(bf16[48,64,128]{2,1,0:T(8,128)(2,1)} %copy-done.15), channel_id=1, source_target_pairs={{0,112},{2,114},{4,116},{6,118},{8,120},{10,122},{12,124},{14,126}... | collective-permute-start | bytes 2359304 | tf_op jit(solution)/shard_map/ppermute | solution.py:360
  41.5 22.0 %collective-permute-start.4 = (bf16[48,64,128]{2,1,0:T(8,128)(2,1)}, bf16[48,64,128]{2,1,0:T(8,128)(2,1)S(1)}, u32[]{:S(2)}, u32[]{:S(2)}) collective-permute-start(bf16[48,64,128]{2,1,0:T(8,128)(2,1)} %copy-done.14), channel_id=1, source_target_pairs={{0,16},{2,18},{4,20},{6,22},{8,24},{10,26},{12,28},{14,30},{16,32}... | collective-permute-start | bytes 2359304 | tf_op jit(solution)/shard_map/ppermute | solution.py:360
  44.8 31.4 %collective-permute-start.5 = (bf16[48,64,128]{2,1,0:T(8,128)(2,1)}, bf16[48,64,128]{2,1,0:T(8,128)(2,1)S(1)}, u32[]{:S(2)}, u32[]{:S(2)}) collective-permute-start(bf16[48,64,128]{2,1,0:T(8,128)(2,1)} %copy-done.11), channel_id=1, source_target_pairs={{0,16},{2,18},{4,20},{6,22},{8,24},{10,26},{12,28},{14,30},{16,32}... | collective-permute-start | bytes 2359304 | tf_op jit(solution)/shard_map/ppermute | solution.py:360
  48.4 39.0 %collective-permute-start.6 = (bf16[48,64,128]{2,1,0:T(8,128)(2,1)}, bf16[48,64,128]{2,1,0:T(8,128)(2,1)S(1)}, u32[]{:S(2)}, u32[]{:S(2)}) collective-permute-start(bf16[48,64,128]{2,1,0:T(8,128)(2,1)} %copy-done.10), channel_id=1, source_target_pairs={{0,32},{2,34},{4,36},{6,38},{8,40},{10,42},{12,44},{14,46},{16,48}... | collective-permute-start | bytes 2359304 | tf_op jit(solution)/shard_map/ppermute | solution.py:360
  54.3 37.2 %collective-permute-start.7 = (bf16[48,64,128]{2,1,0:T(8,128)(2,1)}, bf16[48,64,128]{2,1,0:T(8,128)(2,1)S(1)}, u32[]{:S(2)}, u32[]{:S(2)}) collective-permute-start(bf16[48,64,128]{2,1,0:T(8,128)(2,1)} %copy-done.9), channel_id=1, source_target_pairs={{0,112},{2,114},{4,116},{6,118},{8,120},{10,122},{12,124},{14,126}... | collective-permute-start | bytes 2359304 | tf_op jit(solution)/shard_map/ppermute | solution.py:360
  56.2 35.3 %collective-permute-start.8 = (bf16[48,64,128]{2,1,0:T(8,128)(2,1)}, bf16[48,64,128]{2,1,0:T(8,128)(2,1)S(1)}, u32[]{:S(2)}, u32[]{:S(2)}) collective-permute-start(bf16[48,64,128]{2,1,0:T(8,128)(2,1)} %copy-done.8), channel_id=1, source_target_pairs={{0,96},{2,98},{4,100},{6,102},{8,104},{10,106},{12,108},{14,110},{... | collective-permute-start | bytes 2359304 | tf_op jit(solution)/shard_map/ppermute | solution.py:360
  63.5 0.8 copy-start.3
  64.3 1.1 copy-start.13
  73.4 18.1 %copy-start.2 = (bf16[48,64,128]{2,1,0:T(8,128)(2,1)S(1)}, bf16[48,64,128]{2,1,0:T(8,128)(2,1)}, u32[]{:S(2)}) copy-start(bf16[48,64,128]{2,1,0:T(8,128)(2,1)} %copy-done.1) | copy-start | bytes 2359300
  73.5 34.3 %collective-permute-start.14 = (f16[8,16,16,128]{3,2,1,0:T(8,128)(2,1)S(1)}, f16[8,16,16,128]{3,2,1,0:T(8,128)(2,1)S(1)}, u32[]{:S(2)}, u32[]{:S(2)}) collective-permute-start(f16[8,16,16,128]{3,2,1,0:T(8,128)(2,1)S(1)} %convert_element_type.61), channel_id=1, source_target_pairs={{0,384},{128,0},{256,128},{384,256},{1,385},{129,1},{257,129},{385... | collective-permute-start | bytes 1572872 | tf_op jit(solution)/shard_map/ppermute | solution.py:324
  76.2 35.4 %collective-permute-start.13 = (f16[8,16,16,128]{3,2,1,0:T(8,128)(2,1)S(1)}, f16[8,16,16,128]{3,2,1,0:T(8,128)(2,1)S(1)}, u32[]{:S(2)}, u32[]{:S(2)}) collective-permute-start(f16[8,16,16,128]{3,2,1,0:T(8,128)(2,1)S(1)} %convert_element_type.59), channel_id=1, source_target_pairs={{0,128},{128,256},{256,384},{384,0},{1,129},{129,257},{257,385},{3... | collective-permute-start | bytes 1572872 | tf_op jit(solution)/shard_map/ppermute | solution.py:324
  87.4 24.3 %collective-permute-start.12 = (f16[8,16,16,128]{3,2,1,0:T(8,128)(2,1)S(1)}, f16[8,16,16,128]{3,2,1,0:T(8,128)(2,1)S(1)}, u32[]{:S(2)}, u32[]{:S(2)}) collective-permute-start(f16[8,16,16,128]{3,2,1,0:T(8,128)(2,1)S(1)} %convert_element_type.57), channel_id=1, source_target_pairs={{0,256},{128,384},{256,0},{384,128},{1,257},{129,385},{257,1},{385... | collective-permute-start | bytes 1572872 | tf_op jit(solution)/shard_map/ppermute | solution.py:324
  101.8 21.9 %collective-permute-start.11 = (f16[8,16,16,128]{3,2,1,0:T(8,128)(2,1)S(1)}, f16[8,16,16,128]{3,2,1,0:T(8,128)(2,1)S(1)}, u32[]{:S(2)}, u32[]{:S(2)}) collective-permute-start(f16[8,16,16,128]{3,2,1,0:T(8,128)(2,1)S(1)} %convert_element_type.55), channel_id=1, source_target_pairs={{0,384},{128,0},{256,128},{384,256},{1,385},{129,1},{257,129},{385... | collective-permute-start | bytes 1572872 | tf_op jit(solution)/shard_map/ppermute | solution.py:324
  104.5 19.2 %collective-permute-start.10 = (f16[8,16,16,128]{3,2,1,0:T(8,128)(2,1)S(1)}, f16[8,16,16,128]{3,2,1,0:T(8,128)(2,1)S(1)}, u32[]{:S(2)}, u32[]{:S(2)}) collective-permute-start(f16[8,16,16,128]{3,2,1,0:T(8,128)(2,1)S(1)} %convert_element_type.53), channel_id=1, source_target_pairs={{0,128},{128,256},{256,384},{384,0},{1,129},{129,257},{257,385},{3... | collective-permute-start | bytes 1572872 | tf_op jit(solution)/shard_map/ppermute | solution.py:324
  107.8 15.9 %collective-permute-start.9 = (f16[8,16,16,128]{3,2,1,0:T(8,128)(2,1)S(1)}, f16[8,16,16,128]{3,2,1,0:T(8,128)(2,1)S(1)}, u32[]{:S(2)}, u32[]{:S(2)}) collective-permute-start(f16[8,16,16,128]{3,2,1,0:T(8,128)(2,1)S(1)} %convert_element_type.51), channel_id=1, source_target_pairs={{0,256},{128,384},{256,0},{384,128},{1,257},{129,385},{257,1},{385... | collective-permute-start | bytes 1572872 | tf_op jit(solution)/shard_map/ppermute | solution.py:324
  112.0 18.7 %collective-permute-start.15 = (f16[8,16,16,128]{3,2,1,0:T(8,128)(2,1)S(1)}, f16[8,16,16,128]{3,2,1,0:T(8,128)(2,1)S(1)}, u32[]{:S(2)}, u32[]{:S(2)}) collective-permute-start(f16[8,16,16,128]{3,2,1,0:T(8,128)(2,1)S(1)} %add_convert_fusion.1), channel_id=1, source_target_pairs={{0,64},{2,66},{4,68},{6,70},{8,72},{10,74},{12,76},{14,78},{16,80}... | collective-permute-start | bytes 1572872 | tf_op jit(solution)/shard_map/ppermute | solution.py:372
  130.7 9.9 %copy-start.18 = (s32[16,3]{0,1:T(4,128)S(1)}, s32[16,3]{0,1:T(4,128)}, u32[]{:S(2)}) copy-start(s32[16,3]{0,1:T(4,128)} %param.14) | copy-start | bytes 580
  130.7 9.9 %copy-start.19 = (f32[128]{0:T(128)S(1)}, f32[128]{0:T(128)}, u32[]{:S(2)}) copy-start(f32[128]{0:T(128)} %param.21) | copy-start | bytes 1540
  130.7 10.1 %copy-start.4 = (bf16[16,16,128]{2,1,0:T(8,128)(2,1)S(1)}, bf16[16,16,128]{2,1,0:T(8,128)(2,1)}, u32[]{:S(2)}) copy-start(bf16[16,16,128]{2,1,0:T(8,128)(2,1)} %refs_7_) | copy-start | bytes 196612
  130.7 10.1 %copy-start.17 = (bf16[64,64]{1,0:T(8,128)(2,1)S(1)}, bf16[64,64]{1,0:T(8,128)(2,1)}, u32[]{:S(2)}) copy-start(bf16[64,64]{1,0:T(8,128)(2,1)} %param.17) | copy-start | bytes 24580
  131.8 22.1 %all-to-all-start.1 = ((f16[8,16,16,128]{3,2,1,0:T(8,128)(2,1)}), f16[8,16,16,128]{3,2,1,0:T(8,128)(2,1)S(1)}, u32[]{:S(2)}, u32[]{:S(2)}) async-start(f16[8,16,16,128]{3,2,1,0:T(8,128)(2,1)} %add_convert_fusion), calls=%async_computation.1 | async-start | bytes 1048576 | tf_op jit(solution)/shard_map/all_to_all | solution.py:374

commit v10 on v9

--- a/solution.py
+++ b/solution.py
@@ -13,6 +13,7 @@
 LINK = jnp.float16
 VMEM = pl.BlockSpec(memory_space=pltpu.VMEM)
 SMEM = pl.BlockSpec(memory_space=pltpu.SMEM)
+HBM = pl.BlockSpec(memory_space=pltpu.HBM)
 
 
 def doubled(matrices):
@@ -26,12 +27,14 @@
     width = parts.shape[-1] // 2
     return jnp.concatenate([parts[..., width:], -parts[..., :width]], axis=-1)
 
+
 RINGS = 8
 CAP = 3
 LOT = 4
 SPAN = 2 * CAP * RINGS
-FAR = ((4, 0), (3, -1), (-3, 1))
-NEAR = ((0, 0), (1, 1), (2, 2), (-1, -1), (-2, -2))
+SENDS = ((1, (-3, 1)), (-1, (3, -1)), (2, (2,)), (-2, (-2,)), (0, (4, 0)))
+FAR = tuple((n, group.index((step + 4) % 8 - 8 * ((step + 4) % 8 > 4)), step) for n, (step, group) in enumerate(SENDS) if len(group) == 2)
+NEAR = tuple((n, group.index(step), step) for n, (step, group) in enumerate(SENDS))
 SIBLING = [(i, i ^ 1) for i in range(2 * RINGS * RINGS)]
 
 
@@ -50,41 +53,61 @@
 
 
 def pick_kernel(spot_ref, own_slot, sib_slot, own_ref, sib_hbm, *refs):
-    out_refs, (sib_ref, sem) = refs[:-2], refs[-2:]
+    out_refs, (sib_ref, held, sem, sems) = refs[:-4], refs[-4:]
     copy = pltpu.make_async_copy(sib_hbm, sib_ref, sem)
     copy.start()
     core, along = spot_ref[0], spot_ref[1]
     far = jnp.where(core == 0, 16, 2)
     near = jnp.where(core == 0, 2, 16)
     count = own_slot.shape[0] // CAP
-    for kind, (slots, store) in enumerate(((own_slot, own_ref), (sib_slot, sib_ref))):
-        if kind == 1:
-            copy.wait()
-        for (ahead, _), out_ref in zip(FAR + NEAR, out_refs, strict=True):
-            first = lax.rem(along + ahead + RINGS, RINGS) * far + core
-            for c in range(CAP):
-                for r in range(RINGS):
-                    slot = slots[c * count + first + r * near]
-                    out_ref[kind * CAP * RINGS + c * RINGS + r] = store[jnp.maximum(slot, 0)]
+
+    def fill(ahead, place, kind):
+        slots, store = ((own_slot, own_ref), (sib_slot, sib_ref))[kind]
+        first = lax.rem(along + ahead + RINGS, RINGS) * far + core
+        for c in range(CAP):
+            for r in range(RINGS):
+                slot = slots[c * count + first + r * near]
+                held[place * SPAN + kind * CAP * RINGS + c * RINGS + r] = store[jnp.maximum(slot, 0)]
+
+    aheads = [ahead for _, group in SENDS for ahead in group]
+    for place, ahead in enumerate(aheads):
+        fill(ahead, place, 0)
+    copy.wait()
+    copies, place = [], 0
+    for n, ((_, group), out_ref) in enumerate(zip(SENDS, out_refs, strict=True)):
+        for ahead in group:
+            fill(ahead, place, 1)
+            place += 1
+        begin = (place - len(group)) * SPAN
+        copies.append(pltpu.make_async_copy(held.at[pl.ds(begin, len(group) * SPAN)], out_ref, sems.at[n]))
+        copies[-1].start()
+    for copy in copies:
+        copy.wait()
 
 
 def pick(spot, own_slots, sib_slots, own, sib):
-    shape = jax.ShapeDtypeStruct((SPAN,) + own.shape[1:], own.dtype)
+    tile = own.shape[1:]
+    total = sum(len(group) for _, group in SENDS)
     return pl.pallas_call(
         pick_kernel,
-        in_specs=[SMEM, SMEM, SMEM, VMEM, pl.BlockSpec(memory_space=pl.ANY)],
-        out_specs=[VMEM] * len(FAR + NEAR),
-        out_shape=[shape] * len(FAR + NEAR),
-        scratch_shapes=[pltpu.VMEM(own.shape, own.dtype), pltpu.SemaphoreType.DMA],
+        in_specs=[SMEM, SMEM, SMEM, VMEM, HBM],
+        out_specs=[HBM] * len(SENDS),
+        out_shape=[pltpu.HBM((len(group) * SPAN,) + tile, own.dtype) for _, group in SENDS],
+        scratch_shapes=[
+            pltpu.VMEM(own.shape, own.dtype),
+            pltpu.VMEM((total * SPAN,) + tile, own.dtype),
+            pltpu.SemaphoreType.DMA,
+            pltpu.SemaphoreType.DMA((len(SENDS),)),
+        ],
         compiler_params=pltpu.CompilerParams(vmem_limit_bytes=24 * 2**20),
         cost_estimate=pl.CostEstimate(flops=0, bytes_accessed=10 * 2**20, transcendentals=0),
     )(spot, own_slots, sib_slots, own, sib)
 
 
 def terms_kernel(sources, modes, windows, part, spot_ref, list_ref, re_ref, im_ref, *refs):
-    flat_refs = refs[:sources]
-    wide_ref, ham_ref, rho_ref = refs[sources:sources + 3]
-    out_refs, (flat, acc, sems) = refs[sources + 3:-3], refs[-3:]
+    count = len(sources)
+    state_refs, (wide_ref, ham_ref, rho_ref) = refs[:count], refs[count:count + 3]
+    out_refs, (flat, acc, sems) = refs[count + 3:-3], refs[-3:]
     here, group = spot_ref[2], spot_ref[3]
     share = rho_ref.shape[1]
     width = ham_ref.shape[0]
@@ -95,7 +118,10 @@
     downs, extra, counts = modes, modes + CAP + slot * levels, list_ref.shape[0] - 1
 
     copies = [
-        pltpu.make_async_copy(ref, flat.at[pl.ds(n * SPAN, SPAN)], sems.at[n]) for n, ref in enumerate(flat_refs)
+        pltpu.make_async_copy(
+            state_refs[n].at[pl.ds(place * SPAN, SPAN)], flat.at[pl.ds(n * SPAN, SPAN)], sems.at[n]
+        )
+        for n, (_, place, _) in enumerate(sources)
     ]
     for copy in copies:
         copy.start()
@@ -160,7 +186,7 @@
 
     lax.fori_loop(0, CAP, lower, 0)
 
-    if sources == len(NEAR):
+    if sources is NEAR:
 
         for w in range(windows):
             acc[here * windows + w] += rotate(
@@ -177,23 +203,23 @@
     lax.fori_loop(begin, end, leave, 0)
 
 
-def terms(part, spot, lists, coup_re, coup_im, pieces, maps_wide, head_cols, rho):
+def terms(sources, part, spot, lists, coup_re, coup_im, states, maps_wide, head_cols, rho):
     modes = maps_wide.shape[0] - 1
     windows, share, lanes = rho.shape
     width = head_cols.shape[0]
     return pl.pallas_call(
-        functools.partial(terms_kernel, len(pieces), modes, windows, part),
-        in_specs=[SMEM] * 4 + [pl.BlockSpec(memory_space=pl.ANY)] * len(pieces) + [VMEM] * 3,
+        functools.partial(terms_kernel, sources, modes, windows, part),
+        in_specs=[SMEM] * 4 + [HBM] * len(sources) + [VMEM] * 3,
         out_specs=[VMEM] * (width // share),
         out_shape=[jax.ShapeDtypeStruct((part[1] - part[0], windows, share, lanes), F32)] * (width // share),
         scratch_shapes=[
-            pltpu.VMEM((len(pieces) * SPAN, width, lanes), BF16),
+            pltpu.VMEM((len(sources) * SPAN, width, lanes), BF16),
             pltpu.VMEM((RINGS * windows + 1, width, lanes), F32),
-            pltpu.SemaphoreType.DMA((len(pieces),)),
+            pltpu.SemaphoreType.DMA((len(sources),)),
         ],
         compiler_params=pltpu.CompilerParams(vmem_limit_bytes=28 * 2**20),
         cost_estimate=pl.CostEstimate(flops=10**9, bytes_accessed=10 * 2**20, transcendentals=0),
-    )(spot, lists, coup_re, coup_im, *pieces, maps_wide, head_cols, rho)
+    )(spot, lists, coup_re, coup_im, *[states[n] for n, _, _ in sources], maps_wide, head_cols, rho)
 
 
 def lists_of(steps, parts, modes, spot_ref, heard_ref, out_ref):
@@ -206,7 +232,7 @@
         z, y, c = lax.shift_right_logical(owner, 4), lax.shift_right_logical(owner, 1) & 7, owner & 1
         off = (jnp.where(core == 0, z, y) - along) & (RINGS - 1)
         source = jnp.full_like(off, -1)
-        for n, (_, step) in enumerate(steps):
+        for n, (_, _, step) in enumerate(steps):
             source = jnp.where(off == -step % RINGS, n, source)
         mine = (jnp.where(core == 0, y, z) == across) & (source >= 0)
         kind = jnp.where(c == core, 0, 1)
@@ -343,6 +369,7 @@
     slots = jnp.transpose(send_slot[0, 0]).reshape(-1)
     sib_store = lax.ppermute(states[0, 0], "ado", SIBLING)
     sib_slots = lax.ppermute(slots, "ado", SIBLING)
+    slots, use_up = lax.optimization_barrier((slots, use_up))
     said = say(spot, use_up, use_down, modes_tri)
     said = jnp.concatenate([said, lax.ppermute(said, "ado", onward(4))], axis=0)
     heard = lax.all_to_all(
@@ -355,22 +382,18 @@
     shared = (maps_wide, head_cols, window_tier_states)
     picked, heard, shared = lax.optimization_barrier((picked, heard, shared))
 
-    def send(steps, blocks):
-        return [
-            block if step == 0 else lax.ppermute(block, "ado", onward(step))
-            for (_, step), block in zip(steps, blocks, strict=True)
-        ]
-
-    far_states = send(FAR, picked[:len(FAR)])
-    near_states = send(NEAR, picked[len(FAR):])
+    sent = [
+        block if step == 0 else lax.ppermute(block, "ado", onward(step))
+        for (step, _), block in zip(SENDS, picked, strict=True)
+    ]
     kinds = ((FAR, ((0, RINGS),), 1), (NEAR, ((0, RINGS),), 0))
     far_lists, near_lists = use_lists(kinds, modes, spot, heard)
 
-    far = terms((0, RINGS, 0), spot, far_lists, coup_re, coup_im, far_states, *shared)
+    far = terms(FAR, (0, RINGS, 0), spot, far_lists, coup_re, coup_im, sent, *shared)
     far, near_lists = lax.optimization_barrier((far, near_lists))
     far = over_groups(far)
     far = lax.ppermute(far.astype(LINK), "ado", onward(4))
-    near = over_groups(terms((0, RINGS, 0), spot, near_lists, coup_re, coup_im, near_states, *shared))
+    near = over_groups(terms(NEAR, (0, RINGS, 0), spot, near_lists, coup_re, coup_im, sent, *shared))
     summed = lax.all_to_all(
         (near + far.astype(F32)).astype(LINK), "ado", split_axis=0, concat_axis=0,
         tiled=True, axis_index_groups=DELIVER,

time: 156 us -> 159 us (1.019)
  the two profiles are of different devices: /device:TPU:66 before, /device:TPU:2 now
where the time goes in v10:
time: 159 us; the launch traced here: 158 us
  starting transfers between devices  70.2 us (44%)
  waiting for transfers between devices  51.4 us (32%)
  Pallas kernels  25.7 us (16%)
  other arithmetic  5.92 us (4%)
  local copies, waits for them, and re-layouts  3.92 us (2%)
    ppermute x6, starting transfers between devices, over_groups(): lax.ppermute(parts[shift].astype(LINK), 'grp', ring).astype(F32)  20.4 us
    pallas_call x2, Pallas kernels, terms(): pl.pallas_call(functools.partial(terms_kernel, sources, modes, windows, p...  17.8 us
    ppermute x4, starting transfers between devices, on_device(): lax.ppermute(block, 'ado', onward(step))  17.7 us
    ppermute x4, waiting for transfers between devices, on_device(): lax.ppermute(block, 'ado', onward(step))  17.4 us
    all_to_all x1, waiting for transfers between devices, on_device(): lax.all_to_all((near + far.astype(F32)).astype(LINK), 'ado', split_axis=0...  12.8 us
    ppermute x1, starting transfers between devices, on_device(): said = jnp.concatenate([said, lax.ppermute(said, 'ado', onward(4))], axis=0)  10.9 us
    ppermute x1, waiting for transfers between devices, on_device(): far = lax.ppermute(far.astype(LINK), 'ado', onward(4))  10.2 us
    all_to_all x1, starting transfers between devices, on_device(): lax.all_to_all(jnp.broadcast_to(said, (RINGS,) + said.shape), 'ado', spli...  7.23 us
  transfers between devices with their start and end apart: 16, of which 7 were waited for; matrix products, arithmetic and copies ran while one was open for 4% of the time, Pallas kernels for 16%

profile of v10, /device:TPU:2, one launch (start us, length us, event | category | flops | bytes accessed | tf_op | source)
XLA Modules:
  0.0 157.7 jit_solution(612585971268730063)
XLA Ops:
  0.0 2.0 %collective-permute-start.1 = (bf16[128,64,128]{2,1,0:T(8,128)(2,1)}, bf16[128,64,128]{2,1,0:T(8,128)(2,1)}, u32[]{:S(2)}, u32[]{:S(2)}) collective-permute-start(bf16[128,64,128]{2,1,0:T(8,128)(2,1)} %bitcast.20), channel_id=1, source_target_pairs={{0,1},{1,0},{2,3},{3,2},{4,5},{5,4},{6,7},{7,6},{8,9},{9,8},{10,11... | collective-permute-start | bytes 6291464 | tf_op jit(solution)/shard_map/ppermute | solution.py:370
  2.1 0.7 copy.15
  2.8 0.6 pad_add_fusion.1.spot_ref
  3.3 1.6 %shard_map.110 = s32[40,128]{1,0:T(8,128)} custom-call(s32[4]{0:T(128)} %pad_add_fusion.1.spot_ref, s32[16,32]{1,0:T(8,128)} %up_ref, s32[3,16]{1,0:T(4,128)} %bitcast.25, s32[3,16]{1,0:T(4,128)} %bitcast.24), custom_call_target="tpu_custom_call" | custom-call | flops 1000000 | bytes 262144 | tf_op jit(solution)/shard_map/pallas_call | solution.py:336
  4.9 10.9 %collective-permute-start.2 = (s32[40,128]{1,0:T(8,128)}, s32[40,128]{1,0:T(8,128)S(1)}, u32[]{:S(2)}, u32[]{:S(2)}) collective-permute-start(s32[40,128]{1,0:T(8,128)} %shard_map.110), channel_id=1, source_target_pairs={{0,64},{2,66},{4,68},{6,70},{8,72},{10,74},{12,76},{14,78},{16,80}... | collective-permute-start | bytes 61448 | tf_op jit(solution)/shard_map/ppermute | solution.py:374
  15.8 2.0 %collective-permute-done.2 = s32[40,128]{1,0:T(8,128)S(1)} collective-permute-done((s32[40,128]{1,0:T(8,128)}, s32[40,128]{1,0:T(8,128)S(1)}, u32[]{:S(2)}, u32[]{:S(2)}) %collective-permute-start.2) | collective-permute-done | bytes 20512 | tf_op jit(solution)/shard_map/ppermute | solution.py:374
  17.8 0.7 pad_add_fusion
  18.6 0.8 broadcast_in_dim.10
  19.3 7.2 %all-to-all-start = ((s32[8,80,128]{2,1,0:T(8,128)}), s32[8,80,128]{2,1,0:T(8,128)S(1)}, u32[]{:S(2)}, u32[]{:S(2)}) async-start(s32[8,80,128]{2,1,0:T(8,128)} %broadcast_in_dim.10), calls=%async_computation | async-start | bytes 655360 | tf_op jit(solution)/shard_map/all_to_all | solution.py:375
  26.6 1.9 %collective-permute-start = (s32[384]{0:T(512)S(1)}, s32[384]{0:T(512)S(1)}, u32[]{:S(2)}, u32[]{:S(2)}) collective-permute-start(s32[384]{0:T(512)S(1)} %bitcast.22), channel_id=1, source_target_pairs={{0,1},{1,0},{2,3},{3,2},{4,5},{5,4},{6,7},{7,6},{8,9},{9,8},{10,11... | collective-permute-start | bytes 4616 | tf_op jit(solution)/shard_map/ppermute | solution.py:371
  28.5 1.5 fusion.2
  30.0 0.1 constant_dynamic-slice_fusion.refs_4_.refs_6_
  30.1 0.1 concatenate.31.refs_3_.refs_5_
  30.3 5.0 %shard_map.109 = (bf16[96,64,128]{2,1,0:T(8,128)(2,1)}, bf16[96,64,128]{2,1,0:T(8,128)(2,1)}, bf16[48,64,128]{2,1,0:T(8,128)(2,1)}, bf16[48,64,128]{2,1,0:T(8,128)(2,1)}, bf16[96,64,128]{2,1,0:T(8,128)(2,1)}) custom-call(s32[4]{0:T(128)S(1)} %copy-done.4, s32[384]{0:T(512)S(1)} %bitcast.23, s32[384]{0:T(512)S(1)} %collective-permute-done.sib_slot, ...), custom_call_target="tpu_custom_call" | custom-call | bytes 10485760 | tf_op jit(solution)/shard_map/pallas_call | solution.py:91
  35.3 2.5 %all-to-all-done.heard_ref = s32[8,80,128]{2,1,0:T(8,128)S(1)} async-done(((s32[8,80,128]{2,1,0:T(8,128)}), s32[8,80,128]{2,1,0:T(8,128)S(1)}, u32[]{:S(2)}, u32[]{:S(2)}) %all-to-all-start) | async-done | bytes 327712 | tf_op jit(solution)/shard_map/all_to_all | solution.py:375
  37.8 3.4 %collective-permute-start.3 = (bf16[96,64,128]{2,1,0:T(8,128)(2,1)}, bf16[96,64,128]{2,1,0:T(8,128)(2,1)S(1)}, u32[]{:S(2)}, u32[]{:S(2)}) collective-permute-start(bf16[96,64,128]{2,1,0:T(8,128)(2,1)} %get-tuple-element.45), channel_id=1, source_target_pairs={{0,16},{2,18},{4,20},{6,22},{8,24},{10,26},{12,28},{14,30},{16,32}... | collective-permute-start | bytes 4718600 | tf_op jit(solution)/shard_map/ppermute | solution.py:386
  41.1 6.4 %collective-permute-start.4 = (bf16[96,64,128]{2,1,0:T(8,128)(2,1)}, bf16[96,64,128]{2,1,0:T(8,128)(2,1)S(1)}, u32[]{:S(2)}, u32[]{:S(2)}) collective-permute-start(bf16[96,64,128]{2,1,0:T(8,128)(2,1)} %get-tuple-element.46), channel_id=1, source_target_pairs={{0,112},{2,114},{4,116},{6,118},{8,120},{10,122},{12,124},{14,126}... | collective-permute-start | bytes 4718600 | tf_op jit(solution)/shard_map/ppermute | solution.py:386
  47.5 1.9 %collective-permute-start.5 = (bf16[48,64,128]{2,1,0:T(8,128)(2,1)}, bf16[48,64,128]{2,1,0:T(8,128)(2,1)S(1)}, u32[]{:S(2)}, u32[]{:S(2)}) collective-permute-start(bf16[48,64,128]{2,1,0:T(8,128)(2,1)} %get-tuple-element.57), channel_id=1, source_target_pairs={{0,32},{2,34},{4,36},{6,38},{8,40},{10,42},{12,44},{14,46},{16,48}... | collective-permute-start | bytes 2359304 | tf_op jit(solution)/shard_map/ppermute | solution.py:386
  49.5 6.0 %collective-permute-start.6 = (bf16[48,64,128]{2,1,0:T(8,128)(2,1)}, bf16[48,64,128]{2,1,0:T(8,128)(2,1)S(1)}, u32[]{:S(2)}, u32[]{:S(2)}) collective-permute-start(bf16[48,64,128]{2,1,0:T(8,128)(2,1)} %get-tuple-element.58), channel_id=1, source_target_pairs={{0,96},{2,98},{4,100},{6,102},{8,104},{10,106},{12,108},{14,110},{... | collective-permute-start | bytes 2359304 | tf_op jit(solution)/shard_map/ppermute | solution.py:386
  55.5 1.3 shard_map.111
  56.8 7.4 %collective-permute-done.3.refs_0_ = bf16[96,64,128]{2,1,0:T(8,128)(2,1)S(1)} collective-permute-done((bf16[96,64,128]{2,1,0:T(8,128)(2,1)}, bf16[96,64,128]{2,1,0:T(8,128)(2,1)S(1)}, u32[]{:S(2)}, u32[]{:S(2)}) %collective-permute-start.3) | collective-permute-done | bytes 1572896 | tf_op jit(solution)/shard_map/ppermute | solution.py:386
  64.2 10.0 %collective-permute-done.4.refs_1_ = bf16[96,64,128]{2,1,0:T(8,128)(2,1)S(1)} collective-permute-done((bf16[96,64,128]{2,1,0:T(8,128)(2,1)}, bf16[96,64,128]{2,1,0:T(8,128)(2,1)S(1)}, u32[]{:S(2)}, u32[]{:S(2)}) %collective-permute-start.4) | collective-permute-done | bytes 1572896 | tf_op jit(solution)/shard_map/ppermute | solution.py:386
  74.2 1.4 copy-done
  75.6 0.8 copy-done.2
  76.5 7.6 %shard_map.112 = (f32[8,16,16,128]{3,2,1,0:T(8,128)S(1)}, f32[8,16,16,128]{3,2,1,0:T(8,128)S(1)}, f32[8,16,16,128]{3,2,1,0:T(8,128)S(1)}, f32[8,16,16,128]{3,2,1,0:T(8,128)S(1)}) custom-call(s32[4]{0:T(128)S(1)} %copy-done.4, s32[48,128]{1,0:T(8,128)S(1)} %get-tuple-element.44.list_ref, f32[32]{0:T(128)S(1)} %copy-done.5, f32[32]{0:T(128)S(1)} %copy-done.6, ...), custom_call_target="tpu_custom_call" | custom-call | flops 1000000000 | bytes 10485760 | tf_op jit(solution)/shard_map/pallas_call | solution.py:210
  84.1 0.1 convert_element_type.61
  84.2 2.8 %collective-permute-start.12 = (f16[8,16,16,128]{3,2,1,0:T(8,128)(2,1)S(1)}, f16[8,16,16,128]{3,2,1,0:T(8,128)(2,1)S(1)}, u32[]{:S(2)}, u32[]{:S(2)}) collective-permute-start(f16[8,16,16,128]{3,2,1,0:T(8,128)(2,1)S(1)} %convert_element_type.61), channel_id=1, source_target_pairs={{0,384},{128,0},{256,128},{384,256},{1,385},{129,1},{257,129},{385... | collective-permute-start | bytes 1572872 | tf_op jit(solution)/shard_map/ppermute | solution.py:350
  87.0 0.1 convert_element_type.59
  87.1 3.1 %collective-permute-start.11 = (f16[8,16,16,128]{3,2,1,0:T(8,128)(2,1)S(1)}, f16[8,16,16,128]{3,2,1,0:T(8,128)(2,1)S(1)}, u32[]{:S(2)}, u32[]{:S(2)}) collective-permute-start(f16[8,16,16,128]{3,2,1,0:T(8,128)(2,1)S(1)} %convert_element_type.59), channel_id=1, source_target_pairs={{0,128},{128,256},{256,384},{384,0},{1,129},{129,257},{257,385},{3... | collective-permute-start | bytes 1572872 | tf_op jit(solution)/shard_map/ppermute | solution.py:350
  90.1 0.1 convert_element_type.57
  90.2 5.6 %collective-permute-start.10 = (f16[8,16,16,128]{3,2,1,0:T(8,128)(2,1)S(1)}, f16[8,16,16,128]{3,2,1,0:T(8,128)(2,1)S(1)}, u32[]{:S(2)}, u32[]{:S(2)}) collective-permute-start(f16[8,16,16,128]{3,2,1,0:T(8,128)(2,1)S(1)} %convert_element_type.57), channel_id=1, source_target_pairs={{0,256},{128,384},{256,0},{384,128},{1,257},{129,385},{257,1},{385... | collective-permute-start | bytes 1572872 | tf_op jit(solution)/shard_map/ppermute | solution.py:350
  95.8 10.2 %shard_map.113 = (f32[8,16,16,128]{3,2,1,0:T(8,128)S(1)}, f32[8,16,16,128]{3,2,1,0:T(8,128)S(1)}, f32[8,16,16,128]{3,2,1,0:T(8,128)S(1)}, f32[8,16,16,128]{3,2,1,0:T(8,128)S(1)}) custom-call(s32[4]{0:T(128)S(1)} %copy-done.4, s32[48,128]{1,0:T(8,128)S(1)} %get-tuple-element.56.list_ref, f32[32]{0:T(128)S(1)} %copy-done.5, f32[32]{0:T(128)S(1)} %copy-done.6, ...), custom_call_target="tpu_custom_call" | custom-call | flops 1000000000 | bytes 10485760 | tf_op jit(solution)/shard_map/pallas_call | solution.py:210
  106.0 0.1 convert_element_type.55
  106.1 2.1 %collective-permute-start.9 = (f16[8,16,16,128]{3,2,1,0:T(8,128)(2,1)S(1)}, f16[8,16,16,128]{3,2,1,0:T(8,128)(2,1)S(1)}, u32[]{:S(2)}, u32[]{:S(2)}) collective-permute-start(f16[8,16,16,128]{3,2,1,0:T(8,128)(2,1)S(1)} %convert_element_type.55), channel_id=1, source_target_pairs={{0,384},{128,0},{256,128},{384,256},{1,385},{129,1},{257,129},{385... | collective-permute-start | bytes 1572872 | tf_op jit(solution)/shard_map/ppermute | solution.py:350
  108.2 0.1 convert_element_type.53
  108.2 3.8 %collective-permute-start.8 = (f16[8,16,16,128]{3,2,1,0:T(8,128)(2,1)S(1)}, f16[8,16,16,128]{3,2,1,0:T(8,128)(2,1)S(1)}, u32[]{:S(2)}, u32[]{:S(2)}) collective-permute-start(f16[8,16,16,128]{3,2,1,0:T(8,128)(2,1)S(1)} %convert_element_type.53), channel_id=1, source_target_pairs={{0,128},{128,256},{256,384},{384,0},{1,129},{129,257},{257,385},{3... | collective-permute-start | bytes 1572872 | tf_op jit(solution)/shard_map/ppermute | solution.py:350
  112.1 3.1 %collective-permute-start.7 = (f16[8,16,16,128]{3,2,1,0:T(8,128)(2,1)S(1)}, f16[8,16,16,128]{3,2,1,0:T(8,128)(2,1)S(1)}, u32[]{:S(2)}, u32[]{:S(2)}) collective-permute-start(f16[8,16,16,128]{3,2,1,0:T(8,128)(2,1)S(1)} %convert_element_type.51), channel_id=1, source_target_pairs={{0,256},{128,384},{256,0},{384,128},{1,257},{129,385},{257,1},{385... | collective-permute-start | bytes 1572872 | tf_op jit(solution)/shard_map/ppermute | solution.py:350
  115.3 0.3 add_convert_fusion.1
  115.6 3.4 %collective-permute-start.13 = (f16[8,16,16,128]{3,2,1,0:T(8,128)(2,1)S(1)}, f16[8,16,16,128]{3,2,1,0:T(8,128)(2,1)S(1)}, u32[]{:S(2)}, u32[]{:S(2)}) collective-permute-start(f16[8,16,16,128]{3,2,1,0:T(8,128)(2,1)S(1)} %add_convert_fusion.1), channel_id=1, source_target_pairs={{0,64},{2,66},{4,68},{6,70},{8,72},{10,74},{12,76},{14,78},{16,80}... | collective-permute-start | bytes 1572872 | tf_op jit(solution)/shard_map/ppermute | solution.py:395
  118.9 6.5 %collective-permute-done.9 = f16[8,16,16,128]{3,2,1,0:T(8,128)(2,1)S(1)} collective-permute-done((f16[8,16,16,128]{3,2,1,0:T(8,128)(2,1)S(1)}, f16[8,16,16,128]{3,2,1,0:T(8,128)(2,1)S(1)}, u32[]{:S(2)}, u32[]{:S(2)}) %collective-permute-start.9) | collective-permute-done | bytes 524320 | tf_op jit(solution)/shard_map/ppermute | solution.py:350
  125.5 10.2 %collective-permute-done.13 = f16[8,16,16,128]{3,2,1,0:T(8,128)(2,1)S(1)} collective-permute-done((f16[8,16,16,128]{3,2,1,0:T(8,128)(2,1)S(1)}, f16[8,16,16,128]{3,2,1,0:T(8,128)(2,1)S(1)}, u32[]{:S(2)}, u32[]{:S(2)}) %collective-permute-start.13) | collective-permute-done | bytes 524320 | tf_op jit(solution)/shard_map/ppermute | solution.py:395
  135.7 1.2 add_convert_fusion
  136.9 6.7 %all-to-all-start.1 = ((f16[8,16,16,128]{3,2,1,0:T(8,128)(2,1)}), f16[8,16,16,128]{3,2,1,0:T(8,128)(2,1)S(1)}, u32[]{:S(2)}, u32[]{:S(2)}) async-start(f16[8,16,16,128]{3,2,1,0:T(8,128)(2,1)} %add_convert_fusion), calls=%async_computation.1 | async-start | bytes 1048576 | tf_op jit(solution)/shard_map/all_to_all | solution.py:397
  143.6 0.2 select_reduce_fusion
  143.8 0.2 convolution_bitcast_fusion
  144.0 0.1 fusion.18
  144.1 12.8 %all-to-all-done.1 = f16[8,16,16,128]{3,2,1,0:T(8,128)(2,1)S(1)} async-done(((f16[8,16,16,128]{3,2,1,0:T(8,128)(2,1)}), f16[8,16,16,128]{3,2,1,0:T(8,128)(2,1)S(1)}, u32[]{:S(2)}, u32[]{:S(2)}) %all-to-all-start.1) | async-done | bytes 524320 | tf_op jit(solution)/shard_map/all_to_all | solution.py:397
  156.9 0.8 fusion.4
  (31 shorter events, 0.2 us)
Async XLA Ops:
  0.0 30.0 %copy-start.7 = (bf16[64,64]{1,0:T(8,128)(2,1)S(1)}, bf16[64,64]{1,0:T(8,128)(2,1)}, u32[]{:S(2)}) copy-start(bf16[64,64]{1,0:T(8,128)(2,1)} %param.17) | copy-start | bytes 24580
  0.0 30.3 %collective-permute-start.1 = (bf16[128,64,128]{2,1,0:T(8,128)(2,1)}, bf16[128,64,128]{2,1,0:T(8,128)(2,1)}, u32[]{:S(2)}, u32[]{:S(2)}) collective-permute-start(bf16[128,64,128]{2,1,0:T(8,128)(2,1)} %bitcast.20), channel_id=1, source_target_pairs={{0,1},{1,0},{2,3},{3,2},{4,5},{5,4},{6,7},{7,6},{8,9},{9,8},{10,11... | collective-permute-start | bytes 6291464 | tf_op jit(solution)/shard_map/ppermute | solution.py:370
  4.9 12.9 %collective-permute-start.2 = (s32[40,128]{1,0:T(8,128)}, s32[40,128]{1,0:T(8,128)S(1)}, u32[]{:S(2)}, u32[]{:S(2)}) collective-permute-start(s32[40,128]{1,0:T(8,128)} %shard_map.110), channel_id=1, source_target_pairs={{0,64},{2,66},{4,68},{6,70},{8,72},{10,74},{12,76},{14,78},{16,80}... | collective-permute-start | bytes 61448 | tf_op jit(solution)/shard_map/ppermute | solution.py:374
  19.3 10.9 %copy-start.1 = (bf16[1,1,128,64,128]{4,3,2,1,0:T(8,128)(2,1)S(1)}, bf16[1,1,128,64,128]{4,3,2,1,0:T(8,128)(2,1)}, u32[]{:S(2)}) copy-start(bf16[1,1,128,64,128]{4,3,2,1,0:T(8,128)(2,1)} %param.11) | copy-start | bytes 6291460
  19.3 10.9 %copy-start.4 = (s32[4]{0:T(128)S(1)}, s32[4]{0:T(128)}, u32[]{:S(2)}) copy-start(s32[4]{0:T(128)} %pad_add_fusion.1.spot_ref) | copy-start | bytes 52
  19.3 18.4 %all-to-all-start = ((s32[8,80,128]{2,1,0:T(8,128)}), s32[8,80,128]{2,1,0:T(8,128)S(1)}, u32[]{:S(2)}, u32[]{:S(2)}) async-start(s32[8,80,128]{2,1,0:T(8,128)} %broadcast_in_dim.10), calls=%async_computation | async-start | bytes 655360 | tf_op jit(solution)/shard_map/all_to_all | solution.py:375
  26.6 3.7 %collective-permute-start = (s32[384]{0:T(512)S(1)}, s32[384]{0:T(512)S(1)}, u32[]{:S(2)}, u32[]{:S(2)}) collective-permute-start(s32[384]{0:T(512)S(1)} %bitcast.22), channel_id=1, source_target_pairs={{0,1},{1,0},{2,3},{3,2},{4,5},{5,4},{6,7},{7,6},{8,9},{9,8},{10,11... | collective-permute-start | bytes 4616 | tf_op jit(solution)/shard_map/ppermute | solution.py:371
  30.2 44.0 %copy-start.5 = (f32[32]{0:T(128)S(1)}, f32[32]{0:T(128)}, u32[]{:S(2)}) copy-start(f32[32]{0:T(128)} %re_ref.3) | copy-start | bytes 388
  30.2 44.0 %copy-start.6 = (f32[32]{0:T(128)S(1)}, f32[32]{0:T(128)}, u32[]{:S(2)}) copy-start(f32[32]{0:T(128)} %im_ref.3) | copy-start | bytes 388
  37.8 26.4 %collective-permute-start.3 = (bf16[96,64,128]{2,1,0:T(8,128)(2,1)}, bf16[96,64,128]{2,1,0:T(8,128)(2,1)S(1)}, u32[]{:S(2)}, u32[]{:S(2)}) collective-permute-start(bf16[96,64,128]{2,1,0:T(8,128)(2,1)} %get-tuple-element.45), channel_id=1, source_target_pairs={{0,16},{2,18},{4,20},{6,22},{8,24},{10,26},{12,28},{14,30},{16,32}... | collective-permute-start | bytes 4718600 | tf_op jit(solution)/shard_map/ppermute | solution.py:386
  41.1 33.1 %collective-permute-start.4 = (bf16[96,64,128]{2,1,0:T(8,128)(2,1)}, bf16[96,64,128]{2,1,0:T(8,128)(2,1)S(1)}, u32[]{:S(2)}, u32[]{:S(2)}) collective-permute-start(bf16[96,64,128]{2,1,0:T(8,128)(2,1)} %get-tuple-element.46), channel_id=1, source_target_pairs={{0,112},{2,114},{4,116},{6,118},{8,120},{10,122},{12,124},{14,126}... | collective-permute-start | bytes 4718600 | tf_op jit(solution)/shard_map/ppermute | solution.py:386
  47.5 48.3 %collective-permute-start.5 = (bf16[48,64,128]{2,1,0:T(8,128)(2,1)}, bf16[48,64,128]{2,1,0:T(8,128)(2,1)S(1)}, u32[]{:S(2)}, u32[]{:S(2)}) collective-permute-start(bf16[48,64,128]{2,1,0:T(8,128)(2,1)} %get-tuple-element.57), channel_id=1, source_target_pairs={{0,32},{2,34},{4,36},{6,38},{8,40},{10,42},{12,44},{14,46},{16,48}... | collective-permute-start | bytes 2359304 | tf_op jit(solution)/shard_map/ppermute | solution.py:386
  49.5 46.3 %collective-permute-start.6 = (bf16[48,64,128]{2,1,0:T(8,128)(2,1)}, bf16[48,64,128]{2,1,0:T(8,128)(2,1)S(1)}, u32[]{:S(2)}, u32[]{:S(2)}) collective-permute-start(bf16[48,64,128]{2,1,0:T(8,128)(2,1)} %get-tuple-element.58), channel_id=1, source_target_pairs={{0,96},{2,98},{4,100},{6,102},{8,104},{10,106},{12,108},{14,110},{... | collective-permute-start | bytes 2359304 | tf_op jit(solution)/shard_map/ppermute | solution.py:386
  74.2 1.4 copy-start
  75.6 0.8 copy-start.2
  84.2 27.9 %collective-permute-start.12 = (f16[8,16,16,128]{3,2,1,0:T(8,128)(2,1)S(1)}, f16[8,16,16,128]{3,2,1,0:T(8,128)(2,1)S(1)}, u32[]{:S(2)}, u32[]{:S(2)}) collective-permute-start(f16[8,16,16,128]{3,2,1,0:T(8,128)(2,1)S(1)} %convert_element_type.61), channel_id=1, source_target_pairs={{0,384},{128,0},{256,128},{384,256},{1,385},{129,1},{257,129},{385... | collective-permute-start | bytes 1572872 | tf_op jit(solution)/shard_map/ppermute | solution.py:350
  87.1 28.2 %collective-permute-start.11 = (f16[8,16,16,128]{3,2,1,0:T(8,128)(2,1)S(1)}, f16[8,16,16,128]{3,2,1,0:T(8,128)(2,1)S(1)}, u32[]{:S(2)}, u32[]{:S(2)}) collective-permute-start(f16[8,16,16,128]{3,2,1,0:T(8,128)(2,1)S(1)} %convert_element_type.59), channel_id=1, source_target_pairs={{0,128},{128,256},{256,384},{384,0},{1,129},{129,257},{257,385},{3... | collective-permute-start | bytes 1572872 | tf_op jit(solution)/shard_map/ppermute | solution.py:350
  90.2 25.0 %collective-permute-start.10 = (f16[8,16,16,128]{3,2,1,0:T(8,128)(2,1)S(1)}, f16[8,16,16,128]{3,2,1,0:T(8,128)(2,1)S(1)}, u32[]{:S(2)}, u32[]{:S(2)}) collective-permute-start(f16[8,16,16,128]{3,2,1,0:T(8,128)(2,1)S(1)} %convert_element_type.57), channel_id=1, source_target_pairs={{0,256},{128,384},{256,0},{384,128},{1,257},{129,385},{257,1},{385... | collective-permute-start | bytes 1572872 | tf_op jit(solution)/shard_map/ppermute | solution.py:350
  106.1 19.4 %collective-permute-start.9 = (f16[8,16,16,128]{3,2,1,0:T(8,128)(2,1)S(1)}, f16[8,16,16,128]{3,2,1,0:T(8,128)(2,1)S(1)}, u32[]{:S(2)}, u32[]{:S(2)}) collective-permute-start(f16[8,16,16,128]{3,2,1,0:T(8,128)(2,1)S(1)} %convert_element_type.55), channel_id=1, source_target_pairs={{0,384},{128,0},{256,128},{384,256},{1,385},{129,1},{257,129},{385... | collective-permute-start | bytes 1572872 | tf_op jit(solution)/shard_map/ppermute | solution.py:350
  108.2 17.2 %collective-permute-start.8 = (f16[8,16,16,128]{3,2,1,0:T(8,128)(2,1)S(1)}, f16[8,16,16,128]{3,2,1,0:T(8,128)(2,1)S(1)}, u32[]{:S(2)}, u32[]{:S(2)}) collective-permute-start(f16[8,16,16,128]{3,2,1,0:T(8,128)(2,1)S(1)} %convert_element_type.53), channel_id=1, source_target_pairs={{0,128},{128,256},{256,384},{384,0},{1,129},{129,257},{257,385},{3... | collective-permute-start | bytes 1572872 | tf_op jit(solution)/shard_map/ppermute | solution.py:350
  112.1 13.4 %collective-permute-start.7 = (f16[8,16,16,128]{3,2,1,0:T(8,128)(2,1)S(1)}, f16[8,16,16,128]{3,2,1,0:T(8,128)(2,1)S(1)}, u32[]{:S(2)}, u32[]{:S(2)}) collective-permute-start(f16[8,16,16,128]{3,2,1,0:T(8,128)(2,1)S(1)} %convert_element_type.51), channel_id=1, source_target_pairs={{0,256},{128,384},{256,0},{384,128},{1,257},{129,385},{257,1},{385... | collective-permute-start | bytes 1572872 | tf_op jit(solution)/shard_map/ppermute | solution.py:350
  115.6 20.1 %collective-permute-start.13 = (f16[8,16,16,128]{3,2,1,0:T(8,128)(2,1)S(1)}, f16[8,16,16,128]{3,2,1,0:T(8,128)(2,1)S(1)}, u32[]{:S(2)}, u32[]{:S(2)}) collective-permute-start(f16[8,16,16,128]{3,2,1,0:T(8,128)(2,1)S(1)} %add_convert_fusion.1), channel_id=1, source_target_pairs={{0,64},{2,66},{4,68},{6,70},{8,72},{10,74},{12,76},{14,78},{16,80}... | collective-permute-start | bytes 1572872 | tf_op jit(solution)/shard_map/ppermute | solution.py:395
  135.7 7.9 %copy-start.9 = (s32[16,3]{0,1:T(4,128)S(1)}, s32[16,3]{0,1:T(4,128)}, u32[]{:S(2)}) copy-start(s32[16,3]{0,1:T(4,128)} %param.14) | copy-start | bytes 580
  135.7 7.9 %copy-start.10 = (f32[128]{0:T(128)S(1)}, f32[128]{0:T(128)}, u32[]{:S(2)}) copy-start(f32[128]{0:T(128)} %param.21) | copy-start | bytes 1540
  135.7 8.1 %copy-start.3 = (bf16[16,16,128]{2,1,0:T(8,128)(2,1)S(1)}, bf16[16,16,128]{2,1,0:T(8,128)(2,1)}, u32[]{:S(2)}) copy-start(bf16[16,16,128]{2,1,0:T(8,128)(2,1)} %refs_7_) | copy-start | bytes 196612
  135.7 8.1 %copy-start.8 = (bf16[64,64]{1,0:T(8,128)(2,1)S(1)}, bf16[64,64]{1,0:T(8,128)(2,1)}, u32[]{:S(2)}) copy-start(bf16[64,64]{1,0:T(8,128)(2,1)} %param.17) | copy-start | bytes 24580
  136.9 20.0 %all-to-all-start.1 = ((f16[8,16,16,128]{3,2,1,0:T(8,128)(2,1)}), f16[8,16,16,128]{3,2,1,0:T(8,128)(2,1)S(1)}, u32[]{:S(2)}, u32[]{:S(2)}) async-start(f16[8,16,16,128]{3,2,1,0:T(8,128)(2,1)} %add_convert_fusion), calls=%async_computation.1 | async-start | bytes 1048576 | tf_op jit(solution)/shard_map/all_to_all | solution.py:397

commit v11 on v10

--- a/solution.py
+++ b/solution.py
@@ -32,9 +32,9 @@
 CAP = 3
 LOT = 4
 SPAN = 2 * CAP * RINGS
-SENDS = ((1, (-3, 1)), (-1, (3, -1)), (2, (2,)), (-2, (-2,)), (0, (4, 0)))
-FAR = tuple((n, group.index((step + 4) % 8 - 8 * ((step + 4) % 8 > 4)), step) for n, (step, group) in enumerate(SENDS) if len(group) == 2)
-NEAR = tuple((n, group.index(step), step) for n, (step, group) in enumerate(SENDS))
+SENDS = ((1, (-3,)), (-1, (3,)), (1, (1,)), (-1, (-1,)), (2, (2,)), (-2, (-2,)), (0, (4, 0)))
+FAR = ((0, 0, 1), (1, 0, -1), (6, 0, 0))
+NEAR = ((2, 0, 1), (3, 0, -1), (4, 0, 2), (5, 0, -2), (6, 1, 0))
 SIBLING = [(i, i ^ 1) for i in range(2 * RINGS * RINGS)]
 
 
@@ -50,6 +50,9 @@
 
 
 DELIVER = [[device(c, a, b) for b in range(RINGS)] for c in range(2) for a in range(RINGS)]
+REDUCE = [
+    [g * 2 * RINGS * RINGS + member for g in range(4) for member in members] for members in DELIVER
+]
 
 
 def pick_kernel(spot_ref, own_slot, sib_slot, own_ref, sib_hbm, *refs):
@@ -107,8 +110,8 @@
 def terms_kernel(sources, modes, windows, part, spot_ref, list_ref, re_ref, im_ref, *refs):
     count = len(sources)
     state_refs, (wide_ref, ham_ref, rho_ref) = refs[:count], refs[count:count + 3]
-    out_refs, (flat, acc, sems) = refs[count + 3:-3], refs[-3:]
-    here, group = spot_ref[2], spot_ref[3]
+    out_ref, flat, acc, sems = refs[count + 3:]
+    here = spot_ref[2]
     share = rho_ref.shape[1]
     width = ham_ref.shape[0]
     pairs = RINGS * windows
@@ -195,9 +198,9 @@
 
     def leave(r, carry):
         for w in range(windows):
-            for shift, out_ref in enumerate(out_refs):
-                block = lax.rem(group + shift, blocks) * share
-                out_ref[r - begin, w] = acc[r * windows + w, pl.ds(pl.multiple_of(block, share), share), :]
+            value = acc[r * windows + w]
+            for b in range(blocks):
+                out_ref[b, r - begin, w] = value[b * share:(b + 1) * share]
         return carry
 
     lax.fori_loop(begin, end, leave, 0)
@@ -210,8 +213,8 @@
     return pl.pallas_call(
         functools.partial(terms_kernel, sources, modes, windows, part),
         in_specs=[SMEM] * 4 + [HBM] * len(sources) + [VMEM] * 3,
-        out_specs=[VMEM] * (width // share),
-        out_shape=[jax.ShapeDtypeStruct((part[1] - part[0], windows, share, lanes), F32)] * (width // share),
+        out_specs=VMEM,
+        out_shape=jax.ShapeDtypeStruct((width // share, part[1] - part[0], windows, share, lanes), F32),
         scratch_shapes=[
             pltpu.VMEM((len(sources) * SPAN, width, lanes), BF16),
             pltpu.VMEM((RINGS * windows + 1, width, lanes), F32),
@@ -342,13 +345,12 @@
     )(spot, use_up, use_down.T, modes_tri.T)
 
 
-def over_groups(parts):
-    count = len(parts)
-    total = parts[0]
-    for shift in (2, 1, 3):
-        ring = [(i, (i + shift) % count) for i in range(count)]
-        total = total + lax.ppermute(parts[shift].astype(LINK), "grp", ring).astype(F32)
-    return total
+def reduced(parts):
+    parts = parts.reshape((-1,) + parts.shape[2:]).astype(LINK)
+    parts = lax.all_to_all(
+        parts, ("grp", "ado"), split_axis=0, concat_axis=0, tiled=True, axis_index_groups=REDUCE
+    )
+    return jnp.sum(parts.astype(F32), axis=0)
 
 
 def on_device(
@@ -391,13 +393,8 @@
 
     far = terms(FAR, (0, RINGS, 0), spot, far_lists, coup_re, coup_im, sent, *shared)
     far, near_lists = lax.optimization_barrier((far, near_lists))
-    far = over_groups(far)
-    far = lax.ppermute(far.astype(LINK), "ado", onward(4))
-    near = over_groups(terms(NEAR, (0, RINGS, 0), spot, near_lists, coup_re, coup_im, sent, *shared))
-    summed = lax.all_to_all(
-        (near + far.astype(F32)).astype(LINK), "ado", split_axis=0, concat_axis=0,
-        tiled=True, axis_index_groups=DELIVER,
-    )
+    far = lax.ppermute(reduced(far), "ado", onward(4))
+    near = reduced(terms(NEAR, (0, RINGS, 0), spot, near_lists, coup_re, coup_im, sent, *shared))
 
     ham_wide = doubled(hamiltonian)
     right_part = jnp.einsum("wab,bc->wac", window_tier_states, ham_wide, preferred_element_type=F32)
@@ -405,7 +402,7 @@
     hits = modes_tri[:, :, None] == every_mode
     damping = jnp.sum(jnp.where(hits, decay_rate, 0.0), axis=(1, 2))
     own = rotate(right_part) + damping[:, None, None] * window_tier_states.astype(F32)
-    return STEP_WEIGHT * (jnp.sum(summed.astype(F32), axis=0) - own)
+    return STEP_WEIGHT * (near + far - own)
 
 
 def solution(mesh):

time: 159 us -> 184 us (1.16)
  the two profiles are of different devices: /device:TPU:2 before, /device:TPU:1 now
where the time goes in v11:
time: 184 us; the launch traced here: 183 us
  waiting for transfers between devices  79.2 us (43%)
  starting transfers between devices  63.8 us (35%)
  Pallas kernels  25.7 us (14%)
  other arithmetic  9.63 us (5%)
  local copies, waits for them, and re-layouts  3.89 us (2%)
    ppermute x6, waiting for transfers between devices, on_device(): lax.ppermute(block, 'ado', onward(step))  48.8 us
    all_to_all x2, waiting for transfers between devices, reduced(): lax.all_to_all(parts, ('grp', 'ado'), split_axis=0, concat_axis=0, tiled=...  23.6 us
    ppermute x6, starting transfers between devices, on_device(): lax.ppermute(block, 'ado', onward(step))  20.7 us
    all_to_all x2, starting transfers between devices, reduced(): lax.all_to_all(parts, ('grp', 'ado'), split_axis=0, concat_axis=0, tiled=...  18.3 us
    pallas_call x2, Pallas kernels, terms(): pl.pallas_call(functools.partial(terms_kernel, sources, modes, windows, p...  17.8 us
    ppermute x1, starting transfers between devices, on_device(): sib_store = lax.ppermute(states[0, 0], 'ado', SIBLING)  8.91 us
    ppermute x1, waiting for transfers between devices, on_device(): said = jnp.concatenate([said, lax.ppermute(said, 'ado', onward(4))], axis=0)  6.56 us
    ppermute x1, starting transfers between devices, on_device(): far = lax.ppermute(reduced(far), 'ado', onward(4))  5.78 us
  transfers between devices with their start and end apart: 13, of which 9 were waited for; matrix products, arithmetic and copies ran while one was open for 5% of the time, Pallas kernels for 10%

profile of v11, /device:TPU:1, one launch (start us, length us, event | category | flops | bytes accessed | tf_op | source)
XLA Modules:
  0.0 182.6 jit_solution(12060014497732157877)
XLA Ops:
  0.0 8.9 %collective-permute-start.1 = (bf16[128,64,128]{2,1,0:T(8,128)(2,1)}, bf16[128,64,128]{2,1,0:T(8,128)(2,1)}, u32[]{:S(2)}, u32[]{:S(2)}) collective-permute-start(bf16[128,64,128]{2,1,0:T(8,128)(2,1)} %bitcast.22), channel_id=1, source_target_pairs={{0,1},{1,0},{2,3},{3,2},{4,5},{5,4},{6,7},{7,6},{8,9},{9,8},{10,11... | collective-permute-start | bytes 6291464 | tf_op jit(solution)/shard_map/ppermute | solution.py:372
  8.9 0.7 copy.15
  9.6 0.6 pad_add_fusion.1.spot_ref
  10.3 1.6 shard_map.110
  11.9 2.1 %collective-permute-start.2 = (s32[40,128]{1,0:T(8,128)}, s32[40,128]{1,0:T(8,128)S(1)}, u32[]{:S(2)}, u32[]{:S(2)}) collective-permute-start(s32[40,128]{1,0:T(8,128)} %shard_map.110), channel_id=1, source_target_pairs={{0,64},{2,66},{4,68},{6,70},{8,72},{10,74},{12,76},{14,78},{16,80}... | collective-permute-start | bytes 61448 | tf_op jit(solution)/shard_map/ppermute | solution.py:376
  13.9 6.6 %collective-permute-done.2 = s32[40,128]{1,0:T(8,128)S(1)} collective-permute-done((s32[40,128]{1,0:T(8,128)}, s32[40,128]{1,0:T(8,128)S(1)}, u32[]{:S(2)}, u32[]{:S(2)}) %collective-permute-start.2) | collective-permute-done | bytes 20512 | tf_op jit(solution)/shard_map/ppermute | solution.py:376
  20.5 0.7 pad_add_fusion
  21.2 0.7 broadcast_in_dim.10
  22.0 5.0 %all-to-all-start = ((s32[8,80,128]{2,1,0:T(8,128)}), s32[8,80,128]{2,1,0:T(8,128)S(1)}, u32[]{:S(2)}, u32[]{:S(2)}) async-start(s32[8,80,128]{2,1,0:T(8,128)} %broadcast_in_dim.10), calls=%async_computation | async-start | bytes 655360 | tf_op jit(solution)/shard_map/all_to_all | solution.py:377
  27.0 3.0 %collective-permute-start = (s32[384]{0:T(512)S(1)}, s32[384]{0:T(512)S(1)}, u32[]{:S(2)}, u32[]{:S(2)}) collective-permute-start(s32[384]{0:T(512)S(1)} %bitcast.24), channel_id=1, source_target_pairs={{0,1},{1,0},{2,3},{3,2},{4,5},{5,4},{6,7},{7,6},{8,9},{9,8},{10,11... | collective-permute-start | bytes 4616 | tf_op jit(solution)/shard_map/ppermute | solution.py:373
  30.0 1.5 fusion.2
  31.6 0.1 constant_dynamic-slice_fusion.refs_4_.refs_6_
  31.6 0.1 concatenate.31.refs_3_.refs_5_
  31.7 0.0 copy-start.6
  31.7 0.0 copy-start.7
  31.8 0.0 collective-permute-done.sib_slot
  31.8 0.0 collective-permute-done.1.sib_hbm
  31.8 5.0 %shard_map.109 = (bf16[48,64,128]{2,1,0:T(8,128)(2,1)}, bf16[48,64,128]{2,1,0:T(8,128)(2,1)}, bf16[48,64,128]{2,1,0:T(8,128)(2,1)}, bf16[48,64,128]{2,1,0:T(8,12...) custom-call(s32[4]{0:T(128)S(1)} %copy-done.5, ...), custom_call_target="tpu_custom_call" | custom-call | bytes 10485760 | tf_op jit(solution)/shard_map/pallas_call | solution.py:94
  36.8 0.2 all-to-all-done.heard_ref
  37.0 3.5 %collective-permute-start.3 = (bf16[48,64,128]{2,1,0:T(8,128)(2,1)}, bf16[48,64,128]{2,1,0:T(8,128)(2,1)S(1)}, u32[]{:S(2)}, u32[]{:S(2)}) collective-permute-start(bf16[48,64,128]{2,1,0:T(8,128)(2,1)} %get-tuple-element.40), channel_id=1, source_target_pairs={{0,16},{2,18},{4,20},{6,22},{8,24},{10,26},{12,28},{14,30},{16,32}... | collective-permute-start | bytes 2359304 | tf_op jit(solution)/shard_map/ppermute | solution.py:388
  40.5 3.4 %collective-permute-start.4 = (bf16[48,64,128]{2,1,0:T(8,128)(2,1)}, bf16[48,64,128]{2,1,0:T(8,128)(2,1)S(1)}, u32[]{:S(2)}, u32[]{:S(2)}) collective-permute-start(bf16[48,64,128]{2,1,0:T(8,128)(2,1)} %get-tuple-element.41), channel_id=1, source_target_pairs={{0,112},{2,114},{4,116},{6,118},{8,120},{10,122},{12,124},{14,126}... | collective-permute-start | bytes 2359304 | tf_op jit(solution)/shard_map/ppermute | solution.py:388
  43.8 1.3 shard_map.111
  45.1 6.6 %collective-permute-done.3.refs_0_ = bf16[48,64,128]{2,1,0:T(8,128)(2,1)S(1)} collective-permute-done((bf16[48,64,128]{2,1,0:T(8,128)(2,1)}, bf16[48,64,128]{2,1,0:T(8,128)(2,1)S(1)}, u32[]{:S(2)}, u32[]{:S(2)}) %collective-permute-start.3) | collective-permute-done | bytes 786464 | tf_op jit(solution)/shard_map/ppermute | solution.py:388
  51.8 1.9 %collective-permute-done.4.refs_1_ = bf16[48,64,128]{2,1,0:T(8,128)(2,1)S(1)} collective-permute-done((bf16[48,64,128]{2,1,0:T(8,128)(2,1)}, bf16[48,64,128]{2,1,0:T(8,128)(2,1)S(1)}, u32[]{:S(2)}, u32[]{:S(2)}) %collective-permute-start.4) | collective-permute-done | bytes 786464 | tf_op jit(solution)/shard_map/ppermute | solution.py:388
  53.7 1.4 copy-done
  55.1 0.8 copy-done.3
  56.0 7.9 %shard_map.112 = f32[4,8,16,16,128]{4,3,2,1,0:T(8,128)S(1)} custom-call(s32[4]{0:T(128)S(1)} %copy-done.5, s32[48,128]{1,0:T(8,128)S(1)} %get-tuple-element.39.list_ref, f32[32]{0:T(128)S(1)} %copy-done.6, f32[32]{0:T(128)S(1)} %copy-done.7, bf16[48,64,128]{2,1,0:T(8,128)(2,1)S(1)} %collective-permute-done.3.refs_0_, ...), custom_call_target="tpu_custom_call" | custom-call | flops 1000000000 | bytes 10485760 | tf_op jit(solution)/shard_map/pallas_call | solution.py:213
  63.9 1.7 convert_element_type.24
  65.6 10.6 %all-to-all-start.2 = ((f16[32,16,16,128]{3,2,1,0:T(8,128)(2,1)}), f16[32,16,16,128]{3,2,1,0:T(8,128)(2,1)}, u32[]{:S(2)}, u32[]{:S(2)}) async-start(f16[32,16,16,128]{3,2,1,0:T(8,128)(2,1)} %bitcast.26), calls=%async_computation.2 | async-start | bytes 4194304 | tf_op jit(solution)/shard_map/all_to_all | solution.py:350
  76.2 2.9 %collective-permute-start.5 = (bf16[48,64,128]{2,1,0:T(8,128)(2,1)}, bf16[48,64,128]{2,1,0:T(8,128)(2,1)S(1)}, u32[]{:S(2)}, u32[]{:S(2)}) collective-permute-start(bf16[48,64,128]{2,1,0:T(8,128)(2,1)} %get-tuple-element.48), channel_id=1, source_target_pairs={{0,16},{2,18},{4,20},{6,22},{8,24},{10,26},{12,28},{14,30},{16,32}... | collective-permute-start | bytes 2359304 | tf_op jit(solution)/shard_map/ppermute | solution.py:388
  79.1 3.6 %collective-permute-start.6 = (bf16[48,64,128]{2,1,0:T(8,128)(2,1)}, bf16[48,64,128]{2,1,0:T(8,128)(2,1)S(1)}, u32[]{:S(2)}, u32[]{:S(2)}) collective-permute-start(bf16[48,64,128]{2,1,0:T(8,128)(2,1)} %get-tuple-element.49), channel_id=1, source_target_pairs={{0,112},{2,114},{4,116},{6,118},{8,120},{10,122},{12,124},{14,126}... | collective-permute-start | bytes 2359304 | tf_op jit(solution)/shard_map/ppermute | solution.py:388
  82.7 4.4 %collective-permute-start.7 = (bf16[48,64,128]{2,1,0:T(8,128)(2,1)}, bf16[48,64,128]{2,1,0:T(8,128)(2,1)S(1)}, u32[]{:S(2)}, u32[]{:S(2)}) collective-permute-start(bf16[48,64,128]{2,1,0:T(8,128)(2,1)} %get-tuple-element.50), channel_id=1, source_target_pairs={{0,32},{2,34},{4,36},{6,38},{8,40},{10,42},{12,44},{14,46},{16,48}... | collective-permute-start | bytes 2359304 | tf_op jit(solution)/shard_map/ppermute | solution.py:388
  87.1 3.0 %collective-permute-start.8 = (bf16[48,64,128]{2,1,0:T(8,128)(2,1)}, bf16[48,64,128]{2,1,0:T(8,128)(2,1)S(1)}, u32[]{:S(2)}, u32[]{:S(2)}) collective-permute-start(bf16[48,64,128]{2,1,0:T(8,128)(2,1)} %get-tuple-element.51), channel_id=1, source_target_pairs={{0,96},{2,98},{4,100},{6,102},{8,104},{10,106},{12,108},{14,110},{... | collective-permute-start | bytes 2359304 | tf_op jit(solution)/shard_map/ppermute | solution.py:388
  90.1 16.1 %collective-permute-done.5.refs_0_ = bf16[48,64,128]{2,1,0:T(8,128)(2,1)S(1)} collective-permute-done((bf16[48,64,128]{2,1,0:T(8,128)(2,1)}, bf16[48,64,128]{2,1,0:T(8,128)(2,1)S(1)}, u32[]{:S(2)}, u32[]{:S(2)}) %collective-permute-start.5) | collective-permute-done | bytes 786464 | tf_op jit(solution)/shard_map/ppermute | solution.py:388
  106.2 3.8 %collective-permute-done.6.refs_1_ = bf16[48,64,128]{2,1,0:T(8,128)(2,1)S(1)} collective-permute-done((bf16[48,64,128]{2,1,0:T(8,128)(2,1)}, bf16[48,64,128]{2,1,0:T(8,128)(2,1)S(1)}, u32[]{:S(2)}, u32[]{:S(2)}) %collective-permute-start.6) | collective-permute-done | bytes 786464 | tf_op jit(solution)/shard_map/ppermute | solution.py:388
  110.0 14.7 %collective-permute-done.7.refs_2_ = bf16[48,64,128]{2,1,0:T(8,128)(2,1)S(1)} collective-permute-done((bf16[48,64,128]{2,1,0:T(8,128)(2,1)}, bf16[48,64,128]{2,1,0:T(8,128)(2,1)S(1)}, u32[]{:S(2)}, u32[]{:S(2)}) %collective-permute-start.7) | collective-permute-done | bytes 786464 | tf_op jit(solution)/shard_map/ppermute | solution.py:388
  124.6 5.7 %collective-permute-done.8.refs_3_ = bf16[48,64,128]{2,1,0:T(8,128)(2,1)S(1)} collective-permute-done((bf16[48,64,128]{2,1,0:T(8,128)(2,1)}, bf16[48,64,128]{2,1,0:T(8,128)(2,1)S(1)}, u32[]{:S(2)}, u32[]{:S(2)}) %collective-permute-start.8) | collective-permute-done | bytes 786464 | tf_op jit(solution)/shard_map/ppermute | solution.py:388
  130.3 9.8 %shard_map.113 = f32[4,8,16,16,128]{4,3,2,1,0:T(8,128)S(1)} custom-call(s32[4]{0:T(128)S(1)} %copy-done.5, s32[48,128]{1,0:T(8,128)S(1)} %get-tuple-element.47.list_ref, f32[32]{0:T(128)S(1)} %copy-done.6, f32[32]{0:T(128)S(1)} %copy-done.7, bf16[48,64,128]{2,1,0:T(8,128)(2,1)S(1)} %collective-permute-done.5.refs_0_, ...), custom_call_target="tpu_custom_call" | custom-call | flops 1000000000 | bytes 10485760 | tf_op jit(solution)/shard_map/pallas_call | solution.py:213
  140.2 1.8 convert_element_type.21
  141.9 7.8 %all-to-all-start.1 = ((f16[32,16,16,128]{3,2,1,0:T(8,128)(2,1)}), f16[32,16,16,128]{3,2,1,0:T(8,128)(2,1)S(1)}, u32[]{:S(2)}, u32[]{:S(2)}) async-start(f16[32,16,16,128]{3,2,1,0:T(8,128)(2,1)} %bitcast.10), calls=%async_computation.1 | async-start | bytes 4194304 | tf_op jit(solution)/shard_map/all_to_all | solution.py:350
  149.8 0.2 select_reduce_fusion
  149.9 0.2 convolution_bitcast_fusion
  150.2 0.1 fusion.18
  150.3 1.9 %convert_reduce_fusion = f32[16,16,128]{2,1,0:T(8,128)S(1)} fusion(f16[32,16,16,128]{3,2,1,0:T(8,128)(2,1)} %all-to-all-done.2), kind=kLoop, calls=%fused_computation | loop fusion | flops 2064384 | bytes 2228224 | tf_op jit(solution)/shard_map/reduce_sum | solution.py:353
  152.2 5.8 %collective-permute-start.9 = (f32[16,16,128]{2,1,0:T(8,128)S(1)}, f32[16,16,128]{2,1,0:T(8,128)S(1)}, u32[]{:S(2)}, u32[]{:S(2)}) collective-permute-start(f32[16,16,128]{2,1,0:T(8,128)S(1)} %convert_reduce_fusion), channel_id=1, source_target_pairs={{0,64},{2,66},{4,68},{6,70},{8,72},{10,74},{12,76},{14,78},{16,80}... | collective-permute-start | bytes 393224 | tf_op jit(solution)/shard_map/ppermute | solution.py:396
  157.9 23.6 %all-to-all-done.1 = f16[32,16,16,128]{3,2,1,0:T(8,128)(2,1)S(1)} async-done(((f16[32,16,16,128]{3,2,1,0:T(8,128)(2,1)}), f16[32,16,16,128]{3,2,1,0:T(8,128)(2,1)S(1)}, u32[]{:S(2)}, u32[]{:S(2)}) %all-to-all-start.1) | async-done | bytes 2097184 | tf_op jit(solution)/shard_map/all_to_all | solution.py:350
  181.6 0.3 convert_reduce_fusion.1
  181.8 0.8 fusion.4
  (22 shorter events, 0.0 us)
Async XLA Ops:
  0.0 31.5 %copy-start.8 = (bf16[64,64]{1,0:T(8,128)(2,1)S(1)}, bf16[64,64]{1,0:T(8,128)(2,1)}, u32[]{:S(2)}) copy-start(bf16[64,64]{1,0:T(8,128)(2,1)} %param.17) | copy-start | bytes 24580
  0.0 31.8 %collective-permute-start.1 = (bf16[128,64,128]{2,1,0:T(8,128)(2,1)}, bf16[128,64,128]{2,1,0:T(8,128)(2,1)}, u32[]{:S(2)}, u32[]{:S(2)}) collective-permute-start(bf16[128,64,128]{2,1,0:T(8,128)(2,1)} %bitcast.22), channel_id=1, source_target_pairs={{0,1},{1,0},{2,3},{3,2},{4,5},{5,4},{6,7},{7,6},{8,9},{9,8},{10,11... | collective-permute-start | bytes 6291464 | tf_op jit(solution)/shard_map/ppermute | solution.py:372
  11.9 8.6 %collective-permute-start.2 = (s32[40,128]{1,0:T(8,128)}, s32[40,128]{1,0:T(8,128)S(1)}, u32[]{:S(2)}, u32[]{:S(2)}) collective-permute-start(s32[40,128]{1,0:T(8,128)} %shard_map.110), channel_id=1, source_target_pairs={{0,64},{2,66},{4,68},{6,70},{8,72},{10,74},{12,76},{14,78},{16,80}... | collective-permute-start | bytes 61448 | tf_op jit(solution)/shard_map/ppermute | solution.py:376
  22.0 9.8 %copy-start.2 = (bf16[1,1,128,64,128]{4,3,2,1,0:T(8,128)(2,1)S(1)}, bf16[1,1,128,64,128]{4,3,2,1,0:T(8,128)(2,1)}, u32[]{:S(2)}) copy-start(bf16[1,1,128,64,128]{4,3,2,1,0:T(8,128)(2,1)} %param.11) | copy-start | bytes 6291460
  22.0 9.8 %copy-start.5 = (s32[4]{0:T(128)S(1)}, s32[4]{0:T(128)}, u32[]{:S(2)}) copy-start(s32[4]{0:T(128)} %pad_add_fusion.1.spot_ref) | copy-start | bytes 52
  22.0 15.0 %all-to-all-start = ((s32[8,80,128]{2,1,0:T(8,128)}), s32[8,80,128]{2,1,0:T(8,128)S(1)}, u32[]{:S(2)}, u32[]{:S(2)}) async-start(s32[8,80,128]{2,1,0:T(8,128)} %broadcast_in_dim.10), calls=%async_computation | async-start | bytes 655360 | tf_op jit(solution)/shard_map/all_to_all | solution.py:377
  27.0 4.8 %collective-permute-start = (s32[384]{0:T(512)S(1)}, s32[384]{0:T(512)S(1)}, u32[]{:S(2)}, u32[]{:S(2)}) collective-permute-start(s32[384]{0:T(512)S(1)} %bitcast.24), channel_id=1, source_target_pairs={{0,1},{1,0},{2,3},{3,2},{4,5},{5,4},{6,7},{7,6},{8,9},{9,8},{10,11... | collective-permute-start | bytes 4616 | tf_op jit(solution)/shard_map/ppermute | solution.py:373
  31.7 22.0 %copy-start.6 = (f32[32]{0:T(128)S(1)}, f32[32]{0:T(128)}, u32[]{:S(2)}) copy-start(f32[32]{0:T(128)} %re_ref.3) | copy-start | bytes 388
  31.7 22.0 %copy-start.7 = (f32[32]{0:T(128)S(1)}, f32[32]{0:T(128)}, u32[]{:S(2)}) copy-start(f32[32]{0:T(128)} %im_ref.3) | copy-start | bytes 388
  37.0 14.8 %collective-permute-start.3 = (bf16[48,64,128]{2,1,0:T(8,128)(2,1)}, bf16[48,64,128]{2,1,0:T(8,128)(2,1)S(1)}, u32[]{:S(2)}, u32[]{:S(2)}) collective-permute-start(bf16[48,64,128]{2,1,0:T(8,128)(2,1)} %get-tuple-element.40), channel_id=1, source_target_pairs={{0,16},{2,18},{4,20},{6,22},{8,24},{10,26},{12,28},{14,30},{16,32}... | collective-permute-start | bytes 2359304 | tf_op jit(solution)/shard_map/ppermute | solution.py:388
  40.5 13.2 %collective-permute-start.4 = (bf16[48,64,128]{2,1,0:T(8,128)(2,1)}, bf16[48,64,128]{2,1,0:T(8,128)(2,1)S(1)}, u32[]{:S(2)}, u32[]{:S(2)}) collective-permute-start(bf16[48,64,128]{2,1,0:T(8,128)(2,1)} %get-tuple-element.41), channel_id=1, source_target_pairs={{0,112},{2,114},{4,116},{6,118},{8,120},{10,122},{12,124},{14,126}... | collective-permute-start | bytes 2359304 | tf_op jit(solution)/shard_map/ppermute | solution.py:388
  53.7 1.4 copy-start
  55.1 0.8 copy-start.3
  65.6 64.7 %copy-start.1 = (bf16[96,64,128]{2,1,0:T(8,128)(2,1)S(1)}, bf16[96,64,128]{2,1,0:T(8,128)(2,1)}, u32[]{:S(2)}) copy-start(bf16[96,64,128]{2,1,0:T(8,128)(2,1)} %get-tuple-element.42.refs_2_.refs_4_) | copy-start | bytes 4718596
  65.6 64.7 %copy-start.4 = (bf16[16,16,128]{2,1,0:T(8,128)(2,1)S(1)}, bf16[16,16,128]{2,1,0:T(8,128)(2,1)}, u32[]{:S(2)}) copy-start(bf16[16,16,128]{2,1,0:T(8,128)(2,1)} %refs_7_) | copy-start | bytes 196612
  65.6 76.3 %all-to-all-start.2 = ((f16[32,16,16,128]{3,2,1,0:T(8,128)(2,1)}), f16[32,16,16,128]{3,2,1,0:T(8,128)(2,1)}, u32[]{:S(2)}, u32[]{:S(2)}) async-start(f16[32,16,16,128]{3,2,1,0:T(8,128)(2,1)} %bitcast.26), calls=%async_computation.2 | async-start | bytes 4194304 | tf_op jit(solution)/shard_map/all_to_all | solution.py:350
  76.2 30.0 %collective-permute-start.5 = (bf16[48,64,128]{2,1,0:T(8,128)(2,1)}, bf16[48,64,128]{2,1,0:T(8,128)(2,1)S(1)}, u32[]{:S(2)}, u32[]{:S(2)}) collective-permute-start(bf16[48,64,128]{2,1,0:T(8,128)(2,1)} %get-tuple-element.48), channel_id=1, source_target_pairs={{0,16},{2,18},{4,20},{6,22},{8,24},{10,26},{12,28},{14,30},{16,32}... | collective-permute-start | bytes 2359304 | tf_op jit(solution)/shard_map/ppermute | solution.py:388
  79.1 30.9 %collective-permute-start.6 = (bf16[48,64,128]{2,1,0:T(8,128)(2,1)}, bf16[48,64,128]{2,1,0:T(8,128)(2,1)S(1)}, u32[]{:S(2)}, u32[]{:S(2)}) collective-permute-start(bf16[48,64,128]{2,1,0:T(8,128)(2,1)} %get-tuple-element.49), channel_id=1, source_target_pairs={{0,112},{2,114},{4,116},{6,118},{8,120},{10,122},{12,124},{14,126}... | collective-permute-start | bytes 2359304 | tf_op jit(solution)/shard_map/ppermute | solution.py:388
  82.7 41.9 %collective-permute-start.7 = (bf16[48,64,128]{2,1,0:T(8,128)(2,1)}, bf16[48,64,128]{2,1,0:T(8,128)(2,1)S(1)}, u32[]{:S(2)}, u32[]{:S(2)}) collective-permute-start(bf16[48,64,128]{2,1,0:T(8,128)(2,1)} %get-tuple-element.50), channel_id=1, source_target_pairs={{0,32},{2,34},{4,36},{6,38},{8,40},{10,42},{12,44},{14,46},{16,48}... | collective-permute-start | bytes 2359304 | tf_op jit(solution)/shard_map/ppermute | solution.py:388
  87.1 43.2 %collective-permute-start.8 = (bf16[48,64,128]{2,1,0:T(8,128)(2,1)}, bf16[48,64,128]{2,1,0:T(8,128)(2,1)S(1)}, u32[]{:S(2)}, u32[]{:S(2)}) collective-permute-start(bf16[48,64,128]{2,1,0:T(8,128)(2,1)} %get-tuple-element.51), channel_id=1, source_target_pairs={{0,96},{2,98},{4,100},{6,102},{8,104},{10,106},{12,108},{14,110},{... | collective-permute-start | bytes 2359304 | tf_op jit(solution)/shard_map/ppermute | solution.py:388
  141.9 7.8 %copy-start.10 = (s32[16,3]{0,1:T(4,128)S(1)}, s32[16,3]{0,1:T(4,128)}, u32[]{:S(2)}) copy-start(s32[16,3]{0,1:T(4,128)} %param.14) | copy-start | bytes 580
  141.9 7.8 %copy-start.11 = (f32[128]{0:T(128)S(1)}, f32[128]{0:T(128)}, u32[]{:S(2)}) copy-start(f32[128]{0:T(128)} %param.21) | copy-start | bytes 1540
  141.9 8.0 %copy-start.9 = (bf16[64,64]{1,0:T(8,128)(2,1)S(1)}, bf16[64,64]{1,0:T(8,128)(2,1)}, u32[]{:S(2)}) copy-start(bf16[64,64]{1,0:T(8,128)(2,1)} %param.17) | copy-start | bytes 24580
  141.9 39.6 %all-to-all-start.1 = ((f16[32,16,16,128]{3,2,1,0:T(8,128)(2,1)}), f16[32,16,16,128]{3,2,1,0:T(8,128)(2,1)S(1)}, u32[]{:S(2)}, u32[]{:S(2)}) async-start(f16[32,16,16,128]{3,2,1,0:T(8,128)(2,1)} %bitcast.10), calls=%async_computation.1 | async-start | bytes 4194304 | tf_op jit(solution)/shard_map/all_to_all | solution.py:350
  152.2 29.7 %collective-permute-start.9 = (f32[16,16,128]{2,1,0:T(8,128)S(1)}, f32[16,16,128]{2,1,0:T(8,128)S(1)}, u32[]{:S(2)}, u32[]{:S(2)}) collective-permute-start(f32[16,16,128]{2,1,0:T(8,128)S(1)} %convert_reduce_fusion), channel_id=1, source_target_pairs={{0,64},{2,66},{4,68},{6,70},{8,72},{10,74},{12,76},{14,78},{16,80}... | collective-permute-start | bytes 393224 | tf_op jit(solution)/shard_map/ppermute | solution.py:396

commit v12 on v11

--- a/solution.py
+++ b/solution.py
@@ -290,25 +290,21 @@
     out_ref[last:last + 1] = sums[:1].astype(jnp.int32)
 
 
-def lists_kernel(kinds, modes, spot_ref, heard_ref, *refs):
-    out_refs, sum_ref = refs[:-1], refs[-1]
-    rows = sum_ref.shape[0]
-    for (steps, parts, far), out_ref in zip(kinds, out_refs, strict=True):
-        sum_ref[...] = sum(heard_ref[r, far * rows:(far + 1) * rows] for r in range(RINGS))
-        lists_of(steps, parts, modes, spot_ref, sum_ref, out_ref)
+def lists_kernel(kinds, modes, spot_ref, *refs):
+    for (steps, parts), heard_ref, out_ref in zip(kinds, refs[:len(kinds)], refs[len(kinds):], strict=True):
+        lists_of(steps, parts, modes, spot_ref, heard_ref, out_ref)
 
 
 def use_lists(kinds, modes, spot, heard):
-    rows = [modes + CAP + len(parts) * (modes // LOT + CAP) + 1 for _, parts, _ in kinds]
+    rows = [modes + CAP + len(parts) * (modes // LOT + CAP) + 1 for _, parts in kinds]
     return pl.pallas_call(
         functools.partial(lists_kernel, kinds, modes),
-        in_specs=[SMEM, VMEM],
+        in_specs=[SMEM] + [VMEM] * len(kinds),
         out_specs=[VMEM] * len(kinds),
-        out_shape=[jax.ShapeDtypeStruct((n + -n % 8, heard.shape[2]), jnp.int32) for n in rows],
-        scratch_shapes=[pltpu.VMEM((heard.shape[1] // 2, heard.shape[2]), jnp.int32)],
+        out_shape=[jax.ShapeDtypeStruct((n + -n % 8, heard[0].shape[1]), jnp.int32) for n in rows],
         compiler_params=pltpu.CompilerParams(vmem_limit_bytes=8 * 2**20),
         cost_estimate=pl.CostEstimate(flops=10**7, bytes_accessed=2**18, transcendentals=0),
-    )(spot, heard)
+    )(spot, *heard)
 
 
 def say_kernel(spot_ref, up_ref, down_ref, tri_ref, out_ref):
@@ -373,26 +369,27 @@
     sib_slots = lax.ppermute(slots, "ado", SIBLING)
     slots, use_up = lax.optimization_barrier((slots, use_up))
     said = say(spot, use_up, use_down, modes_tri)
-    said = jnp.concatenate([said, lax.ppermute(said, "ado", onward(4))], axis=0)
     heard = lax.all_to_all(
         jnp.broadcast_to(said, (RINGS,) + said.shape), "ado", split_axis=0, concat_axis=0, tiled=True,
         axis_index_groups=DELIVER,
     )
+    heard, slots = lax.optimization_barrier((jnp.sum(heard, axis=0), slots))
+    heard_far = lax.ppermute(heard, "ado", onward(4))
     picked = pick(spot, slots, sib_slots, states[0, 0], sib_store)
     maps_wide = jnp.concatenate([doubled(coupling), jnp.zeros((1, 2 * width, 2 * width), BF16)], axis=0)
     head_cols = lax.dynamic_slice_in_dim(hamiltonian, group * share, share, 1)
     shared = (maps_wide, head_cols, window_tier_states)
-    picked, heard, shared = lax.optimization_barrier((picked, heard, shared))
+    picked, heard, heard_far, shared = lax.optimization_barrier((picked, heard, heard_far, shared))
 
     sent = [
         block if step == 0 else lax.ppermute(block, "ado", onward(step))
         for (step, _), block in zip(SENDS, picked, strict=True)
     ]
-    kinds = ((FAR, ((0, RINGS),), 1), (NEAR, ((0, RINGS),), 0))
-    far_lists, near_lists = use_lists(kinds, modes, spot, heard)
+    kinds = ((FAR, ((0, RINGS),)), (NEAR, ((0, RINGS),)))
+    far_lists, near_lists = use_lists(kinds, modes, spot, (heard_far, heard))
 
     far = terms(FAR, (0, RINGS, 0), spot, far_lists, coup_re, coup_im, sent, *shared)
-    far, near_lists = lax.optimization_barrier((far, near_lists))
+    far, near_lists, sent = lax.optimization_barrier((far, near_lists, sent))
     far = lax.ppermute(reduced(far), "ado", onward(4))
     near = reduced(terms(NEAR, (0, RINGS, 0), spot, near_lists, coup_re, coup_im, sent, *shared))
 

time: 184 us -> 162 us (0.88)
  the two profiles are of different devices: /device:TPU:1 before, /device:TPU:8 now
where the time goes in v12:
time: 162 us; the launch traced here: 161 us
  starting transfers between devices  61.9 us (38%)
  waiting for transfers between devices  54.4 us (34%)
  Pallas kernels  25 us (15%)
  other arithmetic  9.92 us (6%)
  local copies, waits for them, and re-layouts  9.02 us (6%)
    all_to_all x2, waiting for transfers between devices, reduced(): lax.all_to_all(parts, ('grp', 'ado'), split_axis=0, concat_axis=0, tiled=...  40.7 us
    ppermute x6, starting transfers between devices, on_device(): lax.ppermute(block, 'ado', onward(step))  22.1 us
    pallas_call x2, Pallas kernels, terms(): pl.pallas_call(functools.partial(terms_kernel, sources, modes, windows, p...  17.1 us
    all_to_all x2, starting transfers between devices, reduced(): lax.all_to_all(parts, ('grp', 'ado'), split_axis=0, concat_axis=0, tiled=...  13.1 us
    ppermute x6, waiting for transfers between devices, on_device(): lax.ppermute(block, 'ado', onward(step))  11.5 us
    ppermute x1, starting transfers between devices, on_device(): heard_far = lax.ppermute(heard, 'ado', onward(4))  9.33 us
    all_to_all x1, starting transfers between devices, on_device(): lax.all_to_all(jnp.broadcast_to(said, (RINGS,) + said.shape), 'ado', spli...  9.24 us
    unnamed x41, local copies, waits for them, and re-layouts  6.2 us
  transfers between devices with their start and end apart: 13, of which 5 were waited for; matrix products, arithmetic and copies ran while one was open for 7% of the time, Pallas kernels for 16%

profile of v12, /device:TPU:8, one launch (start us, length us, event | category | flops | bytes accessed | tf_op | source)
XLA Modules:
  0.0 160.8 jit_solution(4878285968919435440)
XLA Ops:
  0.0 2.0 %collective-permute-start.1 = (bf16[128,64,128]{2,1,0:T(8,128)(2,1)}, bf16[128,64,128]{2,1,0:T(8,128)(2,1)}, u32[]{:S(2)}, u32[]{:S(2)}) collective-permute-start(bf16[128,64,128]{2,1,0:T(8,128)(2,1)} %bitcast.22), channel_id=1, source_target_pairs={{0,1},{1,0},{2,3},{3,2},{4,5},{5,4},{6,7},{7,6},{8,9},{9,8},{10,11... | collective-permute-start | bytes 6291464 | tf_op jit(solution)/shard_map/ppermute | solution.py:368
  2.1 0.7 copy.15
  2.8 0.6 pad_add_fusion.spot_ref
  3.4 1.6 shard_map.109
  5.0 1.4 broadcast_in_dim.10
  6.4 9.2 %all-to-all-start = ((s32[8,40,128]{2,1,0:T(8,128)}), s32[8,40,128]{2,1,0:T(8,128)S(1)}, u32[]{:S(2)}, u32[]{:S(2)}) async-start(s32[8,40,128]{2,1,0:T(8,128)} %broadcast_in_dim.10), calls=%async_computation | async-start | bytes 327680 | tf_op jit(solution)/shard_map/all_to_all | solution.py:372
  15.6 3.3 %collective-permute-start = (s32[384]{0:T(512)S(1)}, s32[384]{0:T(512)S(1)}, u32[]{:S(2)}, u32[]{:S(2)}) collective-permute-start(s32[384]{0:T(512)S(1)} %bitcast.24), channel_id=1, source_target_pairs={{0,1},{1,0},{2,3},{3,2},{4,5},{5,4},{6,7},{7,6},{8,9},{9,8},{10,11... | collective-permute-start | bytes 4616 | tf_op jit(solution)/shard_map/ppermute | solution.py:369
  18.9 2.5 %fusion.2 = bf16[32,128,128]{2,1,0:T(8,128)(2,1)} fusion(bf16[32,64,64]{2,1,0:T(8,128)(2,1)} %param.18), kind=kLoop, calls=%fused_computation.7 | loop fusion | flops 4194304 | bytes 1310720 | tf_op jit(solution)/shard_map/concatenate | solution.py:23
  21.5 2.1 %all-to-all-done = s32[8,40,128]{2,1,0:T(8,128)S(1)} async-done(((s32[8,40,128]{2,1,0:T(8,128)}), s32[8,40,128]{2,1,0:T(8,128)S(1)}, u32[]{:S(2)}, u32[]{:S(2)}) %all-to-all-start) | async-done | bytes 163872 | tf_op jit(solution)/shard_map/all_to_all | solution.py:372
  23.6 9.3 %collective-permute-start.2 = (s32[40,128]{1,0:T(8,128)S(1)}, s32[40,128]{1,0:T(8,128)S(1)}, u32[]{:S(2)}, u32[]{:S(2)}) collective-permute-start(s32[40,128]{1,0:T(8,128)S(1)} %reduce_sum.36.refs_1_), channel_id=1, source_target_pairs={{0,64},{2,66},{4,68},{6,70},{8,72},{10,74},{12,76},{14,78},{16,80}... | collective-permute-start | bytes 61448 | tf_op jit(solution)/shard_map/ppermute | solution.py:377
  33.0 0.1 constant_dynamic-slice_fusion.refs_4_.refs_6_
  33.1 1.4 concatenate.27.refs_3_.refs_5_
  34.4 0.0 copy-start.9
  34.4 0.0 copy-start.13
  34.4 0.0 copy-start.14
  34.5 5.0 %shard_map.110 = (bf16[48,64,128]{2,1,0:T(8,128)(2,1)}, bf16[48,64,128]{2,1,0:T(8,128)(2,1)}, bf16[48,64,128]{2,1,0:T(8,128)(2,1)}, bf16[48,64,128]{2,1,0:T(8,12...) custom-call(s32[4]{0:T(128)S(1)} %copy-done.12, ...), custom_call_target="tpu_custom_call" | custom-call | bytes 10485760 | tf_op jit(solution)/shard_map/pallas_call | solution.py:94
  39.5 0.0 collective-permute-done.2.refs_0_
  39.5 3.4 %collective-permute-start.3 = (bf16[48,64,128]{2,1,0:T(8,128)(2,1)}, bf16[48,64,128]{2,1,0:T(8,128)(2,1)S(1)}, u32[]{:S(2)}, u32[]{:S(2)}) collective-permute-start(bf16[48,64,128]{2,1,0:T(8,128)(2,1)} %get-tuple-element.51), channel_id=1, source_target_pairs={{0,16},{2,18},{4,20},{6,22},{8,24},{10,26},{12,28},{14,30},{16,32}... | collective-permute-start | bytes 2359304 | tf_op jit(solution)/shard_map/ppermute | solution.py:385
  42.9 3.7 %collective-permute-start.4 = (bf16[48,64,128]{2,1,0:T(8,128)(2,1)}, bf16[48,64,128]{2,1,0:T(8,128)(2,1)S(1)}, u32[]{:S(2)}, u32[]{:S(2)}) collective-permute-start(bf16[48,64,128]{2,1,0:T(8,128)(2,1)} %get-tuple-element.52), channel_id=1, source_target_pairs={{0,112},{2,114},{4,116},{6,118},{8,120},{10,122},{12,124},{14,126}... | collective-permute-start | bytes 2359304 | tf_op jit(solution)/shard_map/ppermute | solution.py:385
  46.6 2.2 %collective-permute-start.5 = (bf16[48,64,128]{2,1,0:T(8,128)(2,1)}, bf16[48,64,128]{2,1,0:T(8,128)(2,1)S(1)}, u32[]{:S(2)}, u32[]{:S(2)}) collective-permute-start(bf16[48,64,128]{2,1,0:T(8,128)(2,1)} %get-tuple-element.58), channel_id=1, source_target_pairs={{0,16},{2,18},{4,20},{6,22},{8,24},{10,26},{12,28},{14,30},{16,32}... | collective-permute-start | bytes 2359304 | tf_op jit(solution)/shard_map/ppermute | solution.py:385
  48.7 4.9 %collective-permute-start.6 = (bf16[48,64,128]{2,1,0:T(8,128)(2,1)}, bf16[48,64,128]{2,1,0:T(8,128)(2,1)S(1)}, u32[]{:S(2)}, u32[]{:S(2)}) collective-permute-start(bf16[48,64,128]{2,1,0:T(8,128)(2,1)} %get-tuple-element.59), channel_id=1, source_target_pairs={{0,112},{2,114},{4,116},{6,118},{8,120},{10,122},{12,124},{14,126}... | collective-permute-start | bytes 2359304 | tf_op jit(solution)/shard_map/ppermute | solution.py:385
  53.6 1.9 %collective-permute-start.7 = (bf16[48,64,128]{2,1,0:T(8,128)(2,1)}, bf16[48,64,128]{2,1,0:T(8,128)(2,1)S(1)}, u32[]{:S(2)}, u32[]{:S(2)}) collective-permute-start(bf16[48,64,128]{2,1,0:T(8,128)(2,1)} %get-tuple-element.60), channel_id=1, source_target_pairs={{0,32},{2,34},{4,36},{6,38},{8,40},{10,42},{12,44},{14,46},{16,48}... | collective-permute-start | bytes 2359304 | tf_op jit(solution)/shard_map/ppermute | solution.py:385
  55.6 6.0 %collective-permute-start.8 = (bf16[48,64,128]{2,1,0:T(8,128)(2,1)}, bf16[48,64,128]{2,1,0:T(8,128)(2,1)S(1)}, u32[]{:S(2)}, u32[]{:S(2)}) collective-permute-start(bf16[48,64,128]{2,1,0:T(8,128)(2,1)} %get-tuple-element.61), channel_id=1, source_target_pairs={{0,96},{2,98},{4,100},{6,102},{8,104},{10,106},{12,108},{14,110},{... | collective-permute-start | bytes 2359304 | tf_op jit(solution)/shard_map/ppermute | solution.py:385
  61.6 1.3 shard_map.111
  62.9 0.0 copy-start.10
  63.0 1.4 copy-done
  64.4 7.3 %shard_map.112 = f32[4,8,16,16,128]{4,3,2,1,0:T(8,128)S(1)} custom-call(s32[4]{0:T(128)S(1)} %copy-done.12, s32[48,128]{1,0:T(8,128)S(1)} %get-tuple-element.50.list_ref, f32[32]{0:T(128)S(1)} %copy-done.13, f32[32]{0:T(128)S(1)} %copy-done.14, bf16[48,64,128]{2,1,0:T(8,128)(2,1)S(1)} %collective-permute-done.3.refs_0_, ...), custom_call_target="tpu_custom_call" | custom-call | flops 1000000000 | bytes 10485760 | tf_op jit(solution)/shard_map/pallas_call | solution.py:213
  71.7 2.0 %collective-permute-done.7.refs_2_ = bf16[48,64,128]{2,1,0:T(8,128)(2,1)S(1)} collective-permute-done((bf16[48,64,128]{2,1,0:T(8,128)(2,1)}, bf16[48,64,128]{2,1,0:T(8,128)(2,1)S(1)}, u32[]{:S(2)}, u32[]{:S(2)}) %collective-permute-start.7) | collective-permute-done | bytes 786464 | tf_op jit(solution)/shard_map/ppermute | solution.py:385
  73.6 9.5 %collective-permute-done.8.refs_3_ = bf16[48,64,128]{2,1,0:T(8,128)(2,1)S(1)} collective-permute-done((bf16[48,64,128]{2,1,0:T(8,128)(2,1)}, bf16[48,64,128]{2,1,0:T(8,128)(2,1)S(1)}, u32[]{:S(2)}, u32[]{:S(2)}) %collective-permute-start.8) | collective-permute-done | bytes 786464 | tf_op jit(solution)/shard_map/ppermute | solution.py:385
  83.2 1.8 %convert_element_type.24 = f16[4,8,16,16,128]{4,3,2,1,0:T(8,128)(2,1)} convert(f32[4,8,16,16,128]{4,3,2,1,0:T(8,128)S(1)} %shard_map.112) | non-fusion elementwise | flops 1048576 | bytes 6291456 | tf_op jit(solution)/shard_map/convert_element_type | solution.py:345
  84.9 0.0 copy-start.11
  85.0 6.5 %all-to-all-start.2 = ((f16[32,16,16,128]{3,2,1,0:T(8,128)(2,1)}), f16[32,16,16,128]{3,2,1,0:T(8,128)(2,1)}, u32[]{:S(2)}, u32[]{:S(2)}) async-start(f16[32,16,16,128]{3,2,1,0:T(8,128)(2,1)} %bitcast.26), calls=%async_computation.2 | async-start | bytes 4194304 | tf_op jit(solution)/shard_map/all_to_all | solution.py:346
  91.5 1.1 copy-done.4
  92.6 1.1 copy-done.6
  93.7 1.1 copy-done.8
  94.9 0.7 copy-done.15
  95.5 9.8 %shard_map.113 = f32[4,8,16,16,128]{4,3,2,1,0:T(8,128)S(1)} custom-call(s32[4]{0:T(128)S(1)} %copy-done.12, s32[48,128]{1,0:T(8,128)S(1)} %copy-done.11, f32[32]{0:T(128)S(1)} %copy-done.13, f32[32]{0:T(128)S(1)} %copy-done.15, bf16[48,64,128]{2,1,0:T(8,128)(2,1)S(1)} %collective-permute-done.5.refs_0_, bf16[48,64,128]{2,1,0:T(8,128)(2,1)S(1)} %copy-done.4, ...), custom_call_target="tpu_custom_call" | custom-call | flops 1000000000 | bytes 10485760 | tf_op jit(solution)/shard_map/pallas_call | solution.py:213
  105.4 1.8 %convert_element_type.21 = f16[4,8,16,16,128]{4,3,2,1,0:T(8,128)(2,1)} convert(f32[4,8,16,16,128]{4,3,2,1,0:T(8,128)S(1)} %shard_map.113) | non-fusion elementwise | flops 1048576 | bytes 6291456 | tf_op jit(solution)/shard_map/convert_element_type | solution.py:345
  107.1 13.9 %all-to-all-done.2 = f16[32,16,16,128]{3,2,1,0:T(8,128)(2,1)} async-done(((f16[32,16,16,128]{3,2,1,0:T(8,128)(2,1)}), f16[32,16,16,128]{3,2,1,0:T(8,128)(2,1)}, u32[]{:S(2)}, u32[]{:S(2)}) %all-to-all-start.2) | async-done | bytes 2097184 | tf_op jit(solution)/shard_map/all_to_all | solution.py:346
  121.0 6.6 %all-to-all-start.1 = ((f16[32,16,16,128]{3,2,1,0:T(8,128)(2,1)}), f16[32,16,16,128]{3,2,1,0:T(8,128)(2,1)S(1)}, u32[]{:S(2)}, u32[]{:S(2)}) async-start(f16[32,16,16,128]{3,2,1,0:T(8,128)(2,1)} %bitcast.10), calls=%async_computation.1 | async-start | bytes 4194304 | tf_op jit(solution)/shard_map/all_to_all | solution.py:346
  127.7 0.2 select_reduce_fusion
  127.9 0.2 convolution_bitcast_fusion
  128.1 0.1 fusion.18
  128.2 1.9 %convert_reduce_fusion = f32[16,16,128]{2,1,0:T(8,128)S(1)} fusion(f16[32,16,16,128]{3,2,1,0:T(8,128)(2,1)} %all-to-all-done.2), kind=kLoop, calls=%fused_computation | loop fusion | flops 2064384 | bytes 2228224 | tf_op jit(solution)/shard_map/reduce_sum | solution.py:349
  130.1 2.8 %collective-permute-start.9 = (f32[16,16,128]{2,1,0:T(8,128)S(1)}, f32[16,16,128]{2,1,0:T(8,128)S(1)}, u32[]{:S(2)}, u32[]{:S(2)}) collective-permute-start(f32[16,16,128]{2,1,0:T(8,128)S(1)} %convert_reduce_fusion), channel_id=1, source_target_pairs={{0,64},{2,66},{4,68},{6,70},{8,72},{10,74},{12,76},{14,78},{16,80}... | collective-permute-start | bytes 393224 | tf_op jit(solution)/shard_map/ppermute | solution.py:393
  132.9 26.8 %all-to-all-done.1 = f16[32,16,16,128]{3,2,1,0:T(8,128)(2,1)S(1)} async-done(((f16[32,16,16,128]{3,2,1,0:T(8,128)(2,1)}), f16[32,16,16,128]{3,2,1,0:T(8,128)(2,1)S(1)}, u32[]{:S(2)}, u32[]{:S(2)}) %all-to-all-start.1) | async-done | bytes 2097184 | tf_op jit(solution)/shard_map/all_to_all | solution.py:346
  159.7 0.3 convert_reduce_fusion.1
  160.0 0.8 fusion.4
  (38 shorter events, 0.1 us)
Async XLA Ops:
  0.0 33.0 %copy-start.16 = (bf16[64,64]{1,0:T(8,128)(2,1)S(1)}, bf16[64,64]{1,0:T(8,128)(2,1)}, u32[]{:S(2)}) copy-start(bf16[64,64]{1,0:T(8,128)(2,1)} %param.17) | copy-start | bytes 24580
  0.0 34.5 %collective-permute-start.1 = (bf16[128,64,128]{2,1,0:T(8,128)(2,1)}, bf16[128,64,128]{2,1,0:T(8,128)(2,1)}, u32[]{:S(2)}, u32[]{:S(2)}) collective-permute-start(bf16[128,64,128]{2,1,0:T(8,128)(2,1)} %bitcast.22), channel_id=1, source_target_pairs={{0,1},{1,0},{2,3},{3,2},{4,5},{5,4},{6,7},{7,6},{8,9},{9,8},{10,11... | collective-permute-start | bytes 6291464 | tf_op jit(solution)/shard_map/ppermute | solution.py:368
  6.4 28.1 %copy-start.2 = (bf16[1,1,128,64,128]{4,3,2,1,0:T(8,128)(2,1)S(1)}, bf16[1,1,128,64,128]{4,3,2,1,0:T(8,128)(2,1)}, u32[]{:S(2)}) copy-start(bf16[1,1,128,64,128]{4,3,2,1,0:T(8,128)(2,1)} %param.11) | copy-start | bytes 6291460
  6.4 28.1 %copy-start.12 = (s32[4]{0:T(128)S(1)}, s32[4]{0:T(128)}, u32[]{:S(2)}) copy-start(s32[4]{0:T(128)} %pad_add_fusion.spot_ref) | copy-start | bytes 52
  6.4 17.2 %all-to-all-start = ((s32[8,40,128]{2,1,0:T(8,128)}), s32[8,40,128]{2,1,0:T(8,128)S(1)}, u32[]{:S(2)}, u32[]{:S(2)}) async-start(s32[8,40,128]{2,1,0:T(8,128)} %broadcast_in_dim.10), calls=%async_computation | async-start | bytes 327680 | tf_op jit(solution)/shard_map/all_to_all | solution.py:372
  15.6 18.9 %collective-permute-start = (s32[384]{0:T(512)S(1)}, s32[384]{0:T(512)S(1)}, u32[]{:S(2)}, u32[]{:S(2)}) collective-permute-start(s32[384]{0:T(512)S(1)} %bitcast.24), channel_id=1, source_target_pairs={{0,1},{1,0},{2,3},{3,2},{4,5},{5,4},{6,7},{7,6},{8,9},{9,8},{10,11... | collective-permute-start | bytes 4616 | tf_op jit(solution)/shard_map/ppermute | solution.py:369
  23.6 15.9 %collective-permute-start.2 = (s32[40,128]{1,0:T(8,128)S(1)}, s32[40,128]{1,0:T(8,128)S(1)}, u32[]{:S(2)}, u32[]{:S(2)}) collective-permute-start(s32[40,128]{1,0:T(8,128)S(1)} %reduce_sum.36.refs_1_), channel_id=1, source_target_pairs={{0,64},{2,66},{4,68},{6,70},{8,72},{10,74},{12,76},{14,78},{16,80}... | collective-permute-start | bytes 61448 | tf_op jit(solution)/shard_map/ppermute | solution.py:377
  34.4 28.5 %copy-start.9 = (bf16[16,16,128]{2,1,0:T(8,128)(2,1)S(1)}, bf16[16,16,128]{2,1,0:T(8,128)(2,1)}, u32[]{:S(2)}) copy-start(bf16[16,16,128]{2,1,0:T(8,128)(2,1)} %refs_7_) | copy-start | bytes 196612
  34.4 28.5 %copy-start.13 = (f32[32]{0:T(128)S(1)}, f32[32]{0:T(128)}, u32[]{:S(2)}) copy-start(f32[32]{0:T(128)} %re_ref.3) | copy-start | bytes 388
  34.4 28.5 %copy-start.14 = (f32[32]{0:T(128)S(1)}, f32[32]{0:T(128)}, u32[]{:S(2)}) copy-start(f32[32]{0:T(128)} %im_ref.3) | copy-start | bytes 388
  39.5 16.1 %collective-permute-start.3 = (bf16[48,64,128]{2,1,0:T(8,128)(2,1)}, bf16[48,64,128]{2,1,0:T(8,128)(2,1)S(1)}, u32[]{:S(2)}, u32[]{:S(2)}) collective-permute-start(bf16[48,64,128]{2,1,0:T(8,128)(2,1)} %get-tuple-element.51), channel_id=1, source_target_pairs={{0,16},{2,18},{4,20},{6,22},{8,24},{10,26},{12,28},{14,30},{16,32}... | collective-permute-start | bytes 2359304 | tf_op jit(solution)/shard_map/ppermute | solution.py:385
  42.9 20.0 %collective-permute-start.4 = (bf16[48,64,128]{2,1,0:T(8,128)(2,1)}, bf16[48,64,128]{2,1,0:T(8,128)(2,1)S(1)}, u32[]{:S(2)}, u32[]{:S(2)}) collective-permute-start(bf16[48,64,128]{2,1,0:T(8,128)(2,1)} %get-tuple-element.52), channel_id=1, source_target_pairs={{0,112},{2,114},{4,116},{6,118},{8,120},{10,122},{12,124},{14,126}... | collective-permute-start | bytes 2359304 | tf_op jit(solution)/shard_map/ppermute | solution.py:385
  46.6 25.1 %collective-permute-start.5 = (bf16[48,64,128]{2,1,0:T(8,128)(2,1)}, bf16[48,64,128]{2,1,0:T(8,128)(2,1)S(1)}, u32[]{:S(2)}, u32[]{:S(2)}) collective-permute-start(bf16[48,64,128]{2,1,0:T(8,128)(2,1)} %get-tuple-element.58), channel_id=1, source_target_pairs={{0,16},{2,18},{4,20},{6,22},{8,24},{10,26},{12,28},{14,30},{16,32}... | collective-permute-start | bytes 2359304 | tf_op jit(solution)/shard_map/ppermute | solution.py:385
  48.7 22.9 %collective-permute-start.6 = (bf16[48,64,128]{2,1,0:T(8,128)(2,1)}, bf16[48,64,128]{2,1,0:T(8,128)(2,1)S(1)}, u32[]{:S(2)}, u32[]{:S(2)}) collective-permute-start(bf16[48,64,128]{2,1,0:T(8,128)(2,1)} %get-tuple-element.59), channel_id=1, source_target_pairs={{0,112},{2,114},{4,116},{6,118},{8,120},{10,122},{12,124},{14,126}... | collective-permute-start | bytes 2359304 | tf_op jit(solution)/shard_map/ppermute | solution.py:385
  53.6 20.0 %collective-permute-start.7 = (bf16[48,64,128]{2,1,0:T(8,128)(2,1)}, bf16[48,64,128]{2,1,0:T(8,128)(2,1)S(1)}, u32[]{:S(2)}, u32[]{:S(2)}) collective-permute-start(bf16[48,64,128]{2,1,0:T(8,128)(2,1)} %get-tuple-element.60), channel_id=1, source_target_pairs={{0,32},{2,34},{4,36},{6,38},{8,40},{10,42},{12,44},{14,46},{16,48}... | collective-permute-start | bytes 2359304 | tf_op jit(solution)/shard_map/ppermute | solution.py:385
  55.6 27.6 %collective-permute-start.8 = (bf16[48,64,128]{2,1,0:T(8,128)(2,1)}, bf16[48,64,128]{2,1,0:T(8,128)(2,1)S(1)}, u32[]{:S(2)}, u32[]{:S(2)}) collective-permute-start(bf16[48,64,128]{2,1,0:T(8,128)(2,1)} %get-tuple-element.61), channel_id=1, source_target_pairs={{0,96},{2,98},{4,100},{6,102},{8,104},{10,106},{12,108},{14,110},{... | collective-permute-start | bytes 2359304 | tf_op jit(solution)/shard_map/ppermute | solution.py:385
  62.9 8.7 %copy-start.10 = (s32[48,128]{1,0:T(8,128)}, s32[48,128]{1,0:T(8,128)S(1)}, u32[]{:S(2)}) copy-start(s32[48,128]{1,0:T(8,128)S(1)} %get-tuple-element.62.list_ref) | copy-start | bytes 73732
  62.9 1.4 copy-start
  71.7 13.3 %copy-start.3 = (bf16[48,64,128]{2,1,0:T(8,128)(2,1)}, bf16[48,64,128]{2,1,0:T(8,128)(2,1)S(1)}, u32[]{:S(2)}) copy-start(bf16[48,64,128]{2,1,0:T(8,128)(2,1)S(1)} %collective-permute-done.6.refs_1_) | copy-start | bytes 2359300
  73.6 11.3 %copy-start.5 = (bf16[48,64,128]{2,1,0:T(8,128)(2,1)}, bf16[48,64,128]{2,1,0:T(8,128)(2,1)S(1)}, u32[]{:S(2)}) copy-start(bf16[48,64,128]{2,1,0:T(8,128)(2,1)S(1)} %collective-permute-done.7.refs_2_) | copy-start | bytes 2359300
  83.2 1.8 %copy-start.7 = (bf16[48,64,128]{2,1,0:T(8,128)(2,1)}, bf16[48,64,128]{2,1,0:T(8,128)(2,1)S(1)}, u32[]{:S(2)}) copy-start(bf16[48,64,128]{2,1,0:T(8,128)(2,1)S(1)} %collective-permute-done.8.refs_3_) | copy-start | bytes 2359300
  84.9 6.5 %copy-start.1 = (bf16[96,64,128]{2,1,0:T(8,128)(2,1)S(1)}, bf16[96,64,128]{2,1,0:T(8,128)(2,1)}, u32[]{:S(2)}) copy-start(bf16[96,64,128]{2,1,0:T(8,128)(2,1)} %get-tuple-element.67.refs_2_.refs_4_) | copy-start | bytes 4718596
  84.9 6.5 %copy-start.11 = (s32[48,128]{1,0:T(8,128)S(1)}, s32[48,128]{1,0:T(8,128)}, u32[]{:S(2)}) copy-start(s32[48,128]{1,0:T(8,128)} %copy-done.10) | copy-start | bytes 73732
  85.0 36.1 %all-to-all-start.2 = ((f16[32,16,16,128]{3,2,1,0:T(8,128)(2,1)}), f16[32,16,16,128]{3,2,1,0:T(8,128)(2,1)}, u32[]{:S(2)}, u32[]{:S(2)}) async-start(f16[32,16,16,128]{3,2,1,0:T(8,128)(2,1)} %bitcast.26), calls=%async_computation.2 | async-start | bytes 4194304 | tf_op jit(solution)/shard_map/all_to_all | solution.py:346
  91.5 1.1 copy-start.4
  92.6 1.1 copy-start.6
  93.7 1.1 copy-start.8
  94.9 0.7 copy-start.15
  121.0 6.6 %copy-start.18 = (s32[16,3]{0,1:T(4,128)S(1)}, s32[16,3]{0,1:T(4,128)}, u32[]{:S(2)}) copy-start(s32[16,3]{0,1:T(4,128)} %param.14) | copy-start | bytes 580
  121.0 6.6 %copy-start.19 = (f32[128]{0:T(128)S(1)}, f32[128]{0:T(128)}, u32[]{:S(2)}) copy-start(f32[128]{0:T(128)} %param.21) | copy-start | bytes 1540
  121.0 6.8 %copy-start.17 = (bf16[64,64]{1,0:T(8,128)(2,1)S(1)}, bf16[64,64]{1,0:T(8,128)(2,1)}, u32[]{:S(2)}) copy-start(bf16[64,64]{1,0:T(8,128)(2,1)} %param.17) | copy-start | bytes 24580
  121.0 38.6 %all-to-all-start.1 = ((f16[32,16,16,128]{3,2,1,0:T(8,128)(2,1)}), f16[32,16,16,128]{3,2,1,0:T(8,128)(2,1)S(1)}, u32[]{:S(2)}, u32[]{:S(2)}) async-start(f16[32,16,16,128]{3,2,1,0:T(8,128)(2,1)} %bitcast.10), calls=%async_computation.1 | async-start | bytes 4194304 | tf_op jit(solution)/shard_map/all_to_all | solution.py:346
  130.1 29.9 %collective-permute-start.9 = (f32[16,16,128]{2,1,0:T(8,128)S(1)}, f32[16,16,128]{2,1,0:T(8,128)S(1)}, u32[]{:S(2)}, u32[]{:S(2)}) collective-permute-start(f32[16,16,128]{2,1,0:T(8,128)S(1)} %convert_reduce_fusion), channel_id=1, source_target_pairs={{0,64},{2,66},{4,68},{6,70},{8,72},{10,74},{12,76},{14,78},{16,80}... | collective-permute-start | bytes 393224 | tf_op jit(solution)/shard_map/ppermute | solution.py:393

commit v13 on v10

--- a/solution.py
+++ b/solution.py
@@ -32,9 +32,9 @@
 CAP = 3
 LOT = 4
 SPAN = 2 * CAP * RINGS
-SENDS = ((1, (-3, 1)), (-1, (3, -1)), (2, (2,)), (-2, (-2,)), (0, (4, 0)))
-FAR = tuple((n, group.index((step + 4) % 8 - 8 * ((step + 4) % 8 > 4)), step) for n, (step, group) in enumerate(SENDS) if len(group) == 2)
-NEAR = tuple((n, group.index(step), step) for n, (step, group) in enumerate(SENDS))
+SENDS = ((1, (-3,)), (-1, (3,)), (2, (2,)), (-2, (-2,)), (1, (1,)), (-1, (-1,)), (0, (4, 0)))
+FAR = ((0, 0, 1), (1, 0, -1), (6, 0, 0))
+NEAR = ((2, 0, 2), (3, 0, -2), (4, 0, 1), (5, 0, -1), (6, 1, 0))
 SIBLING = [(i, i ^ 1) for i in range(2 * RINGS * RINGS)]
 
 
@@ -287,25 +287,21 @@
     out_ref[last:last + 1] = sums[:1].astype(jnp.int32)
 
 
-def lists_kernel(kinds, modes, spot_ref, heard_ref, *refs):
-    out_refs, sum_ref = refs[:-1], refs[-1]
-    rows = sum_ref.shape[0]
-    for (steps, parts, far), out_ref in zip(kinds, out_refs, strict=True):
-        sum_ref[...] = sum(heard_ref[r, far * rows:(far + 1) * rows] for r in range(RINGS))
-        lists_of(steps, parts, modes, spot_ref, sum_ref, out_ref)
+def lists_kernel(kinds, modes, spot_ref, *refs):
+    for (steps, parts), heard_ref, out_ref in zip(kinds, refs[:len(kinds)], refs[len(kinds):], strict=True):
+        lists_of(steps, parts, modes, spot_ref, heard_ref, out_ref)
 
 
 def use_lists(kinds, modes, spot, heard):
-    rows = [modes + CAP + len(parts) * (modes // LOT + CAP) + 1 for _, parts, _ in kinds]
+    rows = [modes + CAP + len(parts) * (modes // LOT + CAP) + 1 for _, parts in kinds]
     return pl.pallas_call(
         functools.partial(lists_kernel, kinds, modes),
-        in_specs=[SMEM, VMEM],
+        in_specs=[SMEM] + [VMEM] * len(kinds),
         out_specs=[VMEM] * len(kinds),
-        out_shape=[jax.ShapeDtypeStruct((n + -n % 8, heard.shape[2]), jnp.int32) for n in rows],
-        scratch_shapes=[pltpu.VMEM((heard.shape[1] // 2, heard.shape[2]), jnp.int32)],
+        out_shape=[jax.ShapeDtypeStruct((n + -n % 8, heard[0].shape[1]), jnp.int32) for n in rows],
         compiler_params=pltpu.CompilerParams(vmem_limit_bytes=8 * 2**20),
         cost_estimate=pl.CostEstimate(flops=10**7, bytes_accessed=2**18, transcendentals=0),
-    )(spot, heard)
+    )(spot, *heard)
 
 
 def say_kernel(spot_ref, up_ref, down_ref, tri_ref, out_ref):
@@ -371,32 +367,32 @@
     sib_slots = lax.ppermute(slots, "ado", SIBLING)
     slots, use_up = lax.optimization_barrier((slots, use_up))
     said = say(spot, use_up, use_down, modes_tri)
-    said = jnp.concatenate([said, lax.ppermute(said, "ado", onward(4))], axis=0)
     heard = lax.all_to_all(
         jnp.broadcast_to(said, (RINGS,) + said.shape), "ado", split_axis=0, concat_axis=0, tiled=True,
         axis_index_groups=DELIVER,
     )
+    heard, slots = lax.optimization_barrier((jnp.sum(heard, axis=0), slots))
+    heard_far = lax.ppermute(heard, "ado", onward(4))
     picked = pick(spot, slots, sib_slots, states[0, 0], sib_store)
     maps_wide = jnp.concatenate([doubled(coupling), jnp.zeros((1, 2 * width, 2 * width), BF16)], axis=0)
     head_cols = lax.dynamic_slice_in_dim(hamiltonian, group * share, share, 1)
     shared = (maps_wide, head_cols, window_tier_states)
-    picked, heard, shared = lax.optimization_barrier((picked, heard, shared))
+    picked, heard, heard_far, shared = lax.optimization_barrier((picked, heard, heard_far, shared))
 
     sent = [
         block if step == 0 else lax.ppermute(block, "ado", onward(step))
         for (step, _), block in zip(SENDS, picked, strict=True)
     ]
-    kinds = ((FAR, ((0, RINGS),), 1), (NEAR, ((0, RINGS),), 0))
-    far_lists, near_lists = use_lists(kinds, modes, spot, heard)
+    kinds = ((FAR, ((0, RINGS),)), (NEAR, ((0, RINGS),)))
+    far_lists, near_lists = use_lists(kinds, modes, spot, (heard_far, heard))
 
     far = terms(FAR, (0, RINGS, 0), spot, far_lists, coup_re, coup_im, sent, *shared)
     far, near_lists = lax.optimization_barrier((far, near_lists))
-    far = over_groups(far)
-    far = lax.ppermute(far.astype(LINK), "ado", onward(4))
+    far = lax.ppermute(over_groups(far).astype(LINK), "ado", onward(4))
     near = over_groups(terms(NEAR, (0, RINGS, 0), spot, near_lists, coup_re, coup_im, sent, *shared))
     summed = lax.all_to_all(
-        (near + far.astype(F32)).astype(LINK), "ado", split_axis=0, concat_axis=0,
-        tiled=True, axis_index_groups=DELIVER,
+        (near + far.astype(F32)).astype(LINK), "ado", split_axis=0, concat_axis=0, tiled=True,
+        axis_index_groups=DELIVER,
     )
 
     ham_wide = doubled(hamiltonian)

time: 159 us -> 145 us (0.912)
  the two profiles are of different devices: /device:TPU:2 before, /device:TPU:1 now
where the time goes in v13:
time: 145 us; the launch traced here: 144 us
  starting transfers between devices  70.8 us (49%)
  waiting for transfers between devices  39.2 us (27%)
  Pallas kernels  24.7 us (17%)
  other arithmetic  5.27 us (4%)
  local copies, waits for them, and re-layouts  3.72 us (3%)
    ppermute x6, waiting for transfers between devices, over_groups(): lax.ppermute(parts[shift].astype(LINK), 'grp', ring).astype(F32)  20.9 us
    ppermute x6, starting transfers between devices, over_groups(): lax.ppermute(parts[shift].astype(LINK), 'grp', ring).astype(F32)  20.3 us
    ppermute x6, starting transfers between devices, on_device(): lax.ppermute(block, 'ado', onward(step))  18.8 us
    pallas_call x2, Pallas kernels, terms(): pl.pallas_call(functools.partial(terms_kernel, sources, modes, windows, p...  16.9 us
    all_to_all x1, waiting for transfers between devices, on_device(): lax.all_to_all((near + far.astype(F32)).astype(LINK), 'ado', split_axis=0...  11.9 us
    ppermute x1, starting transfers between devices, on_device(): sib_store = lax.ppermute(states[0, 0], 'ado', SIBLING)  8.91 us
    ppermute x1, starting transfers between devices, on_device(): heard_far = lax.ppermute(heard, 'ado', onward(4))  7.45 us
    all_to_all x1, starting transfers between devices, on_device(): lax.all_to_all((near + far.astype(F32)).astype(LINK), 'ado', split_axis=0...  5.33 us
  transfers between devices with their start and end apart: 18, of which 6 were waited for; matrix products, arithmetic and copies ran while one was open for 4% of the time, Pallas kernels for 17%

profile of v13, /device:TPU:1, one launch (start us, length us, event | category | flops | bytes accessed | tf_op | source)
XLA Modules:
  0.0 144.5 jit_solution(16848620408679915709)
XLA Ops:
  0.0 8.9 %collective-permute-start.1 = (bf16[128,64,128]{2,1,0:T(8,128)(2,1)}, bf16[128,64,128]{2,1,0:T(8,128)(2,1)}, u32[]{:S(2)}, u32[]{:S(2)}) collective-permute-start(bf16[128,64,128]{2,1,0:T(8,128)(2,1)} %bitcast.20), channel_id=1, source_target_pairs={{0,1},{1,0},{2,3},{3,2},{4,5},{5,4},{6,7},{7,6},{8,9},{9,8},{10,11... | collective-permute-start | bytes 6291464 | tf_op jit(solution)/shard_map/ppermute | solution.py:366
  8.9 0.7 copy.15
  9.6 0.7 pad_add_fusion.spot_ref
  10.3 1.6 %shard_map.109 = s32[40,128]{1,0:T(8,128)} custom-call(s32[4]{0:T(128)} %pad_add_fusion.spot_ref, s32[16,32]{1,0:T(8,128)} %up_ref, s32[3,16]{1,0:T(4,128)} %bitcast.25, s32[3,16]{1,0:T(4,128)} %bitcast.24), custom_call_target="tpu_custom_call" | custom-call | flops 1000000 | bytes 262144 | tf_op jit(solution)/shard_map/pallas_call | solution.py:332
  11.9 1.4 broadcast_in_dim.10
  13.3 4.8 %all-to-all-start = ((s32[8,40,128]{2,1,0:T(8,128)}), s32[8,40,128]{2,1,0:T(8,128)S(1)}, u32[]{:S(2)}, u32[]{:S(2)}) async-start(s32[8,40,128]{2,1,0:T(8,128)} %broadcast_in_dim.10), calls=%async_computation | async-start | bytes 327680 | tf_op jit(solution)/shard_map/all_to_all | solution.py:370
  18.1 1.9 %collective-permute-start = (s32[384]{0:T(512)S(1)}, s32[384]{0:T(512)S(1)}, u32[]{:S(2)}, u32[]{:S(2)}) collective-permute-start(s32[384]{0:T(512)S(1)} %bitcast.22), channel_id=1, source_target_pairs={{0,1},{1,0},{2,3},{3,2},{4,5},{5,4},{6,7},{7,6},{8,9},{9,8},{10,11... | collective-permute-start | bytes 4616 | tf_op jit(solution)/shard_map/ppermute | solution.py:367
  20.0 1.5 %fusion.2 = bf16[32,128,128]{2,1,0:T(8,128)(2,1)S(1)} fusion(bf16[32,64,64]{2,1,0:T(8,128)(2,1)} %param.18), kind=kLoop, calls=%fused_computation.5 | loop fusion | flops 4194304 | bytes 1310720 | tf_op jit(solution)/shard_map/concatenate | solution.py:23
  21.5 4.8 %all-to-all-done = s32[8,40,128]{2,1,0:T(8,128)S(1)} async-done(((s32[8,40,128]{2,1,0:T(8,128)}), s32[8,40,128]{2,1,0:T(8,128)S(1)}, u32[]{:S(2)}, u32[]{:S(2)}) %all-to-all-start) | async-done | bytes 163872 | tf_op jit(solution)/shard_map/all_to_all | solution.py:370
  26.4 7.5 %collective-permute-start.2 = (s32[40,128]{1,0:T(8,128)S(1)}, s32[40,128]{1,0:T(8,128)S(1)}, u32[]{:S(2)}, u32[]{:S(2)}) collective-permute-start(s32[40,128]{1,0:T(8,128)S(1)} %reduce_sum.27.refs_1_), channel_id=1, source_target_pairs={{0,64},{2,66},{4,68},{6,70},{8,72},{10,74},{12,76},{14,78},{16,80}... | collective-permute-start | bytes 61448 | tf_op jit(solution)/shard_map/ppermute | solution.py:375
  33.9 0.1 constant_dynamic-slice_fusion.refs_4_.refs_6_
  33.9 0.1 concatenate.27.refs_3_.refs_5_
  34.1 4.9 %shard_map.110 = (bf16[48,64,128]{2,1,0:T(8,128)(2,1)}, bf16[48,64,128]{2,1,0:T(8,128)(2,1)}, bf16[48,64,128]{2,1,0:T(8,128)(2,1)}, bf16[48,64,128]{2,1,0:T(8,12...) custom-call(s32[4]{0:T(128)S(1)} %copy-done.3, ...), custom_call_target="tpu_custom_call" | custom-call | bytes 10485760 | tf_op jit(solution)/shard_map/pallas_call | solution.py:91
  39.1 2.3 %collective-permute-start.3 = (bf16[48,64,128]{2,1,0:T(8,128)(2,1)}, bf16[48,64,128]{2,1,0:T(8,128)(2,1)S(1)}, u32[]{:S(2)}, u32[]{:S(2)}) collective-permute-start(bf16[48,64,128]{2,1,0:T(8,128)(2,1)} %get-tuple-element.57), channel_id=1, source_target_pairs={{0,16},{2,18},{4,20},{6,22},{8,24},{10,26},{12,28},{14,30},{16,32}... | collective-permute-start | bytes 2359304 | tf_op jit(solution)/shard_map/ppermute | solution.py:383
  41.4 4.2 %collective-permute-start.4 = (bf16[48,64,128]{2,1,0:T(8,128)(2,1)}, bf16[48,64,128]{2,1,0:T(8,128)(2,1)S(1)}, u32[]{:S(2)}, u32[]{:S(2)}) collective-permute-start(bf16[48,64,128]{2,1,0:T(8,128)(2,1)} %get-tuple-element.58), channel_id=1, source_target_pairs={{0,112},{2,114},{4,116},{6,118},{8,120},{10,122},{12,124},{14,126}... | collective-permute-start | bytes 2359304 | tf_op jit(solution)/shard_map/ppermute | solution.py:383
  45.6 1.9 %collective-permute-start.5 = (bf16[48,64,128]{2,1,0:T(8,128)(2,1)}, bf16[48,64,128]{2,1,0:T(8,128)(2,1)S(1)}, u32[]{:S(2)}, u32[]{:S(2)}) collective-permute-start(bf16[48,64,128]{2,1,0:T(8,128)(2,1)} %get-tuple-element.69), channel_id=1, source_target_pairs={{0,32},{2,34},{4,36},{6,38},{8,40},{10,42},{12,44},{14,46},{16,48}... | collective-permute-start | bytes 2359304 | tf_op jit(solution)/shard_map/ppermute | solution.py:383
  47.5 5.5 %collective-permute-start.6 = (bf16[48,64,128]{2,1,0:T(8,128)(2,1)}, bf16[48,64,128]{2,1,0:T(8,128)(2,1)S(1)}, u32[]{:S(2)}, u32[]{:S(2)}) collective-permute-start(bf16[48,64,128]{2,1,0:T(8,128)(2,1)} %get-tuple-element.70), channel_id=1, source_target_pairs={{0,96},{2,98},{4,100},{6,102},{8,104},{10,106},{12,108},{14,110},{... | collective-permute-start | bytes 2359304 | tf_op jit(solution)/shard_map/ppermute | solution.py:383
  53.0 1.9 %collective-permute-start.7 = (bf16[48,64,128]{2,1,0:T(8,128)(2,1)}, bf16[48,64,128]{2,1,0:T(8,128)(2,1)S(1)}, u32[]{:S(2)}, u32[]{:S(2)}) collective-permute-start(bf16[48,64,128]{2,1,0:T(8,128)(2,1)} %get-tuple-element.71), channel_id=1, source_target_pairs={{0,16},{2,18},{4,20},{6,22},{8,24},{10,26},{12,28},{14,30},{16,32}... | collective-permute-start | bytes 2359304 | tf_op jit(solution)/shard_map/ppermute | solution.py:383
  54.9 1.6 %collective-permute-done.3.refs_0_ = bf16[48,64,128]{2,1,0:T(8,128)(2,1)S(1)} collective-permute-done((bf16[48,64,128]{2,1,0:T(8,128)(2,1)}, bf16[48,64,128]{2,1,0:T(8,128)(2,1)S(1)}, u32[]{:S(2)}, u32[]{:S(2)}) %collective-permute-start.3) | collective-permute-done | bytes 786464 | tf_op jit(solution)/shard_map/ppermute | solution.py:383
  56.5 3.0 %collective-permute-start.8 = (bf16[48,64,128]{2,1,0:T(8,128)(2,1)}, bf16[48,64,128]{2,1,0:T(8,128)(2,1)S(1)}, u32[]{:S(2)}, u32[]{:S(2)}) collective-permute-start(bf16[48,64,128]{2,1,0:T(8,128)(2,1)} %get-tuple-element.72), channel_id=1, source_target_pairs={{0,112},{2,114},{4,116},{6,118},{8,120},{10,122},{12,124},{14,126}... | collective-permute-start | bytes 2359304 | tf_op jit(solution)/shard_map/ppermute | solution.py:383
  59.5 1.3 shard_map.111
  60.9 1.4 copy-done
  62.3 7.2 %shard_map.112 = (f32[8,16,16,128]{3,2,1,0:T(8,128)S(1)}, f32[8,16,16,128]{3,2,1,0:T(8,128)S(1)}, f32[8,16,16,128]{3,2,1,0:T(8,128)S(1)}, f32[8,16,16,128]{3,2,1,0:T(8,128)S(1)}) custom-call(s32[4]{0:T(128)S(1)} %copy-done.3, s32[48,128]{1,0:T(8,128)S(1)} %get-tuple-element.56.list_ref, f32[32]{0:T(128)S(1)} %copy-done.4, f32[32]{0:T(128)S(1)} %copy-done.5, ...), custom_call_target="tpu_custom_call" | custom-call | flops 1000000000 | bytes 10485760 | tf_op jit(solution)/shard_map/pallas_call | solution.py:210
  69.4 0.1 convert_element_type.61
  69.5 5.3 %collective-permute-start.14 = (f16[8,16,16,128]{3,2,1,0:T(8,128)(2,1)S(1)}, f16[8,16,16,128]{3,2,1,0:T(8,128)(2,1)S(1)}, u32[]{:S(2)}, u32[]{:S(2)}) collective-permute-start(f16[8,16,16,128]{3,2,1,0:T(8,128)(2,1)S(1)} %convert_element_type.61), channel_id=1, source_target_pairs={{0,384},{128,0},{256,128},{384,256},{1,385},{129,1},{257,129},{385... | collective-permute-start | bytes 1572872 | tf_op jit(solution)/shard_map/ppermute | solution.py:346
  74.9 0.1 convert_element_type.59
  74.9 0.1 convert_element_type.57
  75.0 1.9 %collective-permute-start.13 = (f16[8,16,16,128]{3,2,1,0:T(8,128)(2,1)S(1)}, f16[8,16,16,128]{3,2,1,0:T(8,128)(2,1)S(1)}, u32[]{:S(2)}, u32[]{:S(2)}) collective-permute-start(f16[8,16,16,128]{3,2,1,0:T(8,128)(2,1)S(1)} %convert_element_type.59), channel_id=1, source_target_pairs={{0,128},{128,256},{256,384},{384,0},{1,129},{129,257},{257,385},{3... | collective-permute-start | bytes 1572872 | tf_op jit(solution)/shard_map/ppermute | solution.py:346
  77.0 3.1 %collective-permute-start.12 = (f16[8,16,16,128]{3,2,1,0:T(8,128)(2,1)S(1)}, f16[8,16,16,128]{3,2,1,0:T(8,128)(2,1)S(1)}, u32[]{:S(2)}, u32[]{:S(2)}) collective-permute-start(f16[8,16,16,128]{3,2,1,0:T(8,128)(2,1)S(1)} %convert_element_type.57), channel_id=1, source_target_pairs={{0,256},{128,384},{256,0},{384,128},{1,257},{129,385},{257,1},{385... | collective-permute-start | bytes 1572872 | tf_op jit(solution)/shard_map/ppermute | solution.py:346
  80.1 9.7 %shard_map.113 = (f32[8,16,16,128]{3,2,1,0:T(8,128)S(1)}, f32[8,16,16,128]{3,2,1,0:T(8,128)S(1)}, f32[8,16,16,128]{3,2,1,0:T(8,128)S(1)}, f32[8,16,16,128]{3,2,1,0:T(8,128)S(1)}) custom-call(s32[4]{0:T(128)S(1)} %copy-done.3, s32[48,128]{1,0:T(8,128)S(1)} %get-tuple-element.68.list_ref, f32[32]{0:T(128)S(1)} %copy-done.4, f32[32]{0:T(128)S(1)} %copy-done.5, ...), custom_call_target="tpu_custom_call" | custom-call | flops 1000000000 | bytes 10485760 | tf_op jit(solution)/shard_map/pallas_call | solution.py:210
  89.9 0.1 convert_element_type.55
  90.0 4.4 %collective-permute-start.11 = (f16[8,16,16,128]{3,2,1,0:T(8,128)(2,1)S(1)}, f16[8,16,16,128]{3,2,1,0:T(8,128)(2,1)S(1)}, u32[]{:S(2)}, u32[]{:S(2)}) collective-permute-start(f16[8,16,16,128]{3,2,1,0:T(8,128)(2,1)S(1)} %convert_element_type.55), channel_id=1, source_target_pairs={{0,384},{128,0},{256,128},{384,256},{1,385},{129,1},{257,129},{385... | collective-permute-start | bytes 1572872 | tf_op jit(solution)/shard_map/ppermute | solution.py:346
  94.4 0.1 convert_element_type.53
  94.4 1.9 %collective-permute-start.10 = (f16[8,16,16,128]{3,2,1,0:T(8,128)(2,1)S(1)}, f16[8,16,16,128]{3,2,1,0:T(8,128)(2,1)S(1)}, u32[]{:S(2)}, u32[]{:S(2)}) collective-permute-start(f16[8,16,16,128]{3,2,1,0:T(8,128)(2,1)S(1)} %convert_element_type.53), channel_id=1, source_target_pairs={{0,128},{128,256},{256,384},{384,0},{1,129},{129,257},{257,385},{3... | collective-permute-start | bytes 1572872 | tf_op jit(solution)/shard_map/ppermute | solution.py:346
  96.4 0.1 convert_element_type.51
  96.5 3.6 %collective-permute-start.9 = (f16[8,16,16,128]{3,2,1,0:T(8,128)(2,1)S(1)}, f16[8,16,16,128]{3,2,1,0:T(8,128)(2,1)S(1)}, u32[]{:S(2)}, u32[]{:S(2)}) collective-permute-start(f16[8,16,16,128]{3,2,1,0:T(8,128)(2,1)S(1)} %convert_element_type.51), channel_id=1, source_target_pairs={{0,256},{128,384},{256,0},{384,128},{1,257},{129,385},{257,1},{385... | collective-permute-start | bytes 1572872 | tf_op jit(solution)/shard_map/ppermute | solution.py:346
  100.1 0.3 add_convert_fusion.1
  100.4 3.3 %collective-permute-start.15 = (f16[8,16,16,128]{3,2,1,0:T(8,128)(2,1)S(1)}, f16[8,16,16,128]{3,2,1,0:T(8,128)(2,1)S(1)}, u32[]{:S(2)}, u32[]{:S(2)}) collective-permute-start(f16[8,16,16,128]{3,2,1,0:T(8,128)(2,1)S(1)} %add_convert_fusion.1), channel_id=1, source_target_pairs={{0,64},{2,66},{4,68},{6,70},{8,72},{10,74},{12,76},{14,78},{16,80}... | collective-permute-start | bytes 1572872 | tf_op jit(solution)/shard_map/ppermute | solution.py:391
  103.8 6.5 %collective-permute-done.11 = f16[8,16,16,128]{3,2,1,0:T(8,128)(2,1)S(1)} collective-permute-done((f16[8,16,16,128]{3,2,1,0:T(8,128)(2,1)S(1)}, f16[8,16,16,128]{3,2,1,0:T(8,128)(2,1)S(1)}, u32[]{:S(2)}, u32[]{:S(2)}) %collective-permute-start.11) | collective-permute-done | bytes 524320 | tf_op jit(solution)/shard_map/ppermute | solution.py:346
  110.3 14.3 %collective-permute-done.10 = f16[8,16,16,128]{3,2,1,0:T(8,128)(2,1)S(1)} collective-permute-done((f16[8,16,16,128]{3,2,1,0:T(8,128)(2,1)S(1)}, f16[8,16,16,128]{3,2,1,0:T(8,128)(2,1)S(1)}, u32[]{:S(2)}, u32[]{:S(2)}) %collective-permute-start.10) | collective-permute-done | bytes 524320 | tf_op jit(solution)/shard_map/ppermute | solution.py:346
  124.7 1.2 add_convert_fusion
  125.8 5.3 %all-to-all-start.1 = ((f16[8,16,16,128]{3,2,1,0:T(8,128)(2,1)}), f16[8,16,16,128]{3,2,1,0:T(8,128)(2,1)S(1)}, u32[]{:S(2)}, u32[]{:S(2)}) async-start(f16[8,16,16,128]{3,2,1,0:T(8,128)(2,1)} %add_convert_fusion), calls=%async_computation.1 | async-start | bytes 1048576 | tf_op jit(solution)/shard_map/all_to_all | solution.py:393
  131.2 0.2 select_reduce_fusion
  131.4 0.2 convolution_bitcast_fusion
  131.6 0.1 fusion.18
  131.7 11.9 %all-to-all-done.1 = f16[8,16,16,128]{3,2,1,0:T(8,128)(2,1)S(1)} async-done(((f16[8,16,16,128]{3,2,1,0:T(8,128)(2,1)}), f16[8,16,16,128]{3,2,1,0:T(8,128)(2,1)S(1)}, u32[]{:S(2)}, u32[]{:S(2)}) %all-to-all-start.1) | async-done | bytes 524320 | tf_op jit(solution)/shard_map/all_to_all | solution.py:393
  143.6 0.1 convert_reduce_fusion
  143.7 0.8 fusion.4
  (31 shorter events, 0.2 us)
Async XLA Ops:
  0.0 33.8 %copy-start.6 = (bf16[64,64]{1,0:T(8,128)(2,1)S(1)}, bf16[64,64]{1,0:T(8,128)(2,1)}, u32[]{:S(2)}) copy-start(bf16[64,64]{1,0:T(8,128)(2,1)} %param.17) | copy-start | bytes 24580
  0.0 34.1 %collective-permute-start.1 = (bf16[128,64,128]{2,1,0:T(8,128)(2,1)}, bf16[128,64,128]{2,1,0:T(8,128)(2,1)}, u32[]{:S(2)}, u32[]{:S(2)}) collective-permute-start(bf16[128,64,128]{2,1,0:T(8,128)(2,1)} %bitcast.20), channel_id=1, source_target_pairs={{0,1},{1,0},{2,3},{3,2},{4,5},{5,4},{6,7},{7,6},{8,9},{9,8},{10,11... | collective-permute-start | bytes 6291464 | tf_op jit(solution)/shard_map/ppermute | solution.py:366
  13.3 20.8 %copy-start.1 = (bf16[1,1,128,64,128]{4,3,2,1,0:T(8,128)(2,1)S(1)}, bf16[1,1,128,64,128]{4,3,2,1,0:T(8,128)(2,1)}, u32[]{:S(2)}) copy-start(bf16[1,1,128,64,128]{4,3,2,1,0:T(8,128)(2,1)} %param.11) | copy-start | bytes 6291460
  13.3 20.8 %copy-start.3 = (s32[4]{0:T(128)S(1)}, s32[4]{0:T(128)}, u32[]{:S(2)}) copy-start(s32[4]{0:T(128)} %pad_add_fusion.spot_ref) | copy-start | bytes 52
  13.3 13.1 %all-to-all-start = ((s32[8,40,128]{2,1,0:T(8,128)}), s32[8,40,128]{2,1,0:T(8,128)S(1)}, u32[]{:S(2)}, u32[]{:S(2)}) async-start(s32[8,40,128]{2,1,0:T(8,128)} %broadcast_in_dim.10), calls=%async_computation | async-start | bytes 327680 | tf_op jit(solution)/shard_map/all_to_all | solution.py:370
  18.1 16.0 %collective-permute-start = (s32[384]{0:T(512)S(1)}, s32[384]{0:T(512)S(1)}, u32[]{:S(2)}, u32[]{:S(2)}) collective-permute-start(s32[384]{0:T(512)S(1)} %bitcast.22), channel_id=1, source_target_pairs={{0,1},{1,0},{2,3},{3,2},{4,5},{5,4},{6,7},{7,6},{8,9},{9,8},{10,11... | collective-permute-start | bytes 4616 | tf_op jit(solution)/shard_map/ppermute | solution.py:367
  26.4 12.7 %collective-permute-start.2 = (s32[40,128]{1,0:T(8,128)S(1)}, s32[40,128]{1,0:T(8,128)S(1)}, u32[]{:S(2)}, u32[]{:S(2)}) collective-permute-start(s32[40,128]{1,0:T(8,128)S(1)} %reduce_sum.27.refs_1_), channel_id=1, source_target_pairs={{0,64},{2,66},{4,68},{6,70},{8,72},{10,74},{12,76},{14,78},{16,80}... | collective-permute-start | bytes 61448 | tf_op jit(solution)/shard_map/ppermute | solution.py:375
  34.1 26.8 %copy-start.2 = (bf16[16,16,128]{2,1,0:T(8,128)(2,1)S(1)}, bf16[16,16,128]{2,1,0:T(8,128)(2,1)}, u32[]{:S(2)}) copy-start(bf16[16,16,128]{2,1,0:T(8,128)(2,1)} %refs_7_) | copy-start | bytes 196612
  34.1 26.8 %copy-start.4 = (f32[32]{0:T(128)S(1)}, f32[32]{0:T(128)}, u32[]{:S(2)}) copy-start(f32[32]{0:T(128)} %re_ref.3) | copy-start | bytes 388
  34.1 26.8 %copy-start.5 = (f32[32]{0:T(128)S(1)}, f32[32]{0:T(128)}, u32[]{:S(2)}) copy-start(f32[32]{0:T(128)} %im_ref.3) | copy-start | bytes 388
  39.1 17.4 %collective-permute-start.3 = (bf16[48,64,128]{2,1,0:T(8,128)(2,1)}, bf16[48,64,128]{2,1,0:T(8,128)(2,1)S(1)}, u32[]{:S(2)}, u32[]{:S(2)}) collective-permute-start(bf16[48,64,128]{2,1,0:T(8,128)(2,1)} %get-tuple-element.57), channel_id=1, source_target_pairs={{0,16},{2,18},{4,20},{6,22},{8,24},{10,26},{12,28},{14,30},{16,32}... | collective-permute-start | bytes 2359304 | tf_op jit(solution)/shard_map/ppermute | solution.py:383
  41.4 19.4 %collective-permute-start.4 = (bf16[48,64,128]{2,1,0:T(8,128)(2,1)}, bf16[48,64,128]{2,1,0:T(8,128)(2,1)S(1)}, u32[]{:S(2)}, u32[]{:S(2)}) collective-permute-start(bf16[48,64,128]{2,1,0:T(8,128)(2,1)} %get-tuple-element.58), channel_id=1, source_target_pairs={{0,112},{2,114},{4,116},{6,118},{8,120},{10,122},{12,124},{14,126}... | collective-permute-start | bytes 2359304 | tf_op jit(solution)/shard_map/ppermute | solution.py:383
  45.6 29.4 %collective-permute-start.5 = (bf16[48,64,128]{2,1,0:T(8,128)(2,1)}, bf16[48,64,128]{2,1,0:T(8,128)(2,1)S(1)}, u32[]{:S(2)}, u32[]{:S(2)}) collective-permute-start(bf16[48,64,128]{2,1,0:T(8,128)(2,1)} %get-tuple-element.69), channel_id=1, source_target_pairs={{0,32},{2,34},{4,36},{6,38},{8,40},{10,42},{12,44},{14,46},{16,48}... | collective-permute-start | bytes 2359304 | tf_op jit(solution)/shard_map/ppermute | solution.py:383
  47.5 29.4 %collective-permute-start.6 = (bf16[48,64,128]{2,1,0:T(8,128)(2,1)}, bf16[48,64,128]{2,1,0:T(8,128)(2,1)S(1)}, u32[]{:S(2)}, u32[]{:S(2)}) collective-permute-start(bf16[48,64,128]{2,1,0:T(8,128)(2,1)} %get-tuple-element.70), channel_id=1, source_target_pairs={{0,96},{2,98},{4,100},{6,102},{8,104},{10,106},{12,108},{14,110},{... | collective-permute-start | bytes 2359304 | tf_op jit(solution)/shard_map/ppermute | solution.py:383
  53.0 27.1 %collective-permute-start.7 = (bf16[48,64,128]{2,1,0:T(8,128)(2,1)}, bf16[48,64,128]{2,1,0:T(8,128)(2,1)S(1)}, u32[]{:S(2)}, u32[]{:S(2)}) collective-permute-start(bf16[48,64,128]{2,1,0:T(8,128)(2,1)} %get-tuple-element.71), channel_id=1, source_target_pairs={{0,16},{2,18},{4,20},{6,22},{8,24},{10,26},{12,28},{14,30},{16,32}... | collective-permute-start | bytes 2359304 | tf_op jit(solution)/shard_map/ppermute | solution.py:383
  56.5 23.7 %collective-permute-start.8 = (bf16[48,64,128]{2,1,0:T(8,128)(2,1)}, bf16[48,64,128]{2,1,0:T(8,128)(2,1)S(1)}, u32[]{:S(2)}, u32[]{:S(2)}) collective-permute-start(bf16[48,64,128]{2,1,0:T(8,128)(2,1)} %get-tuple-element.72), channel_id=1, source_target_pairs={{0,112},{2,114},{4,116},{6,118},{8,120},{10,122},{12,124},{14,126}... | collective-permute-start | bytes 2359304 | tf_op jit(solution)/shard_map/ppermute | solution.py:383
  60.9 1.4 copy-start
  69.5 27.0 %collective-permute-start.14 = (f16[8,16,16,128]{3,2,1,0:T(8,128)(2,1)S(1)}, f16[8,16,16,128]{3,2,1,0:T(8,128)(2,1)S(1)}, u32[]{:S(2)}, u32[]{:S(2)}) collective-permute-start(f16[8,16,16,128]{3,2,1,0:T(8,128)(2,1)S(1)} %convert_element_type.61), channel_id=1, source_target_pairs={{0,384},{128,0},{256,128},{384,256},{1,385},{129,1},{257,129},{385... | collective-permute-start | bytes 1572872 | tf_op jit(solution)/shard_map/ppermute | solution.py:346
  75.0 25.1 %collective-permute-start.13 = (f16[8,16,16,128]{3,2,1,0:T(8,128)(2,1)S(1)}, f16[8,16,16,128]{3,2,1,0:T(8,128)(2,1)S(1)}, u32[]{:S(2)}, u32[]{:S(2)}) collective-permute-start(f16[8,16,16,128]{3,2,1,0:T(8,128)(2,1)S(1)} %convert_element_type.59), channel_id=1, source_target_pairs={{0,128},{128,256},{256,384},{384,0},{1,129},{129,257},{257,385},{3... | collective-permute-start | bytes 1572872 | tf_op jit(solution)/shard_map/ppermute | solution.py:346
  77.0 23.1 %collective-permute-start.12 = (f16[8,16,16,128]{3,2,1,0:T(8,128)(2,1)S(1)}, f16[8,16,16,128]{3,2,1,0:T(8,128)(2,1)S(1)}, u32[]{:S(2)}, u32[]{:S(2)}) collective-permute-start(f16[8,16,16,128]{3,2,1,0:T(8,128)(2,1)S(1)} %convert_element_type.57), channel_id=1, source_target_pairs={{0,256},{128,384},{256,0},{384,128},{1,257},{129,385},{257,1},{385... | collective-permute-start | bytes 1572872 | tf_op jit(solution)/shard_map/ppermute | solution.py:346
  90.0 20.4 %collective-permute-start.11 = (f16[8,16,16,128]{3,2,1,0:T(8,128)(2,1)S(1)}, f16[8,16,16,128]{3,2,1,0:T(8,128)(2,1)S(1)}, u32[]{:S(2)}, u32[]{:S(2)}) collective-permute-start(f16[8,16,16,128]{3,2,1,0:T(8,128)(2,1)S(1)} %convert_element_type.55), channel_id=1, source_target_pairs={{0,384},{128,0},{256,128},{384,256},{1,385},{129,1},{257,129},{385... | collective-permute-start | bytes 1572872 | tf_op jit(solution)/shard_map/ppermute | solution.py:346
  94.4 30.2 %collective-permute-start.10 = (f16[8,16,16,128]{3,2,1,0:T(8,128)(2,1)S(1)}, f16[8,16,16,128]{3,2,1,0:T(8,128)(2,1)S(1)}, u32[]{:S(2)}, u32[]{:S(2)}) collective-permute-start(f16[8,16,16,128]{3,2,1,0:T(8,128)(2,1)S(1)} %convert_element_type.53), channel_id=1, source_target_pairs={{0,128},{128,256},{256,384},{384,0},{1,129},{129,257},{257,385},{3... | collective-permute-start | bytes 1572872 | tf_op jit(solution)/shard_map/ppermute | solution.py:346
  96.5 28.2 %collective-permute-start.9 = (f16[8,16,16,128]{3,2,1,0:T(8,128)(2,1)S(1)}, f16[8,16,16,128]{3,2,1,0:T(8,128)(2,1)S(1)}, u32[]{:S(2)}, u32[]{:S(2)}) collective-permute-start(f16[8,16,16,128]{3,2,1,0:T(8,128)(2,1)S(1)} %convert_element_type.51), channel_id=1, source_target_pairs={{0,256},{128,384},{256,0},{384,128},{1,257},{129,385},{257,1},{385... | collective-permute-start | bytes 1572872 | tf_op jit(solution)/shard_map/ppermute | solution.py:346
  100.4 24.2 %collective-permute-start.15 = (f16[8,16,16,128]{3,2,1,0:T(8,128)(2,1)S(1)}, f16[8,16,16,128]{3,2,1,0:T(8,128)(2,1)S(1)}, u32[]{:S(2)}, u32[]{:S(2)}) collective-permute-start(f16[8,16,16,128]{3,2,1,0:T(8,128)(2,1)S(1)} %add_convert_fusion.1), channel_id=1, source_target_pairs={{0,64},{2,66},{4,68},{6,70},{8,72},{10,74},{12,76},{14,78},{16,80}... | collective-permute-start | bytes 1572872 | tf_op jit(solution)/shard_map/ppermute | solution.py:391
  124.6 6.5 %copy-start.7 = (s32[16,3]{0,1:T(4,128)S(1)}, s32[16,3]{0,1:T(4,128)}, u32[]{:S(2)}) copy-start(s32[16,3]{0,1:T(4,128)} %param.14) | copy-start | bytes 580
  124.6 6.5 %copy-start.8 = (f32[128]{0:T(128)S(1)}, f32[128]{0:T(128)}, u32[]{:S(2)}) copy-start(f32[128]{0:T(128)} %param.21) | copy-start | bytes 1540
  125.8 17.8 %all-to-all-start.1 = ((f16[8,16,16,128]{3,2,1,0:T(8,128)(2,1)}), f16[8,16,16,128]{3,2,1,0:T(8,128)(2,1)S(1)}, u32[]{:S(2)}, u32[]{:S(2)}) async-start(f16[8,16,16,128]{3,2,1,0:T(8,128)(2,1)} %add_convert_fusion), calls=%async_computation.1 | async-start | bytes 1048576 | tf_op jit(solution)/shard_map/all_to_all | solution.py:393

commit v14 on v13

--- a/solution.py
+++ b/solution.py
@@ -53,52 +53,34 @@
 
 
 def pick_kernel(spot_ref, own_slot, sib_slot, own_ref, sib_hbm, *refs):
-    out_refs, (sib_ref, held, sem, sems) = refs[:-4], refs[-4:]
+    out_refs, (sib_ref, sem) = refs[:-2], refs[-2:]
     copy = pltpu.make_async_copy(sib_hbm, sib_ref, sem)
     copy.start()
     core, along = spot_ref[0], spot_ref[1]
     far = jnp.where(core == 0, 16, 2)
     near = jnp.where(core == 0, 2, 16)
     count = own_slot.shape[0] // CAP
-
-    def fill(ahead, place, kind):
-        slots, store = ((own_slot, own_ref), (sib_slot, sib_ref))[kind]
-        first = lax.rem(along + ahead + RINGS, RINGS) * far + core
-        for c in range(CAP):
-            for r in range(RINGS):
-                slot = slots[c * count + first + r * near]
-                held[place * SPAN + kind * CAP * RINGS + c * RINGS + r] = store[jnp.maximum(slot, 0)]
-
-    aheads = [ahead for _, group in SENDS for ahead in group]
-    for place, ahead in enumerate(aheads):
-        fill(ahead, place, 0)
-    copy.wait()
-    copies, place = [], 0
-    for n, ((_, group), out_ref) in enumerate(zip(SENDS, out_refs, strict=True)):
-        for ahead in group:
-            fill(ahead, place, 1)
-            place += 1
-        begin = (place - len(group)) * SPAN
-        copies.append(pltpu.make_async_copy(held.at[pl.ds(begin, len(group) * SPAN)], out_ref, sems.at[n]))
-        copies[-1].start()
-    for copy in copies:
-        copy.wait()
+    for kind, (slots, store) in enumerate(((own_slot, own_ref), (sib_slot, sib_ref))):
+        if kind == 1:
+            copy.wait()
+        for (_, group), out_ref in zip(SENDS, out_refs, strict=True):
+            for place, ahead in enumerate(group):
+                first = lax.rem(along + ahead + RINGS, RINGS) * far + core
+                for c in range(CAP):
+                    for r in range(RINGS):
+                        slot = slots[c * count + first + r * near]
+                        row = place * SPAN + kind * CAP * RINGS + c * RINGS + r
+                        out_ref[row] = store[jnp.maximum(slot, 0)]
 
 
 def pick(spot, own_slots, sib_slots, own, sib):
     tile = own.shape[1:]
-    total = sum(len(group) for _, group in SENDS)
     return pl.pallas_call(
         pick_kernel,
         in_specs=[SMEM, SMEM, SMEM, VMEM, HBM],
-        out_specs=[HBM] * len(SENDS),
-        out_shape=[pltpu.HBM((len(group) * SPAN,) + tile, own.dtype) for _, group in SENDS],
-        scratch_shapes=[
-            pltpu.VMEM(own.shape, own.dtype),
-            pltpu.VMEM((total * SPAN,) + tile, own.dtype),
-            pltpu.SemaphoreType.DMA,
-            pltpu.SemaphoreType.DMA((len(SENDS),)),
-        ],
+        out_specs=[VMEM] * len(SENDS),
+        out_shape=[jax.ShapeDtypeStruct((len(group) * SPAN,) + tile, own.dtype) for _, group in SENDS],
+        scratch_shapes=[pltpu.VMEM(own.shape, own.dtype), pltpu.SemaphoreType.DMA],
         compiler_params=pltpu.CompilerParams(vmem_limit_bytes=24 * 2**20),
         cost_estimate=pl.CostEstimate(flops=0, bytes_accessed=10 * 2**20, transcendentals=0),
     )(spot, own_slots, sib_slots, own, sib)
@@ -306,7 +288,7 @@
 
 def say_kernel(spot_ref, up_ref, down_ref, tri_ref, out_ref):
     windows, modes = up_ref.shape
-    shape = (windows, out_ref.shape[1])
+    shape = (windows, out_ref.shape[2])
     lanes = lax.broadcasted_iota(jnp.int32, shape, 1)
     row = lax.broadcasted_iota(jnp.int32, shape, 0)
     place = jnp.where(lanes == spot_ref[2] * windows + row, 1.0, 0.0)
@@ -321,9 +303,10 @@
         return (half(high) * 32.0 + half(values & 31)).astype(jnp.int32)
 
     up, down, tri = put(up_ref[...], 0), put(down_ref[...], 1), put(tri_ref[...], 1)
-    spare = jnp.zeros((out_ref.shape[0] - modes - 2 * CAP, shape[1]), jnp.int32)
+    spare = jnp.zeros((out_ref.shape[1] - modes - 2 * CAP, shape[1]), jnp.int32)
     whole = jnp.concatenate([up, down, tri, spare], axis=0)
-    out_ref[...] = whole
+    for n in range(RINGS):
+        out_ref[n] = whole
 
 
 def say(spot, use_up, use_down, modes_tri):
@@ -333,7 +316,7 @@
         say_kernel,
         in_specs=[SMEM, VMEM, VMEM, VMEM],
         out_specs=VMEM,
-        out_shape=jax.ShapeDtypeStruct((rows + -rows % 8, RINGS * windows), jnp.int32),
+        out_shape=jax.ShapeDtypeStruct((RINGS, rows + -rows % 8, RINGS * windows), jnp.int32),
         cost_estimate=pl.CostEstimate(flops=10**6, bytes_accessed=2**18, transcendentals=0),
     )(spot, use_up, use_down.T, modes_tri.T)
 
@@ -362,18 +345,17 @@
 
     spot = jnp.stack([core, along, across, group])
 
-    slots = jnp.transpose(send_slot[0, 0]).reshape(-1)
-    sib_store = lax.ppermute(states[0, 0], "ado", SIBLING)
+    said = say(spot, use_up, use_down, modes_tri)
+    said, slots, store = lax.optimization_barrier((said, send_slot[0, 0], states[0, 0]))
+    heard = lax.all_to_all(
+        said, "ado", split_axis=0, concat_axis=0, tiled=True, axis_index_groups=DELIVER
+    )
+    slots = jnp.transpose(slots).reshape(-1)
+    sib_store = lax.ppermute(store, "ado", SIBLING)
     sib_slots = lax.ppermute(slots, "ado", SIBLING)
-    slots, use_up = lax.optimization_barrier((slots, use_up))
-    said = say(spot, use_up, use_down, modes_tri)
-    heard = lax.all_to_all(
-        jnp.broadcast_to(said, (RINGS,) + said.shape), "ado", split_axis=0, concat_axis=0, tiled=True,
-        axis_index_groups=DELIVER,
-    )
     heard, slots = lax.optimization_barrier((jnp.sum(heard, axis=0), slots))
     heard_far = lax.ppermute(heard, "ado", onward(4))
-    picked = pick(spot, slots, sib_slots, states[0, 0], sib_store)
+    picked = pick(spot, slots, sib_slots, store, sib_store)
     maps_wide = jnp.concatenate([doubled(coupling), jnp.zeros((1, 2 * width, 2 * width), BF16)], axis=0)
     head_cols = lax.dynamic_slice_in_dim(hamiltonian, group * share, share, 1)
     shared = (maps_wide, head_cols, window_tier_states)

time: 145 us -> 140 us (0.966)
  the two profiles are of different devices: /device:TPU:1 before, /device:TPU:194 now
where the time goes in v14:
time: 140 us; the launch traced here: 139 us
  starting transfers between devices  72 us (51%)
  waiting for transfers between devices  36.5 us (26%)
  Pallas kernels  23.9 us (17%)
  other arithmetic  5.28 us (4%)
    ppermute x6, starting transfers between devices, on_device(): lax.ppermute(block, 'ado', onward(step))  21 us
    ppermute x6, starting transfers between devices, over_groups(): lax.ppermute(parts[shift].astype(LINK), 'grp', ring).astype(F32)  20.9 us
    pallas_call x2, Pallas kernels, terms(): pl.pallas_call(functools.partial(terms_kernel, sources, modes, windows, p...  18.5 us
    all_to_all x1, waiting for transfers between devices, on_device(): lax.all_to_all((near + far.astype(F32)).astype(LINK), 'ado', split_axis=0...  12.8 us
    ppermute x1, waiting for transfers between devices, on_device(): far = lax.ppermute(over_groups(far).astype(LINK), 'ado', onward(4))  10 us
    ppermute x1, starting transfers between devices, on_device(): heard_far = lax.ppermute(heard, 'ado', onward(4))  8.22 us
    all_to_all x1, starting transfers between devices, on_device(): lax.all_to_all(said, 'ado', split_axis=0, concat_axis=0, tiled=True, axis...  7.11 us
    ppermute x6, waiting for transfers between devices, over_groups(): lax.ppermute(parts[shift].astype(LINK), 'grp', ring).astype(F32)  5.73 us
  transfers between devices with their start and end apart: 18, of which 7 were waited for; matrix products, arithmetic and copies ran while one was open for 2% of the time, Pallas kernels for 16%

profile of v14, /device:TPU:194, one launch (start us, length us, event | category | flops | bytes accessed | tf_op | source)
XLA Modules:
  0.0 139.2 jit_solution(7905875048177131366)
XLA Ops:
  0.0 0.7 copy.15
  0.7 0.6 pad_add_fusion.spot_ref
  1.3 1.7 %shard_map.109 = s32[8,40,128]{2,1,0:T(8,128)} custom-call(s32[4]{0:T(128)} %pad_add_fusion.spot_ref, s32[16,32]{1,0:T(8,128)} %up_ref.1, s32[3,16]{1,0:T(4,128)} %bitcast.24, s32[3,16]{1,0:T(4,128)} %bitcast.23), custom_call_target="tpu_custom_call" | custom-call | flops 1000000 | bytes 262144 | tf_op jit(solution)/shard_map/pallas_call | solution.py:315
  3.0 2.0 %collective-permute-start.1 = (bf16[128,64,128]{2,1,0:T(8,128)(2,1)}, bf16[128,64,128]{2,1,0:T(8,128)(2,1)}, u32[]{:S(2)}, u32[]{:S(2)}) collective-permute-start(bf16[128,64,128]{2,1,0:T(8,128)(2,1)} %bitcast.19), channel_id=1, source_target_pairs={{0,1},{1,0},{2,3},{3,2},{4,5},{5,4},{6,7},{7,6},{8,9},{9,8},{10,11... | collective-permute-start | bytes 6291464 | tf_op jit(solution)/shard_map/ppermute | solution.py:354
  5.1 7.1 %all-to-all-start = ((s32[8,40,128]{2,1,0:T(8,128)}), s32[8,40,128]{2,1,0:T(8,128)S(1)}, u32[]{:S(2)}, u32[]{:S(2)}) async-start(s32[8,40,128]{2,1,0:T(8,128)} %shard_map.109), calls=%async_computation | async-start | bytes 327680 | tf_op jit(solution)/shard_map/all_to_all | solution.py:350
  12.2 2.9 %collective-permute-start = (s32[384]{0:T(512)S(1)}, s32[384]{0:T(512)S(1)}, u32[]{:S(2)}, u32[]{:S(2)}) collective-permute-start(s32[384]{0:T(512)S(1)} %bitcast.21), channel_id=1, source_target_pairs={{0,1},{1,0},{2,3},{3,2},{4,5},{5,4},{6,7},{7,6},{8,9},{9,8},{10,11... | collective-permute-start | bytes 4616 | tf_op jit(solution)/shard_map/ppermute | solution.py:355
  15.1 1.5 %fusion.2 = bf16[32,128,128]{2,1,0:T(8,128)(2,1)S(1)} fusion(bf16[32,64,64]{2,1,0:T(8,128)(2,1)} %param.18), kind=kLoop, calls=%fused_computation.5 | loop fusion | flops 4194304 | bytes 1310720 | tf_op jit(solution)/shard_map/concatenate | solution.py:23
  16.6 5.0 %all-to-all-done = s32[8,40,128]{2,1,0:T(8,128)S(1)} async-done(((s32[8,40,128]{2,1,0:T(8,128)}), s32[8,40,128]{2,1,0:T(8,128)S(1)}, u32[]{:S(2)}, u32[]{:S(2)}) %all-to-all-start) | async-done | bytes 163872 | tf_op jit(solution)/shard_map/all_to_all | solution.py:350
  21.6 8.2 %collective-permute-start.2 = (s32[40,128]{1,0:T(8,128)S(1)}, s32[40,128]{1,0:T(8,128)S(1)}, u32[]{:S(2)}, u32[]{:S(2)}) collective-permute-start(s32[40,128]{1,0:T(8,128)S(1)} %reduce_sum.27.refs_1_), channel_id=1, source_target_pairs={{0,64},{2,66},{4,68},{6,70},{8,72},{10,74},{12,76},{14,78},{16,80}... | collective-permute-start | bytes 61448 | tf_op jit(solution)/shard_map/ppermute | solution.py:357
  29.9 0.1 constant_dynamic-slice_fusion.refs_4_.refs_6_
  29.9 0.1 concatenate.27.refs_3_.refs_5_
  30.2 2.5 %shard_map.110 = (bf16[48,64,128]{2,1,0:T(8,128)(2,1)S(1)}, bf16[48,64,128]{2,1,0:T(8,128)(2,1)S(1)}, bf16[48,64,128]{2,1,0:T(8,128)(2,1)S(1)}, bf16[48,64,128]{...) custom-call(s32[4]{0:T(128)S(1)} %copy-done.2, ...), custom_call_target="tpu_custom_call" | custom-call | bytes 10485760 | tf_op jit(solution)/shard_map/pallas_call | solution.py:78
  32.7 4.0 %collective-permute-start.3 = (bf16[48,64,128]{2,1,0:T(8,128)(2,1)S(1)}, bf16[48,64,128]{2,1,0:T(8,128)(2,1)S(1)}, u32[]{:S(2)}, u32[]{:S(2)}) collective-permute-start(bf16[48,64,128]{2,1,0:T(8,128)(2,1)S(1)} %get-tuple-element.59), channel_id=1, source_target_pairs={{0,16},{2,18},{4,20},{6,22},{8,24},{10,26},{12,28},{14,30},{16,32}... | collective-permute-start | bytes 2359304 | tf_op jit(solution)/shard_map/ppermute | solution.py:365
  36.7 1.9 %collective-permute-start.4 = (bf16[48,64,128]{2,1,0:T(8,128)(2,1)S(1)}, bf16[48,64,128]{2,1,0:T(8,128)(2,1)S(1)}, u32[]{:S(2)}, u32[]{:S(2)}) collective-permute-start(bf16[48,64,128]{2,1,0:T(8,128)(2,1)S(1)} %get-tuple-element.60), channel_id=1, source_target_pairs={{0,112},{2,114},{4,116},{6,118},{8,120},{10,122},{12,124},{14,126}... | collective-permute-start | bytes 2359304 | tf_op jit(solution)/shard_map/ppermute | solution.py:365
  38.6 4.8 %collective-permute-start.5 = (bf16[48,64,128]{2,1,0:T(8,128)(2,1)S(1)}, bf16[48,64,128]{2,1,0:T(8,128)(2,1)S(1)}, u32[]{:S(2)}, u32[]{:S(2)}) collective-permute-start(bf16[48,64,128]{2,1,0:T(8,128)(2,1)S(1)} %get-tuple-element.71), channel_id=1, source_target_pairs={{0,32},{2,34},{4,36},{6,38},{8,40},{10,42},{12,44},{14,46},{16,48}... | collective-permute-start | bytes 2359304 | tf_op jit(solution)/shard_map/ppermute | solution.py:365
  43.5 1.9 %collective-permute-start.6 = (bf16[48,64,128]{2,1,0:T(8,128)(2,1)S(1)}, bf16[48,64,128]{2,1,0:T(8,128)(2,1)S(1)}, u32[]{:S(2)}, u32[]{:S(2)}) collective-permute-start(bf16[48,64,128]{2,1,0:T(8,128)(2,1)S(1)} %get-tuple-element.72), channel_id=1, source_target_pairs={{0,96},{2,98},{4,100},{6,102},{8,104},{10,106},{12,108},{14,110},{... | collective-permute-start | bytes 2359304 | tf_op jit(solution)/shard_map/ppermute | solution.py:365
  45.4 6.3 %collective-permute-start.7 = (bf16[48,64,128]{2,1,0:T(8,128)(2,1)S(1)}, bf16[48,64,128]{2,1,0:T(8,128)(2,1)S(1)}, u32[]{:S(2)}, u32[]{:S(2)}) collective-permute-start(bf16[48,64,128]{2,1,0:T(8,128)(2,1)S(1)} %get-tuple-element.73), channel_id=1, source_target_pairs={{0,16},{2,18},{4,20},{6,22},{8,24},{10,26},{12,28},{14,30},{16,32}... | collective-permute-start | bytes 2359304 | tf_op jit(solution)/shard_map/ppermute | solution.py:365
  51.8 1.9 %collective-permute-start.8 = (bf16[48,64,128]{2,1,0:T(8,128)(2,1)S(1)}, bf16[48,64,128]{2,1,0:T(8,128)(2,1)S(1)}, u32[]{:S(2)}, u32[]{:S(2)}) collective-permute-start(bf16[48,64,128]{2,1,0:T(8,128)(2,1)S(1)} %get-tuple-element.74), channel_id=1, source_target_pairs={{0,112},{2,114},{4,116},{6,118},{8,120},{10,122},{12,124},{14,126}... | collective-permute-start | bytes 2359304 | tf_op jit(solution)/shard_map/ppermute | solution.py:365
  53.7 1.3 shard_map.111
  55.0 8.1 %shard_map.112 = (f32[8,16,16,128]{3,2,1,0:T(8,128)S(1)}, f32[8,16,16,128]{3,2,1,0:T(8,128)S(1)}, f32[8,16,16,128]{3,2,1,0:T(8,128)S(1)}, f32[8,16,16,128]{3,2,1,0:T(8,128)S(1)}) custom-call(s32[4]{0:T(128)S(1)} %copy-done.2, s32[48,128]{1,0:T(8,128)S(1)} %get-tuple-element.58.list_ref, f32[32]{0:T(128)S(1)} %copy-done.3, f32[32]{0:T(128)S(1)} %copy-done.4, ...), custom_call_target="tpu_custom_call" | custom-call | flops 1000000000 | bytes 10485760 | tf_op jit(solution)/shard_map/pallas_call | solution.py:192
  63.1 0.1 convert_element_type.61
  63.2 1.9 %collective-permute-start.14 = (f16[8,16,16,128]{3,2,1,0:T(8,128)(2,1)S(1)}, f16[8,16,16,128]{3,2,1,0:T(8,128)(2,1)S(1)}, u32[]{:S(2)}, u32[]{:S(2)}) collective-permute-start(f16[8,16,16,128]{3,2,1,0:T(8,128)(2,1)S(1)} %convert_element_type.61), channel_id=1, source_target_pairs={{0,384},{128,0},{256,128},{384,256},{1,385},{129,1},{257,129},{385... | collective-permute-start | bytes 1572872 | tf_op jit(solution)/shard_map/ppermute | solution.py:329
  65.2 0.1 convert_element_type.59
  65.2 0.1 convert_element_type.57
  65.3 3.9 %collective-permute-start.13 = (f16[8,16,16,128]{3,2,1,0:T(8,128)(2,1)S(1)}, f16[8,16,16,128]{3,2,1,0:T(8,128)(2,1)S(1)}, u32[]{:S(2)}, u32[]{:S(2)}) collective-permute-start(f16[8,16,16,128]{3,2,1,0:T(8,128)(2,1)S(1)} %convert_element_type.59), channel_id=1, source_target_pairs={{0,128},{128,256},{256,384},{384,0},{1,129},{129,257},{257,385},{3... | collective-permute-start | bytes 1572872 | tf_op jit(solution)/shard_map/ppermute | solution.py:329
  69.3 4.9 %collective-permute-start.12 = (f16[8,16,16,128]{3,2,1,0:T(8,128)(2,1)S(1)}, f16[8,16,16,128]{3,2,1,0:T(8,128)(2,1)S(1)}, u32[]{:S(2)}, u32[]{:S(2)}) collective-permute-start(f16[8,16,16,128]{3,2,1,0:T(8,128)(2,1)S(1)} %convert_element_type.57), channel_id=1, source_target_pairs={{0,256},{128,384},{256,0},{384,128},{1,257},{129,385},{257,1},{385... | collective-permute-start | bytes 1572872 | tf_op jit(solution)/shard_map/ppermute | solution.py:329
  74.2 2.9 %collective-permute-done.8.refs_3_ = bf16[48,64,128]{2,1,0:T(8,128)(2,1)S(1)} collective-permute-done((bf16[48,64,128]{2,1,0:T(8,128)(2,1)S(1)}, bf16[48,64,128]{2,1,0:T(8,128)(2,1)S(1)}, u32[]{:S(2)}, u32[]{:S(2)}) %collective-permute-start.8) | collective-permute-done | bytes 786464 | tf_op jit(solution)/shard_map/ppermute | solution.py:365
  77.1 10.4 %shard_map.113 = (f32[8,16,16,128]{3,2,1,0:T(8,128)S(1)}, f32[8,16,16,128]{3,2,1,0:T(8,128)S(1)}, f32[8,16,16,128]{3,2,1,0:T(8,128)S(1)}, f32[8,16,16,128]{3,2,1,0:T(8,128)S(1)}) custom-call(s32[4]{0:T(128)S(1)} %copy-done.2, s32[48,128]{1,0:T(8,128)S(1)} %get-tuple-element.70.list_ref, f32[32]{0:T(128)S(1)} %copy-done.3, f32[32]{0:T(128)S(1)} %copy-done.4, ...), custom_call_target="tpu_custom_call" | custom-call | flops 1000000000 | bytes 10485760 | tf_op jit(solution)/shard_map/pallas_call | solution.py:192
  87.5 0.1 convert_element_type.55
  87.6 1.9 %collective-permute-start.11 = (f16[8,16,16,128]{3,2,1,0:T(8,128)(2,1)S(1)}, f16[8,16,16,128]{3,2,1,0:T(8,128)(2,1)S(1)}, u32[]{:S(2)}, u32[]{:S(2)}) collective-permute-start(f16[8,16,16,128]{3,2,1,0:T(8,128)(2,1)S(1)} %convert_element_type.55), channel_id=1, source_target_pairs={{0,384},{128,0},{256,128},{384,256},{1,385},{129,1},{257,129},{385... | collective-permute-start | bytes 1572872 | tf_op jit(solution)/shard_map/ppermute | solution.py:329
  89.5 0.1 convert_element_type.53
  89.6 3.9 %collective-permute-start.10 = (f16[8,16,16,128]{3,2,1,0:T(8,128)(2,1)S(1)}, f16[8,16,16,128]{3,2,1,0:T(8,128)(2,1)S(1)}, u32[]{:S(2)}, u32[]{:S(2)}) collective-permute-start(f16[8,16,16,128]{3,2,1,0:T(8,128)(2,1)S(1)} %convert_element_type.53), channel_id=1, source_target_pairs={{0,128},{128,256},{256,384},{384,0},{1,129},{129,257},{257,385},{3... | collective-permute-start | bytes 1572872 | tf_op jit(solution)/shard_map/ppermute | solution.py:329
  93.5 0.1 convert_element_type.51
  93.6 4.2 %collective-permute-start.9 = (f16[8,16,16,128]{3,2,1,0:T(8,128)(2,1)S(1)}, f16[8,16,16,128]{3,2,1,0:T(8,128)(2,1)S(1)}, u32[]{:S(2)}, u32[]{:S(2)}) collective-permute-start(f16[8,16,16,128]{3,2,1,0:T(8,128)(2,1)S(1)} %convert_element_type.51), channel_id=1, source_target_pairs={{0,256},{128,384},{256,0},{384,128},{1,257},{129,385},{257,1},{385... | collective-permute-start | bytes 1572872 | tf_op jit(solution)/shard_map/ppermute | solution.py:329
  97.9 0.3 add_convert_fusion.1
  98.2 4.7 %collective-permute-start.15 = (f16[8,16,16,128]{3,2,1,0:T(8,128)(2,1)S(1)}, f16[8,16,16,128]{3,2,1,0:T(8,128)(2,1)S(1)}, u32[]{:S(2)}, u32[]{:S(2)}) collective-permute-start(f16[8,16,16,128]{3,2,1,0:T(8,128)(2,1)S(1)} %add_convert_fusion.1), channel_id=1, source_target_pairs={{0,64},{2,66},{4,68},{6,70},{8,72},{10,74},{12,76},{14,78},{16,80}... | collective-permute-start | bytes 1572872 | tf_op jit(solution)/shard_map/ppermute | solution.py:373
  102.9 0.1 collective-permute-done.11
  103.0 2.7 %collective-permute-done.10 = f16[8,16,16,128]{3,2,1,0:T(8,128)(2,1)S(1)} collective-permute-done((f16[8,16,16,128]{3,2,1,0:T(8,128)(2,1)S(1)}, f16[8,16,16,128]{3,2,1,0:T(8,128)(2,1)S(1)}, u32[]{:S(2)}, u32[]{:S(2)}) %collective-permute-start.10) | collective-permute-done | bytes 524320 | tf_op jit(solution)/shard_map/ppermute | solution.py:329
  105.7 2.9 %collective-permute-done.9 = f16[8,16,16,128]{3,2,1,0:T(8,128)(2,1)S(1)} collective-permute-done((f16[8,16,16,128]{3,2,1,0:T(8,128)(2,1)S(1)}, f16[8,16,16,128]{3,2,1,0:T(8,128)(2,1)S(1)}, u32[]{:S(2)}, u32[]{:S(2)}) %collective-permute-start.9) | collective-permute-done | bytes 524320 | tf_op jit(solution)/shard_map/ppermute | solution.py:329
  108.6 10.0 %collective-permute-done.15 = f16[8,16,16,128]{3,2,1,0:T(8,128)(2,1)S(1)} collective-permute-done((f16[8,16,16,128]{3,2,1,0:T(8,128)(2,1)S(1)}, f16[8,16,16,128]{3,2,1,0:T(8,128)(2,1)S(1)}, u32[]{:S(2)}, u32[]{:S(2)}) %collective-permute-start.15) | collective-permute-done | bytes 524320 | tf_op jit(solution)/shard_map/ppermute | solution.py:373
  118.7 1.2 add_convert_fusion
  119.9 5.2 %all-to-all-start.1 = ((f16[8,16,16,128]{3,2,1,0:T(8,128)(2,1)}), f16[8,16,16,128]{3,2,1,0:T(8,128)(2,1)S(1)}, u32[]{:S(2)}, u32[]{:S(2)}) async-start(f16[8,16,16,128]{3,2,1,0:T(8,128)(2,1)} %add_convert_fusion), calls=%async_computation.1 | async-start | bytes 1048576 | tf_op jit(solution)/shard_map/all_to_all | solution.py:375
  125.1 0.2 select_reduce_fusion
  125.3 0.2 convolution_bitcast_fusion
  125.5 0.1 fusion.18
  125.6 12.8 %all-to-all-done.1 = f16[8,16,16,128]{3,2,1,0:T(8,128)(2,1)S(1)} async-done(((f16[8,16,16,128]{3,2,1,0:T(8,128)(2,1)}), f16[8,16,16,128]{3,2,1,0:T(8,128)(2,1)S(1)}, u32[]{:S(2)}, u32[]{:S(2)}) %all-to-all-start.1) | async-done | bytes 524320 | tf_op jit(solution)/shard_map/all_to_all | solution.py:375
  138.4 0.1 convert_reduce_fusion
  138.5 0.8 fusion.4
  (28 shorter events, 0.1 us)
Async XLA Ops:
  0.0 29.9 %copy-start.5 = (bf16[64,64]{1,0:T(8,128)(2,1)S(1)}, bf16[64,64]{1,0:T(8,128)(2,1)}, u32[]{:S(2)}) copy-start(bf16[64,64]{1,0:T(8,128)(2,1)} %param.17) | copy-start | bytes 24580
  3.0 27.1 %copy-start = (bf16[1,1,128,64,128]{4,3,2,1,0:T(8,128)(2,1)S(1)}, bf16[1,1,128,64,128]{4,3,2,1,0:T(8,128)(2,1)}, u32[]{:S(2)}) copy-start(bf16[1,1,128,64,128]{4,3,2,1,0:T(8,128)(2,1)} %param.11) | copy-start | bytes 6291460
  3.0 27.1 %copy-start.2 = (s32[4]{0:T(128)S(1)}, s32[4]{0:T(128)}, u32[]{:S(2)}) copy-start(s32[4]{0:T(128)} %pad_add_fusion.spot_ref) | copy-start | bytes 52
  3.0 27.1 %collective-permute-start.1 = (bf16[128,64,128]{2,1,0:T(8,128)(2,1)}, bf16[128,64,128]{2,1,0:T(8,128)(2,1)}, u32[]{:S(2)}, u32[]{:S(2)}) collective-permute-start(bf16[128,64,128]{2,1,0:T(8,128)(2,1)} %bitcast.19), channel_id=1, source_target_pairs={{0,1},{1,0},{2,3},{3,2},{4,5},{5,4},{6,7},{7,6},{8,9},{9,8},{10,11... | collective-permute-start | bytes 6291464 | tf_op jit(solution)/shard_map/ppermute | solution.py:354
  5.1 16.5 %all-to-all-start = ((s32[8,40,128]{2,1,0:T(8,128)}), s32[8,40,128]{2,1,0:T(8,128)S(1)}, u32[]{:S(2)}, u32[]{:S(2)}) async-start(s32[8,40,128]{2,1,0:T(8,128)} %shard_map.109), calls=%async_computation | async-start | bytes 327680 | tf_op jit(solution)/shard_map/all_to_all | solution.py:350
  12.2 17.9 %collective-permute-start = (s32[384]{0:T(512)S(1)}, s32[384]{0:T(512)S(1)}, u32[]{:S(2)}, u32[]{:S(2)}) collective-permute-start(s32[384]{0:T(512)S(1)} %bitcast.21), channel_id=1, source_target_pairs={{0,1},{1,0},{2,3},{3,2},{4,5},{5,4},{6,7},{7,6},{8,9},{9,8},{10,11... | collective-permute-start | bytes 4616 | tf_op jit(solution)/shard_map/ppermute | solution.py:355
  21.6 11.0 %collective-permute-start.2 = (s32[40,128]{1,0:T(8,128)S(1)}, s32[40,128]{1,0:T(8,128)S(1)}, u32[]{:S(2)}, u32[]{:S(2)}) collective-permute-start(s32[40,128]{1,0:T(8,128)S(1)} %reduce_sum.27.refs_1_), channel_id=1, source_target_pairs={{0,64},{2,66},{4,68},{6,70},{8,72},{10,74},{12,76},{14,78},{16,80}... | collective-permute-start | bytes 61448 | tf_op jit(solution)/shard_map/ppermute | solution.py:357
  30.1 24.9 %copy-start.1 = (bf16[16,16,128]{2,1,0:T(8,128)(2,1)S(1)}, bf16[16,16,128]{2,1,0:T(8,128)(2,1)}, u32[]{:S(2)}) copy-start(bf16[16,16,128]{2,1,0:T(8,128)(2,1)} %refs_7_) | copy-start | bytes 196612
  30.1 24.9 %copy-start.3 = (f32[32]{0:T(128)S(1)}, f32[32]{0:T(128)}, u32[]{:S(2)}) copy-start(f32[32]{0:T(128)} %re_ref.3) | copy-start | bytes 388
  30.1 24.9 %copy-start.4 = (f32[32]{0:T(128)S(1)}, f32[32]{0:T(128)}, u32[]{:S(2)}) copy-start(f32[32]{0:T(128)} %im_ref.3) | copy-start | bytes 388
  32.7 19.1 %collective-permute-start.3 = (bf16[48,64,128]{2,1,0:T(8,128)(2,1)S(1)}, bf16[48,64,128]{2,1,0:T(8,128)(2,1)S(1)}, u32[]{:S(2)}, u32[]{:S(2)}) collective-permute-start(bf16[48,64,128]{2,1,0:T(8,128)(2,1)S(1)} %get-tuple-element.59), channel_id=1, source_target_pairs={{0,16},{2,18},{4,20},{6,22},{8,24},{10,26},{12,28},{14,30},{16,32}... | collective-permute-start | bytes 2359304 | tf_op jit(solution)/shard_map/ppermute | solution.py:365
  36.7 18.3 %collective-permute-start.4 = (bf16[48,64,128]{2,1,0:T(8,128)(2,1)S(1)}, bf16[48,64,128]{2,1,0:T(8,128)(2,1)S(1)}, u32[]{:S(2)}, u32[]{:S(2)}) collective-permute-start(bf16[48,64,128]{2,1,0:T(8,128)(2,1)S(1)} %get-tuple-element.60), channel_id=1, source_target_pairs={{0,112},{2,114},{4,116},{6,118},{8,120},{10,122},{12,124},{14,126}... | collective-permute-start | bytes 2359304 | tf_op jit(solution)/shard_map/ppermute | solution.py:365
  38.6 26.7 %collective-permute-start.5 = (bf16[48,64,128]{2,1,0:T(8,128)(2,1)S(1)}, bf16[48,64,128]{2,1,0:T(8,128)(2,1)S(1)}, u32[]{:S(2)}, u32[]{:S(2)}) collective-permute-start(bf16[48,64,128]{2,1,0:T(8,128)(2,1)S(1)} %get-tuple-element.71), channel_id=1, source_target_pairs={{0,32},{2,34},{4,36},{6,38},{8,40},{10,42},{12,44},{14,46},{16,48}... | collective-permute-start | bytes 2359304 | tf_op jit(solution)/shard_map/ppermute | solution.py:365
  43.5 25.8 %collective-permute-start.6 = (bf16[48,64,128]{2,1,0:T(8,128)(2,1)S(1)}, bf16[48,64,128]{2,1,0:T(8,128)(2,1)S(1)}, u32[]{:S(2)}, u32[]{:S(2)}) collective-permute-start(bf16[48,64,128]{2,1,0:T(8,128)(2,1)S(1)} %get-tuple-element.72), channel_id=1, source_target_pairs={{0,96},{2,98},{4,100},{6,102},{8,104},{10,106},{12,108},{14,110},{... | collective-permute-start | bytes 2359304 | tf_op jit(solution)/shard_map/ppermute | solution.py:365
  45.4 28.8 %collective-permute-start.7 = (bf16[48,64,128]{2,1,0:T(8,128)(2,1)S(1)}, bf16[48,64,128]{2,1,0:T(8,128)(2,1)S(1)}, u32[]{:S(2)}, u32[]{:S(2)}) collective-permute-start(bf16[48,64,128]{2,1,0:T(8,128)(2,1)S(1)} %get-tuple-element.73), channel_id=1, source_target_pairs={{0,16},{2,18},{4,20},{6,22},{8,24},{10,26},{12,28},{14,30},{16,32}... | collective-permute-start | bytes 2359304 | tf_op jit(solution)/shard_map/ppermute | solution.py:365
  51.8 25.4 %collective-permute-start.8 = (bf16[48,64,128]{2,1,0:T(8,128)(2,1)S(1)}, bf16[48,64,128]{2,1,0:T(8,128)(2,1)S(1)}, u32[]{:S(2)}, u32[]{:S(2)}) collective-permute-start(bf16[48,64,128]{2,1,0:T(8,128)(2,1)S(1)} %get-tuple-element.74), channel_id=1, source_target_pairs={{0,112},{2,114},{4,116},{6,118},{8,120},{10,122},{12,124},{14,126}... | collective-permute-start | bytes 2359304 | tf_op jit(solution)/shard_map/ppermute | solution.py:365
  63.2 30.4 %collective-permute-start.14 = (f16[8,16,16,128]{3,2,1,0:T(8,128)(2,1)S(1)}, f16[8,16,16,128]{3,2,1,0:T(8,128)(2,1)S(1)}, u32[]{:S(2)}, u32[]{:S(2)}) collective-permute-start(f16[8,16,16,128]{3,2,1,0:T(8,128)(2,1)S(1)} %convert_element_type.61), channel_id=1, source_target_pairs={{0,384},{128,0},{256,128},{384,256},{1,385},{129,1},{257,129},{385... | collective-permute-start | bytes 1572872 | tf_op jit(solution)/shard_map/ppermute | solution.py:329
  65.3 32.6 %collective-permute-start.13 = (f16[8,16,16,128]{3,2,1,0:T(8,128)(2,1)S(1)}, f16[8,16,16,128]{3,2,1,0:T(8,128)(2,1)S(1)}, u32[]{:S(2)}, u32[]{:S(2)}) collective-permute-start(f16[8,16,16,128]{3,2,1,0:T(8,128)(2,1)S(1)} %convert_element_type.59), channel_id=1, source_target_pairs={{0,128},{128,256},{256,384},{384,0},{1,129},{129,257},{257,385},{3... | collective-permute-start | bytes 1572872 | tf_op jit(solution)/shard_map/ppermute | solution.py:329
  69.3 28.6 %collective-permute-start.12 = (f16[8,16,16,128]{3,2,1,0:T(8,128)(2,1)S(1)}, f16[8,16,16,128]{3,2,1,0:T(8,128)(2,1)S(1)}, u32[]{:S(2)}, u32[]{:S(2)}) collective-permute-start(f16[8,16,16,128]{3,2,1,0:T(8,128)(2,1)S(1)} %convert_element_type.57), channel_id=1, source_target_pairs={{0,256},{128,384},{256,0},{384,128},{1,257},{129,385},{257,1},{385... | collective-permute-start | bytes 1572872 | tf_op jit(solution)/shard_map/ppermute | solution.py:329
  87.6 15.4 %collective-permute-start.11 = (f16[8,16,16,128]{3,2,1,0:T(8,128)(2,1)S(1)}, f16[8,16,16,128]{3,2,1,0:T(8,128)(2,1)S(1)}, u32[]{:S(2)}, u32[]{:S(2)}) collective-permute-start(f16[8,16,16,128]{3,2,1,0:T(8,128)(2,1)S(1)} %convert_element_type.55), channel_id=1, source_target_pairs={{0,384},{128,0},{256,128},{384,256},{1,385},{129,1},{257,129},{385... | collective-permute-start | bytes 1572872 | tf_op jit(solution)/shard_map/ppermute | solution.py:329
  89.6 16.1 %collective-permute-start.10 = (f16[8,16,16,128]{3,2,1,0:T(8,128)(2,1)S(1)}, f16[8,16,16,128]{3,2,1,0:T(8,128)(2,1)S(1)}, u32[]{:S(2)}, u32[]{:S(2)}) collective-permute-start(f16[8,16,16,128]{3,2,1,0:T(8,128)(2,1)S(1)} %convert_element_type.53), channel_id=1, source_target_pairs={{0,128},{128,256},{256,384},{384,0},{1,129},{129,257},{257,385},{3... | collective-permute-start | bytes 1572872 | tf_op jit(solution)/shard_map/ppermute | solution.py:329
  93.6 15.0 %collective-permute-start.9 = (f16[8,16,16,128]{3,2,1,0:T(8,128)(2,1)S(1)}, f16[8,16,16,128]{3,2,1,0:T(8,128)(2,1)S(1)}, u32[]{:S(2)}, u32[]{:S(2)}) collective-permute-start(f16[8,16,16,128]{3,2,1,0:T(8,128)(2,1)S(1)} %convert_element_type.51), channel_id=1, source_target_pairs={{0,256},{128,384},{256,0},{384,128},{1,257},{129,385},{257,1},{385... | collective-permute-start | bytes 1572872 | tf_op jit(solution)/shard_map/ppermute | solution.py:329
  98.2 20.4 %collective-permute-start.15 = (f16[8,16,16,128]{3,2,1,0:T(8,128)(2,1)S(1)}, f16[8,16,16,128]{3,2,1,0:T(8,128)(2,1)S(1)}, u32[]{:S(2)}, u32[]{:S(2)}) collective-permute-start(f16[8,16,16,128]{3,2,1,0:T(8,128)(2,1)S(1)} %add_convert_fusion.1), channel_id=1, source_target_pairs={{0,64},{2,66},{4,68},{6,70},{8,72},{10,74},{12,76},{14,78},{16,80}... | collective-permute-start | bytes 1572872 | tf_op jit(solution)/shard_map/ppermute | solution.py:373
  118.7 6.4 %copy-start.6 = (s32[16,3]{0,1:T(4,128)S(1)}, s32[16,3]{0,1:T(4,128)}, u32[]{:S(2)}) copy-start(s32[16,3]{0,1:T(4,128)} %param.14) | copy-start | bytes 580
  118.7 6.4 %copy-start.7 = (f32[128]{0:T(128)S(1)}, f32[128]{0:T(128)}, u32[]{:S(2)}) copy-start(f32[128]{0:T(128)} %param.21) | copy-start | bytes 1540
  119.9 18.5 %all-to-all-start.1 = ((f16[8,16,16,128]{3,2,1,0:T(8,128)(2,1)}), f16[8,16,16,128]{3,2,1,0:T(8,128)(2,1)S(1)}, u32[]{:S(2)}, u32[]{:S(2)}) async-start(f16[8,16,16,128]{3,2,1,0:T(8,128)(2,1)} %add_convert_fusion), calls=%async_computation.1 | async-start | bytes 1048576 | tf_op jit(solution)/shard_map/all_to_all | solution.py:375

commit v15 on v14

--- a/solution.py
+++ b/solution.py
@@ -324,7 +324,7 @@
 def over_groups(parts):
     count = len(parts)
     total = parts[0]
-    for shift in (2, 1, 3):
+    for shift in (1, 3, 2):
         ring = [(i, (i + shift) % count) for i in range(count)]
         total = total + lax.ppermute(parts[shift].astype(LINK), "grp", ring).astype(F32)
     return total

time: 140 us -> 142 us (1.014)
  the two profiles are of different devices: /device:TPU:194 before, /device:TPU:8 now
where the time goes in v15:
time: 142 us; the launch traced here: 141 us
  starting transfers between devices  79.5 us (56%)
  waiting for transfers between devices  32.8 us (23%)
  Pallas kernels  22.3 us (16%)
  other arithmetic  5.28 us (4%)
    ppermute x6, starting transfers between devices, on_device(): lax.ppermute(block, 'ado', onward(step))  23.7 us
    ppermute x6, starting transfers between devices, over_groups(): lax.ppermute(parts[shift].astype(LINK), 'grp', ring).astype(F32)  21.4 us
    pallas_call x2, Pallas kernels, terms(): pl.pallas_call(functools.partial(terms_kernel, sources, modes, windows, p...  16.9 us
    all_to_all x1, waiting for transfers between devices, on_device(): lax.all_to_all((near + far.astype(F32)).astype(LINK), 'ado', split_axis=0...  11.3 us
    ppermute x6, waiting for transfers between devices, over_groups(): lax.ppermute(parts[shift].astype(LINK), 'grp', ring).astype(F32)  10.9 us
    ppermute x1, starting transfers between devices, on_device(): heard_far = lax.ppermute(heard, 'ado', onward(4))  9.33 us
    all_to_all x1, starting transfers between devices, on_device(): lax.all_to_all(said, 'ado', split_axis=0, concat_axis=0, tiled=True, axis...  9.12 us
    ppermute x1, waiting for transfers between devices, on_device(): far = lax.ppermute(over_groups(far).astype(LINK), 'ado', onward(4))  7.3 us
  transfers between devices with their start and end apart: 18, of which 7 were waited for; matrix products, arithmetic and copies ran while one was open for 2% of the time, Pallas kernels for 15%

profile of v15, /device:TPU:8, one launch (start us, length us, event | category | flops | bytes accessed | tf_op | source)
XLA Modules:
  0.0 141.4 jit_solution(16958384290666903840)
XLA Ops:
  0.0 0.7 copy.15
  0.7 0.6 pad_add_fusion.spot_ref
  1.3 1.7 %shard_map.109 = s32[8,40,128]{2,1,0:T(8,128)} custom-call(s32[4]{0:T(128)} %pad_add_fusion.spot_ref, s32[16,32]{1,0:T(8,128)} %up_ref.1, s32[3,16]{1,0:T(4,128)} %bitcast.24, s32[3,16]{1,0:T(4,128)} %bitcast.23), custom_call_target="tpu_custom_call" | custom-call | flops 1000000 | bytes 262144 | tf_op jit(solution)/shard_map/pallas_call | solution.py:315
  3.0 2.0 %collective-permute-start.1 = (bf16[128,64,128]{2,1,0:T(8,128)(2,1)}, bf16[128,64,128]{2,1,0:T(8,128)(2,1)}, u32[]{:S(2)}, u32[]{:S(2)}) collective-permute-start(bf16[128,64,128]{2,1,0:T(8,128)(2,1)} %bitcast.19), channel_id=1, source_target_pairs={{0,1},{1,0},{2,3},{3,2},{4,5},{5,4},{6,7},{7,6},{8,9},{9,8},{10,11... | collective-permute-start | bytes 6291464 | tf_op jit(solution)/shard_map/ppermute | solution.py:354
  5.1 9.1 %all-to-all-start = ((s32[8,40,128]{2,1,0:T(8,128)}), s32[8,40,128]{2,1,0:T(8,128)S(1)}, u32[]{:S(2)}, u32[]{:S(2)}) async-start(s32[8,40,128]{2,1,0:T(8,128)} %shard_map.109), calls=%async_computation | async-start | bytes 327680 | tf_op jit(solution)/shard_map/all_to_all | solution.py:350
  14.2 3.3 %collective-permute-start = (s32[384]{0:T(512)S(1)}, s32[384]{0:T(512)S(1)}, u32[]{:S(2)}, u32[]{:S(2)}) collective-permute-start(s32[384]{0:T(512)S(1)} %bitcast.21), channel_id=1, source_target_pairs={{0,1},{1,0},{2,3},{3,2},{4,5},{5,4},{6,7},{7,6},{8,9},{9,8},{10,11... | collective-permute-start | bytes 4616 | tf_op jit(solution)/shard_map/ppermute | solution.py:355
  17.5 1.5 %fusion.2 = bf16[32,128,128]{2,1,0:T(8,128)(2,1)S(1)} fusion(bf16[32,64,64]{2,1,0:T(8,128)(2,1)} %param.18), kind=kLoop, calls=%fused_computation.5 | loop fusion | flops 4194304 | bytes 1310720 | tf_op jit(solution)/shard_map/concatenate | solution.py:23
  19.0 3.1 %all-to-all-done = s32[8,40,128]{2,1,0:T(8,128)S(1)} async-done(((s32[8,40,128]{2,1,0:T(8,128)}), s32[8,40,128]{2,1,0:T(8,128)S(1)}, u32[]{:S(2)}, u32[]{:S(2)}) %all-to-all-start) | async-done | bytes 163872 | tf_op jit(solution)/shard_map/all_to_all | solution.py:350
  22.2 9.3 %collective-permute-start.2 = (s32[40,128]{1,0:T(8,128)S(1)}, s32[40,128]{1,0:T(8,128)S(1)}, u32[]{:S(2)}, u32[]{:S(2)}) collective-permute-start(s32[40,128]{1,0:T(8,128)S(1)} %reduce_sum.27.refs_1_), channel_id=1, source_target_pairs={{0,64},{2,66},{4,68},{6,70},{8,72},{10,74},{12,76},{14,78},{16,80}... | collective-permute-start | bytes 61448 | tf_op jit(solution)/shard_map/ppermute | solution.py:357
  31.5 0.1 constant_dynamic-slice_fusion.refs_4_.refs_6_
  31.6 0.1 concatenate.27.refs_3_.refs_5_
  31.8 2.5 %shard_map.110 = (bf16[48,64,128]{2,1,0:T(8,128)(2,1)S(1)}, bf16[48,64,128]{2,1,0:T(8,128)(2,1)S(1)}, bf16[48,64,128]{2,1,0:T(8,128)(2,1)S(1)}, bf16[48,64,128]{...) custom-call(s32[4]{0:T(128)S(1)} %copy-done.2, ...), custom_call_target="tpu_custom_call" | custom-call | bytes 10485760 | tf_op jit(solution)/shard_map/pallas_call | solution.py:78
  34.4 3.4 %collective-permute-start.3 = (bf16[48,64,128]{2,1,0:T(8,128)(2,1)S(1)}, bf16[48,64,128]{2,1,0:T(8,128)(2,1)S(1)}, u32[]{:S(2)}, u32[]{:S(2)}) collective-permute-start(bf16[48,64,128]{2,1,0:T(8,128)(2,1)S(1)} %get-tuple-element.59), channel_id=1, source_target_pairs={{0,16},{2,18},{4,20},{6,22},{8,24},{10,26},{12,28},{14,30},{16,32}... | collective-permute-start | bytes 2359304 | tf_op jit(solution)/shard_map/ppermute | solution.py:365
  37.7 5.3 %collective-permute-start.4 = (bf16[48,64,128]{2,1,0:T(8,128)(2,1)S(1)}, bf16[48,64,128]{2,1,0:T(8,128)(2,1)S(1)}, u32[]{:S(2)}, u32[]{:S(2)}) collective-permute-start(bf16[48,64,128]{2,1,0:T(8,128)(2,1)S(1)} %get-tuple-element.60), channel_id=1, source_target_pairs={{0,112},{2,114},{4,116},{6,118},{8,120},{10,122},{12,124},{14,126}... | collective-permute-start | bytes 2359304 | tf_op jit(solution)/shard_map/ppermute | solution.py:365
  43.1 1.9 %collective-permute-start.5 = (bf16[48,64,128]{2,1,0:T(8,128)(2,1)S(1)}, bf16[48,64,128]{2,1,0:T(8,128)(2,1)S(1)}, u32[]{:S(2)}, u32[]{:S(2)}) collective-permute-start(bf16[48,64,128]{2,1,0:T(8,128)(2,1)S(1)} %get-tuple-element.71), channel_id=1, source_target_pairs={{0,32},{2,34},{4,36},{6,38},{8,40},{10,42},{12,44},{14,46},{16,48}... | collective-permute-start | bytes 2359304 | tf_op jit(solution)/shard_map/ppermute | solution.py:365
  45.0 6.0 %collective-permute-start.6 = (bf16[48,64,128]{2,1,0:T(8,128)(2,1)S(1)}, bf16[48,64,128]{2,1,0:T(8,128)(2,1)S(1)}, u32[]{:S(2)}, u32[]{:S(2)}) collective-permute-start(bf16[48,64,128]{2,1,0:T(8,128)(2,1)S(1)} %get-tuple-element.72), channel_id=1, source_target_pairs={{0,96},{2,98},{4,100},{6,102},{8,104},{10,106},{12,108},{14,110},{... | collective-permute-start | bytes 2359304 | tf_op jit(solution)/shard_map/ppermute | solution.py:365
  51.0 1.9 %collective-permute-start.7 = (bf16[48,64,128]{2,1,0:T(8,128)(2,1)S(1)}, bf16[48,64,128]{2,1,0:T(8,128)(2,1)S(1)}, u32[]{:S(2)}, u32[]{:S(2)}) collective-permute-start(bf16[48,64,128]{2,1,0:T(8,128)(2,1)S(1)} %get-tuple-element.73), channel_id=1, source_target_pairs={{0,16},{2,18},{4,20},{6,22},{8,24},{10,26},{12,28},{14,30},{16,32}... | collective-permute-start | bytes 2359304 | tf_op jit(solution)/shard_map/ppermute | solution.py:365
  53.0 5.1 %collective-permute-start.8 = (bf16[48,64,128]{2,1,0:T(8,128)(2,1)S(1)}, bf16[48,64,128]{2,1,0:T(8,128)(2,1)S(1)}, u32[]{:S(2)}, u32[]{:S(2)}) collective-permute-start(bf16[48,64,128]{2,1,0:T(8,128)(2,1)S(1)} %get-tuple-element.74), channel_id=1, source_target_pairs={{0,112},{2,114},{4,116},{6,118},{8,120},{10,122},{12,124},{14,126}... | collective-permute-start | bytes 2359304 | tf_op jit(solution)/shard_map/ppermute | solution.py:365
  58.1 1.3 shard_map.111
  59.5 7.8 %shard_map.112 = (f32[8,16,16,128]{3,2,1,0:T(8,128)S(1)}, f32[8,16,16,128]{3,2,1,0:T(8,128)S(1)}, f32[8,16,16,128]{3,2,1,0:T(8,128)S(1)}, f32[8,16,16,128]{3,2,1,0:T(8,128)S(1)}) custom-call(s32[4]{0:T(128)S(1)} %copy-done.2, s32[48,128]{1,0:T(8,128)S(1)} %get-tuple-element.58.list_ref, f32[32]{0:T(128)S(1)} %copy-done.3, f32[32]{0:T(128)S(1)} %copy-done.4, ...), custom_call_target="tpu_custom_call" | custom-call | flops 1000000000 | bytes 10485760 | tf_op jit(solution)/shard_map/pallas_call | solution.py:192
  67.2 0.1 convert_element_type.61
  67.3 5.0 %collective-permute-start.14 = (f16[8,16,16,128]{3,2,1,0:T(8,128)(2,1)S(1)}, f16[8,16,16,128]{3,2,1,0:T(8,128)(2,1)S(1)}, u32[]{:S(2)}, u32[]{:S(2)}) collective-permute-start(f16[8,16,16,128]{3,2,1,0:T(8,128)(2,1)S(1)} %convert_element_type.61), channel_id=1, source_target_pairs={{0,256},{128,384},{256,0},{384,128},{1,257},{129,385},{257,1},{385... | collective-permute-start | bytes 1572872 | tf_op jit(solution)/shard_map/ppermute | solution.py:329
  72.3 0.1 convert_element_type.59
  72.4 0.1 convert_element_type.57
  72.5 3.4 %collective-permute-start.13 = (f16[8,16,16,128]{3,2,1,0:T(8,128)(2,1)S(1)}, f16[8,16,16,128]{3,2,1,0:T(8,128)(2,1)S(1)}, u32[]{:S(2)}, u32[]{:S(2)}) collective-permute-start(f16[8,16,16,128]{3,2,1,0:T(8,128)(2,1)S(1)} %convert_element_type.59), channel_id=1, source_target_pairs={{0,384},{128,0},{256,128},{384,256},{1,385},{129,1},{257,129},{385... | collective-permute-start | bytes 1572872 | tf_op jit(solution)/shard_map/ppermute | solution.py:329
  75.9 2.5 %collective-permute-start.12 = (f16[8,16,16,128]{3,2,1,0:T(8,128)(2,1)S(1)}, f16[8,16,16,128]{3,2,1,0:T(8,128)(2,1)S(1)}, u32[]{:S(2)}, u32[]{:S(2)}) collective-permute-start(f16[8,16,16,128]{3,2,1,0:T(8,128)(2,1)S(1)} %convert_element_type.57), channel_id=1, source_target_pairs={{0,128},{128,256},{256,384},{384,0},{1,129},{129,257},{257,385},{3... | collective-permute-start | bytes 1572872 | tf_op jit(solution)/shard_map/ppermute | solution.py:329
  78.4 9.1 %shard_map.113 = (f32[8,16,16,128]{3,2,1,0:T(8,128)S(1)}, f32[8,16,16,128]{3,2,1,0:T(8,128)S(1)}, f32[8,16,16,128]{3,2,1,0:T(8,128)S(1)}, f32[8,16,16,128]{3,2,1,0:T(8,128)S(1)}) custom-call(s32[4]{0:T(128)S(1)} %copy-done.2, s32[48,128]{1,0:T(8,128)S(1)} %get-tuple-element.70.list_ref, f32[32]{0:T(128)S(1)} %copy-done.3, f32[32]{0:T(128)S(1)} %copy-done.4, ...), custom_call_target="tpu_custom_call" | custom-call | flops 1000000000 | bytes 10485760 | tf_op jit(solution)/shard_map/pallas_call | solution.py:192
  87.5 0.1 convert_element_type.55
  87.6 4.0 %collective-permute-start.11 = (f16[8,16,16,128]{3,2,1,0:T(8,128)(2,1)S(1)}, f16[8,16,16,128]{3,2,1,0:T(8,128)(2,1)S(1)}, u32[]{:S(2)}, u32[]{:S(2)}) collective-permute-start(f16[8,16,16,128]{3,2,1,0:T(8,128)(2,1)S(1)} %convert_element_type.55), channel_id=1, source_target_pairs={{0,256},{128,384},{256,0},{384,128},{1,257},{129,385},{257,1},{385... | collective-permute-start | bytes 1572872 | tf_op jit(solution)/shard_map/ppermute | solution.py:329
  91.6 0.1 convert_element_type.53
  91.7 4.1 %collective-permute-start.10 = (f16[8,16,16,128]{3,2,1,0:T(8,128)(2,1)S(1)}, f16[8,16,16,128]{3,2,1,0:T(8,128)(2,1)S(1)}, u32[]{:S(2)}, u32[]{:S(2)}) collective-permute-start(f16[8,16,16,128]{3,2,1,0:T(8,128)(2,1)S(1)} %convert_element_type.53), channel_id=1, source_target_pairs={{0,384},{128,0},{256,128},{384,256},{1,385},{129,1},{257,129},{385... | collective-permute-start | bytes 1572872 | tf_op jit(solution)/shard_map/ppermute | solution.py:329
  95.8 0.1 convert_element_type.51
  95.9 2.4 %collective-permute-start.9 = (f16[8,16,16,128]{3,2,1,0:T(8,128)(2,1)S(1)}, f16[8,16,16,128]{3,2,1,0:T(8,128)(2,1)S(1)}, u32[]{:S(2)}, u32[]{:S(2)}) collective-permute-start(f16[8,16,16,128]{3,2,1,0:T(8,128)(2,1)S(1)} %convert_element_type.51), channel_id=1, source_target_pairs={{0,128},{128,256},{256,384},{384,0},{1,129},{129,257},{257,385},{3... | collective-permute-start | bytes 1572872 | tf_op jit(solution)/shard_map/ppermute | solution.py:329
  98.3 2.1 %collective-permute-done.12 = f16[8,16,16,128]{3,2,1,0:T(8,128)(2,1)S(1)} collective-permute-done((f16[8,16,16,128]{3,2,1,0:T(8,128)(2,1)S(1)}, f16[8,16,16,128]{3,2,1,0:T(8,128)(2,1)S(1)}, u32[]{:S(2)}, u32[]{:S(2)}) %collective-permute-start.12) | collective-permute-done | bytes 524320 | tf_op jit(solution)/shard_map/ppermute | solution.py:329
  100.4 0.3 add_convert_fusion.1
  100.8 4.4 %collective-permute-start.15 = (f16[8,16,16,128]{3,2,1,0:T(8,128)(2,1)S(1)}, f16[8,16,16,128]{3,2,1,0:T(8,128)(2,1)S(1)}, u32[]{:S(2)}, u32[]{:S(2)}) collective-permute-start(f16[8,16,16,128]{3,2,1,0:T(8,128)(2,1)S(1)} %add_convert_fusion.1), channel_id=1, source_target_pairs={{0,64},{2,66},{4,68},{6,70},{8,72},{10,74},{12,76},{14,78},{16,80}... | collective-permute-start | bytes 1572872 | tf_op jit(solution)/shard_map/ppermute | solution.py:373
  105.2 0.7 collective-permute-done.11
  105.8 6.7 %collective-permute-done.10 = f16[8,16,16,128]{3,2,1,0:T(8,128)(2,1)S(1)} collective-permute-done((f16[8,16,16,128]{3,2,1,0:T(8,128)(2,1)S(1)}, f16[8,16,16,128]{3,2,1,0:T(8,128)(2,1)S(1)}, u32[]{:S(2)}, u32[]{:S(2)}) %collective-permute-start.10) | collective-permute-done | bytes 524320 | tf_op jit(solution)/shard_map/ppermute | solution.py:329
  112.5 1.5 %collective-permute-done.9 = f16[8,16,16,128]{3,2,1,0:T(8,128)(2,1)S(1)} collective-permute-done((f16[8,16,16,128]{3,2,1,0:T(8,128)(2,1)S(1)}, f16[8,16,16,128]{3,2,1,0:T(8,128)(2,1)S(1)}, u32[]{:S(2)}, u32[]{:S(2)}) %collective-permute-start.9) | collective-permute-done | bytes 524320 | tf_op jit(solution)/shard_map/ppermute | solution.py:329
  114.0 7.3 %collective-permute-done.15 = f16[8,16,16,128]{3,2,1,0:T(8,128)(2,1)S(1)} collective-permute-done((f16[8,16,16,128]{3,2,1,0:T(8,128)(2,1)S(1)}, f16[8,16,16,128]{3,2,1,0:T(8,128)(2,1)S(1)}, u32[]{:S(2)}, u32[]{:S(2)}) %collective-permute-start.15) | collective-permute-done | bytes 524320 | tf_op jit(solution)/shard_map/ppermute | solution.py:373
  121.3 1.2 add_convert_fusion
  122.5 6.2 %all-to-all-start.1 = ((f16[8,16,16,128]{3,2,1,0:T(8,128)(2,1)}), f16[8,16,16,128]{3,2,1,0:T(8,128)(2,1)S(1)}, u32[]{:S(2)}, u32[]{:S(2)}) async-start(f16[8,16,16,128]{3,2,1,0:T(8,128)(2,1)} %add_convert_fusion), calls=%async_computation.1 | async-start | bytes 1048576 | tf_op jit(solution)/shard_map/all_to_all | solution.py:375
  128.7 0.2 select_reduce_fusion
  128.9 0.2 convolution_bitcast_fusion
  129.1 0.1 fusion.18
  129.2 11.3 %all-to-all-done.1 = f16[8,16,16,128]{3,2,1,0:T(8,128)(2,1)S(1)} async-done(((f16[8,16,16,128]{3,2,1,0:T(8,128)(2,1)}), f16[8,16,16,128]{3,2,1,0:T(8,128)(2,1)S(1)}, u32[]{:S(2)}, u32[]{:S(2)}) %all-to-all-start.1) | async-done | bytes 524320 | tf_op jit(solution)/shard_map/all_to_all | solution.py:375
  140.6 0.1 convert_reduce_fusion
  140.7 0.8 fusion.4
  (28 shorter events, 0.1 us)
Async XLA Ops:
  0.0 31.5 %copy-start.5 = (bf16[64,64]{1,0:T(8,128)(2,1)S(1)}, bf16[64,64]{1,0:T(8,128)(2,1)}, u32[]{:S(2)}) copy-start(bf16[64,64]{1,0:T(8,128)(2,1)} %param.17) | copy-start | bytes 24580
  3.0 28.8 %copy-start = (bf16[1,1,128,64,128]{4,3,2,1,0:T(8,128)(2,1)S(1)}, bf16[1,1,128,64,128]{4,3,2,1,0:T(8,128)(2,1)}, u32[]{:S(2)}) copy-start(bf16[1,1,128,64,128]{4,3,2,1,0:T(8,128)(2,1)} %param.11) | copy-start | bytes 6291460
  3.0 28.8 %copy-start.2 = (s32[4]{0:T(128)S(1)}, s32[4]{0:T(128)}, u32[]{:S(2)}) copy-start(s32[4]{0:T(128)} %pad_add_fusion.spot_ref) | copy-start | bytes 52
  3.0 28.8 %collective-permute-start.1 = (bf16[128,64,128]{2,1,0:T(8,128)(2,1)}, bf16[128,64,128]{2,1,0:T(8,128)(2,1)}, u32[]{:S(2)}, u32[]{:S(2)}) collective-permute-start(bf16[128,64,128]{2,1,0:T(8,128)(2,1)} %bitcast.19), channel_id=1, source_target_pairs={{0,1},{1,0},{2,3},{3,2},{4,5},{5,4},{6,7},{7,6},{8,9},{9,8},{10,11... | collective-permute-start | bytes 6291464 | tf_op jit(solution)/shard_map/ppermute | solution.py:354
  5.1 17.1 %all-to-all-start = ((s32[8,40,128]{2,1,0:T(8,128)}), s32[8,40,128]{2,1,0:T(8,128)S(1)}, u32[]{:S(2)}, u32[]{:S(2)}) async-start(s32[8,40,128]{2,1,0:T(8,128)} %shard_map.109), calls=%async_computation | async-start | bytes 327680 | tf_op jit(solution)/shard_map/all_to_all | solution.py:350
  14.2 17.6 %collective-permute-start = (s32[384]{0:T(512)S(1)}, s32[384]{0:T(512)S(1)}, u32[]{:S(2)}, u32[]{:S(2)}) collective-permute-start(s32[384]{0:T(512)S(1)} %bitcast.21), channel_id=1, source_target_pairs={{0,1},{1,0},{2,3},{3,2},{4,5},{5,4},{6,7},{7,6},{8,9},{9,8},{10,11... | collective-permute-start | bytes 4616 | tf_op jit(solution)/shard_map/ppermute | solution.py:355
  22.2 12.1 %collective-permute-start.2 = (s32[40,128]{1,0:T(8,128)S(1)}, s32[40,128]{1,0:T(8,128)S(1)}, u32[]{:S(2)}, u32[]{:S(2)}) collective-permute-start(s32[40,128]{1,0:T(8,128)S(1)} %reduce_sum.27.refs_1_), channel_id=1, source_target_pairs={{0,64},{2,66},{4,68},{6,70},{8,72},{10,74},{12,76},{14,78},{16,80}... | collective-permute-start | bytes 61448 | tf_op jit(solution)/shard_map/ppermute | solution.py:357
  31.8 27.7 %copy-start.1 = (bf16[16,16,128]{2,1,0:T(8,128)(2,1)S(1)}, bf16[16,16,128]{2,1,0:T(8,128)(2,1)}, u32[]{:S(2)}) copy-start(bf16[16,16,128]{2,1,0:T(8,128)(2,1)} %refs_7_) | copy-start | bytes 196612
  31.8 27.7 %copy-start.3 = (f32[32]{0:T(128)S(1)}, f32[32]{0:T(128)}, u32[]{:S(2)}) copy-start(f32[32]{0:T(128)} %re_ref.3) | copy-start | bytes 388
  31.8 27.7 %copy-start.4 = (f32[32]{0:T(128)S(1)}, f32[32]{0:T(128)}, u32[]{:S(2)}) copy-start(f32[32]{0:T(128)} %im_ref.3) | copy-start | bytes 388
  34.4 18.6 %collective-permute-start.3 = (bf16[48,64,128]{2,1,0:T(8,128)(2,1)S(1)}, bf16[48,64,128]{2,1,0:T(8,128)(2,1)S(1)}, u32[]{:S(2)}, u32[]{:S(2)}) collective-permute-start(bf16[48,64,128]{2,1,0:T(8,128)(2,1)S(1)} %get-tuple-element.59), channel_id=1, source_target_pairs={{0,16},{2,18},{4,20},{6,22},{8,24},{10,26},{12,28},{14,30},{16,32}... | collective-permute-start | bytes 2359304 | tf_op jit(solution)/shard_map/ppermute | solution.py:365
  37.7 21.7 %collective-permute-start.4 = (bf16[48,64,128]{2,1,0:T(8,128)(2,1)S(1)}, bf16[48,64,128]{2,1,0:T(8,128)(2,1)S(1)}, u32[]{:S(2)}, u32[]{:S(2)}) collective-permute-start(bf16[48,64,128]{2,1,0:T(8,128)(2,1)S(1)} %get-tuple-element.60), channel_id=1, source_target_pairs={{0,112},{2,114},{4,116},{6,118},{8,120},{10,122},{12,124},{14,126}... | collective-permute-start | bytes 2359304 | tf_op jit(solution)/shard_map/ppermute | solution.py:365
  43.1 29.4 %collective-permute-start.5 = (bf16[48,64,128]{2,1,0:T(8,128)(2,1)S(1)}, bf16[48,64,128]{2,1,0:T(8,128)(2,1)S(1)}, u32[]{:S(2)}, u32[]{:S(2)}) collective-permute-start(bf16[48,64,128]{2,1,0:T(8,128)(2,1)S(1)} %get-tuple-element.71), channel_id=1, source_target_pairs={{0,32},{2,34},{4,36},{6,38},{8,40},{10,42},{12,44},{14,46},{16,48}... | collective-permute-start | bytes 2359304 | tf_op jit(solution)/shard_map/ppermute | solution.py:365
  45.0 30.9 %collective-permute-start.6 = (bf16[48,64,128]{2,1,0:T(8,128)(2,1)S(1)}, bf16[48,64,128]{2,1,0:T(8,128)(2,1)S(1)}, u32[]{:S(2)}, u32[]{:S(2)}) collective-permute-start(bf16[48,64,128]{2,1,0:T(8,128)(2,1)S(1)} %get-tuple-element.72), channel_id=1, source_target_pairs={{0,96},{2,98},{4,100},{6,102},{8,104},{10,106},{12,108},{14,110},{... | collective-permute-start | bytes 2359304 | tf_op jit(solution)/shard_map/ppermute | solution.py:365
  51.0 27.3 %collective-permute-start.7 = (bf16[48,64,128]{2,1,0:T(8,128)(2,1)S(1)}, bf16[48,64,128]{2,1,0:T(8,128)(2,1)S(1)}, u32[]{:S(2)}, u32[]{:S(2)}) collective-permute-start(bf16[48,64,128]{2,1,0:T(8,128)(2,1)S(1)} %get-tuple-element.73), channel_id=1, source_target_pairs={{0,16},{2,18},{4,20},{6,22},{8,24},{10,26},{12,28},{14,30},{16,32}... | collective-permute-start | bytes 2359304 | tf_op jit(solution)/shard_map/ppermute | solution.py:365
  53.0 25.4 %collective-permute-start.8 = (bf16[48,64,128]{2,1,0:T(8,128)(2,1)S(1)}, bf16[48,64,128]{2,1,0:T(8,128)(2,1)S(1)}, u32[]{:S(2)}, u32[]{:S(2)}) collective-permute-start(bf16[48,64,128]{2,1,0:T(8,128)(2,1)S(1)} %get-tuple-element.74), channel_id=1, source_target_pairs={{0,112},{2,114},{4,116},{6,118},{8,120},{10,122},{12,124},{14,126}... | collective-permute-start | bytes 2359304 | tf_op jit(solution)/shard_map/ppermute | solution.py:365
  67.3 28.6 %collective-permute-start.14 = (f16[8,16,16,128]{3,2,1,0:T(8,128)(2,1)S(1)}, f16[8,16,16,128]{3,2,1,0:T(8,128)(2,1)S(1)}, u32[]{:S(2)}, u32[]{:S(2)}) collective-permute-start(f16[8,16,16,128]{3,2,1,0:T(8,128)(2,1)S(1)} %convert_element_type.61), channel_id=1, source_target_pairs={{0,256},{128,384},{256,0},{384,128},{1,257},{129,385},{257,1},{385... | collective-permute-start | bytes 1572872 | tf_op jit(solution)/shard_map/ppermute | solution.py:329
  72.5 25.9 %collective-permute-start.13 = (f16[8,16,16,128]{3,2,1,0:T(8,128)(2,1)S(1)}, f16[8,16,16,128]{3,2,1,0:T(8,128)(2,1)S(1)}, u32[]{:S(2)}, u32[]{:S(2)}) collective-permute-start(f16[8,16,16,128]{3,2,1,0:T(8,128)(2,1)S(1)} %convert_element_type.59), channel_id=1, source_target_pairs={{0,384},{128,0},{256,128},{384,256},{1,385},{129,1},{257,129},{385... | collective-permute-start | bytes 1572872 | tf_op jit(solution)/shard_map/ppermute | solution.py:329
  75.9 24.6 %collective-permute-start.12 = (f16[8,16,16,128]{3,2,1,0:T(8,128)(2,1)S(1)}, f16[8,16,16,128]{3,2,1,0:T(8,128)(2,1)S(1)}, u32[]{:S(2)}, u32[]{:S(2)}) collective-permute-start(f16[8,16,16,128]{3,2,1,0:T(8,128)(2,1)S(1)} %convert_element_type.57), channel_id=1, source_target_pairs={{0,128},{128,256},{256,384},{384,0},{1,129},{129,257},{257,385},{3... | collective-permute-start | bytes 1572872 | tf_op jit(solution)/shard_map/ppermute | solution.py:329
  87.6 18.3 %collective-permute-start.11 = (f16[8,16,16,128]{3,2,1,0:T(8,128)(2,1)S(1)}, f16[8,16,16,128]{3,2,1,0:T(8,128)(2,1)S(1)}, u32[]{:S(2)}, u32[]{:S(2)}) collective-permute-start(f16[8,16,16,128]{3,2,1,0:T(8,128)(2,1)S(1)} %convert_element_type.55), channel_id=1, source_target_pairs={{0,256},{128,384},{256,0},{384,128},{1,257},{129,385},{257,1},{385... | collective-permute-start | bytes 1572872 | tf_op jit(solution)/shard_map/ppermute | solution.py:329
  91.7 20.8 %collective-permute-start.10 = (f16[8,16,16,128]{3,2,1,0:T(8,128)(2,1)S(1)}, f16[8,16,16,128]{3,2,1,0:T(8,128)(2,1)S(1)}, u32[]{:S(2)}, u32[]{:S(2)}) collective-permute-start(f16[8,16,16,128]{3,2,1,0:T(8,128)(2,1)S(1)} %convert_element_type.53), channel_id=1, source_target_pairs={{0,384},{128,0},{256,128},{384,256},{1,385},{129,1},{257,129},{385... | collective-permute-start | bytes 1572872 | tf_op jit(solution)/shard_map/ppermute | solution.py:329
  95.9 18.1 %collective-permute-start.9 = (f16[8,16,16,128]{3,2,1,0:T(8,128)(2,1)S(1)}, f16[8,16,16,128]{3,2,1,0:T(8,128)(2,1)S(1)}, u32[]{:S(2)}, u32[]{:S(2)}) collective-permute-start(f16[8,16,16,128]{3,2,1,0:T(8,128)(2,1)S(1)} %convert_element_type.51), channel_id=1, source_target_pairs={{0,128},{128,256},{256,384},{384,0},{1,129},{129,257},{257,385},{3... | collective-permute-start | bytes 1572872 | tf_op jit(solution)/shard_map/ppermute | solution.py:329
  100.8 20.5 %collective-permute-start.15 = (f16[8,16,16,128]{3,2,1,0:T(8,128)(2,1)S(1)}, f16[8,16,16,128]{3,2,1,0:T(8,128)(2,1)S(1)}, u32[]{:S(2)}, u32[]{:S(2)}) collective-permute-start(f16[8,16,16,128]{3,2,1,0:T(8,128)(2,1)S(1)} %add_convert_fusion.1), channel_id=1, source_target_pairs={{0,64},{2,66},{4,68},{6,70},{8,72},{10,74},{12,76},{14,78},{16,80}... | collective-permute-start | bytes 1572872 | tf_op jit(solution)/shard_map/ppermute | solution.py:373
  121.3 7.4 %copy-start.6 = (s32[16,3]{0,1:T(4,128)S(1)}, s32[16,3]{0,1:T(4,128)}, u32[]{:S(2)}) copy-start(s32[16,3]{0,1:T(4,128)} %param.14) | copy-start | bytes 580
  121.3 7.4 %copy-start.7 = (f32[128]{0:T(128)S(1)}, f32[128]{0:T(128)}, u32[]{:S(2)}) copy-start(f32[128]{0:T(128)} %param.21) | copy-start | bytes 1540
  122.5 18.1 %all-to-all-start.1 = ((f16[8,16,16,128]{3,2,1,0:T(8,128)(2,1)}), f16[8,16,16,128]{3,2,1,0:T(8,128)(2,1)S(1)}, u32[]{:S(2)}, u32[]{:S(2)}) async-start(f16[8,16,16,128]{3,2,1,0:T(8,128)(2,1)} %add_convert_fusion), calls=%async_computation.1 | async-start | bytes 1048576 | tf_op jit(solution)/shard_map/all_to_all | solution.py:375

commit v16 on v15

--- a/solution.py
+++ b/solution.py
@@ -330,6 +330,13 @@
     return total
 
 
+def along_row(sums):
+    sums = lax.all_to_all(
+        sums.astype(LINK), "ado", split_axis=0, concat_axis=0, tiled=True, axis_index_groups=DELIVER
+    )
+    return jnp.sum(sums.astype(F32), axis=0)
+
+
 def on_device(
     states, send_slot, window_tier_states, modes_tri, use_up, use_down,
     hamiltonian, coupling, coup_re, coup_im, decay_rate,
@@ -370,12 +377,9 @@
 
     far = terms(FAR, (0, RINGS, 0), spot, far_lists, coup_re, coup_im, sent, *shared)
     far, near_lists = lax.optimization_barrier((far, near_lists))
-    far = lax.ppermute(over_groups(far).astype(LINK), "ado", onward(4))
-    near = over_groups(terms(NEAR, (0, RINGS, 0), spot, near_lists, coup_re, coup_im, sent, *shared))
-    summed = lax.all_to_all(
-        (near + far.astype(F32)).astype(LINK), "ado", split_axis=0, concat_axis=0, tiled=True,
-        axis_index_groups=DELIVER,
-    )
+    far = lax.ppermute(along_row(over_groups(far)), "ado", onward(4))
+    near = terms(NEAR, (0, RINGS, 0), spot, near_lists, coup_re, coup_im, sent, *shared)
+    near = along_row(over_groups(near))
 
     ham_wide = doubled(hamiltonian)
     right_part = jnp.einsum("wab,bc->wac", window_tier_states, ham_wide, preferred_element_type=F32)
@@ -383,7 +387,7 @@
     hits = modes_tri[:, :, None] == every_mode
     damping = jnp.sum(jnp.where(hits, decay_rate, 0.0), axis=(1, 2))
     own = rotate(right_part) + damping[:, None, None] * window_tier_states.astype(F32)
-    return STEP_WEIGHT * (jnp.sum(summed.astype(F32), axis=0) - own)
+    return STEP_WEIGHT * (near + far - own)
 
 
 def solution(mesh):

time: 142 us -> 182 us (1.28)
  the two profiles are of different devices: /device:TPU:8 before, /device:TPU:1 now
where the time goes in v16:
time: 182 us; the launch traced here: 180 us
  starting transfers between devices  81.9 us (45%)
  waiting for transfers between devices  57.7 us (32%)
  Pallas kernels  24.8 us (14%)
  other arithmetic  8.14 us (4%)
  local copies, waits for them, and re-layouts  7.31 us (4%)
    ppermute x6, waiting for transfers between devices, on_device(): lax.ppermute(block, 'ado', onward(step))  24.7 us
    ppermute x6, starting transfers between devices, on_device(): lax.ppermute(block, 'ado', onward(step))  20.4 us
    pallas_call x2, Pallas kernels, terms(): pl.pallas_call(functools.partial(terms_kernel, sources, modes, windows, p...  18.9 us
    ppermute x6, starting transfers between devices, over_groups(): lax.ppermute(parts[shift].astype(LINK), 'grp', ring).astype(F32)  18.9 us
    all_to_all x2, starting transfers between devices, along_row(): lax.all_to_all(sums.astype(LINK), 'ado', split_axis=0, concat_axis=0, til...  17.7 us
    ppermute x6, waiting for transfers between devices, over_groups(): lax.ppermute(parts[shift].astype(LINK), 'grp', ring).astype(F32)  17.7 us
    all_to_all x2, waiting for transfers between devices, along_row(): lax.all_to_all(sums.astype(LINK), 'ado', split_axis=0, concat_axis=0, til...  11.5 us
    ppermute x1, starting transfers between devices, on_device(): sib_store = lax.ppermute(store, 'ado', SIBLING)  8.91 us
  transfers between devices with their start and end apart: 19, of which 11 were waited for; matrix products, arithmetic and copies ran while one was open for 5% of the time, Pallas kernels for 8%

profile of v16, /device:TPU:1, one launch (start us, length us, event | category | flops | bytes accessed | tf_op | source)
XLA Modules:
  0.0 180.4 jit_solution(614437782093595234)
XLA Ops:
  0.0 0.7 copy.15
  0.7 0.6 pad_add_fusion.spot_ref
  1.3 1.6 shard_map.109
  3.0 8.9 %collective-permute-start.1 = (bf16[128,64,128]{2,1,0:T(8,128)(2,1)}, bf16[128,64,128]{2,1,0:T(8,128)(2,1)S(1)}, u32[]{:S(2)}, u32[]{:S(2)}) collective-permute-start(bf16[128,64,128]{2,1,0:T(8,128)(2,1)} %bitcast.19), channel_id=1, source_target_pairs={{0,1},{1,0},{2,3},{3,2},{4,5},{5,4},{6,7},{7,6},{8,9},{9,8},{10,11... | collective-permute-start | bytes 6291464 | tf_op jit(solution)/shard_map/ppermute | solution.py:361
  11.9 4.7 %all-to-all-start = ((s32[8,40,128]{2,1,0:T(8,128)}), s32[8,40,128]{2,1,0:T(8,128)S(1)}, u32[]{:S(2)}, u32[]{:S(2)}) async-start(s32[8,40,128]{2,1,0:T(8,128)} %shard_map.109), calls=%async_computation | async-start | bytes 327680 | tf_op jit(solution)/shard_map/all_to_all | solution.py:357
  16.6 1.9 %collective-permute-start = (s32[384]{0:T(512)S(1)}, s32[384]{0:T(512)S(1)}, u32[]{:S(2)}, u32[]{:S(2)}) collective-permute-start(s32[384]{0:T(512)S(1)} %bitcast.21), channel_id=1, source_target_pairs={{0,1},{1,0},{2,3},{3,2},{4,5},{5,4},{6,7},{7,6},{8,9},{9,8},{10,11... | collective-permute-start | bytes 4616 | tf_op jit(solution)/shard_map/ppermute | solution.py:362
  18.5 2.5 %fusion.2 = bf16[32,128,128]{2,1,0:T(8,128)(2,1)} fusion(bf16[32,64,64]{2,1,0:T(8,128)(2,1)} %param.18), kind=kLoop, calls=%fused_computation.5 | loop fusion | flops 4194304 | bytes 1310720 | tf_op jit(solution)/shard_map/concatenate | solution.py:23
  21.0 3.8 %all-to-all-done = s32[8,40,128]{2,1,0:T(8,128)S(1)} async-done(((s32[8,40,128]{2,1,0:T(8,128)}), s32[8,40,128]{2,1,0:T(8,128)S(1)}, u32[]{:S(2)}, u32[]{:S(2)}) %all-to-all-start) | async-done | bytes 163872 | tf_op jit(solution)/shard_map/all_to_all | solution.py:357
  24.9 7.5 %collective-permute-start.2 = (s32[40,128]{1,0:T(8,128)S(1)}, s32[40,128]{1,0:T(8,128)S(1)}, u32[]{:S(2)}, u32[]{:S(2)}) collective-permute-start(s32[40,128]{1,0:T(8,128)S(1)} %reduce_sum.36.refs_1_), channel_id=1, source_target_pairs={{0,64},{2,66},{4,68},{6,70},{8,72},{10,74},{12,76},{14,78},{16,80}... | collective-permute-start | bytes 61448 | tf_op jit(solution)/shard_map/ppermute | solution.py:364
  32.4 1.3 concatenate.27.refs_3_.refs_5_
  33.8 1.3 copy-done.1
  35.1 1.6 copy-done
  36.7 1.6 copy-done.2
  38.3 2.9 %shard_map.110 = (bf16[48,64,128]{2,1,0:T(8,128)(2,1)S(1)}, bf16[48,64,128]{2,1,0:T(8,128)(2,1)S(1)}, bf16[48,64,128]{2,1,0:T(8,128)(2,1)}, bf16[48,64,128]{2,1,...) custom-call(s32[4]{0:T(128)S(1)} %copy-done.4, ...), custom_call_target="tpu_custom_call" | custom-call | bytes 10485760 | tf_op jit(solution)/shard_map/pallas_call | solution.py:78
  41.3 2.3 %collective-permute-start.3 = (bf16[48,64,128]{2,1,0:T(8,128)(2,1)S(1)}, bf16[48,64,128]{2,1,0:T(8,128)(2,1)S(1)}, u32[]{:S(2)}, u32[]{:S(2)}) collective-permute-start(bf16[48,64,128]{2,1,0:T(8,128)(2,1)S(1)} %get-tuple-element.59), channel_id=1, source_target_pairs={{0,16},{2,18},{4,20},{6,22},{8,24},{10,26},{12,28},{14,30},{16,32}... | collective-permute-start | bytes 2359304 | tf_op jit(solution)/shard_map/ppermute | solution.py:372
  43.6 4.2 %collective-permute-start.4 = (bf16[48,64,128]{2,1,0:T(8,128)(2,1)S(1)}, bf16[48,64,128]{2,1,0:T(8,128)(2,1)S(1)}, u32[]{:S(2)}, u32[]{:S(2)}) collective-permute-start(bf16[48,64,128]{2,1,0:T(8,128)(2,1)S(1)} %get-tuple-element.60), channel_id=1, source_target_pairs={{0,112},{2,114},{4,116},{6,118},{8,120},{10,122},{12,124},{14,126}... | collective-permute-start | bytes 2359304 | tf_op jit(solution)/shard_map/ppermute | solution.py:372
  47.8 1.3 shard_map.111
  49.1 6.4 %collective-permute-done.3.refs_0_ = bf16[48,64,128]{2,1,0:T(8,128)(2,1)S(1)} collective-permute-done((bf16[48,64,128]{2,1,0:T(8,128)(2,1)S(1)}, bf16[48,64,128]{2,1,0:T(8,128)(2,1)S(1)}, u32[]{:S(2)}, u32[]{:S(2)}) %collective-permute-start.3) | collective-permute-done | bytes 786464 | tf_op jit(solution)/shard_map/ppermute | solution.py:372
  55.5 1.2 collective-permute-done.4.refs_1_
  56.7 8.1 %shard_map.112 = (f32[8,16,16,128]{3,2,1,0:T(8,128)S(1)}, f32[8,16,16,128]{3,2,1,0:T(8,128)S(1)}, f32[8,16,16,128]{3,2,1,0:T(8,128)S(1)}, f32[8,16,16,128]{3,2,1,0:T(8,128)S(1)}) custom-call(s32[4]{0:T(128)S(1)} %copy-done.4, s32[48,128]{1,0:T(8,128)S(1)} %get-tuple-element.58.list_ref, f32[32]{0:T(128)S(1)} %copy-done.5, f32[32]{0:T(128)S(1)} %copy-done.6, ...), custom_call_target="tpu_custom_call" | custom-call | flops 1000000000 | bytes 10485760 | tf_op jit(solution)/shard_map/pallas_call | solution.py:192
  64.9 2.8 %collective-permute-start.12 = (f16[8,16,16,128]{3,2,1,0:T(8,128)(2,1)S(1)}, f16[8,16,16,128]{3,2,1,0:T(8,128)(2,1)S(1)}, u32[]{:S(2)}, u32[]{:S(2)}) collective-permute-start(f16[8,16,16,128]{3,2,1,0:T(8,128)(2,1)S(1)} %convert_element_type.59), channel_id=1, source_target_pairs={{0,128},{128,256},{256,384},{384,0},{1,129},{129,257},{257,385},{3... | collective-permute-start | bytes 1572872 | tf_op jit(solution)/shard_map/ppermute | solution.py:329
  67.8 3.7 %collective-permute-start.13 = (f16[8,16,16,128]{3,2,1,0:T(8,128)(2,1)S(1)}, f16[8,16,16,128]{3,2,1,0:T(8,128)(2,1)S(1)}, u32[]{:S(2)}, u32[]{:S(2)}) collective-permute-start(f16[8,16,16,128]{3,2,1,0:T(8,128)(2,1)S(1)} %convert_element_type.61), channel_id=1, source_target_pairs={{0,384},{128,0},{256,128},{384,256},{1,385},{129,1},{257,129},{385... | collective-permute-start | bytes 1572872 | tf_op jit(solution)/shard_map/ppermute | solution.py:329
  71.6 3.1 %collective-permute-start.14 = (f16[8,16,16,128]{3,2,1,0:T(8,128)(2,1)S(1)}, f16[8,16,16,128]{3,2,1,0:T(8,128)(2,1)S(1)}, u32[]{:S(2)}, u32[]{:S(2)}) collective-permute-start(f16[8,16,16,128]{3,2,1,0:T(8,128)(2,1)S(1)} %convert_element_type.63), channel_id=1, source_target_pairs={{0,256},{128,384},{256,0},{384,128},{1,257},{129,385},{257,1},{385... | collective-permute-start | bytes 1572872 | tf_op jit(solution)/shard_map/ppermute | solution.py:329
  74.7 2.7 %collective-permute-start.5 = (bf16[48,64,128]{2,1,0:T(8,128)(2,1)}, bf16[48,64,128]{2,1,0:T(8,128)(2,1)S(1)}, u32[]{:S(2)}, u32[]{:S(2)}) collective-permute-start(bf16[48,64,128]{2,1,0:T(8,128)(2,1)} %get-tuple-element.71), channel_id=1, source_target_pairs={{0,32},{2,34},{4,36},{6,38},{8,40},{10,42},{12,44},{14,46},{16,48}... | collective-permute-start | bytes 2359304 | tf_op jit(solution)/shard_map/ppermute | solution.py:372
  77.4 4.7 %collective-permute-start.6 = (bf16[48,64,128]{2,1,0:T(8,128)(2,1)}, bf16[48,64,128]{2,1,0:T(8,128)(2,1)}, u32[]{:S(2)}, u32[]{:S(2)}) collective-permute-start(bf16[48,64,128]{2,1,0:T(8,128)(2,1)} %get-tuple-element.72), channel_id=1, source_target_pairs={{0,96},{2,98},{4,100},{6,102},{8,104},{10,106},{12,108},{14,110},{... | collective-permute-start | bytes 2359304 | tf_op jit(solution)/shard_map/ppermute | solution.py:372
  82.1 2.4 %collective-permute-start.7 = (bf16[48,64,128]{2,1,0:T(8,128)(2,1)}, bf16[48,64,128]{2,1,0:T(8,128)(2,1)}, u32[]{:S(2)}, u32[]{:S(2)}) collective-permute-start(bf16[48,64,128]{2,1,0:T(8,128)(2,1)} %get-tuple-element.73), channel_id=1, source_target_pairs={{0,16},{2,18},{4,20},{6,22},{8,24},{10,26},{12,28},{14,30},{16,32}... | collective-permute-start | bytes 2359304 | tf_op jit(solution)/shard_map/ppermute | solution.py:372
  84.5 4.2 %collective-permute-start.8 = (bf16[48,64,128]{2,1,0:T(8,128)(2,1)}, bf16[48,64,128]{2,1,0:T(8,128)(2,1)}, u32[]{:S(2)}, u32[]{:S(2)}) collective-permute-start(bf16[48,64,128]{2,1,0:T(8,128)(2,1)} %get-tuple-element.74), channel_id=1, source_target_pairs={{0,112},{2,114},{4,116},{6,118},{8,120},{10,122},{12,124},{14,126}... | collective-permute-start | bytes 2359304 | tf_op jit(solution)/shard_map/ppermute | solution.py:372
  88.7 1.1 collective-permute-done.14
  89.8 1.1 add_convert_fusion
  90.9 5.1 %all-to-all-start.2 = ((f16[8,16,16,128]{3,2,1,0:T(8,128)(2,1)}), f16[8,16,16,128]{3,2,1,0:T(8,128)(2,1)}, u32[]{:S(2)}, u32[]{:S(2)}) async-start(f16[8,16,16,128]{3,2,1,0:T(8,128)(2,1)} %add_convert_fusion), calls=%async_computation.2 | async-start | bytes 1048576 | tf_op jit(solution)/shard_map/all_to_all | solution.py:334
  96.0 3.8 %collective-permute-done.6.refs_1_ = bf16[48,64,128]{2,1,0:T(8,128)(2,1)} collective-permute-done((bf16[48,64,128]{2,1,0:T(8,128)(2,1)}, bf16[48,64,128]{2,1,0:T(8,128)(2,1)}, u32[]{:S(2)}, u32[]{:S(2)}) %collective-permute-start.6) | collective-permute-done | bytes 786464 | tf_op jit(solution)/shard_map/ppermute | solution.py:372
  99.8 6.3 %collective-permute-done.7.refs_2_ = bf16[48,64,128]{2,1,0:T(8,128)(2,1)} collective-permute-done((bf16[48,64,128]{2,1,0:T(8,128)(2,1)}, bf16[48,64,128]{2,1,0:T(8,128)(2,1)}, u32[]{:S(2)}, u32[]{:S(2)}) %collective-permute-start.7) | collective-permute-done | bytes 786464 | tf_op jit(solution)/shard_map/ppermute | solution.py:372
  106.0 7.0 %collective-permute-done.8.refs_3_ = bf16[48,64,128]{2,1,0:T(8,128)(2,1)} collective-permute-done((bf16[48,64,128]{2,1,0:T(8,128)(2,1)}, bf16[48,64,128]{2,1,0:T(8,128)(2,1)}, u32[]{:S(2)}, u32[]{:S(2)}) %collective-permute-start.8) | collective-permute-done | bytes 786464 | tf_op jit(solution)/shard_map/ppermute | solution.py:372
  113.0 0.7 copy-done.7
  113.7 10.8 %shard_map.113 = (f32[8,16,16,128]{3,2,1,0:T(8,128)S(1)}, f32[8,16,16,128]{3,2,1,0:T(8,128)S(1)}, f32[8,16,16,128]{3,2,1,0:T(8,128)S(1)}, f32[8,16,16,128]{3,2,1,0:T(8,128)S(1)}) custom-call(s32[4]{0:T(128)S(1)} %copy-done.4, s32[48,128]{1,0:T(8,128)S(1)} %get-tuple-element.70.list_ref, f32[32]{0:T(128)S(1)} %copy-done.5, f32[32]{0:T(128)S(1)} %copy-done.7, ...), custom_call_target="tpu_custom_call" | custom-call | flops 1000000000 | bytes 10485760 | tf_op jit(solution)/shard_map/pallas_call | solution.py:192
  124.6 1.9 %collective-permute-start.10 = (f16[8,16,16,128]{3,2,1,0:T(8,128)(2,1)S(1)}, f16[8,16,16,128]{3,2,1,0:T(8,128)(2,1)S(1)}, u32[]{:S(2)}, u32[]{:S(2)}) collective-permute-start(f16[8,16,16,128]{3,2,1,0:T(8,128)(2,1)S(1)} %convert_element_type.53), channel_id=1, source_target_pairs={{0,384},{128,0},{256,128},{384,256},{1,385},{129,1},{257,129},{385... | collective-permute-start | bytes 1572872 | tf_op jit(solution)/shard_map/ppermute | solution.py:329
  126.6 5.5 %collective-permute-start.11 = (f16[8,16,16,128]{3,2,1,0:T(8,128)(2,1)S(1)}, f16[8,16,16,128]{3,2,1,0:T(8,128)(2,1)S(1)}, u32[]{:S(2)}, u32[]{:S(2)}) collective-permute-start(f16[8,16,16,128]{3,2,1,0:T(8,128)(2,1)S(1)} %convert_element_type.55), channel_id=1, source_target_pairs={{0,256},{128,384},{256,0},{384,128},{1,257},{129,385},{257,1},{385... | collective-permute-start | bytes 1572872 | tf_op jit(solution)/shard_map/ppermute | solution.py:329
  132.2 1.9 %collective-permute-start.9 = (f16[8,16,16,128]{3,2,1,0:T(8,128)(2,1)S(1)}, f16[8,16,16,128]{3,2,1,0:T(8,128)(2,1)S(1)}, u32[]{:S(2)}, u32[]{:S(2)}) collective-permute-start(f16[8,16,16,128]{3,2,1,0:T(8,128)(2,1)S(1)} %convert_element_type.51), channel_id=1, source_target_pairs={{0,128},{128,256},{256,384},{384,0},{1,129},{129,257},{257,385},{3... | collective-permute-start | bytes 1572872 | tf_op jit(solution)/shard_map/ppermute | solution.py:329
  134.1 0.8 collective-permute-done.10
  134.9 3.9 %collective-permute-done.11 = f16[8,16,16,128]{3,2,1,0:T(8,128)(2,1)S(1)} collective-permute-done((f16[8,16,16,128]{3,2,1,0:T(8,128)(2,1)S(1)}, f16[8,16,16,128]{3,2,1,0:T(8,128)(2,1)S(1)}, u32[]{:S(2)}, u32[]{:S(2)}) %collective-permute-start.11) | collective-permute-done | bytes 524320 | tf_op jit(solution)/shard_map/ppermute | solution.py:329
  138.8 11.9 %collective-permute-done.9 = f16[8,16,16,128]{3,2,1,0:T(8,128)(2,1)S(1)} collective-permute-done((f16[8,16,16,128]{3,2,1,0:T(8,128)(2,1)S(1)}, f16[8,16,16,128]{3,2,1,0:T(8,128)(2,1)S(1)}, u32[]{:S(2)}, u32[]{:S(2)}) %collective-permute-start.9) | collective-permute-done | bytes 524320 | tf_op jit(solution)/shard_map/ppermute | solution.py:329
  150.7 1.1 add_convert_fusion.1
  151.8 12.6 %all-to-all-start.1 = ((f16[8,16,16,128]{3,2,1,0:T(8,128)(2,1)}), f16[8,16,16,128]{3,2,1,0:T(8,128)(2,1)S(1)}, u32[]{:S(2)}, u32[]{:S(2)}) async-start(f16[8,16,16,128]{3,2,1,0:T(8,128)(2,1)} %add_convert_fusion.1), calls=%async_computation.1 | async-start | bytes 1048576 | tf_op jit(solution)/shard_map/all_to_all | solution.py:334
  164.7 0.2 convolution_bitcast_fusion
  165.0 1.1 convert_reduce_fusion
  166.1 1.9 %collective-permute-start.15 = (f32[16,16,128]{2,1,0:T(8,128)S(1)}, f32[16,16,128]{2,1,0:T(8,128)S(1)}, u32[]{:S(2)}, u32[]{:S(2)}) collective-permute-start(f32[16,16,128]{2,1,0:T(8,128)S(1)} %convert_reduce_fusion), channel_id=1, source_target_pairs={{0,64},{2,66},{4,68},{6,70},{8,72},{10,74},{12,76},{14,78},{16,80}... | collective-permute-start | bytes 393224 | tf_op jit(solution)/shard_map/ppermute | solution.py:380
  168.1 11.5 %all-to-all-done.1 = f16[8,16,16,128]{3,2,1,0:T(8,128)(2,1)S(1)} async-done(((f16[8,16,16,128]{3,2,1,0:T(8,128)(2,1)}), f16[8,16,16,128]{3,2,1,0:T(8,128)(2,1)S(1)}, u32[]{:S(2)}, u32[]{:S(2)}) %all-to-all-start.1) | async-done | bytes 524320 | tf_op jit(solution)/shard_map/all_to_all | solution.py:334
  179.6 0.8 fusion.4
  (39 shorter events, 1.0 us)
Async XLA Ops:
  0.0 32.3 %copy-start.8 = (bf16[64,64]{1,0:T(8,128)(2,1)S(1)}, bf16[64,64]{1,0:T(8,128)(2,1)}, u32[]{:S(2)}) copy-start(bf16[64,64]{1,0:T(8,128)(2,1)} %param.17) | copy-start | bytes 24580
  3.0 32.2 %copy-start.4 = (s32[4]{0:T(128)S(1)}, s32[4]{0:T(128)}, u32[]{:S(2)}) copy-start(s32[4]{0:T(128)} %pad_add_fusion.spot_ref) | copy-start | bytes 52
  3.0 30.8 %collective-permute-start.1 = (bf16[128,64,128]{2,1,0:T(8,128)(2,1)}, bf16[128,64,128]{2,1,0:T(8,128)(2,1)S(1)}, u32[]{:S(2)}, u32[]{:S(2)}) collective-permute-start(bf16[128,64,128]{2,1,0:T(8,128)(2,1)} %bitcast.19), channel_id=1, source_target_pairs={{0,1},{1,0},{2,3},{3,2},{4,5},{5,4},{6,7},{7,6},{8,9},{9,8},{10,11... | collective-permute-start | bytes 6291464 | tf_op jit(solution)/shard_map/ppermute | solution.py:361
  11.9 13.0 %all-to-all-start = ((s32[8,40,128]{2,1,0:T(8,128)}), s32[8,40,128]{2,1,0:T(8,128)S(1)}, u32[]{:S(2)}, u32[]{:S(2)}) async-start(s32[8,40,128]{2,1,0:T(8,128)} %shard_map.109), calls=%async_computation | async-start | bytes 327680 | tf_op jit(solution)/shard_map/all_to_all | solution.py:357
  16.6 17.2 %collective-permute-start = (s32[384]{0:T(512)S(1)}, s32[384]{0:T(512)S(1)}, u32[]{:S(2)}, u32[]{:S(2)}) collective-permute-start(s32[384]{0:T(512)S(1)} %bitcast.21), channel_id=1, source_target_pairs={{0,1},{1,0},{2,3},{3,2},{4,5},{5,4},{6,7},{7,6},{8,9},{9,8},{10,11... | collective-permute-start | bytes 4616 | tf_op jit(solution)/shard_map/ppermute | solution.py:362
  24.9 16.4 %collective-permute-start.2 = (s32[40,128]{1,0:T(8,128)S(1)}, s32[40,128]{1,0:T(8,128)S(1)}, u32[]{:S(2)}, u32[]{:S(2)}) collective-permute-start(s32[40,128]{1,0:T(8,128)S(1)} %reduce_sum.36.refs_1_), channel_id=1, source_target_pairs={{0,64},{2,66},{4,68},{6,70},{8,72},{10,74},{12,76},{14,78},{16,80}... | collective-permute-start | bytes 61448 | tf_op jit(solution)/shard_map/ppermute | solution.py:364
  32.4 24.3 %copy-start.3 = (bf16[16,16,128]{2,1,0:T(8,128)(2,1)S(1)}, bf16[16,16,128]{2,1,0:T(8,128)(2,1)}, u32[]{:S(2)}) copy-start(bf16[16,16,128]{2,1,0:T(8,128)(2,1)} %refs_7_) | copy-start | bytes 196612
  32.4 24.3 %copy-start.5 = (f32[32]{0:T(128)S(1)}, f32[32]{0:T(128)}, u32[]{:S(2)}) copy-start(f32[32]{0:T(128)} %re_ref.3) | copy-start | bytes 388
  32.4 24.3 %copy-start.6 = (f32[32]{0:T(128)S(1)}, f32[32]{0:T(128)}, u32[]{:S(2)}) copy-start(f32[32]{0:T(128)} %im_ref.3) | copy-start | bytes 388
  33.8 1.3 copy-start.1
  35.1 1.6 copy-start
  36.7 1.6 copy-start.2
  41.3 14.2 %collective-permute-start.3 = (bf16[48,64,128]{2,1,0:T(8,128)(2,1)S(1)}, bf16[48,64,128]{2,1,0:T(8,128)(2,1)S(1)}, u32[]{:S(2)}, u32[]{:S(2)}) collective-permute-start(bf16[48,64,128]{2,1,0:T(8,128)(2,1)S(1)} %get-tuple-element.59), channel_id=1, source_target_pairs={{0,16},{2,18},{4,20},{6,22},{8,24},{10,26},{12,28},{14,30},{16,32}... | collective-permute-start | bytes 2359304 | tf_op jit(solution)/shard_map/ppermute | solution.py:372
  43.6 13.1 %collective-permute-start.4 = (bf16[48,64,128]{2,1,0:T(8,128)(2,1)S(1)}, bf16[48,64,128]{2,1,0:T(8,128)(2,1)S(1)}, u32[]{:S(2)}, u32[]{:S(2)}) collective-permute-start(bf16[48,64,128]{2,1,0:T(8,128)(2,1)S(1)} %get-tuple-element.60), channel_id=1, source_target_pairs={{0,112},{2,114},{4,116},{6,118},{8,120},{10,122},{12,124},{14,126}... | collective-permute-start | bytes 2359304 | tf_op jit(solution)/shard_map/ppermute | solution.py:372
  64.9 17.2 %collective-permute-start.12 = (f16[8,16,16,128]{3,2,1,0:T(8,128)(2,1)S(1)}, f16[8,16,16,128]{3,2,1,0:T(8,128)(2,1)S(1)}, u32[]{:S(2)}, u32[]{:S(2)}) collective-permute-start(f16[8,16,16,128]{3,2,1,0:T(8,128)(2,1)S(1)} %convert_element_type.59), channel_id=1, source_target_pairs={{0,128},{128,256},{256,384},{384,0},{1,129},{129,257},{257,385},{3... | collective-permute-start | bytes 1572872 | tf_op jit(solution)/shard_map/ppermute | solution.py:329
  67.8 16.7 %collective-permute-start.13 = (f16[8,16,16,128]{3,2,1,0:T(8,128)(2,1)S(1)}, f16[8,16,16,128]{3,2,1,0:T(8,128)(2,1)S(1)}, u32[]{:S(2)}, u32[]{:S(2)}) collective-permute-start(f16[8,16,16,128]{3,2,1,0:T(8,128)(2,1)S(1)} %convert_element_type.61), channel_id=1, source_target_pairs={{0,384},{128,0},{256,128},{384,256},{1,385},{129,1},{257,129},{385... | collective-permute-start | bytes 1572872 | tf_op jit(solution)/shard_map/ppermute | solution.py:329
  71.6 18.2 %collective-permute-start.14 = (f16[8,16,16,128]{3,2,1,0:T(8,128)(2,1)S(1)}, f16[8,16,16,128]{3,2,1,0:T(8,128)(2,1)S(1)}, u32[]{:S(2)}, u32[]{:S(2)}) collective-permute-start(f16[8,16,16,128]{3,2,1,0:T(8,128)(2,1)S(1)} %convert_element_type.63), channel_id=1, source_target_pairs={{0,256},{128,384},{256,0},{384,128},{1,257},{129,385},{257,1},{385... | collective-permute-start | bytes 1572872 | tf_op jit(solution)/shard_map/ppermute | solution.py:329
  74.7 21.3 %collective-permute-start.5 = (bf16[48,64,128]{2,1,0:T(8,128)(2,1)}, bf16[48,64,128]{2,1,0:T(8,128)(2,1)S(1)}, u32[]{:S(2)}, u32[]{:S(2)}) collective-permute-start(bf16[48,64,128]{2,1,0:T(8,128)(2,1)} %get-tuple-element.71), channel_id=1, source_target_pairs={{0,32},{2,34},{4,36},{6,38},{8,40},{10,42},{12,44},{14,46},{16,48}... | collective-permute-start | bytes 2359304 | tf_op jit(solution)/shard_map/ppermute | solution.py:372
  77.4 22.4 %collective-permute-start.6 = (bf16[48,64,128]{2,1,0:T(8,128)(2,1)}, bf16[48,64,128]{2,1,0:T(8,128)(2,1)}, u32[]{:S(2)}, u32[]{:S(2)}) collective-permute-start(bf16[48,64,128]{2,1,0:T(8,128)(2,1)} %get-tuple-element.72), channel_id=1, source_target_pairs={{0,96},{2,98},{4,100},{6,102},{8,104},{10,106},{12,108},{14,110},{... | collective-permute-start | bytes 2359304 | tf_op jit(solution)/shard_map/ppermute | solution.py:372
  82.1 23.9 %collective-permute-start.7 = (bf16[48,64,128]{2,1,0:T(8,128)(2,1)}, bf16[48,64,128]{2,1,0:T(8,128)(2,1)}, u32[]{:S(2)}, u32[]{:S(2)}) collective-permute-start(bf16[48,64,128]{2,1,0:T(8,128)(2,1)} %get-tuple-element.73), channel_id=1, source_target_pairs={{0,16},{2,18},{4,20},{6,22},{8,24},{10,26},{12,28},{14,30},{16,32}... | collective-permute-start | bytes 2359304 | tf_op jit(solution)/shard_map/ppermute | solution.py:372
  84.5 28.6 %collective-permute-start.8 = (bf16[48,64,128]{2,1,0:T(8,128)(2,1)}, bf16[48,64,128]{2,1,0:T(8,128)(2,1)}, u32[]{:S(2)}, u32[]{:S(2)}) collective-permute-start(bf16[48,64,128]{2,1,0:T(8,128)(2,1)} %get-tuple-element.74), channel_id=1, source_target_pairs={{0,112},{2,114},{4,116},{6,118},{8,120},{10,122},{12,124},{14,126}... | collective-permute-start | bytes 2359304 | tf_op jit(solution)/shard_map/ppermute | solution.py:372
  90.9 61.0 %all-to-all-start.2 = ((f16[8,16,16,128]{3,2,1,0:T(8,128)(2,1)}), f16[8,16,16,128]{3,2,1,0:T(8,128)(2,1)}, u32[]{:S(2)}, u32[]{:S(2)}) async-start(f16[8,16,16,128]{3,2,1,0:T(8,128)(2,1)} %add_convert_fusion), calls=%async_computation.2 | async-start | bytes 1048576 | tf_op jit(solution)/shard_map/all_to_all | solution.py:334
  113.0 0.7 copy-start.7
  124.6 10.3 %collective-permute-start.10 = (f16[8,16,16,128]{3,2,1,0:T(8,128)(2,1)S(1)}, f16[8,16,16,128]{3,2,1,0:T(8,128)(2,1)S(1)}, u32[]{:S(2)}, u32[]{:S(2)}) collective-permute-start(f16[8,16,16,128]{3,2,1,0:T(8,128)(2,1)S(1)} %convert_element_type.53), channel_id=1, source_target_pairs={{0,384},{128,0},{256,128},{384,256},{1,385},{129,1},{257,129},{385... | collective-permute-start | bytes 1572872 | tf_op jit(solution)/shard_map/ppermute | solution.py:329
  126.6 12.2 %collective-permute-start.11 = (f16[8,16,16,128]{3,2,1,0:T(8,128)(2,1)S(1)}, f16[8,16,16,128]{3,2,1,0:T(8,128)(2,1)S(1)}, u32[]{:S(2)}, u32[]{:S(2)}) collective-permute-start(f16[8,16,16,128]{3,2,1,0:T(8,128)(2,1)S(1)} %convert_element_type.55), channel_id=1, source_target_pairs={{0,256},{128,384},{256,0},{384,128},{1,257},{129,385},{257,1},{385... | collective-permute-start | bytes 1572872 | tf_op jit(solution)/shard_map/ppermute | solution.py:329
  132.2 18.5 %collective-permute-start.9 = (f16[8,16,16,128]{3,2,1,0:T(8,128)(2,1)S(1)}, f16[8,16,16,128]{3,2,1,0:T(8,128)(2,1)S(1)}, u32[]{:S(2)}, u32[]{:S(2)}) collective-permute-start(f16[8,16,16,128]{3,2,1,0:T(8,128)(2,1)S(1)} %convert_element_type.51), channel_id=1, source_target_pairs={{0,128},{128,256},{256,384},{384,0},{1,129},{129,257},{257,385},{3... | collective-permute-start | bytes 1572872 | tf_op jit(solution)/shard_map/ppermute | solution.py:329
  150.7 13.8 %copy-start.10 = (s32[16,3]{0,1:T(4,128)S(1)}, s32[16,3]{0,1:T(4,128)}, u32[]{:S(2)}) copy-start(s32[16,3]{0,1:T(4,128)} %param.14) | copy-start | bytes 580
  150.7 13.8 %copy-start.11 = (f32[128]{0:T(128)S(1)}, f32[128]{0:T(128)}, u32[]{:S(2)}) copy-start(f32[128]{0:T(128)} %param.21) | copy-start | bytes 1540
  150.7 14.0 %copy-start.9 = (bf16[64,64]{1,0:T(8,128)(2,1)S(1)}, bf16[64,64]{1,0:T(8,128)(2,1)}, u32[]{:S(2)}) copy-start(bf16[64,64]{1,0:T(8,128)(2,1)} %param.17) | copy-start | bytes 24580
  151.8 27.7 %all-to-all-start.1 = ((f16[8,16,16,128]{3,2,1,0:T(8,128)(2,1)}), f16[8,16,16,128]{3,2,1,0:T(8,128)(2,1)S(1)}, u32[]{:S(2)}, u32[]{:S(2)}) async-start(f16[8,16,16,128]{3,2,1,0:T(8,128)(2,1)} %add_convert_fusion.1), calls=%async_computation.1 | async-start | bytes 1048576 | tf_op jit(solution)/shard_map/all_to_all | solution.py:334
  166.1 13.5 %collective-permute-start.15 = (f32[16,16,128]{2,1,0:T(8,128)S(1)}, f32[16,16,128]{2,1,0:T(8,128)S(1)}, u32[]{:S(2)}, u32[]{:S(2)}) collective-permute-start(f32[16,16,128]{2,1,0:T(8,128)S(1)} %convert_reduce_fusion), channel_id=1, source_target_pairs={{0,64},{2,66},{4,68},{6,70},{8,72},{10,74},{12,76},{14,78},{16,80}... | collective-permute-start | bytes 393224 | tf_op jit(solution)/shard_map/ppermute | solution.py:380

commit v17 on v15

--- a/solution.py
+++ b/solution.py
@@ -321,10 +321,10 @@
     )(spot, use_up, use_down.T, modes_tri.T)
 
 
-def over_groups(parts):
+def over_groups(parts, shifts):
     count = len(parts)
     total = parts[0]
-    for shift in (1, 3, 2):
+    for shift in shifts:
         ring = [(i, (i + shift) % count) for i in range(count)]
         total = total + lax.ppermute(parts[shift].astype(LINK), "grp", ring).astype(F32)
     return total
@@ -370,8 +370,9 @@
 
     far = terms(FAR, (0, RINGS, 0), spot, far_lists, coup_re, coup_im, sent, *shared)
     far, near_lists = lax.optimization_barrier((far, near_lists))
-    far = lax.ppermute(over_groups(far).astype(LINK), "ado", onward(4))
-    near = over_groups(terms(NEAR, (0, RINGS, 0), spot, near_lists, coup_re, coup_im, sent, *shared))
+    far = lax.ppermute(over_groups(far, (2, 1, 3)).astype(LINK), "ado", onward(4))
+    near = terms(NEAR, (0, RINGS, 0), spot, near_lists, coup_re, coup_im, sent, *shared)
+    near = over_groups(near, (1, 3, 2))
     summed = lax.all_to_all(
         (near + far.astype(F32)).astype(LINK), "ado", split_axis=0, concat_axis=0, tiled=True,
         axis_index_groups=DELIVER,

time: 142 us -> 151 us (1.063)
  starting transfers between devices: 79.5 us -> 85.9 us
  waiting for transfers between devices: 32.8 us -> 35.4 us
    all_to_all x1, starting transfers between devices: 6.23 us -> 12.4 us  [on_device(): lax.all_to_all((near + far.astype(F32)).astype(LINK), 'ado', split_axis=0...]
    ppermute x6, waiting for transfers between devices: 10.9 us -> 14.4 us  [over_groups(): lax.ppermute(parts[shift].astype(LINK), 'grp', ring).astype(F32)]
  transfers between devices with their start and end apart: 18 -> 18, of which waited for: 7 -> 8; matrix products, arithmetic and copies ran while one was open for 2% -> 2% of each run, Pallas kernels for 15% -> 13%
where the time goes in v17:
time: 151 us; the launch traced here: 150 us
  starting transfers between devices  85.9 us (57%)
  waiting for transfers between devices  35.4 us (23%)
  Pallas kernels  21.7 us (14%)
  other arithmetic  5.28 us (3%)
    ppermute x6, starting transfers between devices, on_device(): lax.ppermute(block, 'ado', onward(step))  23.7 us
    ppermute x6, starting transfers between devices, over_groups(): lax.ppermute(parts[shift].astype(LINK), 'grp', ring).astype(F32)  21.6 us
    pallas_call x2, Pallas kernels, terms(): pl.pallas_call(functools.partial(terms_kernel, sources, modes, windows, p...  16.3 us
    ppermute x6, waiting for transfers between devices, over_groups(): lax.ppermute(parts[shift].astype(LINK), 'grp', ring).astype(F32)  14.4 us
    all_to_all x1, starting transfers between devices, on_device(): lax.all_to_all((near + far.astype(F32)).astype(LINK), 'ado', split_axis=0...  12.4 us
    all_to_all x1, waiting for transfers between devices, on_device(): lax.all_to_all((near + far.astype(F32)).astype(LINK), 'ado', split_axis=0...  11.3 us
    ppermute x1, starting transfers between devices, on_device(): heard_far = lax.ppermute(heard, 'ado', onward(4))  9.33 us
    all_to_all x1, starting transfers between devices, on_device(): lax.all_to_all(said, 'ado', split_axis=0, concat_axis=0, tiled=True, axis...  9.12 us
  transfers between devices with their start and end apart: 18, of which 8 were waited for; matrix products, arithmetic and copies ran while one was open for 2% of the time, Pallas kernels for 13%

profile of v17, /device:TPU:8, one launch (start us, length us, event | category | flops | bytes accessed | tf_op | source)
XLA Modules:
  0.0 149.8 jit_solution(2973862412265025331)
XLA Ops:
  0.0 0.7 copy.15
  0.7 0.6 pad_add_fusion.spot_ref
  1.3 1.7 %shard_map.109 = s32[8,40,128]{2,1,0:T(8,128)} custom-call(s32[4]{0:T(128)} %pad_add_fusion.spot_ref, s32[16,32]{1,0:T(8,128)} %up_ref.1, s32[3,16]{1,0:T(4,128)} %bitcast.24, s32[3,16]{1,0:T(4,128)} %bitcast.23), custom_call_target="tpu_custom_call" | custom-call | flops 1000000 | bytes 262144 | tf_op jit(solution)/shard_map/pallas_call | solution.py:315
  3.0 2.0 %collective-permute-start.1 = (bf16[128,64,128]{2,1,0:T(8,128)(2,1)}, bf16[128,64,128]{2,1,0:T(8,128)(2,1)}, u32[]{:S(2)}, u32[]{:S(2)}) collective-permute-start(bf16[128,64,128]{2,1,0:T(8,128)(2,1)} %bitcast.19), channel_id=1, source_target_pairs={{0,1},{1,0},{2,3},{3,2},{4,5},{5,4},{6,7},{7,6},{8,9},{9,8},{10,11... | collective-permute-start | bytes 6291464 | tf_op jit(solution)/shard_map/ppermute | solution.py:354
  5.1 9.1 %all-to-all-start = ((s32[8,40,128]{2,1,0:T(8,128)}), s32[8,40,128]{2,1,0:T(8,128)S(1)}, u32[]{:S(2)}, u32[]{:S(2)}) async-start(s32[8,40,128]{2,1,0:T(8,128)} %shard_map.109), calls=%async_computation | async-start | bytes 327680 | tf_op jit(solution)/shard_map/all_to_all | solution.py:350
  14.2 3.3 %collective-permute-start = (s32[384]{0:T(512)S(1)}, s32[384]{0:T(512)S(1)}, u32[]{:S(2)}, u32[]{:S(2)}) collective-permute-start(s32[384]{0:T(512)S(1)} %bitcast.21), channel_id=1, source_target_pairs={{0,1},{1,0},{2,3},{3,2},{4,5},{5,4},{6,7},{7,6},{8,9},{9,8},{10,11... | collective-permute-start | bytes 4616 | tf_op jit(solution)/shard_map/ppermute | solution.py:355
  17.5 1.5 %fusion.2 = bf16[32,128,128]{2,1,0:T(8,128)(2,1)S(1)} fusion(bf16[32,64,64]{2,1,0:T(8,128)(2,1)} %param.18), kind=kLoop, calls=%fused_computation.5 | loop fusion | flops 4194304 | bytes 1310720 | tf_op jit(solution)/shard_map/concatenate | solution.py:23
  19.0 3.1 %all-to-all-done = s32[8,40,128]{2,1,0:T(8,128)S(1)} async-done(((s32[8,40,128]{2,1,0:T(8,128)}), s32[8,40,128]{2,1,0:T(8,128)S(1)}, u32[]{:S(2)}, u32[]{:S(2)}) %all-to-all-start) | async-done | bytes 163872 | tf_op jit(solution)/shard_map/all_to_all | solution.py:350
  22.2 9.3 %collective-permute-start.2 = (s32[40,128]{1,0:T(8,128)S(1)}, s32[40,128]{1,0:T(8,128)S(1)}, u32[]{:S(2)}, u32[]{:S(2)}) collective-permute-start(s32[40,128]{1,0:T(8,128)S(1)} %reduce_sum.27.refs_1_), channel_id=1, source_target_pairs={{0,64},{2,66},{4,68},{6,70},{8,72},{10,74},{12,76},{14,78},{16,80}... | collective-permute-start | bytes 61448 | tf_op jit(solution)/shard_map/ppermute | solution.py:357
  31.5 0.1 constant_dynamic-slice_fusion.refs_4_.refs_6_
  31.6 0.1 concatenate.27.refs_3_.refs_5_
  31.8 2.5 %shard_map.110 = (bf16[48,64,128]{2,1,0:T(8,128)(2,1)S(1)}, bf16[48,64,128]{2,1,0:T(8,128)(2,1)S(1)}, bf16[48,64,128]{2,1,0:T(8,128)(2,1)S(1)}, bf16[48,64,128]{...) custom-call(s32[4]{0:T(128)S(1)} %copy-done.2, ...), custom_call_target="tpu_custom_call" | custom-call | bytes 10485760 | tf_op jit(solution)/shard_map/pallas_call | solution.py:78
  34.4 3.4 %collective-permute-start.3 = (bf16[48,64,128]{2,1,0:T(8,128)(2,1)S(1)}, bf16[48,64,128]{2,1,0:T(8,128)(2,1)S(1)}, u32[]{:S(2)}, u32[]{:S(2)}) collective-permute-start(bf16[48,64,128]{2,1,0:T(8,128)(2,1)S(1)} %get-tuple-element.59), channel_id=1, source_target_pairs={{0,16},{2,18},{4,20},{6,22},{8,24},{10,26},{12,28},{14,30},{16,32}... | collective-permute-start | bytes 2359304 | tf_op jit(solution)/shard_map/ppermute | solution.py:365
  37.7 5.3 %collective-permute-start.4 = (bf16[48,64,128]{2,1,0:T(8,128)(2,1)S(1)}, bf16[48,64,128]{2,1,0:T(8,128)(2,1)S(1)}, u32[]{:S(2)}, u32[]{:S(2)}) collective-permute-start(bf16[48,64,128]{2,1,0:T(8,128)(2,1)S(1)} %get-tuple-element.60), channel_id=1, source_target_pairs={{0,112},{2,114},{4,116},{6,118},{8,120},{10,122},{12,124},{14,126}... | collective-permute-start | bytes 2359304 | tf_op jit(solution)/shard_map/ppermute | solution.py:365
  43.1 1.9 %collective-permute-start.5 = (bf16[48,64,128]{2,1,0:T(8,128)(2,1)S(1)}, bf16[48,64,128]{2,1,0:T(8,128)(2,1)S(1)}, u32[]{:S(2)}, u32[]{:S(2)}) collective-permute-start(bf16[48,64,128]{2,1,0:T(8,128)(2,1)S(1)} %get-tuple-element.71), channel_id=1, source_target_pairs={{0,32},{2,34},{4,36},{6,38},{8,40},{10,42},{12,44},{14,46},{16,48}... | collective-permute-start | bytes 2359304 | tf_op jit(solution)/shard_map/ppermute | solution.py:365
  45.0 6.0 %collective-permute-start.6 = (bf16[48,64,128]{2,1,0:T(8,128)(2,1)S(1)}, bf16[48,64,128]{2,1,0:T(8,128)(2,1)S(1)}, u32[]{:S(2)}, u32[]{:S(2)}) collective-permute-start(bf16[48,64,128]{2,1,0:T(8,128)(2,1)S(1)} %get-tuple-element.72), channel_id=1, source_target_pairs={{0,96},{2,98},{4,100},{6,102},{8,104},{10,106},{12,108},{14,110},{... | collective-permute-start | bytes 2359304 | tf_op jit(solution)/shard_map/ppermute | solution.py:365
  51.0 1.9 %collective-permute-start.7 = (bf16[48,64,128]{2,1,0:T(8,128)(2,1)S(1)}, bf16[48,64,128]{2,1,0:T(8,128)(2,1)S(1)}, u32[]{:S(2)}, u32[]{:S(2)}) collective-permute-start(bf16[48,64,128]{2,1,0:T(8,128)(2,1)S(1)} %get-tuple-element.73), channel_id=1, source_target_pairs={{0,16},{2,18},{4,20},{6,22},{8,24},{10,26},{12,28},{14,30},{16,32}... | collective-permute-start | bytes 2359304 | tf_op jit(solution)/shard_map/ppermute | solution.py:365
  53.0 5.1 %collective-permute-start.8 = (bf16[48,64,128]{2,1,0:T(8,128)(2,1)S(1)}, bf16[48,64,128]{2,1,0:T(8,128)(2,1)S(1)}, u32[]{:S(2)}, u32[]{:S(2)}) collective-permute-start(bf16[48,64,128]{2,1,0:T(8,128)(2,1)S(1)} %get-tuple-element.74), channel_id=1, source_target_pairs={{0,112},{2,114},{4,116},{6,118},{8,120},{10,122},{12,124},{14,126}... | collective-permute-start | bytes 2359304 | tf_op jit(solution)/shard_map/ppermute | solution.py:365
  58.1 1.3 shard_map.111
  59.5 7.5 %shard_map.112 = (f32[8,16,16,128]{3,2,1,0:T(8,128)S(1)}, f32[8,16,16,128]{3,2,1,0:T(8,128)S(1)}, f32[8,16,16,128]{3,2,1,0:T(8,128)S(1)}, f32[8,16,16,128]{3,2,1,0:T(8,128)S(1)}) custom-call(s32[4]{0:T(128)S(1)} %copy-done.2, s32[48,128]{1,0:T(8,128)S(1)} %get-tuple-element.58.list_ref, f32[32]{0:T(128)S(1)} %copy-done.3, f32[32]{0:T(128)S(1)} %copy-done.4, ...), custom_call_target="tpu_custom_call" | custom-call | flops 1000000000 | bytes 10485760 | tf_op jit(solution)/shard_map/pallas_call | solution.py:192
  67.0 0.1 convert_element_type.61
  67.1 5.0 %collective-permute-start.14 = (f16[8,16,16,128]{3,2,1,0:T(8,128)(2,1)S(1)}, f16[8,16,16,128]{3,2,1,0:T(8,128)(2,1)S(1)}, u32[]{:S(2)}, u32[]{:S(2)}) collective-permute-start(f16[8,16,16,128]{3,2,1,0:T(8,128)(2,1)S(1)} %convert_element_type.61), channel_id=1, source_target_pairs={{0,384},{128,0},{256,128},{384,256},{1,385},{129,1},{257,129},{385... | collective-permute-start | bytes 1572872 | tf_op jit(solution)/shard_map/ppermute | solution.py:329
  72.0 0.1 convert_element_type.59
  72.1 0.1 convert_element_type.57
  72.2 1.9 %collective-permute-start.13 = (f16[8,16,16,128]{3,2,1,0:T(8,128)(2,1)S(1)}, f16[8,16,16,128]{3,2,1,0:T(8,128)(2,1)S(1)}, u32[]{:S(2)}, u32[]{:S(2)}) collective-permute-start(f16[8,16,16,128]{3,2,1,0:T(8,128)(2,1)S(1)} %convert_element_type.59), channel_id=1, source_target_pairs={{0,128},{128,256},{256,384},{384,0},{1,129},{129,257},{257,385},{3... | collective-permute-start | bytes 1572872 | tf_op jit(solution)/shard_map/ppermute | solution.py:329
  74.1 4.2 %collective-permute-start.12 = (f16[8,16,16,128]{3,2,1,0:T(8,128)(2,1)S(1)}, f16[8,16,16,128]{3,2,1,0:T(8,128)(2,1)S(1)}, u32[]{:S(2)}, u32[]{:S(2)}) collective-permute-start(f16[8,16,16,128]{3,2,1,0:T(8,128)(2,1)S(1)} %convert_element_type.57), channel_id=1, source_target_pairs={{0,256},{128,384},{256,0},{384,128},{1,257},{129,385},{257,1},{385... | collective-permute-start | bytes 1572872 | tf_op jit(solution)/shard_map/ppermute | solution.py:329
  78.3 8.8 %shard_map.113 = (f32[8,16,16,128]{3,2,1,0:T(8,128)S(1)}, f32[8,16,16,128]{3,2,1,0:T(8,128)S(1)}, f32[8,16,16,128]{3,2,1,0:T(8,128)S(1)}, f32[8,16,16,128]{3,2,1,0:T(8,128)S(1)}) custom-call(s32[4]{0:T(128)S(1)} %copy-done.2, s32[48,128]{1,0:T(8,128)S(1)} %get-tuple-element.70.list_ref, f32[32]{0:T(128)S(1)} %copy-done.3, f32[32]{0:T(128)S(1)} %copy-done.4, ...), custom_call_target="tpu_custom_call" | custom-call | flops 1000000000 | bytes 10485760 | tf_op jit(solution)/shard_map/pallas_call | solution.py:192
  87.1 0.1 convert_element_type.55
  87.2 5.3 %collective-permute-start.11 = (f16[8,16,16,128]{3,2,1,0:T(8,128)(2,1)S(1)}, f16[8,16,16,128]{3,2,1,0:T(8,128)(2,1)S(1)}, u32[]{:S(2)}, u32[]{:S(2)}) collective-permute-start(f16[8,16,16,128]{3,2,1,0:T(8,128)(2,1)S(1)} %convert_element_type.55), channel_id=1, source_target_pairs={{0,256},{128,384},{256,0},{384,128},{1,257},{129,385},{257,1},{385... | collective-permute-start | bytes 1572872 | tf_op jit(solution)/shard_map/ppermute | solution.py:329
  92.6 0.1 convert_element_type.53
  92.6 3.3 %collective-permute-start.10 = (f16[8,16,16,128]{3,2,1,0:T(8,128)(2,1)S(1)}, f16[8,16,16,128]{3,2,1,0:T(8,128)(2,1)S(1)}, u32[]{:S(2)}, u32[]{:S(2)}) collective-permute-start(f16[8,16,16,128]{3,2,1,0:T(8,128)(2,1)S(1)} %convert_element_type.53), channel_id=1, source_target_pairs={{0,384},{128,0},{256,128},{384,256},{1,385},{129,1},{257,129},{385... | collective-permute-start | bytes 1572872 | tf_op jit(solution)/shard_map/ppermute | solution.py:329
  95.9 0.1 convert_element_type.51
  96.0 2.8 %collective-permute-done.14 = f16[8,16,16,128]{3,2,1,0:T(8,128)(2,1)S(1)} collective-permute-done((f16[8,16,16,128]{3,2,1,0:T(8,128)(2,1)S(1)}, f16[8,16,16,128]{3,2,1,0:T(8,128)(2,1)S(1)}, u32[]{:S(2)}, u32[]{:S(2)}) %collective-permute-start.14) | collective-permute-done | bytes 524320 | tf_op jit(solution)/shard_map/ppermute | solution.py:329
  98.8 1.9 %collective-permute-start.9 = (f16[8,16,16,128]{3,2,1,0:T(8,128)(2,1)S(1)}, f16[8,16,16,128]{3,2,1,0:T(8,128)(2,1)S(1)}, u32[]{:S(2)}, u32[]{:S(2)}) collective-permute-start(f16[8,16,16,128]{3,2,1,0:T(8,128)(2,1)S(1)} %convert_element_type.51), channel_id=1, source_target_pairs={{0,128},{128,256},{256,384},{384,0},{1,129},{129,257},{257,385},{3... | collective-permute-start | bytes 1572872 | tf_op jit(solution)/shard_map/ppermute | solution.py:329
  100.7 1.9 %collective-permute-done.13 = f16[8,16,16,128]{3,2,1,0:T(8,128)(2,1)S(1)} collective-permute-done((f16[8,16,16,128]{3,2,1,0:T(8,128)(2,1)S(1)}, f16[8,16,16,128]{3,2,1,0:T(8,128)(2,1)S(1)}, u32[]{:S(2)}, u32[]{:S(2)}) %collective-permute-start.13) | collective-permute-done | bytes 524320 | tf_op jit(solution)/shard_map/ppermute | solution.py:329
  102.6 0.3 add_convert_fusion.1
  102.9 4.4 %collective-permute-start.15 = (f16[8,16,16,128]{3,2,1,0:T(8,128)(2,1)S(1)}, f16[8,16,16,128]{3,2,1,0:T(8,128)(2,1)S(1)}, u32[]{:S(2)}, u32[]{:S(2)}) collective-permute-start(f16[8,16,16,128]{3,2,1,0:T(8,128)(2,1)S(1)} %add_convert_fusion.1), channel_id=1, source_target_pairs={{0,64},{2,66},{4,68},{6,70},{8,72},{10,74},{12,76},{14,78},{16,80}... | collective-permute-start | bytes 1572872 | tf_op jit(solution)/shard_map/ppermute | solution.py:373
  107.3 2.3 %collective-permute-done.11 = f16[8,16,16,128]{3,2,1,0:T(8,128)(2,1)S(1)} collective-permute-done((f16[8,16,16,128]{3,2,1,0:T(8,128)(2,1)S(1)}, f16[8,16,16,128]{3,2,1,0:T(8,128)(2,1)S(1)}, u32[]{:S(2)}, u32[]{:S(2)}) %collective-permute-start.11) | collective-permute-done | bytes 524320 | tf_op jit(solution)/shard_map/ppermute | solution.py:329
  109.6 2.7 %collective-permute-done.10 = f16[8,16,16,128]{3,2,1,0:T(8,128)(2,1)S(1)} collective-permute-done((f16[8,16,16,128]{3,2,1,0:T(8,128)(2,1)S(1)}, f16[8,16,16,128]{3,2,1,0:T(8,128)(2,1)S(1)}, u32[]{:S(2)}, u32[]{:S(2)}) %collective-permute-start.10) | collective-permute-done | bytes 524320 | tf_op jit(solution)/shard_map/ppermute | solution.py:329
  112.3 4.7 %collective-permute-done.9 = f16[8,16,16,128]{3,2,1,0:T(8,128)(2,1)S(1)} collective-permute-done((f16[8,16,16,128]{3,2,1,0:T(8,128)(2,1)S(1)}, f16[8,16,16,128]{3,2,1,0:T(8,128)(2,1)S(1)}, u32[]{:S(2)}, u32[]{:S(2)}) %collective-permute-start.9) | collective-permute-done | bytes 524320 | tf_op jit(solution)/shard_map/ppermute | solution.py:329
  117.0 6.5 %collective-permute-done.15 = f16[8,16,16,128]{3,2,1,0:T(8,128)(2,1)S(1)} collective-permute-done((f16[8,16,16,128]{3,2,1,0:T(8,128)(2,1)S(1)}, f16[8,16,16,128]{3,2,1,0:T(8,128)(2,1)S(1)}, u32[]{:S(2)}, u32[]{:S(2)}) %collective-permute-start.15) | collective-permute-done | bytes 524320 | tf_op jit(solution)/shard_map/ppermute | solution.py:373
  123.5 1.2 add_convert_fusion
  124.7 12.4 %all-to-all-start.1 = ((f16[8,16,16,128]{3,2,1,0:T(8,128)(2,1)}), f16[8,16,16,128]{3,2,1,0:T(8,128)(2,1)S(1)}, u32[]{:S(2)}, u32[]{:S(2)}) async-start(f16[8,16,16,128]{3,2,1,0:T(8,128)(2,1)} %add_convert_fusion), calls=%async_computation.1 | async-start | bytes 1048576 | tf_op jit(solution)/shard_map/all_to_all | solution.py:376
  137.2 0.2 select_reduce_fusion
  137.3 0.2 convolution_bitcast_fusion
  137.6 0.1 fusion.18
  137.7 11.3 %all-to-all-done.1 = f16[8,16,16,128]{3,2,1,0:T(8,128)(2,1)S(1)} async-done(((f16[8,16,16,128]{3,2,1,0:T(8,128)(2,1)}), f16[8,16,16,128]{3,2,1,0:T(8,128)(2,1)S(1)}, u32[]{:S(2)}, u32[]{:S(2)}) %all-to-all-start.1) | async-done | bytes 524320 | tf_op jit(solution)/shard_map/all_to_all | solution.py:376
  149.1 0.8 fusion.4
  (28 shorter events, 0.1 us)
Async XLA Ops:
  0.0 31.5 %copy-start.5 = (bf16[64,64]{1,0:T(8,128)(2,1)S(1)}, bf16[64,64]{1,0:T(8,128)(2,1)}, u32[]{:S(2)}) copy-start(bf16[64,64]{1,0:T(8,128)(2,1)} %param.17) | copy-start | bytes 24580
  3.0 28.8 %copy-start = (bf16[1,1,128,64,128]{4,3,2,1,0:T(8,128)(2,1)S(1)}, bf16[1,1,128,64,128]{4,3,2,1,0:T(8,128)(2,1)}, u32[]{:S(2)}) copy-start(bf16[1,1,128,64,128]{4,3,2,1,0:T(8,128)(2,1)} %param.11) | copy-start | bytes 6291460
  3.0 28.8 %copy-start.2 = (s32[4]{0:T(128)S(1)}, s32[4]{0:T(128)}, u32[]{:S(2)}) copy-start(s32[4]{0:T(128)} %pad_add_fusion.spot_ref) | copy-start | bytes 52
  3.0 28.8 %collective-permute-start.1 = (bf16[128,64,128]{2,1,0:T(8,128)(2,1)}, bf16[128,64,128]{2,1,0:T(8,128)(2,1)}, u32[]{:S(2)}, u32[]{:S(2)}) collective-permute-start(bf16[128,64,128]{2,1,0:T(8,128)(2,1)} %bitcast.19), channel_id=1, source_target_pairs={{0,1},{1,0},{2,3},{3,2},{4,5},{5,4},{6,7},{7,6},{8,9},{9,8},{10,11... | collective-permute-start | bytes 6291464 | tf_op jit(solution)/shard_map/ppermute | solution.py:354
  5.1 17.1 %all-to-all-start = ((s32[8,40,128]{2,1,0:T(8,128)}), s32[8,40,128]{2,1,0:T(8,128)S(1)}, u32[]{:S(2)}, u32[]{:S(2)}) async-start(s32[8,40,128]{2,1,0:T(8,128)} %shard_map.109), calls=%async_computation | async-start | bytes 327680 | tf_op jit(solution)/shard_map/all_to_all | solution.py:350
  14.2 17.6 %collective-permute-start = (s32[384]{0:T(512)S(1)}, s32[384]{0:T(512)S(1)}, u32[]{:S(2)}, u32[]{:S(2)}) collective-permute-start(s32[384]{0:T(512)S(1)} %bitcast.21), channel_id=1, source_target_pairs={{0,1},{1,0},{2,3},{3,2},{4,5},{5,4},{6,7},{7,6},{8,9},{9,8},{10,11... | collective-permute-start | bytes 4616 | tf_op jit(solution)/shard_map/ppermute | solution.py:355
  22.2 12.1 %collective-permute-start.2 = (s32[40,128]{1,0:T(8,128)S(1)}, s32[40,128]{1,0:T(8,128)S(1)}, u32[]{:S(2)}, u32[]{:S(2)}) collective-permute-start(s32[40,128]{1,0:T(8,128)S(1)} %reduce_sum.27.refs_1_), channel_id=1, source_target_pairs={{0,64},{2,66},{4,68},{6,70},{8,72},{10,74},{12,76},{14,78},{16,80}... | collective-permute-start | bytes 61448 | tf_op jit(solution)/shard_map/ppermute | solution.py:357
  31.8 27.7 %copy-start.1 = (bf16[16,16,128]{2,1,0:T(8,128)(2,1)S(1)}, bf16[16,16,128]{2,1,0:T(8,128)(2,1)}, u32[]{:S(2)}) copy-start(bf16[16,16,128]{2,1,0:T(8,128)(2,1)} %refs_7_) | copy-start | bytes 196612
  31.8 27.7 %copy-start.3 = (f32[32]{0:T(128)S(1)}, f32[32]{0:T(128)}, u32[]{:S(2)}) copy-start(f32[32]{0:T(128)} %re_ref.3) | copy-start | bytes 388
  31.8 27.7 %copy-start.4 = (f32[32]{0:T(128)S(1)}, f32[32]{0:T(128)}, u32[]{:S(2)}) copy-start(f32[32]{0:T(128)} %im_ref.3) | copy-start | bytes 388
  34.4 18.6 %collective-permute-start.3 = (bf16[48,64,128]{2,1,0:T(8,128)(2,1)S(1)}, bf16[48,64,128]{2,1,0:T(8,128)(2,1)S(1)}, u32[]{:S(2)}, u32[]{:S(2)}) collective-permute-start(bf16[48,64,128]{2,1,0:T(8,128)(2,1)S(1)} %get-tuple-element.59), channel_id=1, source_target_pairs={{0,16},{2,18},{4,20},{6,22},{8,24},{10,26},{12,28},{14,30},{16,32}... | collective-permute-start | bytes 2359304 | tf_op jit(solution)/shard_map/ppermute | solution.py:365
  37.7 21.7 %collective-permute-start.4 = (bf16[48,64,128]{2,1,0:T(8,128)(2,1)S(1)}, bf16[48,64,128]{2,1,0:T(8,128)(2,1)S(1)}, u32[]{:S(2)}, u32[]{:S(2)}) collective-permute-start(bf16[48,64,128]{2,1,0:T(8,128)(2,1)S(1)} %get-tuple-element.60), channel_id=1, source_target_pairs={{0,112},{2,114},{4,116},{6,118},{8,120},{10,122},{12,124},{14,126}... | collective-permute-start | bytes 2359304 | tf_op jit(solution)/shard_map/ppermute | solution.py:365
  43.1 29.1 %collective-permute-start.5 = (bf16[48,64,128]{2,1,0:T(8,128)(2,1)S(1)}, bf16[48,64,128]{2,1,0:T(8,128)(2,1)S(1)}, u32[]{:S(2)}, u32[]{:S(2)}) collective-permute-start(bf16[48,64,128]{2,1,0:T(8,128)(2,1)S(1)} %get-tuple-element.71), channel_id=1, source_target_pairs={{0,32},{2,34},{4,36},{6,38},{8,40},{10,42},{12,44},{14,46},{16,48}... | collective-permute-start | bytes 2359304 | tf_op jit(solution)/shard_map/ppermute | solution.py:365
  45.0 29.1 %collective-permute-start.6 = (bf16[48,64,128]{2,1,0:T(8,128)(2,1)S(1)}, bf16[48,64,128]{2,1,0:T(8,128)(2,1)S(1)}, u32[]{:S(2)}, u32[]{:S(2)}) collective-permute-start(bf16[48,64,128]{2,1,0:T(8,128)(2,1)S(1)} %get-tuple-element.72), channel_id=1, source_target_pairs={{0,96},{2,98},{4,100},{6,102},{8,104},{10,106},{12,108},{14,110},{... | collective-permute-start | bytes 2359304 | tf_op jit(solution)/shard_map/ppermute | solution.py:365
  51.0 27.3 %collective-permute-start.7 = (bf16[48,64,128]{2,1,0:T(8,128)(2,1)S(1)}, bf16[48,64,128]{2,1,0:T(8,128)(2,1)S(1)}, u32[]{:S(2)}, u32[]{:S(2)}) collective-permute-start(bf16[48,64,128]{2,1,0:T(8,128)(2,1)S(1)} %get-tuple-element.73), channel_id=1, source_target_pairs={{0,16},{2,18},{4,20},{6,22},{8,24},{10,26},{12,28},{14,30},{16,32}... | collective-permute-start | bytes 2359304 | tf_op jit(solution)/shard_map/ppermute | solution.py:365
  53.0 25.3 %collective-permute-start.8 = (bf16[48,64,128]{2,1,0:T(8,128)(2,1)S(1)}, bf16[48,64,128]{2,1,0:T(8,128)(2,1)S(1)}, u32[]{:S(2)}, u32[]{:S(2)}) collective-permute-start(bf16[48,64,128]{2,1,0:T(8,128)(2,1)S(1)} %get-tuple-element.74), channel_id=1, source_target_pairs={{0,112},{2,114},{4,116},{6,118},{8,120},{10,122},{12,124},{14,126}... | collective-permute-start | bytes 2359304 | tf_op jit(solution)/shard_map/ppermute | solution.py:365
  67.1 31.7 %collective-permute-start.14 = (f16[8,16,16,128]{3,2,1,0:T(8,128)(2,1)S(1)}, f16[8,16,16,128]{3,2,1,0:T(8,128)(2,1)S(1)}, u32[]{:S(2)}, u32[]{:S(2)}) collective-permute-start(f16[8,16,16,128]{3,2,1,0:T(8,128)(2,1)S(1)} %convert_element_type.61), channel_id=1, source_target_pairs={{0,384},{128,0},{256,128},{384,256},{1,385},{129,1},{257,129},{385... | collective-permute-start | bytes 1572872 | tf_op jit(solution)/shard_map/ppermute | solution.py:329
  72.2 30.4 %collective-permute-start.13 = (f16[8,16,16,128]{3,2,1,0:T(8,128)(2,1)S(1)}, f16[8,16,16,128]{3,2,1,0:T(8,128)(2,1)S(1)}, u32[]{:S(2)}, u32[]{:S(2)}) collective-permute-start(f16[8,16,16,128]{3,2,1,0:T(8,128)(2,1)S(1)} %convert_element_type.59), channel_id=1, source_target_pairs={{0,128},{128,256},{256,384},{384,0},{1,129},{129,257},{257,385},{3... | collective-permute-start | bytes 1572872 | tf_op jit(solution)/shard_map/ppermute | solution.py:329
  74.1 28.5 %collective-permute-start.12 = (f16[8,16,16,128]{3,2,1,0:T(8,128)(2,1)S(1)}, f16[8,16,16,128]{3,2,1,0:T(8,128)(2,1)S(1)}, u32[]{:S(2)}, u32[]{:S(2)}) collective-permute-start(f16[8,16,16,128]{3,2,1,0:T(8,128)(2,1)S(1)} %convert_element_type.57), channel_id=1, source_target_pairs={{0,256},{128,384},{256,0},{384,128},{1,257},{129,385},{257,1},{385... | collective-permute-start | bytes 1572872 | tf_op jit(solution)/shard_map/ppermute | solution.py:329
  87.2 22.4 %collective-permute-start.11 = (f16[8,16,16,128]{3,2,1,0:T(8,128)(2,1)S(1)}, f16[8,16,16,128]{3,2,1,0:T(8,128)(2,1)S(1)}, u32[]{:S(2)}, u32[]{:S(2)}) collective-permute-start(f16[8,16,16,128]{3,2,1,0:T(8,128)(2,1)S(1)} %convert_element_type.55), channel_id=1, source_target_pairs={{0,256},{128,384},{256,0},{384,128},{1,257},{129,385},{257,1},{385... | collective-permute-start | bytes 1572872 | tf_op jit(solution)/shard_map/ppermute | solution.py:329
  92.6 19.7 %collective-permute-start.10 = (f16[8,16,16,128]{3,2,1,0:T(8,128)(2,1)S(1)}, f16[8,16,16,128]{3,2,1,0:T(8,128)(2,1)S(1)}, u32[]{:S(2)}, u32[]{:S(2)}) collective-permute-start(f16[8,16,16,128]{3,2,1,0:T(8,128)(2,1)S(1)} %convert_element_type.53), channel_id=1, source_target_pairs={{0,384},{128,0},{256,128},{384,256},{1,385},{129,1},{257,129},{385... | collective-permute-start | bytes 1572872 | tf_op jit(solution)/shard_map/ppermute | solution.py:329
  98.8 18.3 %collective-permute-start.9 = (f16[8,16,16,128]{3,2,1,0:T(8,128)(2,1)S(1)}, f16[8,16,16,128]{3,2,1,0:T(8,128)(2,1)S(1)}, u32[]{:S(2)}, u32[]{:S(2)}) collective-permute-start(f16[8,16,16,128]{3,2,1,0:T(8,128)(2,1)S(1)} %convert_element_type.51), channel_id=1, source_target_pairs={{0,128},{128,256},{256,384},{384,0},{1,129},{129,257},{257,385},{3... | collective-permute-start | bytes 1572872 | tf_op jit(solution)/shard_map/ppermute | solution.py:329
  102.9 20.6 %collective-permute-start.15 = (f16[8,16,16,128]{3,2,1,0:T(8,128)(2,1)S(1)}, f16[8,16,16,128]{3,2,1,0:T(8,128)(2,1)S(1)}, u32[]{:S(2)}, u32[]{:S(2)}) collective-permute-start(f16[8,16,16,128]{3,2,1,0:T(8,128)(2,1)S(1)} %add_convert_fusion.1), channel_id=1, source_target_pairs={{0,64},{2,66},{4,68},{6,70},{8,72},{10,74},{12,76},{14,78},{16,80}... | collective-permute-start | bytes 1572872 | tf_op jit(solution)/shard_map/ppermute | solution.py:373
  123.5 13.6 %copy-start.6 = (s32[16,3]{0,1:T(4,128)S(1)}, s32[16,3]{0,1:T(4,128)}, u32[]{:S(2)}) copy-start(s32[16,3]{0,1:T(4,128)} %param.14) | copy-start | bytes 580
  123.5 13.6 %copy-start.7 = (f32[128]{0:T(128)S(1)}, f32[128]{0:T(128)}, u32[]{:S(2)}) copy-start(f32[128]{0:T(128)} %param.21) | copy-start | bytes 1540
  124.7 24.2 %all-to-all-start.1 = ((f16[8,16,16,128]{3,2,1,0:T(8,128)(2,1)}), f16[8,16,16,128]{3,2,1,0:T(8,128)(2,1)S(1)}, u32[]{:S(2)}, u32[]{:S(2)}) async-start(f16[8,16,16,128]{3,2,1,0:T(8,128)(2,1)} %add_convert_fusion), calls=%async_computation.1 | async-start | bytes 1048576 | tf_op jit(solution)/shard_map/all_to_all | solution.py:376

commit v18 on v14

--- a/solution.py
+++ b/solution.py
@@ -127,7 +127,7 @@
         )
         return rotate(left - right)
 
-    together = 16
+    together = 32
 
     def first(index, carry):
         for j in range(together):

time: 140 us -> 140 us (level); the launches traced: 139 us -> 137 us
  Pallas kernels: 23.9 us -> 20.6 us
    pallas_call x2, Pallas kernels: 18.5 us -> 15.1 us  [terms(): pl.pallas_call(functools.partial(terms_kernel, sources, modes, windows, p...]
    all_to_all x1, starting transfers between devices: 5.22 us -> 3.49 us  [on_device(): lax.all_to_all((near + far.astype(F32)).astype(LINK), 'ado', split_axis=0...]
    ppermute x6, starting transfers between devices: 20.9 us -> 22.6 us  [over_groups(): lax.ppermute(parts[shift].astype(LINK), 'grp', ring).astype(F32)]
  transfers between devices with their start and end apart: 18 -> 18, of which waited for: 7 -> 6; matrix products, arithmetic and copies ran while one was open for 2% -> 2% of each run, Pallas kernels for 16% -> 14%
where the time goes in v18:
time: 140 us; the launch traced here: 137 us
  starting transfers between devices  72.3 us (52%)
  waiting for transfers between devices  37.2 us (27%)
  Pallas kernels  20.6 us (15%)
  other arithmetic  5.28 us (4%)
    ppermute x6, starting transfers between devices, over_groups(): lax.ppermute(parts[shift].astype(LINK), 'grp', ring).astype(F32)  22.6 us
    ppermute x6, starting transfers between devices, on_device(): lax.ppermute(block, 'ado', onward(step))  21 us
    pallas_call x2, Pallas kernels, terms(): pl.pallas_call(functools.partial(terms_kernel, sources, modes, windows, p...  15.1 us
    all_to_all x1, waiting for transfers between devices, on_device(): lax.all_to_all((near + far.astype(F32)).astype(LINK), 'ado', split_axis=0...  12.7 us
    ppermute x1, waiting for transfers between devices, on_device(): far = lax.ppermute(over_groups(far).astype(LINK), 'ado', onward(4))  10.2 us
    ppermute x1, starting transfers between devices, on_device(): heard_far = lax.ppermute(heard, 'ado', onward(4))  8.22 us
    all_to_all x1, starting transfers between devices, on_device(): lax.all_to_all(said, 'ado', split_axis=0, concat_axis=0, tiled=True, axis...  7.11 us
    ppermute x6, waiting for transfers between devices, over_groups(): lax.ppermute(parts[shift].astype(LINK), 'grp', ring).astype(F32)  5.27 us
  transfers between devices with their start and end apart: 18, of which 6 were waited for; matrix products, arithmetic and copies ran while one was open for 2% of the time, Pallas kernels for 14%

profile of v18, /device:TPU:194, one launch (start us, length us, event | category | flops | bytes accessed | tf_op | source)
XLA Modules:
  0.0 136.9 jit_solution(15008705040609810047)
XLA Ops:
  0.0 0.7 copy.15
  0.7 0.6 pad_add_fusion.spot_ref
  1.3 1.7 %shard_map.109 = s32[8,40,128]{2,1,0:T(8,128)} custom-call(s32[4]{0:T(128)} %pad_add_fusion.spot_ref, s32[16,32]{1,0:T(8,128)} %up_ref.1, s32[3,16]{1,0:T(4,128)} %bitcast.24, s32[3,16]{1,0:T(4,128)} %bitcast.23), custom_call_target="tpu_custom_call" | custom-call | flops 1000000 | bytes 262144 | tf_op jit(solution)/shard_map/pallas_call | solution.py:315
  3.0 2.0 %collective-permute-start.1 = (bf16[128,64,128]{2,1,0:T(8,128)(2,1)}, bf16[128,64,128]{2,1,0:T(8,128)(2,1)}, u32[]{:S(2)}, u32[]{:S(2)}) collective-permute-start(bf16[128,64,128]{2,1,0:T(8,128)(2,1)} %bitcast.19), channel_id=1, source_target_pairs={{0,1},{1,0},{2,3},{3,2},{4,5},{5,4},{6,7},{7,6},{8,9},{9,8},{10,11... | collective-permute-start | bytes 6291464 | tf_op jit(solution)/shard_map/ppermute | solution.py:354
  5.1 7.1 %all-to-all-start = ((s32[8,40,128]{2,1,0:T(8,128)}), s32[8,40,128]{2,1,0:T(8,128)S(1)}, u32[]{:S(2)}, u32[]{:S(2)}) async-start(s32[8,40,128]{2,1,0:T(8,128)} %shard_map.109), calls=%async_computation | async-start | bytes 327680 | tf_op jit(solution)/shard_map/all_to_all | solution.py:350
  12.2 2.9 %collective-permute-start = (s32[384]{0:T(512)S(1)}, s32[384]{0:T(512)S(1)}, u32[]{:S(2)}, u32[]{:S(2)}) collective-permute-start(s32[384]{0:T(512)S(1)} %bitcast.21), channel_id=1, source_target_pairs={{0,1},{1,0},{2,3},{3,2},{4,5},{5,4},{6,7},{7,6},{8,9},{9,8},{10,11... | collective-permute-start | bytes 4616 | tf_op jit(solution)/shard_map/ppermute | solution.py:355
  15.1 1.5 %fusion.2 = bf16[32,128,128]{2,1,0:T(8,128)(2,1)S(1)} fusion(bf16[32,64,64]{2,1,0:T(8,128)(2,1)} %param.18), kind=kLoop, calls=%fused_computation.5 | loop fusion | flops 4194304 | bytes 1310720 | tf_op jit(solution)/shard_map/concatenate | solution.py:23
  16.6 5.0 %all-to-all-done = s32[8,40,128]{2,1,0:T(8,128)S(1)} async-done(((s32[8,40,128]{2,1,0:T(8,128)}), s32[8,40,128]{2,1,0:T(8,128)S(1)}, u32[]{:S(2)}, u32[]{:S(2)}) %all-to-all-start) | async-done | bytes 163872 | tf_op jit(solution)/shard_map/all_to_all | solution.py:350
  21.6 8.2 %collective-permute-start.2 = (s32[40,128]{1,0:T(8,128)S(1)}, s32[40,128]{1,0:T(8,128)S(1)}, u32[]{:S(2)}, u32[]{:S(2)}) collective-permute-start(s32[40,128]{1,0:T(8,128)S(1)} %reduce_sum.27.refs_1_), channel_id=1, source_target_pairs={{0,64},{2,66},{4,68},{6,70},{8,72},{10,74},{12,76},{14,78},{16,80}... | collective-permute-start | bytes 61448 | tf_op jit(solution)/shard_map/ppermute | solution.py:357
  29.9 0.1 constant_dynamic-slice_fusion.refs_4_.refs_6_
  29.9 0.1 concatenate.27.refs_3_.refs_5_
  30.1 0.0 copy-start.1
  30.2 2.5 %shard_map.110 = (bf16[48,64,128]{2,1,0:T(8,128)(2,1)S(1)}, bf16[48,64,128]{2,1,0:T(8,128)(2,1)S(1)}, bf16[48,64,128]{2,1,0:T(8,128)(2,1)S(1)}, bf16[48,64,128]{...) custom-call(s32[4]{0:T(128)S(1)} %copy-done.2, ...), custom_call_target="tpu_custom_call" | custom-call | bytes 10485760 | tf_op jit(solution)/shard_map/pallas_call | solution.py:78
  32.7 4.0 %collective-permute-start.3 = (bf16[48,64,128]{2,1,0:T(8,128)(2,1)S(1)}, bf16[48,64,128]{2,1,0:T(8,128)(2,1)S(1)}, u32[]{:S(2)}, u32[]{:S(2)}) collective-permute-start(bf16[48,64,128]{2,1,0:T(8,128)(2,1)S(1)} %get-tuple-element.59), channel_id=1, source_target_pairs={{0,16},{2,18},{4,20},{6,22},{8,24},{10,26},{12,28},{14,30},{16,32}... | collective-permute-start | bytes 2359304 | tf_op jit(solution)/shard_map/ppermute | solution.py:365
  36.7 1.9 %collective-permute-start.4 = (bf16[48,64,128]{2,1,0:T(8,128)(2,1)S(1)}, bf16[48,64,128]{2,1,0:T(8,128)(2,1)S(1)}, u32[]{:S(2)}, u32[]{:S(2)}) collective-permute-start(bf16[48,64,128]{2,1,0:T(8,128)(2,1)S(1)} %get-tuple-element.60), channel_id=1, source_target_pairs={{0,112},{2,114},{4,116},{6,118},{8,120},{10,122},{12,124},{14,126}... | collective-permute-start | bytes 2359304 | tf_op jit(solution)/shard_map/ppermute | solution.py:365
  38.6 4.8 %collective-permute-start.5 = (bf16[48,64,128]{2,1,0:T(8,128)(2,1)S(1)}, bf16[48,64,128]{2,1,0:T(8,128)(2,1)S(1)}, u32[]{:S(2)}, u32[]{:S(2)}) collective-permute-start(bf16[48,64,128]{2,1,0:T(8,128)(2,1)S(1)} %get-tuple-element.71), channel_id=1, source_target_pairs={{0,32},{2,34},{4,36},{6,38},{8,40},{10,42},{12,44},{14,46},{16,48}... | collective-permute-start | bytes 2359304 | tf_op jit(solution)/shard_map/ppermute | solution.py:365
  43.5 1.9 %collective-permute-start.6 = (bf16[48,64,128]{2,1,0:T(8,128)(2,1)S(1)}, bf16[48,64,128]{2,1,0:T(8,128)(2,1)S(1)}, u32[]{:S(2)}, u32[]{:S(2)}) collective-permute-start(bf16[48,64,128]{2,1,0:T(8,128)(2,1)S(1)} %get-tuple-element.72), channel_id=1, source_target_pairs={{0,96},{2,98},{4,100},{6,102},{8,104},{10,106},{12,108},{14,110},{... | collective-permute-start | bytes 2359304 | tf_op jit(solution)/shard_map/ppermute | solution.py:365
  45.4 6.3 %collective-permute-start.7 = (bf16[48,64,128]{2,1,0:T(8,128)(2,1)S(1)}, bf16[48,64,128]{2,1,0:T(8,128)(2,1)S(1)}, u32[]{:S(2)}, u32[]{:S(2)}) collective-permute-start(bf16[48,64,128]{2,1,0:T(8,128)(2,1)S(1)} %get-tuple-element.73), channel_id=1, source_target_pairs={{0,16},{2,18},{4,20},{6,22},{8,24},{10,26},{12,28},{14,30},{16,32}... | collective-permute-start | bytes 2359304 | tf_op jit(solution)/shard_map/ppermute | solution.py:365
  51.8 1.9 %collective-permute-start.8 = (bf16[48,64,128]{2,1,0:T(8,128)(2,1)S(1)}, bf16[48,64,128]{2,1,0:T(8,128)(2,1)S(1)}, u32[]{:S(2)}, u32[]{:S(2)}) collective-permute-start(bf16[48,64,128]{2,1,0:T(8,128)(2,1)S(1)} %get-tuple-element.74), channel_id=1, source_target_pairs={{0,112},{2,114},{4,116},{6,118},{8,120},{10,122},{12,124},{14,126}... | collective-permute-start | bytes 2359304 | tf_op jit(solution)/shard_map/ppermute | solution.py:365
  53.7 1.3 shard_map.111
  55.0 6.9 %shard_map.112 = (f32[8,16,16,128]{3,2,1,0:T(8,128)S(1)}, f32[8,16,16,128]{3,2,1,0:T(8,128)S(1)}, f32[8,16,16,128]{3,2,1,0:T(8,128)S(1)}, f32[8,16,16,128]{3,2,1,0:T(8,128)S(1)}) custom-call(s32[4]{0:T(128)S(1)} %copy-done.2, s32[48,128]{1,0:T(8,128)S(1)} %get-tuple-element.58.list_ref, f32[32]{0:T(128)S(1)} %copy-done.3, f32[32]{0:T(128)S(1)} %copy-done.4, ...), custom_call_target="tpu_custom_call" | custom-call | flops 1000000000 | bytes 10485760 | tf_op jit(solution)/shard_map/pallas_call | solution.py:192
  62.0 0.1 convert_element_type.61
  62.1 2.5 %collective-permute-start.14 = (f16[8,16,16,128]{3,2,1,0:T(8,128)(2,1)S(1)}, f16[8,16,16,128]{3,2,1,0:T(8,128)(2,1)S(1)}, u32[]{:S(2)}, u32[]{:S(2)}) collective-permute-start(f16[8,16,16,128]{3,2,1,0:T(8,128)(2,1)S(1)} %convert_element_type.61), channel_id=1, source_target_pairs={{0,384},{128,0},{256,128},{384,256},{1,385},{129,1},{257,129},{385... | collective-permute-start | bytes 1572872 | tf_op jit(solution)/shard_map/ppermute | solution.py:329
  64.6 0.1 convert_element_type.59
  64.6 0.1 convert_element_type.57
  64.7 3.4 %collective-permute-start.13 = (f16[8,16,16,128]{3,2,1,0:T(8,128)(2,1)S(1)}, f16[8,16,16,128]{3,2,1,0:T(8,128)(2,1)S(1)}, u32[]{:S(2)}, u32[]{:S(2)}) collective-permute-start(f16[8,16,16,128]{3,2,1,0:T(8,128)(2,1)S(1)} %convert_element_type.59), channel_id=1, source_target_pairs={{0,128},{128,256},{256,384},{384,0},{1,129},{129,257},{257,385},{3... | collective-permute-start | bytes 1572872 | tf_op jit(solution)/shard_map/ppermute | solution.py:329
  68.1 4.9 %collective-permute-start.12 = (f16[8,16,16,128]{3,2,1,0:T(8,128)(2,1)S(1)}, f16[8,16,16,128]{3,2,1,0:T(8,128)(2,1)S(1)}, u32[]{:S(2)}, u32[]{:S(2)}) collective-permute-start(f16[8,16,16,128]{3,2,1,0:T(8,128)(2,1)S(1)} %convert_element_type.57), channel_id=1, source_target_pairs={{0,256},{128,384},{256,0},{384,128},{1,257},{129,385},{257,1},{385... | collective-permute-start | bytes 1572872 | tf_op jit(solution)/shard_map/ppermute | solution.py:329
  73.1 4.1 %collective-permute-done.8.refs_3_ = bf16[48,64,128]{2,1,0:T(8,128)(2,1)S(1)} collective-permute-done((bf16[48,64,128]{2,1,0:T(8,128)(2,1)S(1)}, bf16[48,64,128]{2,1,0:T(8,128)(2,1)S(1)}, u32[]{:S(2)}, u32[]{:S(2)}) %collective-permute-start.8) | collective-permute-done | bytes 786464 | tf_op jit(solution)/shard_map/ppermute | solution.py:365
  77.1 8.2 %shard_map.113 = (f32[8,16,16,128]{3,2,1,0:T(8,128)S(1)}, f32[8,16,16,128]{3,2,1,0:T(8,128)S(1)}, f32[8,16,16,128]{3,2,1,0:T(8,128)S(1)}, f32[8,16,16,128]{3,2,1,0:T(8,128)S(1)}) custom-call(s32[4]{0:T(128)S(1)} %copy-done.2, s32[48,128]{1,0:T(8,128)S(1)} %get-tuple-element.70.list_ref, f32[32]{0:T(128)S(1)} %copy-done.3, f32[32]{0:T(128)S(1)} %copy-done.4, ...), custom_call_target="tpu_custom_call" | custom-call | flops 1000000000 | bytes 10485760 | tf_op jit(solution)/shard_map/pallas_call | solution.py:192
  85.3 0.1 convert_element_type.55
  85.4 3.4 %collective-permute-start.11 = (f16[8,16,16,128]{3,2,1,0:T(8,128)(2,1)S(1)}, f16[8,16,16,128]{3,2,1,0:T(8,128)(2,1)S(1)}, u32[]{:S(2)}, u32[]{:S(2)}) collective-permute-start(f16[8,16,16,128]{3,2,1,0:T(8,128)(2,1)S(1)} %convert_element_type.55), channel_id=1, source_target_pairs={{0,384},{128,0},{256,128},{384,256},{1,385},{129,1},{257,129},{385... | collective-permute-start | bytes 1572872 | tf_op jit(solution)/shard_map/ppermute | solution.py:329
  88.8 0.1 convert_element_type.53
  88.9 2.6 %collective-permute-start.10 = (f16[8,16,16,128]{3,2,1,0:T(8,128)(2,1)S(1)}, f16[8,16,16,128]{3,2,1,0:T(8,128)(2,1)S(1)}, u32[]{:S(2)}, u32[]{:S(2)}) collective-permute-start(f16[8,16,16,128]{3,2,1,0:T(8,128)(2,1)S(1)} %convert_element_type.53), channel_id=1, source_target_pairs={{0,128},{128,256},{256,384},{384,0},{1,129},{129,257},{257,385},{3... | collective-permute-start | bytes 1572872 | tf_op jit(solution)/shard_map/ppermute | solution.py:329
  91.5 0.1 convert_element_type.51
  91.6 5.8 %collective-permute-start.9 = (f16[8,16,16,128]{3,2,1,0:T(8,128)(2,1)S(1)}, f16[8,16,16,128]{3,2,1,0:T(8,128)(2,1)S(1)}, u32[]{:S(2)}, u32[]{:S(2)}) collective-permute-start(f16[8,16,16,128]{3,2,1,0:T(8,128)(2,1)S(1)} %convert_element_type.51), channel_id=1, source_target_pairs={{0,256},{128,384},{256,0},{384,128},{1,257},{129,385},{257,1},{385... | collective-permute-start | bytes 1572872 | tf_op jit(solution)/shard_map/ppermute | solution.py:329
  97.4 0.3 add_convert_fusion.1
  97.7 5.0 %collective-permute-start.15 = (f16[8,16,16,128]{3,2,1,0:T(8,128)(2,1)S(1)}, f16[8,16,16,128]{3,2,1,0:T(8,128)(2,1)S(1)}, u32[]{:S(2)}, u32[]{:S(2)}) collective-permute-start(f16[8,16,16,128]{3,2,1,0:T(8,128)(2,1)S(1)} %add_convert_fusion.1), channel_id=1, source_target_pairs={{0,64},{2,66},{4,68},{6,70},{8,72},{10,74},{12,76},{14,78},{16,80}... | collective-permute-start | bytes 1572872 | tf_op jit(solution)/shard_map/ppermute | solution.py:373
  102.7 1.8 %collective-permute-done.10 = f16[8,16,16,128]{3,2,1,0:T(8,128)(2,1)S(1)} collective-permute-done((f16[8,16,16,128]{3,2,1,0:T(8,128)(2,1)S(1)}, f16[8,16,16,128]{3,2,1,0:T(8,128)(2,1)S(1)}, u32[]{:S(2)}, u32[]{:S(2)}) %collective-permute-start.10) | collective-permute-done | bytes 524320 | tf_op jit(solution)/shard_map/ppermute | solution.py:329
  104.5 3.5 %collective-permute-done.9 = f16[8,16,16,128]{3,2,1,0:T(8,128)(2,1)S(1)} collective-permute-done((f16[8,16,16,128]{3,2,1,0:T(8,128)(2,1)S(1)}, f16[8,16,16,128]{3,2,1,0:T(8,128)(2,1)S(1)}, u32[]{:S(2)}, u32[]{:S(2)}) %collective-permute-start.9) | collective-permute-done | bytes 524320 | tf_op jit(solution)/shard_map/ppermute | solution.py:329
  108.0 10.2 %collective-permute-done.15 = f16[8,16,16,128]{3,2,1,0:T(8,128)(2,1)S(1)} collective-permute-done((f16[8,16,16,128]{3,2,1,0:T(8,128)(2,1)S(1)}, f16[8,16,16,128]{3,2,1,0:T(8,128)(2,1)S(1)}, u32[]{:S(2)}, u32[]{:S(2)}) %collective-permute-start.15) | collective-permute-done | bytes 524320 | tf_op jit(solution)/shard_map/ppermute | solution.py:373
  118.2 1.2 add_convert_fusion
  119.4 3.5 %all-to-all-start.1 = ((f16[8,16,16,128]{3,2,1,0:T(8,128)(2,1)}), f16[8,16,16,128]{3,2,1,0:T(8,128)(2,1)S(1)}, u32[]{:S(2)}, u32[]{:S(2)}) async-start(f16[8,16,16,128]{3,2,1,0:T(8,128)(2,1)} %add_convert_fusion), calls=%async_computation.1 | async-start | bytes 1048576 | tf_op jit(solution)/shard_map/all_to_all | solution.py:375
  122.9 0.2 select_reduce_fusion
  123.1 0.2 convolution_bitcast_fusion
  123.3 0.1 fusion.18
  123.4 12.7 %all-to-all-done.1 = f16[8,16,16,128]{3,2,1,0:T(8,128)(2,1)S(1)} async-done(((f16[8,16,16,128]{3,2,1,0:T(8,128)(2,1)}), f16[8,16,16,128]{3,2,1,0:T(8,128)(2,1)S(1)}, u32[]{:S(2)}, u32[]{:S(2)}) %all-to-all-start.1) | async-done | bytes 524320 | tf_op jit(solution)/shard_map/all_to_all | solution.py:375
  136.1 0.1 convert_reduce_fusion
  136.2 0.8 fusion.4
  (28 shorter events, 0.1 us)
Async XLA Ops:
  0.0 29.9 %copy-start.5 = (bf16[64,64]{1,0:T(8,128)(2,1)S(1)}, bf16[64,64]{1,0:T(8,128)(2,1)}, u32[]{:S(2)}) copy-start(bf16[64,64]{1,0:T(8,128)(2,1)} %param.17) | copy-start | bytes 24580
  3.0 27.1 %copy-start = (bf16[1,1,128,64,128]{4,3,2,1,0:T(8,128)(2,1)S(1)}, bf16[1,1,128,64,128]{4,3,2,1,0:T(8,128)(2,1)}, u32[]{:S(2)}) copy-start(bf16[1,1,128,64,128]{4,3,2,1,0:T(8,128)(2,1)} %param.11) | copy-start | bytes 6291460
  3.0 27.1 %copy-start.2 = (s32[4]{0:T(128)S(1)}, s32[4]{0:T(128)}, u32[]{:S(2)}) copy-start(s32[4]{0:T(128)} %pad_add_fusion.spot_ref) | copy-start | bytes 52
  3.0 27.1 %collective-permute-start.1 = (bf16[128,64,128]{2,1,0:T(8,128)(2,1)}, bf16[128,64,128]{2,1,0:T(8,128)(2,1)}, u32[]{:S(2)}, u32[]{:S(2)}) collective-permute-start(bf16[128,64,128]{2,1,0:T(8,128)(2,1)} %bitcast.19), channel_id=1, source_target_pairs={{0,1},{1,0},{2,3},{3,2},{4,5},{5,4},{6,7},{7,6},{8,9},{9,8},{10,11... | collective-permute-start | bytes 6291464 | tf_op jit(solution)/shard_map/ppermute | solution.py:354
  5.1 16.5 %all-to-all-start = ((s32[8,40,128]{2,1,0:T(8,128)}), s32[8,40,128]{2,1,0:T(8,128)S(1)}, u32[]{:S(2)}, u32[]{:S(2)}) async-start(s32[8,40,128]{2,1,0:T(8,128)} %shard_map.109), calls=%async_computation | async-start | bytes 327680 | tf_op jit(solution)/shard_map/all_to_all | solution.py:350
  12.2 17.9 %collective-permute-start = (s32[384]{0:T(512)S(1)}, s32[384]{0:T(512)S(1)}, u32[]{:S(2)}, u32[]{:S(2)}) collective-permute-start(s32[384]{0:T(512)S(1)} %bitcast.21), channel_id=1, source_target_pairs={{0,1},{1,0},{2,3},{3,2},{4,5},{5,4},{6,7},{7,6},{8,9},{9,8},{10,11... | collective-permute-start | bytes 4616 | tf_op jit(solution)/shard_map/ppermute | solution.py:355
  21.6 11.0 %collective-permute-start.2 = (s32[40,128]{1,0:T(8,128)S(1)}, s32[40,128]{1,0:T(8,128)S(1)}, u32[]{:S(2)}, u32[]{:S(2)}) collective-permute-start(s32[40,128]{1,0:T(8,128)S(1)} %reduce_sum.27.refs_1_), channel_id=1, source_target_pairs={{0,64},{2,66},{4,68},{6,70},{8,72},{10,74},{12,76},{14,78},{16,80}... | collective-permute-start | bytes 61448 | tf_op jit(solution)/shard_map/ppermute | solution.py:357
  30.1 24.9 %copy-start.1 = (bf16[16,16,128]{2,1,0:T(8,128)(2,1)S(1)}, bf16[16,16,128]{2,1,0:T(8,128)(2,1)}, u32[]{:S(2)}) copy-start(bf16[16,16,128]{2,1,0:T(8,128)(2,1)} %refs_7_) | copy-start | bytes 196612
  30.1 24.9 %copy-start.3 = (f32[32]{0:T(128)S(1)}, f32[32]{0:T(128)}, u32[]{:S(2)}) copy-start(f32[32]{0:T(128)} %re_ref.3) | copy-start | bytes 388
  30.1 24.9 %copy-start.4 = (f32[32]{0:T(128)S(1)}, f32[32]{0:T(128)}, u32[]{:S(2)}) copy-start(f32[32]{0:T(128)} %im_ref.3) | copy-start | bytes 388
  32.7 19.1 %collective-permute-start.3 = (bf16[48,64,128]{2,1,0:T(8,128)(2,1)S(1)}, bf16[48,64,128]{2,1,0:T(8,128)(2,1)S(1)}, u32[]{:S(2)}, u32[]{:S(2)}) collective-permute-start(bf16[48,64,128]{2,1,0:T(8,128)(2,1)S(1)} %get-tuple-element.59), channel_id=1, source_target_pairs={{0,16},{2,18},{4,20},{6,22},{8,24},{10,26},{12,28},{14,30},{16,32}... | collective-permute-start | bytes 2359304 | tf_op jit(solution)/shard_map/ppermute | solution.py:365
  36.7 18.3 %collective-permute-start.4 = (bf16[48,64,128]{2,1,0:T(8,128)(2,1)S(1)}, bf16[48,64,128]{2,1,0:T(8,128)(2,1)S(1)}, u32[]{:S(2)}, u32[]{:S(2)}) collective-permute-start(bf16[48,64,128]{2,1,0:T(8,128)(2,1)S(1)} %get-tuple-element.60), channel_id=1, source_target_pairs={{0,112},{2,114},{4,116},{6,118},{8,120},{10,122},{12,124},{14,126}... | collective-permute-start | bytes 2359304 | tf_op jit(solution)/shard_map/ppermute | solution.py:365
  38.6 26.1 %collective-permute-start.5 = (bf16[48,64,128]{2,1,0:T(8,128)(2,1)S(1)}, bf16[48,64,128]{2,1,0:T(8,128)(2,1)S(1)}, u32[]{:S(2)}, u32[]{:S(2)}) collective-permute-start(bf16[48,64,128]{2,1,0:T(8,128)(2,1)S(1)} %get-tuple-element.71), channel_id=1, source_target_pairs={{0,32},{2,34},{4,36},{6,38},{8,40},{10,42},{12,44},{14,46},{16,48}... | collective-permute-start | bytes 2359304 | tf_op jit(solution)/shard_map/ppermute | solution.py:365
  43.5 24.6 %collective-permute-start.6 = (bf16[48,64,128]{2,1,0:T(8,128)(2,1)S(1)}, bf16[48,64,128]{2,1,0:T(8,128)(2,1)S(1)}, u32[]{:S(2)}, u32[]{:S(2)}) collective-permute-start(bf16[48,64,128]{2,1,0:T(8,128)(2,1)S(1)} %get-tuple-element.72), channel_id=1, source_target_pairs={{0,96},{2,98},{4,100},{6,102},{8,104},{10,106},{12,108},{14,110},{... | collective-permute-start | bytes 2359304 | tf_op jit(solution)/shard_map/ppermute | solution.py:365
  45.4 27.7 %collective-permute-start.7 = (bf16[48,64,128]{2,1,0:T(8,128)(2,1)S(1)}, bf16[48,64,128]{2,1,0:T(8,128)(2,1)S(1)}, u32[]{:S(2)}, u32[]{:S(2)}) collective-permute-start(bf16[48,64,128]{2,1,0:T(8,128)(2,1)S(1)} %get-tuple-element.73), channel_id=1, source_target_pairs={{0,16},{2,18},{4,20},{6,22},{8,24},{10,26},{12,28},{14,30},{16,32}... | collective-permute-start | bytes 2359304 | tf_op jit(solution)/shard_map/ppermute | solution.py:365
  51.8 25.4 %collective-permute-start.8 = (bf16[48,64,128]{2,1,0:T(8,128)(2,1)S(1)}, bf16[48,64,128]{2,1,0:T(8,128)(2,1)S(1)}, u32[]{:S(2)}, u32[]{:S(2)}) collective-permute-start(bf16[48,64,128]{2,1,0:T(8,128)(2,1)S(1)} %get-tuple-element.74), channel_id=1, source_target_pairs={{0,112},{2,114},{4,116},{6,118},{8,120},{10,122},{12,124},{14,126}... | collective-permute-start | bytes 2359304 | tf_op jit(solution)/shard_map/ppermute | solution.py:365
  62.1 29.5 %collective-permute-start.14 = (f16[8,16,16,128]{3,2,1,0:T(8,128)(2,1)S(1)}, f16[8,16,16,128]{3,2,1,0:T(8,128)(2,1)S(1)}, u32[]{:S(2)}, u32[]{:S(2)}) collective-permute-start(f16[8,16,16,128]{3,2,1,0:T(8,128)(2,1)S(1)} %convert_element_type.61), channel_id=1, source_target_pairs={{0,384},{128,0},{256,128},{384,256},{1,385},{129,1},{257,129},{385... | collective-permute-start | bytes 1572872 | tf_op jit(solution)/shard_map/ppermute | solution.py:329
  64.7 32.6 %collective-permute-start.13 = (f16[8,16,16,128]{3,2,1,0:T(8,128)(2,1)S(1)}, f16[8,16,16,128]{3,2,1,0:T(8,128)(2,1)S(1)}, u32[]{:S(2)}, u32[]{:S(2)}) collective-permute-start(f16[8,16,16,128]{3,2,1,0:T(8,128)(2,1)S(1)} %convert_element_type.59), channel_id=1, source_target_pairs={{0,128},{128,256},{256,384},{384,0},{1,129},{129,257},{257,385},{3... | collective-permute-start | bytes 1572872 | tf_op jit(solution)/shard_map/ppermute | solution.py:329
  68.1 29.3 %collective-permute-start.12 = (f16[8,16,16,128]{3,2,1,0:T(8,128)(2,1)S(1)}, f16[8,16,16,128]{3,2,1,0:T(8,128)(2,1)S(1)}, u32[]{:S(2)}, u32[]{:S(2)}) collective-permute-start(f16[8,16,16,128]{3,2,1,0:T(8,128)(2,1)S(1)} %convert_element_type.57), channel_id=1, source_target_pairs={{0,256},{128,384},{256,0},{384,128},{1,257},{129,385},{257,1},{385... | collective-permute-start | bytes 1572872 | tf_op jit(solution)/shard_map/ppermute | solution.py:329
  85.4 17.3 %collective-permute-start.11 = (f16[8,16,16,128]{3,2,1,0:T(8,128)(2,1)S(1)}, f16[8,16,16,128]{3,2,1,0:T(8,128)(2,1)S(1)}, u32[]{:S(2)}, u32[]{:S(2)}) collective-permute-start(f16[8,16,16,128]{3,2,1,0:T(8,128)(2,1)S(1)} %convert_element_type.55), channel_id=1, source_target_pairs={{0,384},{128,0},{256,128},{384,256},{1,385},{129,1},{257,129},{385... | collective-permute-start | bytes 1572872 | tf_op jit(solution)/shard_map/ppermute | solution.py:329
  88.9 15.6 %collective-permute-start.10 = (f16[8,16,16,128]{3,2,1,0:T(8,128)(2,1)S(1)}, f16[8,16,16,128]{3,2,1,0:T(8,128)(2,1)S(1)}, u32[]{:S(2)}, u32[]{:S(2)}) collective-permute-start(f16[8,16,16,128]{3,2,1,0:T(8,128)(2,1)S(1)} %convert_element_type.53), channel_id=1, source_target_pairs={{0,128},{128,256},{256,384},{384,0},{1,129},{129,257},{257,385},{3... | collective-permute-start | bytes 1572872 | tf_op jit(solution)/shard_map/ppermute | solution.py:329
  91.6 16.4 %collective-permute-start.9 = (f16[8,16,16,128]{3,2,1,0:T(8,128)(2,1)S(1)}, f16[8,16,16,128]{3,2,1,0:T(8,128)(2,1)S(1)}, u32[]{:S(2)}, u32[]{:S(2)}) collective-permute-start(f16[8,16,16,128]{3,2,1,0:T(8,128)(2,1)S(1)} %convert_element_type.51), channel_id=1, source_target_pairs={{0,256},{128,384},{256,0},{384,128},{1,257},{129,385},{257,1},{385... | collective-permute-start | bytes 1572872 | tf_op jit(solution)/shard_map/ppermute | solution.py:329
  97.7 20.5 %collective-permute-start.15 = (f16[8,16,16,128]{3,2,1,0:T(8,128)(2,1)S(1)}, f16[8,16,16,128]{3,2,1,0:T(8,128)(2,1)S(1)}, u32[]{:S(2)}, u32[]{:S(2)}) collective-permute-start(f16[8,16,16,128]{3,2,1,0:T(8,128)(2,1)S(1)} %add_convert_fusion.1), channel_id=1, source_target_pairs={{0,64},{2,66},{4,68},{6,70},{8,72},{10,74},{12,76},{14,78},{16,80}... | collective-permute-start | bytes 1572872 | tf_op jit(solution)/shard_map/ppermute | solution.py:373
  118.2 4.7 %copy-start.6 = (s32[16,3]{0,1:T(4,128)S(1)}, s32[16,3]{0,1:T(4,128)}, u32[]{:S(2)}) copy-start(s32[16,3]{0,1:T(4,128)} %param.14) | copy-start | bytes 580
  118.2 4.7 %copy-start.7 = (f32[128]{0:T(128)S(1)}, f32[128]{0:T(128)}, u32[]{:S(2)}) copy-start(f32[128]{0:T(128)} %param.21) | copy-start | bytes 1540
  119.4 16.7 %all-to-all-start.1 = ((f16[8,16,16,128]{3,2,1,0:T(8,128)(2,1)}), f16[8,16,16,128]{3,2,1,0:T(8,128)(2,1)S(1)}, u32[]{:S(2)}, u32[]{:S(2)}) async-start(f16[8,16,16,128]{3,2,1,0:T(8,128)(2,1)} %add_convert_fusion), calls=%async_computation.1 | async-start | bytes 1048576 | tf_op jit(solution)/shard_map/all_to_all | solution.py:375
